TPU v7x, 32 devices: a whole 2x2x4 slice. The times are simulated.
32 devices in a mesh: dp: 2 (over core), head: 4 (over z), ffn: 4 (over y, x).
Axes of the slice: x: 2, y: 2, z: 4, core: 2. Of those that a mesh axis runs over, the one named last changes fastest.
Arguments:
- tokens: bfloat16 [12, 2048, 1024], P('dp', 'ffn', 'head'), may hold values from -6 to 6
- first_values: bfloat16 [12, 2048, 1024], P('dp', 'ffn', 'head'), may hold values from -6 to 6
- segment_ids: int32 [12, 2048], P('dp'), may hold values from 0 to 7, as said below
- cotangent: bfloat16 [12, 2048, 1024], P('dp', 'ffn', 'head'), may hold values from -6 to 6
- qkv_weight: bfloat16 [1024, 3, 1024], P(('dp', 'ffn'), None, 'head'), may hold values from -0.1875 to 0.1875
- out_weight: bfloat16 [1024, 1024], P('head', ('dp', 'ffn')), may hold values from -0.75 to 0.75
- gate_up_weight: bfloat16 [1024, 2, 2816], P(('dp', 'ffn'), None, 'head'), may hold values from -0.1875 to 0.1875
- down_weight: bfloat16 [2816, 1024], P('head', ('dp', 'ffn')), may hold values from -0.109375 to 0.109375
- attn_gain: float32 [1024], P('head'), may hold values from 0.1 to 1.9
- mlp_gain: float32 [1024], P('head'), may hold values from 0.1 to 1.9
Outputs:
- out_tokens: bfloat16 [12, 2048, 1024], P('dp', 'ffn', 'head')
- grad_tokens: bfloat16 [12, 2048, 1024], P('dp', 'ffn', 'head')
- grad_first_values: bfloat16 [12, 2048, 1024], P('dp', 'ffn', 'head')
- grad_qkv_weight: float32 [1024, 3, 1024], P(('dp', 'ffn'), None, 'head')
- grad_out_weight: float32 [1024, 1024], P('head', ('dp', 'ffn'))
- grad_gate_up_weight: float32 [1024, 2, 2816], P(('dp', 'ffn'), None, 'head')
- grad_down_weight: float32 [2816, 1024], P('head', ('dp', 'ffn'))
- grad_attn_gain: float32 [1024], P('head')
- grad_mlp_gain: float32 [1024], P('head')
Inputs may be any that keep to these rules, and one draw needn't show every extreme that they name: `segment_ids`: in each sequence the numbers start at 0 and never fall; of the 6 sequences of each index of dp, one drawn from the seed is a single document, and every other sequence reaches the largest number.
All inputs are finite; a program needn't handle non-finite values.
Results may differ from a plain program's by a relative error of at most 0.024.
Values may be sent and summed in bfloat16 or wider, within the bound.
No kernel may reach another device: no remote copies, remote signals or barrier semaphores. Data moves between devices by JAX's collectives and lax.ppermute only.
A program may use at most 320 MiB of HBM per device.

v0:
```python
import math

import jax
import jax.numpy as jnp
from jax import lax
from jax.sharding import PartitionSpec as P

HD = 64
MICRO = 4


EPSILON = 1e-06
MASKED = -1e30


def rope_tables(positions, head_size):
    half_size = head_size // 2
    exponent = jnp.arange(half_size, dtype=jnp.float32) * (2.0 / head_size)
    frequency = jnp.exp(exponent * -jnp.log(jnp.float32(10000.0)))
    angles = positions.astype(jnp.float32)[:, None] * frequency[None, :]
    angles = jnp.concatenate([angles, angles], axis=1)
    return (jnp.cos(angles), jnp.sin(angles))


def rotate(vectors, cos_table, sin_table):
    half_size = vectors.shape[-1] // 2
    turned = jnp.concatenate([-vectors[..., half_size:], vectors[..., :half_size]], axis=-1)
    return vectors * cos_table + turned * sin_table


def unrotate(gradient, cos_table, sin_table):
    half_size = gradient.shape[-1] // 2
    scaled = gradient * sin_table
    turned = jnp.concatenate([scaled[..., half_size:], -scaled[..., :half_size]], axis=-1)
    return gradient * cos_table + turned


def swiglu(gate_up):
    return jax.nn.silu(gate_up[:, 0]) * gate_up[:, 1]


def contract_rows(former, latter):
    return lax.dot_general(
        former, latter, (((0,), (0,)), ((), ())), preferred_element_type=jnp.float32
    )


def contract_last(former, latter):
    return lax.dot_general(
        former, latter, (((1,), (1,)), ((), ())), preferred_element_type=jnp.float32
    )


def gather_weights(qkv_weight, out_weight, gate_up_weight, down_weight):
    return (
        lax.all_gather(qkv_weight, ("dp", "ffn"), axis=0, tiled=True),
        lax.all_gather(out_weight, ("dp", "ffn"), axis=1, tiled=True),
        lax.all_gather(gate_up_weight, ("dp", "ffn"), axis=0, tiled=True),
        lax.all_gather(down_weight, ("dp", "ffn"), axis=1, tiled=True),
    )


def row_total(values):
    return lax.psum(values, "head")


def spread_rows(values):
    return lax.all_gather(values, "head", axis=1, tiled=True)


def spread_grads(values):
    return lax.all_gather(values, "head", axis=1, tiled=True)


def collect_rows(values):
    return lax.psum_scatter(
        values.astype(jnp.bfloat16), "head", scatter_dimension=1, tiled=True
    ).astype(jnp.float32)


def collect_grads(values):
    return lax.psum_scatter(
        values.astype(jnp.bfloat16), "head", scatter_dimension=1, tiled=True
    ).astype(jnp.float32)


def norm_forward(values, gain_vector, full_width):
    factor = lax.rsqrt(row_total(jnp.sum(values * values, axis=1)) / full_width + EPSILON)
    return (factor, values * factor[:, None] * gain_vector)


def norm_backward(values, factor, gain_vector, gradient, full_width):
    weighted = gradient * gain_vector
    row_inner = row_total(jnp.sum(weighted * values, axis=1))
    norm_grad = (
        factor[:, None] * weighted
        - values * (factor * factor * factor * row_inner / full_width)[:, None]
    )
    gain_grad = jnp.sum(gradient * values * factor[:, None], axis=0)
    return (norm_grad, gain_grad)


def masked_scores(queries, key_rows, query_places, key_places, query_ids, key_ids, score_scale):
    scores = (
        jnp.einsum("qhd,khd->hqk", queries, key_rows, preferred_element_type=jnp.float32)
        * score_scale
    )
    allowed = (key_places[None, :] <= query_places[:, None]) & (
        key_ids[None, :] == query_ids[:, None]
    )
    return jnp.where(allowed[None], scores, MASKED)


def attend_forward(
    queries, key_rows, value_rows, query_places, key_places, query_ids, key_ids, score_scale
):
    scores = masked_scores(
        queries, key_rows, query_places, key_places, query_ids, key_ids, score_scale
    )
    highest = jnp.max(scores, axis=2, keepdims=True)
    log_total = highest + jnp.log(jnp.sum(jnp.exp(scores - highest), axis=2, keepdims=True))
    weights = jnp.exp(scores - log_total).astype(jnp.bfloat16)
    attended = jnp.einsum("hqk,khd->qhd", weights, value_rows, preferred_element_type=jnp.float32)
    return (attended, log_total[:, :, 0])


def query_side(
    queries,
    key_rows,
    value_rows,
    grad_rows,
    log_total,
    query_places,
    key_places,
    query_ids,
    key_ids,
    score_scale,
):
    scores = masked_scores(
        queries, key_rows, query_places, key_places, query_ids, key_ids, score_scale
    )
    weights = jnp.exp(scores - log_total[:, :, None])
    weight_grad = jnp.einsum(
        "qhd,khd->hqk", grad_rows, value_rows, preferred_element_type=jnp.float32
    )
    row_inner = jnp.sum(weights * weight_grad, axis=2)
    score_grad = (weights * (weight_grad - row_inner[:, :, None])).astype(jnp.bfloat16)
    query_grad = (
        jnp.einsum("hqk,khd->qhd", score_grad, key_rows, preferred_element_type=jnp.float32)
        * score_scale
    )
    return (weights, score_grad, row_inner, query_grad)


def per_device(
    tokens,
    first_values,
    segment_ids,
    cotangent,
    qkv_weight,
    out_weight,
    gate_up_weight,
    down_weight,
    attn_gain,
    mlp_gain,
):
    seq_total = tokens.shape[0]
    local_len = tokens.shape[1]
    local_width = tokens.shape[2]
    full_width = local_width * lax.axis_size("head")
    seq_len = local_len * lax.axis_size("ffn")
    head_width = first_values.shape[2]
    head_local = head_width // HD
    hidden_local = down_weight.shape[0]
    score_scale = 1.0 / math.sqrt(HD)
    offset = lax.axis_index("ffn") * local_len
    own_places = offset + jnp.arange(local_len, dtype=jnp.int32)
    all_places = jnp.arange(seq_len, dtype=jnp.int32)
    cos_table, sin_table = rope_tables(own_places, HD)
    cos_table = cos_table[:, None, :]
    sin_table = sin_table[:, None, :]
    base_count = seq_total // MICRO
    remainder = seq_total % MICRO
    qkv_grads = jnp.zeros((full_width, 3, head_width), jnp.float32)
    out_grads = jnp.zeros((head_width, full_width), jnp.float32)
    gate_grads = jnp.zeros((full_width, 2, hidden_local), jnp.float32)
    down_grads = jnp.zeros((hidden_local, full_width), jnp.float32)
    attn_gain_grads = jnp.zeros((local_width,), jnp.float32)
    mlp_gain_grads = jnp.zeros((local_width,), jnp.float32)
    outputs = []
    token_grads = []
    value_grads = []
    seq_start = 0
    for micro_index in range(MICRO):
        seq_count = base_count + (1 if micro_index < remainder else 0)
        row_count = seq_count * local_len
        gathered = gather_weights(qkv_weight, out_weight, gate_up_weight, down_weight)
        qkv_matrix = gathered[0].reshape(full_width, 3 * head_width)
        out_matrix = gathered[1]
        gate_matrix = gathered[2].reshape(full_width, 2 * hidden_local)
        down_matrix = gathered[3]
        token_rows = (
            tokens[seq_start : seq_start + seq_count]
            .reshape(row_count, local_width)
            .astype(jnp.float32)
        )
        factor_one, normed_one = norm_forward(token_rows, attn_gain, full_width)
        normed_full = spread_rows(normed_one.astype(jnp.bfloat16))
        projected = jnp.dot(normed_full, qkv_matrix, preferred_element_type=jnp.float32)
        projected = projected.reshape(seq_count, local_len, 3, head_local, HD)
        queries = rotate(projected[:, :, 0], cos_table, sin_table).astype(jnp.bfloat16)
        key_local = rotate(projected[:, :, 1], cos_table, sin_table).astype(jnp.bfloat16)
        first_block = first_values[seq_start : seq_start + seq_count].reshape(
            seq_count, local_len, head_local, HD
        )
        value_local = (0.5 * projected[:, :, 2] + 0.5 * first_block.astype(jnp.float32)).astype(
            jnp.bfloat16
        )
        key_full, value_full = (
            lax.all_gather(
                key_local.reshape(seq_count, local_len, head_width), "ffn", axis=1, tiled=True
            ),
            lax.all_gather(
                value_local.reshape(seq_count, local_len, head_width), "ffn", axis=1, tiled=True
            ),
        )
        key_full = key_full.reshape(seq_count, seq_len, head_local, HD)
        value_full = value_full.reshape(seq_count, seq_len, head_local, HD)
        ids_full = segment_ids[seq_start : seq_start + seq_count]
        ids_own = lax.dynamic_slice_in_dim(ids_full, offset, local_len, axis=1)

        def forward_one(pieces):
            return attend_forward(
                pieces[0],
                pieces[1],
                pieces[2],
                own_places,
                all_places,
                pieces[3],
                pieces[4],
                score_scale,
            )

        attended, log_totals = lax.map(
            forward_one, (queries, key_full, value_full, ids_own, ids_full)
        )
        attended_low = attended.reshape(row_count, head_width).astype(jnp.bfloat16)
        branch = collect_rows(jnp.dot(attended_low, out_matrix, preferred_element_type=jnp.float32))
        hidden = token_rows + branch
        factor_two, normed_two = norm_forward(hidden, mlp_gain, full_width)
        normed_mlp = spread_rows(normed_two.astype(jnp.bfloat16))
        gate_up = jnp.dot(normed_mlp, gate_matrix, preferred_element_type=jnp.float32).reshape(
            row_count, 2, hidden_local
        )
        active, swiglu_back = jax.vjp(swiglu, gate_up)
        active_low = active.astype(jnp.bfloat16)
        mlp_branch = collect_rows(
            jnp.dot(active_low, down_matrix, preferred_element_type=jnp.float32)
        )
        outputs.append(
            (hidden + mlp_branch).astype(jnp.bfloat16).reshape(seq_count, local_len, local_width)
        )
        grad_out = cotangent[seq_start : seq_start + seq_count].reshape(row_count, local_width)
        grad_full = spread_grads(grad_out)
        active_grad = contract_last(grad_full, down_matrix)
        down_grads = down_grads + contract_rows(active_low, grad_full)
        gate_grad = (
            swiglu_back(active_grad)[0].astype(jnp.bfloat16).reshape(row_count, 2 * hidden_local)
        )
        gate_grads = gate_grads + contract_rows(normed_mlp, gate_grad).reshape(
            full_width, 2, hidden_local
        )
        normed_grad = collect_grads(contract_last(gate_grad, gate_matrix))
        back_two, gain_two = norm_backward(hidden, factor_two, mlp_gain, normed_grad, full_width)
        mlp_gain_grads = mlp_gain_grads + gain_two
        hidden_grad = grad_out.astype(jnp.float32) + back_two
        hidden_full = spread_grads(hidden_grad.astype(jnp.bfloat16))
        attended_grad = contract_last(hidden_full, out_matrix).astype(jnp.bfloat16)
        out_grads = out_grads + contract_rows(attended_low, hidden_full)
        grad_blocks = attended_grad.reshape(seq_count, local_len, head_local, HD)

        def backward_one(pieces):
            (
                queries_one,
                key_one,
                value_one,
                grad_one,
                total_one,
                own_ids,
                full_ids,
                own_key,
                own_value,
            ) = pieces
            weights, score_grad, row_inner, query_grad = query_side(
                queries_one,
                key_one,
                value_one,
                grad_one,
                total_one,
                own_places,
                all_places,
                own_ids,
                full_ids,
                score_scale,
            )
            key_grad = (
                jnp.einsum(
                    "hqk,qhd->khd", score_grad, queries_one, preferred_element_type=jnp.float32
                )
                * score_scale
            )
            value_grad = jnp.einsum(
                "hqk,qhd->khd",
                weights.astype(jnp.bfloat16),
                grad_one,
                preferred_element_type=jnp.float32,
            )
            key_value = jnp.stack([key_grad, value_grad], axis=1).reshape(seq_len, 2, head_width)
            return (
                query_grad,
                lax.psum_scatter(
                    key_value.astype(jnp.bfloat16), "ffn", scatter_dimension=0, tiled=True
                ).astype(jnp.float32),
            )

        query_grads, key_value_grads = lax.map(
            backward_one,
            (
                queries,
                key_full,
                value_full,
                grad_blocks,
                log_totals,
                ids_own,
                ids_full,
                key_local,
                value_local,
            ),
        )
        key_rot_grad = key_value_grads[:, :, 0].reshape(seq_count, local_len, head_local, HD)
        value_mix_grad = key_value_grads[:, :, 1].reshape(seq_count, local_len, head_local, HD)
        value_grads.append(
            (0.5 * value_mix_grad).astype(jnp.bfloat16).reshape(seq_count, local_len, head_width)
        )
        projected_grad = (
            jnp.stack(
                [
                    unrotate(query_grads, cos_table, sin_table),
                    unrotate(key_rot_grad, cos_table, sin_table),
                    0.5 * value_mix_grad,
                ],
                axis=2,
            )
            .astype(jnp.bfloat16)
            .reshape(row_count, 3 * head_width)
        )
        qkv_grads = qkv_grads + contract_rows(normed_full, projected_grad).reshape(
            full_width, 3, head_width
        )
        normed_grad_one = collect_grads(contract_last(projected_grad, qkv_matrix))
        back_one, gain_one = norm_backward(
            token_rows, factor_one, attn_gain, normed_grad_one, full_width
        )
        attn_gain_grads = attn_gain_grads + gain_one
        token_grads.append(
            (hidden_grad + back_one).astype(jnp.bfloat16).reshape(seq_count, local_len, local_width)
        )
        seq_start = seq_start + seq_count
    weight_sums = (
        lax.psum_scatter(
            qkv_grads.astype(jnp.bfloat16), ("dp", "ffn"), scatter_dimension=0, tiled=True
        ).astype(jnp.float32),
        lax.psum_scatter(
            out_grads.astype(jnp.bfloat16), ("dp", "ffn"), scatter_dimension=1, tiled=True
        ).astype(jnp.float32),
        lax.psum_scatter(
            gate_grads.astype(jnp.bfloat16), ("dp", "ffn"), scatter_dimension=0, tiled=True
        ).astype(jnp.float32),
        lax.psum_scatter(
            down_grads.astype(jnp.bfloat16), ("dp", "ffn"), scatter_dimension=1, tiled=True
        ).astype(jnp.float32),
    )
    gain_sums = lax.psum((attn_gain_grads, mlp_gain_grads), ("dp", "ffn"))
    return (
        jnp.concatenate(outputs, axis=0),
        jnp.concatenate(token_grads, axis=0),
        jnp.concatenate(value_grads, axis=0),
        weight_sums[0],
        weight_sums[1],
        weight_sums[2],
        weight_sums[3],
        gain_sums[0],
        gain_sums[1],
    )


def solution(mesh):
    in_specs = (
        P("dp", "ffn", "head"),
        P("dp", "ffn", "head"),
        P("dp", None),
        P("dp", "ffn", "head"),
        P(("dp", "ffn"), None, "head"),
        P("head", ("dp", "ffn")),
        P(("dp", "ffn"), None, "head"),
        P("head", ("dp", "ffn")),
        P("head"),
        P("head"),
    )
    out_specs = (
        P("dp", "ffn", "head"),
        P("dp", "ffn", "head"),
        P("dp", "ffn", "head"),
        P(("dp", "ffn"), None, "head"),
        P("head", ("dp", "ffn")),
        P(("dp", "ffn"), None, "head"),
        P("head", ("dp", "ffn")),
        P("head"),
        P("head"),
    )
    return jax.shard_map(
        per_device, mesh=mesh, in_specs=in_specs, out_specs=out_specs, check_vma=False
    )
```

profile of v0, /device:TPU:0, one launch (start us, length us, event | category | flops | bytes accessed | tf_op | source)
XLA Modules:
  0.0 2182.2 jit_solution(15343066074441733611)
XLA Ops:
  10.2 20.4 all-reduce.12
  38.2 24.4 %all-gather.52.cloned.1.call-done = bf16[512,1024]{1,0:T(8,128)(2,1)} async-done(((bf16[512,256]{1,0:T(8,128)(2,1)}), bf16[512,1024]{1,0:T(8,128)(2,1)}) %all-gather.52.cloned.1.call-update) | async-done | bytes 1048592 | tf_op jit(solution)/shard_map/all_gather | solution.py:68
  62.6 25.6 %all-gather.32.cloned.1.call-done = bf16[1024,3,256]{0,2,1:T(8,128)(2,1)} async-done(((bf16[128,3,256]{0,2,1:T(8,128)(2,1)}), bf16[1024,3,256]{0,2,1:T(8,128)(2,1)}) %all-gather.32.cloned.1.call-update) | async-done | bytes 1572880 | tf_op jit(solution)/shard_map/all_gather | solution.py:56
  94.0 26.6 %all-gather.60.cloned.1.call-done = bf16[512,1024]{1,0:T(8,128)(2,1)} async-done(((bf16[512,256]{1,0:T(8,128)(2,1)}), bf16[512,1024]{1,0:T(8,128)(2,1)}) %all-gather.60.cloned.1.call-update) | async-done | bytes 1048592 | tf_op jit(solution)/shard_map/all_gather | solution.py:68
  130.0 37.2 %all-gather.44.cloned.1.call-done = bf16[1024,1024]{1,0:T(8,128)(2,1)} async-done(((bf16[1024,256]{1,0:T(8,128)(2,1)}), bf16[1024,1024]{1,0:T(8,128)(2,1)}) %all-gather.44.cloned.1.call-update) | async-done | bytes 2097168 | tf_op jit(solution)/shard_map/all_gather | solution.py:68
  173.9 39.2 %all-gather.30.cloned.1.call-done = bf16[1024,1024]{1,0:T(8,128)(2,1)} async-done(((bf16[1024,256]{1,0:T(8,128)(2,1)}), bf16[1024,1024]{1,0:T(8,128)(2,1)}) %all-gather.30.cloned.1.call-update) | async-done | bytes 2097168 | tf_op jit(solution)/shard_map/all_gather | solution.py:68
  231.3 26.0 %all_gather.100 = bf16[256,1024]{1,0:T(8,128)(2,1)} all-gather(bf16[256,128]{1,0:T(8,128)(2,1)S(1)} %copy-done.143), channel_id=1, replica_groups=mesh['dp'=2,'head'=4,'ffn'=4] {'dp','ffn'}, dimensions={1}, use_global_device_ids=true | all-gather | bytes 589824 | tf_op jit(solution)/shard_map/all_gather | solution.py:57
  269.3 10.1 fusion.118
  281.7 8.9 exponential_reduce_fusion.3
  315.0 14.4 all-gather.62.cloned.1.call-done
  342.1 24.3 %all-gather.46.cloned.1.call-done = bf16[2,2048,256]{2,1,0:T(8,128)(2,1)} async-done(((bf16[2,512,256]{2,1,0:T(8,128)(2,1)}), bf16[2,2048,256]{2,1,0:T(8,128)(2,1)}) %all-gather.46.cloned.1.call-update) | async-done | bytes 2097168 | tf_op jit(solution)/shard_map/all_gather | solution.py:223
  369.4 34.1 %all-gather.48.cloned.1.call-done = bf16[2,2048,256]{1,2,0:T(8,128)(2,1)} async-done(((bf16[2,512,256]{1,2,0:T(8,128)(2,1)}), bf16[2,2048,256]{1,2,0:T(8,128)(2,1)}) %all-gather.48.cloned.1.call-update) | async-done | bytes 2097168 | tf_op jit(solution)/shard_map/all_gather | solution.py:220
  403.5 30.6 %while.13 = (s32[]{:T(128)}, bf16[2,512,4,64]{1,3,2,0:T(8,128)(2,1)}, f32[2,4,512]{2,1,0:T(4,128)S(1)}, bf16[2,2048,4,64]{1,3,2,0:T(8,128)(2,1)S(1)}, s32[2,2048...) while((s32[]{:T(128)}, ...), condition=%wide.region_15.16_spmd.clone, body=%wide.region_12.15_spmd.clone.sunk | while | flops 1123023360 | bytes 61706420 | solution.py:244
  443.5 34.1 %all-gather.36.cloned.1.call-done = bf16[2,2048,256]{1,2,0:T(8,128)(2,1)} async-done(((bf16[2,512,256]{1,2,0:T(8,128)(2,1)}), bf16[2,2048,256]{1,2,0:T(8,128)(2,1)}) %all-gather.36.cloned.1.call-update) | async-done | bytes 2097168 | tf_op jit(solution)/shard_map/all_gather | solution.py:220
  477.6 30.6 %while.12 = (s32[]{:T(128)}, bf16[2,512,4,64]{1,3,2,0:T(8,128)(2,1)}, f32[2,4,512]{2,1,0:T(4,128)S(1)}, bf16[2,2048,4,64]{1,3,2,0:T(8,128)(2,1)S(1)}, s32[2,2048...) while((s32[]{:T(128)}, ...), condition=%wide.region_5.6_spmd.clone, body=%wide.region_2.5_spmd.clone.sunk | while | flops 1123023360 | bytes 61706420 | solution.py:244
  513.8 22.4 %reduce-scatter.43.cloned.1.call-done = bf16[512,256]{1,0:T(8,128)(2,1)} async-done(((bf16[512,1024]{1,0:T(8,128)(2,1)}), bf16[512,256]{1,0:T(8,128)(2,1)}) %reduce-scatter.43.cloned.1.call-update) | async-done | bytes 262160 | tf_op jit(solution)/shard_map/reduce_scatter | solution.py:76
  537.5 43.4 %reduce-scatter.35.cloned.1.call-done = bf16[1024,256]{1,0:T(8,128)(2,1)} async-done(((bf16[1024,1024]{1,0:T(8,128)(2,1)}), bf16[1024,256]{1,0:T(8,128)(2,1)}) %reduce-scatter.35.cloned.1.call-update) | async-done | bytes 524304 | tf_op jit(solution)/shard_map/reduce_scatter | solution.py:76
  580.9 45.5 %reduce-scatter.31.cloned.1.call-done = bf16[1024,256]{1,0:T(8,128)(2,1)} async-done(((bf16[1024,1024]{1,0:T(8,128)(2,1)}), bf16[1024,256]{1,0:T(8,128)(2,1)}) %reduce-scatter.31.cloned.1.call-update) | async-done | bytes 524304 | tf_op jit(solution)/shard_map/reduce_scatter | solution.py:76
  628.0 16.8 all-reduce.11
  659.1 32.4 %all-gather.66.cloned.1.call-done = bf16[512,1024]{1,0:T(8,128)(2,1)} async-done(((bf16[512,256]{1,0:T(8,128)(2,1)}), bf16[512,1024]{1,0:T(8,128)(2,1)}) %all-gather.66.cloned.1.call-update) | async-done | bytes 1048592 | tf_op jit(solution)/shard_map/all_gather | solution.py:68
  696.9 25.1 %all-gather.82.cloned.1.call-done = bf16[1,512,1024]{2,1,0:T(8,128)(2,1)} async-done(((bf16[1,512,256]{2,1,0:T(8,128)(2,1)}), bf16[1,512,1024]{2,1,0:T(8,128)(2,1)}) %all-gather.82.cloned.1.call-update) | async-done | bytes 1048592 | tf_op jit(solution)/shard_map/all_gather | solution.py:72
  722.0 25.5 %all-gather.42.cloned.1.call-done = bf16[704,1024]{1,0:T(8,128)(2,1)} async-done(((bf16[704,128]{1,0:T(8,128)(2,1)}), bf16[704,1024]{1,0:T(8,128)(2,1)}) %all-gather.42.cloned.1.call-update) | async-done | bytes 1441808 | tf_op jit(solution)/shard_map/all_gather | solution.py:59
  757.1 22.8 %all-gather.58.cloned.1.call-done = bf16[512,1024]{1,0:T(8,128)(2,1)} async-done(((bf16[512,256]{1,0:T(8,128)(2,1)}), bf16[512,1024]{1,0:T(8,128)(2,1)}) %all-gather.58.cloned.1.call-update) | async-done | bytes 1048592 | tf_op jit(solution)/shard_map/all_gather | solution.py:68
  785.3 25.3 %all-gather.80.cloned.1.call-done = bf16[1,512,1024]{2,1,0:T(8,128)(2,1)} async-done(((bf16[1,512,256]{2,1,0:T(8,128)(2,1)}), bf16[1,512,1024]{2,1,0:T(8,128)(2,1)}) %all-gather.80.cloned.1.call-update) | async-done | bytes 1048592 | tf_op jit(solution)/shard_map/all_gather | solution.py:72
  820.5 36.1 %all-gather.50.cloned.1.call-done = bf16[1024,1024]{1,0:T(8,128)(2,1)} async-done(((bf16[1024,256]{1,0:T(8,128)(2,1)}), bf16[1024,1024]{1,0:T(8,128)(2,1)}) %all-gather.50.cloned.1.call-update) | async-done | bytes 2097168 | tf_op jit(solution)/shard_map/all_gather | solution.py:68
  864.6 38.0 %all-gather.72.cloned.1.call-done = bf16[1024,1024]{1,0:T(8,128)(2,1)} async-done(((bf16[1024,256]{1,0:T(8,128)(2,1)}), bf16[1024,1024]{1,0:T(8,128)(2,1)}) %all-gather.72.cloned.1.call-update) | async-done | bytes 2097168 | tf_op jit(solution)/shard_map/all_gather | solution.py:72
  917.7 30.8 %all-gather.38.cloned.1.call-done = bf16[1024,1024]{1,0:T(8,128)(2,1)} async-done(((bf16[1024,256]{1,0:T(8,128)(2,1)}), bf16[1024,1024]{1,0:T(8,128)(2,1)}) %all-gather.38.cloned.1.call-update) | async-done | bytes 2097168 | tf_op jit(solution)/shard_map/all_gather | solution.py:68
  956.6 37.8 %all-gather.68.cloned.1.call-done = bf16[1024,1024]{1,0:T(8,128)(2,1)} async-done(((bf16[1024,256]{1,0:T(8,128)(2,1)}), bf16[1024,1024]{1,0:T(8,128)(2,1)}) %all-gather.68.cloned.1.call-update) | async-done | bytes 2097168 | tf_op jit(solution)/shard_map/all_gather | solution.py:72
  1013.0 9.2 reduce-scatter.61.cloned.1.call-done
  1022.2 28.2 %reduce-scatter.55.cloned.1.call-done = bf16[512,256]{1,0:T(8,128)(2,1)} async-done(((bf16[512,1024]{1,0:T(8,128)(2,1)}), bf16[512,256]{1,0:T(8,128)(2,1)}) %reduce-scatter.55.cloned.1.call-update) | async-done | bytes 262160 | tf_op jit(solution)/shard_map/reduce_scatter | solution.py:82
  1052.5 42.5 %reduce-scatter.51.cloned.1.call-done = bf16[1024,256]{1,0:T(8,128)(2,1)} async-done(((bf16[1024,1024]{1,0:T(8,128)(2,1)}), bf16[1024,256]{1,0:T(8,128)(2,1)}) %reduce-scatter.51.cloned.1.call-update) | async-done | bytes 524304 | tf_op jit(solution)/shard_map/reduce_scatter | solution.py:82
  1095.1 45.6 %reduce-scatter.47.cloned.1.call-done = bf16[1024,256]{1,0:T(8,128)(2,1)} async-done(((bf16[1024,1024]{1,0:T(8,128)(2,1)}), bf16[1024,256]{1,0:T(8,128)(2,1)}) %reduce-scatter.47.cloned.1.call-update) | async-done | bytes 524304 | tf_op jit(solution)/shard_map/reduce_scatter | solution.py:82
  1143.5 17.4 all-reduce.10
  1172.4 43.7 %all-gather.74.cloned.1.call-done = bf16[1024,1024]{1,0:T(8,128)(2,1)} async-done(((bf16[1024,256]{1,0:T(8,128)(2,1)}), bf16[1024,1024]{1,0:T(8,128)(2,1)}) %all-gather.74.cloned.1.call-update) | async-done | bytes 2097168 | tf_op jit(solution)/shard_map/all_gather | solution.py:72
  1220.3 42.0 %all-gather.70.cloned.1.call-done = bf16[1024,1024]{1,0:T(8,128)(2,1)} async-done(((bf16[1024,256]{1,0:T(8,128)(2,1)}), bf16[1024,1024]{1,0:T(8,128)(2,1)}) %all-gather.70.cloned.1.call-update) | async-done | bytes 2097168 | tf_op jit(solution)/shard_map/all_gather | solution.py:72
  1271.7 155.1 %while.15 = (s32[]{:T(128)}, f32[2,512,4,64]{1,3,2,0:T(8,128)}, f32[2,512,2,256]{1,3,2,0:T(8,128)}, bf16[2,2048,4,64]{1,3,2,0:T(8,128)(2,1)S(1)}, s32[2,2048]{1,...) while((s32[]{:T(128)}, f32[2,512,4,64]{1,3,2,0:T(8,128)}, ...), condition=%wide.region_52.53_spmd.clone, body=%wide.region_49.52_spmd.clone.sunk | while | flops 2753427968 | bytes 253326592 | solution.py:326
  1283.1 12.9 multiply_reduce_fusion.11
  1296.0 12.1 multiply_convert_fusion.19
  1319.8 26.7 %reduce-scatter.77.cloned.1.call-done = bf16[512,2,256]{0,2,1:T(8,128)(2,1)} async-done(((bf16[2048,2,256]{0,2,1:T(8,128)(2,1)}), bf16[512,2,256]{0,2,1:T(8,128)(2,1)}) %reduce-scatter.77.cloned.1.call-update) | async-done | bytes 524304 | tf_op jit(solution)/shard_map/while/body/eval_jaxpr/reduce_scatter | solution.py:321
  1359.6 12.9 multiply_reduce_fusion.11
  1372.4 12.1 multiply_convert_fusion.19
  1396.2 28.5 %reduce-scatter.77.cloned.1.call-done = bf16[512,2,256]{0,2,1:T(8,128)(2,1)} async-done(((bf16[2048,2,256]{0,2,1:T(8,128)(2,1)}), bf16[512,2,256]{0,2,1:T(8,128)(2,1)}) %reduce-scatter.77.cloned.1.call-update) | async-done | bytes 524304 | tf_op jit(solution)/shard_map/while/body/eval_jaxpr/reduce_scatter | solution.py:321
  1429.6 157.4 %while.14 = (s32[]{:T(128)}, f32[2,512,4,64]{1,3,2,0:T(8,128)}, f32[2,512,2,256]{1,3,2,0:T(8,128)}, bf16[2,2048,4,64]{1,3,2,0:T(8,128)(2,1)S(1)}, s32[2,2048]{1,...) while((s32[]{:T(128)}, f32[2,512,4,64]{1,3,2,0:T(8,128)}, ...), condition=%wide.region_42.43_spmd.clone, body=%wide.region_39.42_spmd.clone.sunk | while | flops 2753427968 | bytes 253326592 | solution.py:326
  1440.8 12.9 multiply_reduce_fusion.10
  1453.6 12.1 multiply_convert_fusion.18
  1477.5 28.5 %reduce-scatter.75.cloned.1.call-done = bf16[512,2,256]{0,2,1:T(8,128)(2,1)} async-done(((bf16[2048,2,256]{0,2,1:T(8,128)(2,1)}), bf16[512,2,256]{0,2,1:T(8,128)(2,1)}) %reduce-scatter.75.cloned.1.call-update) | async-done | bytes 524304 | tf_op jit(solution)/shard_map/while/body/eval_jaxpr/reduce_scatter | solution.py:321
  1519.1 12.9 multiply_reduce_fusion.10
  1532.0 12.1 multiply_convert_fusion.18
  1555.9 28.5 %reduce-scatter.75.cloned.1.call-done = bf16[512,2,256]{0,2,1:T(8,128)(2,1)} async-done(((bf16[2048,2,256]{0,2,1:T(8,128)(2,1)}), bf16[512,2,256]{0,2,1:T(8,128)(2,1)}) %reduce-scatter.75.cloned.1.call-update) | async-done | bytes 524304 | tf_op jit(solution)/shard_map/while/body/eval_jaxpr/reduce_scatter | solution.py:321
  1588.3 31.6 %all-gather.78.cloned.1.call-done = bf16[512,1024]{1,0:T(8,128)(2,1)} async-done(((bf16[512,256]{1,0:T(8,128)(2,1)}), bf16[512,1024]{1,0:T(8,128)(2,1)}) %all-gather.78.cloned.1.call-update) | async-done | bytes 1048592 | tf_op jit(solution)/shard_map/all_gather | solution.py:72
  1622.5 15.6 multiply_reduce_fusion.2
  1639.6 10.9 multiply_convert_fusion.2
  1677.1 10.9 multiply_reduce_fusion.3
  1818.8 9.4 reduce-scatter.71.cloned.1.call-done
  1841.0 24.2 %reduce-scatter.69.cloned.1.call-done = bf16[128,256]{1,0:T(8,128)(2,1)} async-done(((bf16[1024,256]{1,0:T(8,128)(2,1)}), bf16[128,256]{1,0:T(8,128)(2,1)}) %reduce-scatter.69.cloned.1.call-update) | async-done | bytes 65552
  1876.2 35.2 %reduce-scatter.49.cloned.1.call-done = bf16[1024,256]{1,0:T(8,128)(2,1)} async-done(((bf16[1024,1024]{1,0:T(8,128)(2,1)}), bf16[1024,256]{1,0:T(8,128)(2,1)}) %reduce-scatter.49.cloned.1.call-update) | async-done | bytes 524304 | tf_op jit(solution)/shard_map/reduce_scatter | solution.py:82
  1911.4 45.4 %reduce-scatter.53.cloned.1.call-done = bf16[1024,256]{1,0:T(8,128)(2,1)} async-done(((bf16[1024,1024]{1,0:T(8,128)(2,1)}), bf16[1024,256]{1,0:T(8,128)(2,1)}) %reduce-scatter.53.cloned.1.call-update) | async-done | bytes 524304 | tf_op jit(solution)/shard_map/reduce_scatter | solution.py:82
  1958.9 26.6 %reduce-scatter.65.cloned.1.call-done = bf16[512,256]{1,0:T(8,128)(2,1)} async-done(((bf16[512,1024]{1,0:T(8,128)(2,1)}), bf16[512,256]{1,0:T(8,128)(2,1)}) %reduce-scatter.65.cloned.1.call-update) | async-done | bytes 262160 | tf_op jit(solution)/shard_map/reduce_scatter | solution.py:82
  1985.5 28.0 %reduce-scatter.59.cloned.1.call-done = bf16[512,256]{1,0:T(8,128)(2,1)} async-done(((bf16[512,1024]{1,0:T(8,128)(2,1)}), bf16[512,256]{1,0:T(8,128)(2,1)}) %reduce-scatter.59.cloned.1.call-update) | async-done | bytes 262160 | tf_op jit(solution)/shard_map/reduce_scatter | solution.py:82
  2015.0 15.2 all-reduce.8
  2030.2 16.4 all-reduce.9
  2051.5 35.2 %reduce-scatter.33.cloned.1.call-done = bf16[1024,256]{1,0:T(8,128)(2,1)} async-done(((bf16[1024,1024]{1,0:T(8,128)(2,1)}), bf16[1024,256]{1,0:T(8,128)(2,1)}) %reduce-scatter.33.cloned.1.call-update) | async-done | bytes 524304 | tf_op jit(solution)/shard_map/reduce_scatter | solution.py:76
  2089.5 42.7 %reduce-scatter.37.cloned.1.call-done = bf16[1024,256]{1,0:T(8,128)(2,1)} async-done(((bf16[1024,1024]{1,0:T(8,128)(2,1)}), bf16[1024,256]{1,0:T(8,128)(2,1)}) %reduce-scatter.37.cloned.1.call-update) | async-done | bytes 524304 | tf_op jit(solution)/shard_map/reduce_scatter | solution.py:76
  2137.3 36.0 %reduce-scatter.67.cloned.1.call-done = bf16[128,3,256]{2,0,1:T(8,128)(2,1)} async-done(((bf16[1024,3,256]{2,0,1:T(8,128)(2,1)}), bf16[128,3,256]{2,0,1:T(8,128)(2,1)}) %reduce-scatter.67.cloned.1.call-update) | async-done | bytes 196624 | tf_op jit(solution)/shard_map/reduce_scatter | solution.py:370
  (849 shorter events, 611.7 us)
Async XLA Ops:
  7.2 55.4 %all-gather.52.cloned.1.call-start = ((), (), s32[]{:S(2)}) async-start(), calls=%async_computation.39 | async-start | bytes 1310720 | tf_op jit(solution)/shard_map/all_gather | solution.py:68
  33.4 54.8 %all-gather.32.cloned.1.call-start = ((), (), s32[]{:S(2)}) async-start(), calls=%async_computation.25 | async-start | bytes 1769472 | tf_op jit(solution)/shard_map/all_gather | solution.py:56
  34.3 86.3 %all-gather.60.cloned.1.call-start = ((), (), s32[]{:S(2)}) async-start(), calls=%async_computation.45 | async-start | bytes 1310720 | tf_op jit(solution)/shard_map/all_gather | solution.py:68
  35.0 132.1 %all-gather.44.cloned.1.call-start = ((), (), s32[]{:S(2)}) async-start(), calls=%async_computation.33 | async-start | bytes 2621440 | tf_op jit(solution)/shard_map/all_gather | solution.py:68
  36.5 176.6 %all-gather.30.cloned.1.call-start = ((), (), s32[]{:S(2)}) async-start(), calls=%async_computation.24 | async-start | bytes 2621440 | tf_op jit(solution)/shard_map/all_gather | solution.py:68
  37.1 232.2 %all-gather.56.cloned.1.call-start = ((), (), s32[]{:S(2)}) async-start(), calls=%async_computation.41 | async-start | bytes 1310720 | tf_op jit(solution)/shard_map/all_gather | solution.py:220
  38.2 228.3 %copy-start.32 = (f32[512,64]{0,1:T(8,128)}, f32[512,64]{0,1:T(8,128)S(1)}, u32[]{:S(2)}) copy-start(f32[512,64]{0,1:T(8,128)S(1)} %get-tuple-element.815) | copy-start | bytes 393220
  38.2 228.3 %copy-start.44 = (f32[512,64]{0,1:T(8,128)}, f32[512,64]{0,1:T(8,128)S(1)}, u32[]{:S(2)}) copy-start(f32[512,64]{0,1:T(8,128)S(1)} %get-tuple-element.814) | copy-start | bytes 393220
  126.0 153.5 %all-gather.54.cloned.1.call-start = ((), (), s32[]{:S(2)}) async-start(), calls=%async_computation.40 | async-start | bytes 1310720 | tf_op jit(solution)/shard_map/all_gather | solution.py:223
  128.5 171.8 %all-gather.64.cloned.1.call-start = ((), (), s32[]{:S(2)}) async-start(), calls=%async_computation.47 | async-start | bytes 1310720 | tf_op jit(solution)/shard_map/all_gather | solution.py:220
  129.2 200.2 %all-gather.62.cloned.1.call-start = ((), (), s32[]{:S(2)}) async-start(), calls=%async_computation.46 | async-start | bytes 1310720 | tf_op jit(solution)/shard_map/all_gather | solution.py:223
  130.0 236.5 %all-gather.46.cloned.1.call-start = ((), (), s32[]{:S(2)}) async-start(), calls=%async_computation.34 | async-start | bytes 2621440 | tf_op jit(solution)/shard_map/all_gather | solution.py:223
  225.3 178.2 %all-gather.48.cloned.1.call-start = ((), (), s32[]{:S(2)}) async-start(), calls=%async_computation.35 | async-start | bytes 2621440 | tf_op jit(solution)/shard_map/all_gather | solution.py:220
  228.8 211.7 %all-gather.34.cloned.1.call-start = ((), (), s32[]{:S(2)}) async-start(), calls=%async_computation.26 | async-start | bytes 2621440 | tf_op jit(solution)/shard_map/all_gather | solution.py:223
  230.6 247.0 %all-gather.36.cloned.1.call-start = ((), (), s32[]{:S(2)}) async-start(), calls=%async_computation.27 | async-start | bytes 2621440 | tf_op jit(solution)/shard_map/all_gather | solution.py:220
  266.4 247.4 %reduce-scatter.39.cloned.1.call-start = ((), (), s32[]{:S(2)}) async-start(), calls=%async_computation.42 | async-start | bytes 1310720 | tf_op jit(solution)/shard_map/reduce_scatter | solution.py:76
  299.0 237.2 %reduce-scatter.43.cloned.1.call-start = ((), (), s32[]{:S(2)}) async-start(), calls=%async_computation.48 | async-start | bytes 1310720 | tf_op jit(solution)/shard_map/reduce_scatter | solution.py:76
  341.6 239.3 %reduce-scatter.35.cloned.1.call-start = ((), (), s32[]{:S(2)}) async-start(), calls=%async_computation.36 | async-start | bytes 2621440 | tf_op jit(solution)/shard_map/reduce_scatter | solution.py:76
  440.1 186.3 %reduce-scatter.31.cloned.1.call-start = ((), (), s32[]{:S(2)}) async-start(), calls=%async_computation.28 | async-start | bytes 2621440 | tf_op jit(solution)/shard_map/reduce_scatter | solution.py:76
  513.2 145.9 %all-gather.40.cloned.1.call-start = ((), (), s32[]{:S(2)}) async-start(), calls=%async_computation.30 | async-start | bytes 3244032 | tf_op jit(solution)/shard_map/all_gather | solution.py:58
  513.7 177.7 %all-gather.66.cloned.1.call-start = ((), (), s32[]{:S(2)}) async-start(), calls=%async_computation.49 | async-start | bytes 1310720 | tf_op jit(solution)/shard_map/all_gather | solution.py:68
  644.9 524.9 %copy-start.152 = (f32[512]{0:T(512)}, f32[512]{0:T(512)S(1)}, u32[]{:S(2)}) copy-start(f32[512]{0:T(512)S(1)} %add_rsqrt_fusion.4) | copy-start | bytes 6148
  644.9 524.9 %copy-start.150 = (f32[512]{0:T(512)}, f32[512]{0:T(512)S(1)}, u32[]{:S(2)}) copy-start(f32[512]{0:T(512)S(1)} %add_rsqrt_fusion.6) | copy-start | bytes 6148
  646.9 75.1 %all-gather.82.cloned.1.call-start = ((), (), s32[]{:S(2)}) async-start(), calls=%async_computation.69 | async-start | bytes 1310720 | tf_op jit(solution)/shard_map/all_gather | solution.py:72
  648.8 98.7 %all-gather.42.cloned.1.call-start = ((), (), s32[]{:S(2)}) async-start(), calls=%async_computation.31 | async-start | bytes 1622016 | tf_op jit(solution)/shard_map/all_gather | solution.py:59
  649.6 130.3 %all-gather.58.cloned.1.call-start = ((), (), s32[]{:S(2)}) async-start(), calls=%async_computation.43 | async-start | bytes 1310720 | tf_op jit(solution)/shard_map/all_gather | solution.py:68
  650.3 160.2 %all-gather.80.cloned.1.call-start = ((), (), s32[]{:S(2)}) async-start(), calls=%async_computation.68 | async-start | bytes 1310720 | tf_op jit(solution)/shard_map/all_gather | solution.py:72
  651.1 205.5 %all-gather.50.cloned.1.call-start = ((), (), s32[]{:S(2)}) async-start(), calls=%async_computation.37 | async-start | bytes 2621440 | tf_op jit(solution)/shard_map/all_gather | solution.py:68
  651.1 509.8 %copy-start.133 = (f32[1024]{0:T(1024)}, f32[1024]{0:T(1024)S(1)}, u32[]{:S(2)}) copy-start(f32[1024]{0:T(1024)S(1)} %add_rsqrt_fusion) | copy-start | bytes 12292
  651.2 509.7 %copy-start.135 = (f32[1024]{0:T(1024)}, f32[1024]{0:T(1024)S(1)}, u32[]{:S(2)}) copy-start(f32[1024]{0:T(1024)S(1)} %add_rsqrt_fusion.2) | copy-start | bytes 12292
  652.6 250.0 %all-gather.72.cloned.1.call-start = ((), (), s32[]{:S(2)}) async-start(), calls=%async_computation.55 | async-start | bytes 2621440 | tf_op jit(solution)/shard_map/all_gather | solution.py:72
  654.9 293.6 %all-gather.38.cloned.1.call-start = ((), (), s32[]{:S(2)}) async-start(), calls=%async_computation.29 | async-start | bytes 2621440 | tf_op jit(solution)/shard_map/all_gather | solution.py:68
  655.5 339.0 %all-gather.68.cloned.1.call-start = ((), (), s32[]{:S(2)}) async-start(), calls=%async_computation.51 | async-start | bytes 2621440 | tf_op jit(solution)/shard_map/all_gather | solution.py:72
  656.1 366.1 %reduce-scatter.61.cloned.1.call-start = ((), (), s32[]{:S(2)}) async-start(), calls=%async_computation.63 | async-start | bytes 1310720 | tf_op jit(solution)/shard_map/reduce_scatter | solution.py:82
  757.0 293.4 %reduce-scatter.55.cloned.1.call-start = ((), (), s32[]{:S(2)}) async-start(), calls=%async_computation.59 | async-start | bytes 1310720 | tf_op jit(solution)/shard_map/reduce_scatter | solution.py:82
  820.0 275.1 %reduce-scatter.51.cloned.1.call-start = ((), (), s32[]{:S(2)}) async-start(), calls=%async_computation.56 | async-start | bytes 2621440 | tf_op jit(solution)/shard_map/reduce_scatter | solution.py:82
  917.5 223.2 %reduce-scatter.47.cloned.1.call-start = ((), (), s32[]{:S(2)}) async-start(), calls=%async_computation.52 | async-start | bytes 2621440 | tf_op jit(solution)/shard_map/reduce_scatter | solution.py:82
  1009.3 160.5 %reduce-scatter.45.cloned.1.call-start = ((), (), s32[]{:S(2)}) async-start(), calls=%async_computation.50 | async-start | bytes 1310720 | tf_op jit(solution)/shard_map/reduce_scatter | solution.py:76
  1012.9 203.2 %all-gather.74.cloned.1.call-start = ((), (), s32[]{:S(2)}) async-start(), calls=%async_computation.57 | async-start | bytes 2621440 | tf_op jit(solution)/shard_map/all_gather | solution.py:72
  1163.9 98.4 %all-gather.70.cloned.1.call-start = ((), (), s32[]{:S(2)}) async-start(), calls=%async_computation.53 | async-start | bytes 2621440 | tf_op jit(solution)/shard_map/all_gather | solution.py:72
  1272.1 74.3 %reduce-scatter.77.cloned.1.call-start = ((), (), s32[]{:S(2)}) async-start(), calls=%async_computation.74 | async-start | bytes 2621440 | tf_op jit(solution)/shard_map/while/body/eval_jaxpr/reduce_scatter | solution.py:321
  1348.6 76.0 %reduce-scatter.77.cloned.1.call-start = ((), (), s32[]{:S(2)}) async-start(), calls=%async_computation.74 | async-start | bytes 2621440 | tf_op jit(solution)/shard_map/while/body/eval_jaxpr/reduce_scatter | solution.py:321
  1429.7 76.3 %reduce-scatter.75.cloned.1.call-start = ((), (), s32[]{:S(2)}) async-start(), calls=%async_computation.73 | async-start | bytes 2621440 | tf_op jit(solution)/shard_map/while/body/eval_jaxpr/reduce_scatter | solution.py:321
  1508.2 76.2 %reduce-scatter.75.cloned.1.call-start = ((), (), s32[]{:S(2)}) async-start(), calls=%async_computation.73 | async-start | bytes 2621440 | tf_op jit(solution)/shard_map/while/body/eval_jaxpr/reduce_scatter | solution.py:321
  1587.0 33.0 %all-gather.78.cloned.1.call-start = ((), (), s32[]{:S(2)}) async-start(), calls=%async_computation.64 | async-start | bytes 1310720 | tf_op jit(solution)/shard_map/all_gather | solution.py:72
  1587.6 77.6 %all-gather.76.cloned.1.call-start = ((), (), s32[]{:S(2)}) async-start(), calls=%async_computation.60 | async-start | bytes 1310720 | tf_op jit(solution)/shard_map/all_gather | solution.py:72
  1588.3 203.5 %reduce-scatter.63.cloned.1.call-start = ((), (), s32[]{:S(2)}) async-start(), calls=%async_computation.65 | async-start | bytes 2621440 | tf_op jit(solution)/shard_map/while/body/eval_jaxpr/reduce_scatter | solution.py:321
  1665.1 128.3 %reduce-scatter.57.cloned.1.call-start = ((), (), s32[]{:S(2)}) async-start(), calls=%async_computation.61 | async-start | bytes 2621440 | tf_op jit(solution)/shard_map/while/body/eval_jaxpr/reduce_scatter | solution.py:321
  1702.2 114.4 %reduce-scatter.73.cloned.1.call-start = ((), (), s32[]{:S(2)}) async-start(), calls=%async_computation.72 | async-start | bytes 1769472
  1715.0 113.1 %reduce-scatter.71.cloned.1.call-start = ((), (), s32[]{:S(2)}) async-start(), calls=%async_computation.71 | async-start | bytes 3244032
  1730.8 134.4 %reduce-scatter.69.cloned.1.call-start = ((), (), s32[]{:S(2)}) async-start(), calls=%async_computation.70 | async-start | bytes 589824
  1754.3 157.0 %reduce-scatter.49.cloned.1.call-start = ((), (), s32[]{:S(2)}) async-start(), calls=%async_computation.54 | async-start | bytes 2621440 | tf_op jit(solution)/shard_map/reduce_scatter | solution.py:82
  1766.3 190.4 %reduce-scatter.53.cloned.1.call-start = ((), (), s32[]{:S(2)}) async-start(), calls=%async_computation.58 | async-start | bytes 2621440 | tf_op jit(solution)/shard_map/reduce_scatter | solution.py:82
  1783.4 202.0 %reduce-scatter.65.cloned.1.call-start = ((), (), s32[]{:S(2)}) async-start(), calls=%async_computation.66 | async-start | bytes 1310720 | tf_op jit(solution)/shard_map/reduce_scatter | solution.py:82
  1799.2 214.2 %reduce-scatter.59.cloned.1.call-start = ((), (), s32[]{:S(2)}) async-start(), calls=%async_computation.62 | async-start | bytes 1310720 | tf_op jit(solution)/shard_map/reduce_scatter | solution.py:82
  1803.1 245.9 %reduce-scatter.41.cloned.1.call-start = ((), (), s32[]{:S(2)}) async-start(), calls=%async_computation.44 | async-start | bytes 1310720 | tf_op jit(solution)/shard_map/reduce_scatter | solution.py:76
  1806.5 280.1 %reduce-scatter.33.cloned.1.call-start = ((), (), s32[]{:S(2)}) async-start(), calls=%async_computation.32 | async-start | bytes 2621440 | tf_op jit(solution)/shard_map/reduce_scatter | solution.py:76
  1811.7 320.6 %reduce-scatter.37.cloned.1.call-start = ((), (), s32[]{:S(2)}) async-start(), calls=%async_computation.38 | async-start | bytes 2621440 | tf_op jit(solution)/shard_map/reduce_scatter | solution.py:76
  1816.3 356.9 %reduce-scatter.67.cloned.1.call-start = ((), (), s32[]{:S(2)}) async-start(), calls=%async_computation.67 | async-start | bytes 1769472 | tf_op jit(solution)/shard_map/reduce_scatter | solution.py:370
  1873.6 173.2 %copy-start.41 = (bf16[512,256]{1,0:T(8,128)(2,1)S(1)}, bf16[512,256]{1,0:T(8,128)(2,1)}, u32[]{:S(2)}) copy-start(bf16[512,256]{1,0:T(8,128)(2,1)} %reduce-scatter.43.cloned.1.call-done) | copy-start | bytes 786436
  1873.6 173.2 %copy-start.73 = (bf16[512,256]{1,0:T(8,128)(2,1)S(1)}, bf16[512,256]{1,0:T(8,128)(2,1)}, u32[]{:S(2)}) copy-start(bf16[512,256]{1,0:T(8,128)(2,1)} %reduce-scatter.61.cloned.1.call-done) | copy-start | bytes 786436
  1873.6 173.2 %copy-start.138 = (f32[256]{0:T(256)S(1)}, f32[256]{0:T(256)}, u32[]{:S(2)}) copy-start(f32[256]{0:T(256)} %param.27) | copy-start | bytes 3076
  1873.6 173.2 %copy-start.153 = (f32[512]{0:T(512)S(1)}, f32[512]{0:T(512)}, u32[]{:S(2)}) copy-start(f32[512]{0:T(512)} %copy-done.152) | copy-start | bytes 6148
  1873.6 173.2 %copy-start.166 = (f32[512]{0:T(512)S(1)}, f32[512]{0:T(512)}, u32[]{:S(2)}) copy-start(f32[512]{0:T(512)} %copy-done.165) | copy-start | bytes 6148
  (206 other events, 4441.4 us)
Sparse Core Ops, SparseCore 0:
  33.5 29.0 all-gather.51
  65.1 23.1 all-gather.31
  90.4 30.1 all-gather.59
  122.6 44.5 all-gather.43
  168.6 44.4 all-gather.29
  214.8 27.0 all-gather.55
  244.3 27.6 all-gather.53
  273.8 26.4 all-gather.63
  302.7 26.6 all-gather.61
  331.1 35.2 all-gather.45
  368.3 35.1 all-gather.47
  405.2 35.3 all-gather.33
  442.4 35.1 all-gather.35
  480.3 27.1 reduce-scatter.38
  510.3 25.8 reduce-scatter.42
  538.3 42.4 reduce-scatter.34
  583.1 43.1 reduce-scatter.30
  628.1 30.9 all-gather.39
  661.2 30.1 all-gather.65
  693.4 28.4 all-gather.81
  723.9 23.5 all-gather.41
  749.6 30.1 all-gather.57
  782.0 28.4 all-gather.79
  812.0 44.5 all-gather.49
  858.1 44.4 all-gather.71
  904.0 44.4 all-gather.37
  949.9 44.4 all-gather.67
  996.7 25.3 reduce-scatter.60
  1024.6 25.7 reduce-scatter.54
  1052.5 42.4 reduce-scatter.50
  1097.5 43.1 reduce-scatter.46
  1143.0 26.7 reduce-scatter.44
  1171.3 44.8 all-gather.73
  1217.8 44.4 all-gather.69
  1313.0 33.3 reduce-scatter.76
  1389.5 35.1 reduce-scatter.76
  1470.8 35.1 reduce-scatter.74
  1549.2 35.1 reduce-scatter.74
  1589.7 30.1 all-gather.77
  1622.2 28.5 all-gather.75
  1665.2 33.4 reduce-scatter.62
  1702.3 34.5 reduce-scatter.56
  1741.0 38.4 reduce-scatter.72
  1783.2 44.8 reduce-scatter.70
  1831.1 34.0 reduce-scatter.68
  1867.4 43.8 reduce-scatter.48
  1913.5 43.1 reduce-scatter.52
  1959.0 26.4 reduce-scatter.64
  1987.6 25.7 reduce-scatter.58
  2015.8 26.0 reduce-scatter.40
  2044.1 42.5 reduce-scatter.32
  2089.1 43.1 reduce-scatter.36
  2135.4 37.7 reduce-scatter.66
where the time goes:
time: 2190 us; the launch traced here: 2180 us
  waiting for transfers between devices  1300 us (59%)
  matrix products  414 us (19%)
  other arithmetic  217 us (10%)
  local copies, waits for them, and re-layouts  115 us (5%)
  blocking collectives  112 us (5%)
    reduce_scatter x8, waiting for transfers between devices, collect_grads(): lax.psum_scatter(values.astype(jnp.bfloat16), 'head', scatter_dimension=1...  261 us
    all_gather x8, waiting for transfers between devices, spread_rows(): return lax.all_gather(values, 'head', axis=1, tiled=True)  249 us
    all_gather x8, waiting for transfers between devices, spread_grads(): return lax.all_gather(values, 'head', axis=1, tiled=True)  244 us
    reduce_scatter x8, waiting for transfers between devices, collect_rows(): lax.psum_scatter(values.astype(jnp.bfloat16), 'head', scatter_dimension=1...  194 us
    reduce_scatter x6, waiting for transfers between devices, backward_one(): lax.psum_scatter(key_value.astype(jnp.bfloat16), 'ffn', scatter_dimension...  112 us
    dot_general x6, matrix products, query_side(): jnp.einsum('qhd,khd->hqk', grad_rows, value_rows, preferred_element_type=...  77.9 us
    psum x4, blocking collectives, row_total(): return lax.psum(values, 'head')  71.1 us
    all_gather x4, waiting for transfers between devices, per_device(): lax.all_gather(key_local.reshape(seq_count, local_len, head_width), 'ffn'...  69.2 us
  transfers between devices with their start and end apart: 53, of which 45 were waited for; matrix products, arithmetic and copies ran while one was open for 24% of the time, Pallas kernels for 0%

commit v1 on v0

--- a/solution.py
+++ b/solution.py
@@ -3,6 +3,8 @@
 import jax
 import jax.numpy as jnp
 from jax import lax
+from jax.experimental import pallas as pl
+from jax.experimental.pallas import tpu as pltpu
 from jax.sharding import PartitionSpec as P
 
 HD = 64
@@ -394,6 +396,760 @@
     )
 
 
+BF16 = jnp.bfloat16
+F32 = jnp.float32
+BQ = 256
+BK = 512
+MASKED_SCORE = -1e30
+
+
+def matmul(former, latter):
+    return lax.dot_general(former, latter, (((1,), (0,)), ((), ())), preferred_element_type=F32)
+
+
+def compiler_params(mib):
+    return pltpu.CompilerParams(vmem_limit_bytes=mib * 1024 * 1024)
+
+
+def exchange(blocks, axes, count):
+    me = lax.axis_index(axes)
+    out = blocks
+    for step in range(1, count):
+        send = lax.dynamic_index_in_dim(blocks, me ^ step, 0, keepdims=False)
+        got = lax.ppermute(send, axes, [(j, j ^ step) for j in range(count)])
+        out = lax.dynamic_update_index_in_dim(out, got, me ^ step, 0)
+    return out
+
+
+def swap(values):
+    return lax.ppermute(values, "dp", [(0, 1), (1, 0)])
+
+
+def halves(turned_by, lanes):
+    return (lax.broadcasted_iota(jnp.int32, (1, lanes), 1) % HD) < turned_by
+
+
+def swap_halves(values):
+    low = (lax.broadcasted_iota(jnp.int32, values.shape, 1) % HD) < HD // 2
+    lanes = values.shape[1]
+    return jnp.where(
+        low, pltpu.roll(values, lanes - HD // 2, 1), pltpu.roll(values, HD // 2, 1)
+    )
+
+
+def norm_kernel(main_ref, shared_ref, gain_ref, main_out, shared_out):
+    width = main_ref.shape[2]
+    blocks = main_ref.shape[0]
+    for ref, out in ((main_ref, main_out), (shared_ref, shared_out)):
+        rows = ref.shape[1]
+        for start in range(0, rows, 256):
+            part = pl.ds(start, 256)
+            values = [ref[b, part, :].astype(F32) for b in range(blocks)]
+            total = sum(jnp.sum(v * v, axis=1, keepdims=True) for v in values)
+            factor = lax.rsqrt(total / (width * blocks) + EPSILON)
+            for b in range(blocks):
+                cols = pl.ds(b * width, width)
+                out[part, cols] = (values[b] * factor * gain_ref[:, cols]).astype(BF16)
+
+
+def head_masks():
+    lane = lax.broadcasted_iota(jnp.int32, (1, 2 * HD), 1)
+    first = jnp.where(lane < HD, 1.0, 0.0).astype(BF16)
+    return first, (1.0 - first.astype(F32)).astype(BF16)
+
+
+def attend_kernel(
+    low_ref, n_ref, w_ref, fv_ref, start_ref, cos_ref, sin_ref, q_ref, k_ref, v_ref, o_ref, lse_ref
+):
+    length = n_ref.shape[0]
+    lanes = 2 * HD
+    for begin in range(0, length, 512):
+        rows = pl.ds(begin, 512)
+        made = matmul(n_ref[rows, :], w_ref[...])
+        cos, sin = cos_ref[rows, :], sin_ref[rows, :]
+        q = made[:, :lanes]
+        k = made[:, lanes : 2 * lanes]
+        q_ref[rows, :] = ((q * cos + swap_halves(q) * sin) * (1.0 / math.sqrt(HD))).astype(BF16)
+        k_ref[rows, :] = (k * cos + swap_halves(k) * sin).astype(BF16)
+        v_ref[rows, :] = (0.5 * made[:, 2 * lanes :] + 0.5 * fv_ref[rows, :].astype(F32)).astype(
+            BF16
+        )
+    mask_a, mask_b = head_masks()
+    lane = lax.broadcasted_iota(jnp.int32, (BQ, lanes), 1)
+    for i in range(length // BQ):
+        rows = pl.ds(i * BQ, BQ)
+        q = q_ref[rows, :]
+        both = jnp.concatenate([q * mask_a, q * mask_b], axis=0)
+        start = start_ref[rows, :]
+        start = jnp.concatenate([start, start], axis=0)
+        place = i * BQ + lax.broadcasted_iota(jnp.int32, (BQ, 1), 0)
+        place = jnp.concatenate([place, place], axis=0)
+
+        def step(j, carry):
+            top, total, acc = carry
+            keys = pl.ds(pl.multiple_of(j * BK, BK), BK)
+            s = contract_last(both, k_ref[keys, :])
+            key = j * BK + lax.broadcasted_iota(jnp.int32, s.shape, 1)
+            s = jnp.where((key >= start) & (key <= place), s, MASKED_SCORE)
+            new_top = jnp.maximum(top, jnp.max(s, axis=1, keepdims=True))
+            p = jnp.exp(s - new_top)
+            scale = jnp.exp(top - new_top)
+            total = total * scale + jnp.sum(p, axis=1, keepdims=True)
+            acc = acc * scale + matmul(p.astype(BF16), v_ref[keys, :])
+            return new_top, total, acc
+
+        top, total, acc = lax.fori_loop(
+            low_ref[i],
+            (i * BQ) // BK + 1,
+            step,
+            (
+                jnp.full((2 * BQ, 1), MASKED_SCORE, F32),
+                jnp.zeros((2 * BQ, 1), F32),
+                jnp.zeros((2 * BQ, lanes), F32),
+            ),
+        )
+        acc = acc / total
+        lse = top + jnp.log(total)
+        o_ref[rows, :] = jnp.where(lane < HD, acc[:BQ], acc[BQ:]).astype(BF16)
+        lse_ref[rows, :] = jnp.where(
+            lane < HD, jnp.broadcast_to(lse[:BQ], (BQ, lanes)), jnp.broadcast_to(lse[BQ:], (BQ, lanes))
+        )
+
+
+def attend(low, normed, weight, first, start_col, cos, sin):
+    length = normed.shape[0]
+    small = jax.ShapeDtypeStruct((length, 2 * HD), BF16)
+    vmem = pl.BlockSpec(memory_space=pltpu.VMEM)
+    return pl.pallas_call(
+        attend_kernel,
+        out_shape=(small, small, small, small, jax.ShapeDtypeStruct((length, 2 * HD), F32)),
+        in_specs=[pl.BlockSpec(memory_space=pltpu.SMEM)] + [vmem] * 6,
+        out_specs=(vmem,) * 5,
+        compiler_params=compiler_params(48),
+    )(low, normed, weight, first, start_col, cos, sin)
+
+
+def attend_back_kernel(
+    low_ref,
+    n_ref,
+    w_ref,
+    q_ref,
+    k_ref,
+    v_ref,
+    o_ref,
+    lse_ref,
+    do_ref,
+    start_ref,
+    cos_ref,
+    sin_ref,
+    dn_ref,
+    gw_ref,
+    gfv_ref,
+    dq_ref,
+    dk_ref,
+    dv_ref,
+    dp_ref,
+):
+    length = n_ref.shape[0]
+    lanes = 2 * HD
+    dk_ref[...] = jnp.zeros_like(dk_ref)
+    dv_ref[...] = jnp.zeros_like(dv_ref)
+    mask_a, mask_b = head_masks()
+    lane = lax.broadcasted_iota(jnp.int32, (BQ, lanes), 1)
+    for i in range(length // BQ):
+        rows = pl.ds(i * BQ, BQ)
+        q, do = q_ref[rows, :], do_ref[rows, :]
+        q2 = jnp.concatenate([q * mask_a, q * mask_b], axis=0)
+        do2 = jnp.concatenate([do * mask_a, do * mask_b], axis=0)
+        lse = jnp.transpose(lse_ref[rows, :])
+        lse = jnp.concatenate([lse[0:1, :], lse[HD : HD + 1, :]], axis=1)
+        inner = jnp.transpose(do.astype(F32) * o_ref[rows, :].astype(F32))
+        inner = jnp.concatenate(
+            [
+                jnp.sum(inner[:HD], axis=0, keepdims=True),
+                jnp.sum(inner[HD:], axis=0, keepdims=True),
+            ],
+            axis=1,
+        )
+        start = start_ref[:, rows]
+        start = jnp.concatenate([start, start], axis=1)
+        place = i * BQ + lax.broadcasted_iota(jnp.int32, (1, BQ), 1)
+        place = jnp.concatenate([place, place], axis=1)
+
+        def step(j, acc):
+            keys = pl.ds(pl.multiple_of(j * BK, BK), BK)
+            k, v = k_ref[keys, :], v_ref[keys, :]
+            s = contract_last(k, q2)
+            key = j * BK + lax.broadcasted_iota(jnp.int32, s.shape, 0)
+            s = jnp.where((key >= start) & (key <= place), s, MASKED_SCORE)
+            p = jnp.exp(s - lse)
+            dp = contract_last(v, do2)
+            ds = (p * (dp - inner)).astype(BF16)
+            dv_ref[keys, :] += matmul(p.astype(BF16), do2)
+            dk_ref[keys, :] += matmul(ds, q2)
+            return acc + contract_rows(ds, k)
+
+        acc = lax.fori_loop(
+            low_ref[i], (i * BQ) // BK + 1, step, jnp.zeros((2 * BQ, lanes), F32)
+        )
+        dq_ref[rows, :] = jnp.where(lane < HD, acc[:BQ], acc[BQ:]) * (1.0 / math.sqrt(HD))
+    for begin in range(0, length, 512):
+        rows = pl.ds(begin, 512)
+        cos, sin = cos_ref[rows, :], sin_ref[rows, :]
+        dq, dk = dq_ref[rows, :], dk_ref[rows, :]
+        dv = (0.5 * dv_ref[rows, :]).astype(BF16)
+        gfv_ref[rows, :] = dv
+        dp_ref[rows, 0:lanes] = (dq * cos - swap_halves(dq) * sin).astype(BF16)
+        dp_ref[rows, lanes : 2 * lanes] = (dk * cos - swap_halves(dk) * sin).astype(BF16)
+        dp_ref[rows, 2 * lanes :] = dv
+        dn_ref[rows, :] = contract_last(dp_ref[rows, :], w_ref[...]).astype(BF16)
+    for begin in range(0, n_ref.shape[1], 256):
+        cols = pl.ds(begin, 256)
+        gw_ref[:, cols] = contract_rows(dp_ref[...], n_ref[:, cols])
+
+
+def attend_back(low, normed, weight, kept, grad, start_row, cos, sin):
+    length, width = normed.shape
+    lanes = 2 * HD
+    vmem = pl.BlockSpec(memory_space=pltpu.VMEM)
+    return pl.pallas_call(
+        attend_back_kernel,
+        out_shape=(
+            jax.ShapeDtypeStruct((length, width), BF16),
+            jax.ShapeDtypeStruct((3 * lanes, width), F32),
+            jax.ShapeDtypeStruct((length, lanes), BF16),
+        ),
+        in_specs=[pl.BlockSpec(memory_space=pltpu.SMEM)] + [vmem] * 11,
+        out_specs=(vmem,) * 3,
+        scratch_shapes=[
+            pltpu.VMEM((length, lanes), F32),
+            pltpu.VMEM((length, lanes), F32),
+            pltpu.VMEM((length, lanes), F32),
+            pltpu.VMEM((length, 3 * lanes), BF16),
+        ],
+        compiler_params=compiler_params(56),
+    )(low, normed, weight, *kept, grad, start_row, cos, sin)
+
+
+def fill_out_weight(wall_ref, ow_ref):
+    groups, depth, high, wide = wall_ref.shape
+    for g in range(groups):
+        for z in range(depth):
+            ow_ref[z * high : (z + 1) * high, g * wide : (g + 1) * wide] = wall_ref[g, z]
+
+
+def pair_column(index, ffn_size):
+    return (index % ffn_size) * 2 + index // ffn_size
+
+
+def hidden_kernel(
+    om_ref, os_ref, xm_ref, xs_ref, cm_ref, cs_ref, wall_ref, gain_ref,
+    h_ref, n_ref, ob_ref, dy_ref, ow_ref,
+):
+    fill_out_weight(wall_ref, ow_ref)
+    groups, lanes = om_ref.shape[0], om_ref.shape[2]
+    blocks, width = xm_ref.shape[0], xm_ref.shape[2]
+    base = 0
+    for o, x, c in ((om_ref, xm_ref, cm_ref), (os_ref, xs_ref, cs_ref)):
+        rows = x.shape[1]
+        for begin in range(0, rows, 256):
+            part = pl.ds(begin, 256)
+            here = pl.ds(base + begin, 256)
+            for g in range(groups):
+                column = pair_column(g, groups // 2) * lanes
+                ob_ref[here, column : column + lanes] = o[g, part, :]
+            for b in range(blocks):
+                dy_ref[here, b * width : (b + 1) * width] = c[b, part, :]
+            branch = matmul(ob_ref[here, :], ow_ref[...])
+            total = jnp.zeros((256, 1), F32)
+            for b in range(blocks):
+                cols = slice(b * width, (b + 1) * width)
+                h = x[b, part, :].astype(F32) + branch[:, cols]
+                h_ref[here, cols] = h
+                total = total + jnp.sum(h * h, axis=1, keepdims=True)
+            factor = lax.rsqrt(total / (width * blocks) + EPSILON)
+            n_ref[here, :] = (h_ref[here, :] * factor * gain_ref[...]).astype(BF16)
+        base += rows
+
+
+def mlp_kernel(
+    n_ref, dy_ref, wall_ref, y_ref, dn_ref, grad_ref, g_ref, d_ref, nt_ref, act_ref, dgu_ref
+):
+    groups, rows_in, lanes = wall_ref.shape[0], wall_ref.shape[2], wall_ref.shape[3]
+    rows, width = n_ref.shape
+    padded = d_ref.shape[0]
+    deep = width // groups
+    tiles = 2 * padded // lanes
+    up_to = rows_in - (tiles * deep)
+    skip = grad_ref.shape[2] - tiles * deep
+    hidden = skip
+    first = up_to - hidden
+
+    @pl.when(pl.program_id(0) == 0)
+    def _():
+        y_ref[...] = jnp.zeros_like(y_ref)
+        dn_ref[...] = jnp.zeros_like(dn_ref)
+        nt_ref[...] = jnp.transpose(n_ref[...])
+        d_ref[hidden:, :] = jnp.zeros((padded - hidden, width), BF16)
+
+    for g in range(groups):
+        for t in range(tiles):
+            at = first + t * deep
+            g_ref[g * deep : (g + 1) * deep, t * lanes : (t + 1) * lanes] = wall_ref[
+                g, 0, at : at + deep, :
+            ]
+        at = first + tiles * deep
+        d_ref[0:hidden, g * lanes : (g + 1) * lanes] = wall_ref[g, 0, at : at + hidden, :]
+    for begin in range(0, rows, 256):
+        part = pl.ds(begin, 256)
+        gu = matmul(n_ref[part, :], g_ref[...])
+        gate, up = gu[:, :padded], gu[:, padded:]
+        sig = 1.0 / (1.0 + jnp.exp(-gate))
+        silu = gate * sig
+        act_ref[part, :] = (silu * up).astype(BF16)
+        dact = contract_last(dy_ref[part, :], d_ref[...])
+        dgu_ref[part, :padded] = (dact * up * sig * (1.0 + gate * (1.0 - sig))).astype(BF16)
+        dgu_ref[part, padded:] = (dact * silu).astype(BF16)
+        y_ref[part, :] += matmul(act_ref[part, :], d_ref[...])
+        dn_ref[part, :] += contract_last(dgu_ref[part, :], g_ref[...])
+    for begin in range(0, 2 * padded, 512):
+        made = matmul(nt_ref[...], dgu_ref[:, begin : begin + 512]).astype(BF16)
+        for g in range(groups):
+            for t in range(512 // lanes):
+                at = (begin // lanes + t) * deep
+                grad_ref[g, 0, at : at + deep, :] = made[
+                    g * deep : (g + 1) * deep, t * lanes : (t + 1) * lanes
+                ]
+    for begin in range(0, width, 512):
+        made = contract_rows(act_ref[...], dy_ref[:, begin : begin + 512]).astype(BF16)
+        for t in range(512 // lanes):
+            grad_ref[begin // lanes + t, 0, tiles * deep :, :] = made[
+                :hidden, t * lanes : (t + 1) * lanes
+            ]
+
+
+def hidden_back_kernel(
+    h_ref, y_ref, dn_ref, dy_ref, ob_ref, wall_ref, gain_ref,
+    outm_ref, outs_ref, dh_ref, dom_ref, dos_ref, gout_ref, ggain_ref, ow_ref, low_ref,
+):
+    fill_out_weight(wall_ref, ow_ref)
+    groups, lanes = dom_ref.shape[0], dom_ref.shape[2]
+    blocks, width = outm_ref.shape[0], outm_ref.shape[2]
+    full = width * blocks
+    gain = gain_ref[...]
+    ggain = jnp.zeros((1, full), F32)
+    base = 0
+    for out, dob in ((outm_ref, dom_ref), (outs_ref, dos_ref)):
+        rows = out.shape[1]
+        for begin in range(0, rows, 256):
+            part = pl.ds(begin, 256)
+            here = pl.ds(base + begin, 256)
+            h = h_ref[here, :]
+            factor = lax.rsqrt(jnp.sum(h * h, axis=1, keepdims=True) / full + EPSILON)
+            dn = dn_ref[here, :]
+            result = (h + y_ref[here, :]).astype(BF16)
+            for b in range(blocks):
+                out[b, part, :] = result[:, b * width : (b + 1) * width]
+            weighted = dn * gain
+            ggain = ggain + jnp.sum(dn * (h * factor), axis=0, keepdims=True)
+            row_inner = jnp.sum(weighted * h, axis=1, keepdims=True)
+            dh = (
+                dy_ref[here, :].astype(F32)
+                + factor * weighted
+                - h * (factor * factor * factor * row_inner / full)
+            )
+            dh_ref[here, :] = dh
+            low_ref[here, :] = dh.astype(BF16)
+            made = contract_last(low_ref[here, :], ow_ref[...]).astype(BF16)
+            for g in range(groups):
+                column = pair_column(g, groups // 2) * lanes
+                dob[g, part, :] = made[:, column : column + lanes]
+        base += rows
+    ggain_ref[...] = ggain
+    high, wide = gout_ref.shape[2], gout_ref.shape[3]
+    for z in range(gout_ref.shape[1]):
+        made = contract_rows(ob_ref[:, z * high : (z + 1) * high], low_ref[...]).astype(BF16)
+        for g in range(groups):
+            gout_ref[g, z] = made[:, g * wide : (g + 1) * wide]
+
+
+def last_kernel(
+    xm_ref, xs_ref, dh_ref, am_ref, bm_ref, as_ref, bs_ref, gain_ref,
+    outm_ref, outs_ref, ggain_ref,
+):
+    blocks, width = xm_ref.shape[0], xm_ref.shape[2]
+    full = width * blocks
+    ggain_ref[...] = jnp.zeros_like(ggain_ref)
+    base = 0
+    for x, out, own, others in (
+        (xm_ref, outm_ref, am_ref, bm_ref),
+        (xs_ref, outs_ref, as_ref, bs_ref),
+    ):
+        rows = x.shape[1]
+        for begin in range(0, rows, 256):
+            part = pl.ds(begin, 256)
+            here = pl.ds(base + begin, 256)
+            dn = own[part, :].astype(F32)
+            for other in range(others.shape[0]):
+                dn = dn + others[other, part, :].astype(F32)
+            weighted = dn * gain_ref[...]
+            total = jnp.zeros((256, 1), F32)
+            inner = jnp.zeros((256, 1), F32)
+            for b in range(blocks):
+                cols = slice(b * width, (b + 1) * width)
+                value = x[b, part, :].astype(F32)
+                total = total + jnp.sum(value * value, axis=1, keepdims=True)
+                inner = inner + jnp.sum(weighted[:, cols] * value, axis=1, keepdims=True)
+            factor = lax.rsqrt(total / full + EPSILON)
+            slope = factor * factor * factor * inner / full
+            for b in range(blocks):
+                cols = slice(b * width, (b + 1) * width)
+                value = x[b, part, :].astype(F32)
+                ggain_ref[:, cols] += jnp.sum(dn[:, cols] * value * factor, axis=0, keepdims=True)
+                out[b, part, :] = (
+                    dh_ref[here, cols] + factor * weighted[:, cols] - value * slope
+                ).astype(BF16)
+        base += rows
+
+
+def by_layers():
+    def run(
+        tokens,
+        first_values,
+        segment_ids,
+        cotangent,
+        qkv_weight,
+        out_weight,
+        gate_up_weight,
+        down_weight,
+        attn_gain,
+        mlp_gain,
+    ):
+        dp, z, f = (lax.axis_index(a) for a in ("dp", "head", "ffn"))
+        depth, side = lax.axis_size("head"), lax.axis_size("ffn")
+        group = 2 * side
+        length, width = tokens.shape[1], tokens.shape[2]
+        half = length // 2
+        full_width = width * depth
+        seq_len = length * side
+        lanes = 2 * HD
+        hidden = down_weight.shape[0]
+        padded = -(-hidden // lanes) * lanes
+        layer = ("dp", "ffn")
+        vmem = pl.BlockSpec(memory_space=pltpu.VMEM)
+
+        def to_layers(values):
+            keep = lax.dynamic_slice(values, (depth, dp * half, 0), (2, half, width))
+            give = lax.dynamic_slice(values, (depth, (1 - dp) * half, 0), (2, half, width))
+            got = swap(give)
+            early = jnp.where(dp == 0, keep, got)
+            late = jnp.where(dp == 0, got, keep)
+            shared = jnp.stack([early[0], late[0], early[1], late[1]])
+            return (
+                exchange(values[:depth], "head", depth),
+                exchange(shared, "head", depth),
+            )
+
+        def from_layers(main, shared):
+            main = exchange(main, "head", depth)
+            shared = exchange(shared, "head", depth)
+            keep = jnp.where(dp == 0, shared[0::2], shared[1::2])
+            got = swap(jnp.where(dp == 0, shared[1::2], shared[0::2]))
+            early = jnp.where(dp == 0, keep, got)
+            late = jnp.where(dp == 0, got, keep)
+            return jnp.concatenate([main, jnp.concatenate([early, late], axis=1)], axis=0)
+
+        def tiles(values):
+            values = jnp.pad(values, ((0, 0), (0, padded - hidden)))
+            return values.reshape(-1, padded // lanes, lanes).transpose(1, 0, 2).reshape(-1, lanes)
+
+        wall = jnp.concatenate(
+            [out_weight, tiles(gate_up_weight[:, 0]), tiles(gate_up_weight[:, 1]), down_weight],
+            axis=0,
+        )
+        wall = lax.all_gather(wall, ("dp", "ffn", "head"), axis=0, tiled=False)
+        wall = wall.reshape(group, depth, wall.shape[1], lanes)
+        out_rows = out_weight.shape[0]
+
+        deep = qkv_weight.shape[0]
+        part = qkv_weight.reshape(deep, 3, 2, lanes).transpose(2, 1, 0, 3)
+        part = exchange(jnp.broadcast_to(part[None], (depth,) + part.shape), "head", depth)
+        part = part.transpose(1, 0, 2, 3, 4).reshape(group, 3, deep, lanes)
+        part = exchange(part, layer, group)
+        weight = part.transpose(0, 2, 1, 3).reshape(group * deep, 3 * lanes)
+        gains = jnp.stack([attn_gain, mlp_gain])
+        gains = exchange(jnp.broadcast_to(gains[None], (depth,) + gains.shape), "head", depth)
+        gains = gains.transpose(1, 0, 2).reshape(2, 1, full_width)
+
+        other_ids = swap(segment_ids)
+        pick = depth + z // 2
+        ids = [
+            lax.dynamic_index_in_dim(segment_ids, z, 0, keepdims=False),
+            lax.dynamic_index_in_dim(other_ids, z, 0, keepdims=False),
+            jnp.where(
+                z % 2 == dp,
+                lax.dynamic_index_in_dim(segment_ids, pick, 0, keepdims=False),
+                lax.dynamic_index_in_dim(other_ids, pick, 0, keepdims=False),
+            ),
+        ]
+        ids = jnp.stack(ids)
+        starts = jnp.sum((ids[:, None, :] < ids[:, :, None]).astype(jnp.int32), axis=2)
+        lows = starts[:, ::BQ] // BK
+
+        places = jnp.arange(seq_len, dtype=jnp.int32)
+        cos, sin = rope_tables(places, HD)
+        cos = jnp.concatenate([cos, cos], axis=1)
+        sin = jnp.concatenate([-sin[:, : HD // 2], sin[:, HD // 2 :]], axis=1)
+        sin = jnp.concatenate([sin, sin], axis=1)
+
+        xm, xs = to_layers(tokens)
+        nm, ns = pl.pallas_call(
+            norm_kernel,
+            out_shape=(
+                jax.ShapeDtypeStruct((length, full_width), BF16),
+                jax.ShapeDtypeStruct((half, full_width), BF16),
+            ),
+            in_specs=[vmem] * 3,
+            out_specs=(vmem,) * 2,
+            compiler_params=compiler_params(32),
+        )(xm, xs, gains[0])
+
+        def spread(values):
+            blocks = jnp.broadcast_to(values[None], (side,) + values.shape)
+            own = exchange(blocks, "ffn", side)
+            return own, swap(own)
+
+        own, other = spread(nm)
+        normed = [own.reshape(seq_len, full_width), other.reshape(seq_len, full_width)]
+        own, other = spread(ns)
+        mixed = jnp.stack(
+            [jnp.where(dp == 0, own, other), jnp.where(dp == 0, other, own)], axis=1
+        )
+        normed.append(mixed.reshape(seq_len, full_width))
+
+        fm, fs = to_layers(first_values)
+
+        def to_pairs(values):
+            rows = values.shape[1]
+            values = values.reshape(depth, rows, 2, lanes).transpose(2, 0, 1, 3)
+            return exchange(values.reshape(group, rows, lanes), layer, group)
+
+        def positions(main, shared):
+            main = main.reshape(2, seq_len, lanes)
+            shared = shared.reshape(2, side, half, lanes).transpose(1, 0, 2, 3)
+            return [
+                lax.dynamic_index_in_dim(main, dp, 0, keepdims=False),
+                lax.dynamic_index_in_dim(main, 1 - dp, 0, keepdims=False),
+                shared.reshape(seq_len, lanes),
+            ]
+
+        def owners(values):
+            mine = values[0].reshape(1, side, length, lanes)
+            theirs = values[1].reshape(1, side, length, lanes)
+            main = jnp.where(
+                dp == 0,
+                jnp.concatenate([mine, theirs], axis=0),
+                jnp.concatenate([theirs, mine], axis=0),
+            ).reshape(group, length, lanes)
+            shared = values[2].reshape(side, 2, half, lanes).transpose(1, 0, 2, 3)
+            return (
+                exchange(main, layer, group),
+                exchange(shared.reshape(group, half, lanes), layer, group),
+            )
+
+        firsts = positions(to_pairs(fm), to_pairs(fs))
+        kept = [
+            attend(lows[i], normed[i], weight, firsts[i], starts[i][:, None], cos, sin)
+            for i in range(3)
+        ]
+        om, os_ = owners([k[3] for k in kept])
+        cm, cs = to_layers(cotangent)
+
+        rows = length + half
+        whole = jax.ShapeDtypeStruct((rows, full_width), F32)
+        whole_low = jax.ShapeDtypeStruct((rows, full_width), BF16)
+        out_spec = pl.BlockSpec((group, depth, out_rows, lanes), lambda i: (0, 0, 0, 0))
+
+        def fixed(shape):
+            return pl.BlockSpec(
+                shape, lambda i: (0,) * len(shape), pipeline_mode=pl.Buffered(1)
+            )
+
+        ow_scratch = pltpu.VMEM((out_rows * depth, group * lanes), BF16)
+        h, n2, ob, dy = pl.pallas_call(
+            hidden_kernel,
+            grid=(1,),
+            out_shape=(whole, whole_low, whole_low, whole_low),
+            in_specs=[fixed(a.shape) for a in (om, os_, xm, xs, cm, cs)]
+            + [out_spec, fixed((1, full_width))],
+            out_specs=tuple(fixed((rows, full_width)) for _ in range(4)),
+            scratch_shapes=[ow_scratch],
+            compiler_params=compiler_params(56),
+        )(om, os_, xm, xs, cm, cs, wall, gains[1])
+
+        high = wall.shape[2]
+        grad_rows = high - out_rows
+        y, dn2, grads = pl.pallas_call(
+            mlp_kernel,
+            grid=(depth,),
+            out_shape=(
+                whole,
+                whole,
+                jax.ShapeDtypeStruct((group, depth, grad_rows, lanes), BF16),
+            ),
+            in_specs=[
+                fixed((rows, full_width)),
+                fixed((rows, full_width)),
+                pl.BlockSpec((group, 1, high, lanes), lambda i: (0, i, 0, 0)),
+            ],
+            out_specs=(
+                fixed((rows, full_width)),
+                fixed((rows, full_width)),
+                pl.BlockSpec((group, 1, grad_rows, lanes), lambda i: (0, i, 0, 0)),
+            ),
+            scratch_shapes=[
+                pltpu.VMEM((full_width, 2 * padded), BF16),
+                pltpu.VMEM((padded, full_width), BF16),
+                pltpu.VMEM((full_width, rows), BF16),
+                pltpu.VMEM((rows, padded), BF16),
+                pltpu.VMEM((rows, 2 * padded), BF16),
+            ],
+            compiler_params=compiler_params(60),
+        )(n2, dy, wall)
+
+        grads = grads.reshape(group * depth * grad_rows, lanes)
+        grads = lax.psum_scatter(grads, layer, scatter_dimension=0, tiled=True)
+        grads = lax.psum_scatter(grads, "head", scatter_dimension=0, tiled=True)
+
+        outm, outs, dh, dom, dos, gout, gain_two = pl.pallas_call(
+            hidden_back_kernel,
+            grid=(1,),
+            out_shape=(
+                jax.ShapeDtypeStruct(xm.shape, BF16),
+                jax.ShapeDtypeStruct(xs.shape, BF16),
+                whole,
+                jax.ShapeDtypeStruct(om.shape, BF16),
+                jax.ShapeDtypeStruct(os_.shape, BF16),
+                jax.ShapeDtypeStruct((group, depth, out_rows, lanes), BF16),
+                jax.ShapeDtypeStruct((1, full_width), F32),
+            ),
+            in_specs=[fixed((rows, full_width))] * 5 + [out_spec, fixed((1, full_width))],
+            out_specs=tuple(
+                fixed(s)
+                for s in (
+                    xm.shape,
+                    xs.shape,
+                    (rows, full_width),
+                    om.shape,
+                    os_.shape,
+                    (group, depth, out_rows, lanes),
+                    (1, full_width),
+                )
+            ),
+            scratch_shapes=[ow_scratch, pltpu.VMEM((rows, full_width), BF16)],
+            compiler_params=compiler_params(60),
+        )(h, y, dn2, dy, ob, wall, gains[1])
+        out_tokens = from_layers(outm, outs)
+
+        douts = positions(exchange(dom, layer, group), exchange(dos, layer, group))
+        back = [
+            attend_back(
+                lows[i], normed[i], weight, kept[i], douts[i], starts[i][None], cos, sin
+            )
+            for i in range(3)
+        ]
+
+        gout = exchange(gout, layer, group)
+        gout = jnp.sum(gout.astype(F32), axis=0).astype(BF16)
+        grad_out = jnp.sum(exchange(gout, "head", depth).astype(F32), axis=0)
+
+        gvm, gvs = owners([b[2] for b in back])
+
+        def to_columns(values):
+            rows = values.shape[1]
+            values = values.reshape(2, side, rows, lanes).transpose(1, 2, 0, 3)
+            return values.reshape(depth, rows, width)
+
+        value_grads = from_layers(to_columns(gvm), to_columns(gvs))
+
+        def summed(mine, theirs):
+            chip = (mine.astype(F32) + theirs.astype(F32)).astype(BF16)
+            own = lax.dynamic_index_in_dim(chip, f, 0, keepdims=False)
+            got = []
+            for step in range(1, side):
+                send = lax.dynamic_index_in_dim(chip, f ^ step, 0, keepdims=False)
+                got.append(lax.ppermute(send, "ffn", [(j, j ^ step) for j in range(side)]))
+            return own, jnp.stack(got)
+
+        dn = [b[0] for b in back]
+        main_parts = summed(
+            dn[0].reshape(side, length, full_width),
+            swap(dn[1].reshape(side, length, full_width)),
+        )
+        shared = dn[2].reshape(side, 2, half, full_width)
+        shared_parts = summed(
+            lax.dynamic_index_in_dim(shared, dp, 1, keepdims=False),
+            swap(lax.dynamic_index_in_dim(shared, 1 - dp, 1, keepdims=False)),
+        )
+        tokm, toks, gain_one = pl.pallas_call(
+            last_kernel,
+            out_shape=(
+                jax.ShapeDtypeStruct(xm.shape, BF16),
+                jax.ShapeDtypeStruct(xs.shape, BF16),
+                jax.ShapeDtypeStruct((1, full_width), F32),
+            ),
+            in_specs=[vmem] * 8,
+            out_specs=(vmem,) * 3,
+            compiler_params=compiler_params(56),
+        )(xm, xs, dh, *main_parts, *shared_parts, gains[0])
+        token_grads = from_layers(tokm, toks)
+
+        grad_w = (back[0][1] + back[1][1] + back[2][1]).astype(BF16)
+        grad_w = grad_w.reshape(3, lanes, group, deep).transpose(2, 0, 3, 1)
+        grad_w = exchange(grad_w, layer, group)
+        grad_w = grad_w.reshape(2, side, 3, deep, lanes).transpose(1, 3, 2, 0, 4)
+        grad_w = grad_w.reshape(depth, deep, 3, width)
+        grad_qkv = jnp.sum(exchange(grad_w, "head", depth).astype(F32), axis=0)
+
+        gain_sums = lax.psum(jnp.concatenate([gain_one, gain_two]), ("dp", "ffn", "head"))
+        gain_sums = lax.dynamic_slice_in_dim(gain_sums, z * width, width, axis=1)
+
+        grads = grads.astype(F32)
+        count = padded // lanes * deep
+
+        def untile(values):
+            values = values.reshape(padded // lanes, deep, lanes).transpose(1, 0, 2)
+            return values.reshape(deep, padded)[:, :hidden]
+
+        grad_gate = jnp.stack([untile(grads[:count]), untile(grads[count : 2 * count])], axis=1)
+        return (
+            out_tokens,
+            token_grads,
+            value_grads,
+            grad_qkv,
+            grad_out,
+            grad_gate,
+            grads[2 * count :],
+            gain_sums[0],
+            gain_sums[1],
+        )
+
+    return run
+
+
+def fits_layers(mesh, seqs, seq_len, full_width, heads):
+    sizes = dict(mesh.shape)
+    return (
+        sizes["dp"] == 2
+        and sizes["head"] == 4
+        and sizes["ffn"] == 4
+        and seqs == 12
+        and seq_len % (512 * 4) == 0
+        and full_width == 1024
+        and heads == 16
+    )
+
+
 def solution(mesh):
     in_specs = (
         P("dp", "ffn", "head"),
@@ -418,6 +1174,14 @@
         P("head"),
         P("head"),
     )
-    return jax.shard_map(
-        per_device, mesh=mesh, in_specs=in_specs, out_specs=out_specs, check_vma=False
-    )
+
+    def program(*args):
+        seqs, seq_len, full_width = args[0].shape
+        heads = args[5].shape[0] // HD
+        fast = fits_layers(mesh, seqs, seq_len, full_width, heads)
+        body = by_layers() if fast else per_device
+        return jax.shard_map(
+            body, mesh=mesh, in_specs=in_specs, out_specs=out_specs, check_vma=False
+        )(*args)
+
+    return program

time: 2190 us -> 1100 us (0.50)
  waiting for transfers between devices: 1300 us -> 457 us
  matrix products: 414 us -> 0 us
  Pallas kernels: 0 us -> 239 us
  starting transfers between devices: 4.89 us -> 172 us
  other arithmetic: 217 us -> 50.7 us
  blocking collectives: 112 us -> 39.5 us
    all_gather x27 -> x1, waiting for transfers between devices: 655 us -> 0.02 us  [run(): wall = lax.all_gather(wall, ('dp', 'ffn', 'head'), axis=0, tiled=False)]
    reduce_scatter x23 -> x2, waiting for transfers between devices: 603 us -> 0.01 us  [the longest x1 0.01 us: run(): grads = lax.psum_scatter(grads, layer, scatter_dimension=0, tiled=True)]
    ppermute x0 -> x148, waiting for transfers between devices: none -> 457 us  [the longest x131 406 us: exchange(): got = lax.ppermute(send, axes, [(j, j ^ step) for j in range(count)])]
    dot_general x88 -> x0, matrix products: 414 us -> none  [the longest x6 77.9 us: query_side(): jnp.einsum('qhd,khd->hqk', grad_rows, value_rows, preferred_element_type=...]
    pallas_call x0 -> x11, Pallas kernels: none -> 239 us  [the longest x3 85.8 us: attend_back(): pl.pallas_call(attend_back_kernel, out_shape=(jax.ShapeDtypeStruct((lengt...]
    ppermute x0 -> x148, starting transfers between devices: none -> 172 us  [the longest x131 161 us: exchange(): got = lax.ppermute(send, axes, [(j, j ^ step) for j in range(count)])]
    convert_element_type x28 -> x3, other arithmetic: 104 us -> 8.12 us  [the longest x2 8.11 us: summed(): chip = (mine.astype(F32) + theirs.astype(F32)).astype(BF16)]
    psum x5 -> x1, blocking collectives: 86.3 us -> 39.5 us  [run(): lax.psum(jnp.concatenate([gain_one, gain_two]), ('dp', 'ffn', 'head'))]
  transfers between devices with their start and end apart: 53 -> 151, of which waited for: 45 -> 71; matrix products, arithmetic and copies ran while one was open for 24% -> 14% of each run, Pallas kernels for 0% -> 16%
where the time goes in v1:
time: 1100 us; the launch traced here: 1090 us
  waiting for transfers between devices  457 us (42%)
  Pallas kernels  239 us (22%)
  starting transfers between devices  172 us (16%)
  local copies, waits for them, and re-layouts  113 us (10%)
  other arithmetic  50.7 us (5%)
  blocking collectives  39.5 us (4%)
  between operations  16 us (1%)
    ppermute x131, waiting for transfers between devices, exchange(): got = lax.ppermute(send, axes, [(j, j ^ step) for j in range(count)])  406 us
    ppermute x131, starting transfers between devices, exchange(): got = lax.ppermute(send, axes, [(j, j ^ step) for j in range(count)])  161 us
    pallas_call x3, Pallas kernels, attend_back(): pl.pallas_call(attend_back_kernel, out_shape=(jax.ShapeDtypeStruct((lengt...  85.8 us
    pallas_call x3, Pallas kernels, attend(): pl.pallas_call(attend_kernel, out_shape=(small, small, small, small, jax....  67.7 us
    pallas_call x1, Pallas kernels, run(): pl.pallas_call(mlp_kernel, grid=(depth,), out_shape=(whole, whole, jax.Sh...  54.1 us
    ppermute x6, waiting for transfers between devices, summed(): got.append(lax.ppermute(send, 'ffn', [(j, j ^ step) for j in range(side)]))  51.1 us
    psum x1, blocking collectives, run(): lax.psum(jnp.concatenate([gain_one, gain_two]), ('dp', 'ffn', 'head'))  39.5 us
    dynamic_update_slice x107, local copies, waits for them, and re-layouts, exchange(): out = lax.dynamic_update_index_in_dim(out, got, me ^ step, 0)  33.4 us
  transfers between devices with their start and end apart: 151, of which 71 were waited for; matrix products, arithmetic and copies ran while one was open for 14% of the time, Pallas kernels for 16%

profile of v1, /device:TPU:0, one launch (start us, length us, event | category | flops | bytes accessed | tf_op | source)
XLA Modules:
  0.0 1088.5 jit_solution(608002424861009478)
XLA Ops:
  9.8 3.1 collective-permute-start.8
  16.5 3.5 collective-permute-start.15
  33.0 4.0 fusion.2
  42.0 5.8 convert_reduce_fusion
  64.6 10.0 collective-permute-done.1
  75.5 13.7 %collective-permute-done.24 = bf16[512,256]{0,1:T(8,128)(2,1)S(1)} collective-permute-done((bf16[512,256]{0,1:T(8,128)(2,1)}, bf16[512,256]{0,1:T(8,128)(2,1)S(1)}, u32[]{:S(2)}, u32[]{:S(2)}) %collective-permute-start.24) | collective-permute-done | bytes 262176 | tf_op jit(solution)/shard_map/ppermute | solution.py:419
  91.3 13.9 %collective-permute-done.64 = bf16[512,256]{1,0:T(8,128)(2,1)S(1)} collective-permute-done((bf16[512,256]{1,0:T(8,128)(2,1)S(1)}, bf16[512,256]{1,0:T(8,128)(2,1)S(1)}, u32[]{:S(2)}, u32[]{:S(2)}) %collective-permute-start.64) | collective-permute-done | bytes 262176 | tf_op jit(solution)/shard_map/ppermute | solution.py:419
  113.8 26.7 %collective-permute-done.68 = bf16[256,256]{1,0:T(8,128)(2,1)S(1)} collective-permute-done((bf16[256,256]{1,0:T(8,128)(2,1)S(1)}, bf16[256,256]{1,0:T(8,128)(2,1)S(1)}, u32[]{:S(2)}, u32[]{:S(2)}) %collective-permute-start.68) | collective-permute-done | bytes 131104 | tf_op jit(solution)/shard_map/ppermute | solution.py:419
  143.7 4.1 collective-permute-done.18
  150.1 5.6 collective-permute-done.19
  157.9 3.8 collective-permute-done.21
  171.3 5.1 collective-permute-start.65
  181.5 51.7 %collective-permute-done.6 = bf16[256,256]{1,0:T(8,128)(2,1)S(1)} collective-permute-done((bf16[256,256]{1,0:T(8,128)(2,1)S(1)}, bf16[256,256]{1,0:T(8,128)(2,1)S(1)}, u32[]{:S(2)}, u32[]{:S(2)}) %collective-permute-start.6) | collective-permute-done | bytes 131104 | tf_op jit(solution)/shard_map/ppermute | solution.py:419
  234.3 5.7 collective-permute-done.7
  260.1 14.8 %collective-permute-done.50 = bf16[256,128]{1,0:T(8,128)(2,1)S(1)} collective-permute-done((bf16[256,128]{1,0:T(8,128)(2,1)S(1)}, bf16[256,128]{1,0:T(8,128)(2,1)S(1)}, u32[]{:S(2)}, u32[]{:S(2)}) %collective-permute-start.50) | collective-permute-done | bytes 65568 | tf_op jit(solution)/shard_map/ppermute | solution.py:419
  284.0 12.6 %collective-permute-done.52 = bf16[256,128]{1,0:T(8,128)(2,1)S(1)} collective-permute-done((bf16[256,128]{1,0:T(8,128)(2,1)S(1)}, bf16[256,128]{1,0:T(8,128)(2,1)S(1)}, u32[]{:S(2)}, u32[]{:S(2)}) %collective-permute-start.52) | collective-permute-done | bytes 65568 | tf_op jit(solution)/shard_map/ppermute | solution.py:419
  314.2 37.5 %collective-permute-done.12 = bf16[512,1024]{1,0:T(8,128)(2,1)S(1)} collective-permute-done((bf16[512,1024]{1,0:T(8,128)(2,1)S(1)}, bf16[512,1024]{1,0:T(8,128)(2,1)S(1)}, u32[]{:S(2)}, u32[]{:S(2)}) %collective-permute-start.12) | collective-permute-done | bytes 1048608 | tf_op jit(solution)/shard_map/ppermute | solution.py:419
  355.9 5.2 collective-permute-done.28
  370.2 19.8 %shard_map.172 = (bf16[2048,128]{1,0:T(8,128)(2,1)S(1)}, bf16[2048,128]{1,0:T(8,128)(2,1)S(1)}, bf16[2048,128]{1,0:T(8,128)(2,1)S(1)}, bf16[2048,128]{1,0:T(8,128)(2,1)S(1)}, f32[2048,128]{1,0:T(8,128)S(1)}) custom-call(s32[8]{0:T(128)S(1)} %get-tuple-element.300.low_ref, bf16[2048,1024]{1,0:T(8,128)(2,1)} %bitcast.700, bf16[1024,384]{1,0:T(8,128)(2,1)S(1)} %bitcast.685, ...), custom_call_target="tpu_custom_call" | custom-call | tf_op jit(solution)/shard_map/pallas_call | solution.py:523
  390.1 3.7 collective-permute-start.57
  399.0 24.1 %shard_map.170 = (bf16[2048,128]{1,0:T(8,128)(2,1)S(1)}, bf16[2048,128]{1,0:T(8,128)(2,1)S(1)}, bf16[2048,128]{1,0:T(8,128)(2,1)S(1)}, bf16[2048,128]{1,0:T(8,128)(2,1)S(1)}, f32[2048,128]{1,0:T(8,128)S(1)}) custom-call(s32[8]{0:T(128)S(1)} %get-tuple-element.302.low_ref, bf16[2048,1024]{1,0:T(8,128)(2,1)} %bitcast.702, bf16[1024,384]{1,0:T(8,128)(2,1)S(1)} %bitcast.686, ...), custom_call_target="tpu_custom_call" | custom-call | tf_op jit(solution)/shard_map/pallas_call | solution.py:523
  436.8 23.8 %shard_map.171 = (bf16[2048,128]{1,0:T(8,128)(2,1)S(1)}, bf16[2048,128]{1,0:T(8,128)(2,1)S(1)}, bf16[2048,128]{1,0:T(8,128)(2,1)S(1)}, bf16[2048,128]{1,0:T(8,128)(2,1)S(1)}, f32[2048,128]{1,0:T(8,128)S(1)}) custom-call(s32[8]{0:T(128)S(1)} %get-tuple-element.301.low_ref, bf16[2048,1024]{1,0:T(8,128)(2,1)} %bitcast.705, bf16[1024,384]{1,0:T(8,128)(2,1)S(1)} %bitcast.687, ...), custom_call_target="tpu_custom_call" | custom-call | tf_op jit(solution)/shard_map/pallas_call | solution.py:523
  462.6 3.7 collective-permute-done.35
  471.7 4.0 collective-permute-done.36
  478.3 4.2 collective-permute-done.41
  483.4 8.4 shard_map.173
  491.8 54.1 %shard_map.174 = (f32[768,1024]{1,0:T(8,128)}, f32[768,1024]{1,0:T(8,128)}, bf16[8,4,2240,128]{3,2,1,0:T(8,128)(2,1)}) custom-call(bf16[768,1024]{1,0:T(8,128)(2,1)} %get-tuple-element.58.n_ref, bf16[768,1024]{1,0:T(8,128)(2,1)} %get-tuple-element.59.dy_ref, bf16[8,4,2496,128]{3,2,1,0:T(8,128)(2,1)} %bitcast.698), custom_call_target="tpu_custom_call" | custom-call | tf_op jit(solution)/shard_map/pallas_call | solution.py:992
  546.4 14.4 %shard_map.175 = (bf16[4,512,256]{2,1,0:T(8,128)(2,1)}, bf16[4,256,256]{2,1,0:T(8,128)(2,1)}, f32[768,1024]{1,0:T(8,128)}, bf16[8,512,128]{2,1,0:T(8,128)(2,1)},...) custom-call(f32[768,1024]{1,0:T(8,128)} %get-tuple-element.57.h_ref, ...), custom_call_target="tpu_custom_call" | custom-call | tf_op jit(solution)/shard_map/pallas_call | solution.py:1024
  576.3 3.1 collective-permute-done.91
  583.0 3.3 collective-permute-done.93
  587.6 4.2 collective-permute-done.94
  594.5 3.4 collective-permute-done.95
  600.5 25.5 %shard_map.178 = (bf16[2048,1024]{1,0:T(8,128)(2,1)}, f32[384,1024]{1,0:T(8,128)}, bf16[2048,128]{1,0:T(8,128)(2,1)}) custom-call(s32[8]{0:T(128)} %copy-done.27, bf16[2048,1024]{1,0:T(8,128)(2,1)} %bitcast.701, bf16[1024,384]{1,0:T(8,128)(2,1)} %bitcast.688, bf16[2048,128]{1,0:T(8,128)(2,1)} %copy-done.21, bf16[2048,128]{1,0:T(8,128)(2,1)} %copy-done.22, ...), custom_call_target="tpu_custom_call" | custom-call | tf_op jit(solution)/shard_map/pallas_call | solution.py:615
  626.0 3.2 dynamic-slice_bitcast_fusion
  649.5 7.1 collective-permute-done.84
  658.8 3.9 collective-permute-done.118
  663.7 5.8 collective-permute-done.119
  671.0 5.3 collective-permute-done.121
  681.2 30.0 %shard_map.177 = (bf16[2048,1024]{1,0:T(8,128)(2,1)}, f32[384,1024]{1,0:T(8,128)}, bf16[2048,128]{1,0:T(8,128)(2,1)}) custom-call(s32[8]{0:T(128)} %copy-done.26, bf16[2048,1024]{1,0:T(8,128)(2,1)} %bitcast.706, bf16[1024,384]{1,0:T(8,128)(2,1)} %bitcast.689, bf16[2048,128]{1,0:T(8,128)(2,1)} %copy-done.18, bf16[2048,128]{1,0:T(8,128)(2,1)} %copy-done.19, ...), custom_call_target="tpu_custom_call" | custom-call | tf_op jit(solution)/shard_map/pallas_call | solution.py:615
  711.2 30.3 %shard_map.176 = (bf16[2048,1024]{1,0:T(8,128)(2,1)}, f32[384,1024]{1,0:T(8,128)}, bf16[2048,128]{1,0:T(8,128)(2,1)}) custom-call(s32[8]{0:T(128)} %copy-done.25, bf16[2048,1024]{1,0:T(8,128)(2,1)} %bitcast.703, bf16[1024,384]{1,0:T(8,128)(2,1)} %bitcast.690, bf16[2048,128]{1,0:T(8,128)(2,1)} %copy-done.15, bf16[2048,128]{1,0:T(8,128)(2,1)} %copy-done.16, ...), custom_call_target="tpu_custom_call" | custom-call | tf_op jit(solution)/shard_map/pallas_call | solution.py:615
  777.3 6.5 collective-permute-done.108
  785.2 4.4 collective-permute-done.109
  792.4 4.0 collective-permute-done.111
  796.8 5.0 collective-permute-done.112
  803.3 5.0 collective-permute-done.113
  808.3 3.3 collective-permute-start.125
  812.3 6.1 collective-permute-done.125
  820.8 4.7 collective-permute-done.126
  838.7 8.6 collective-permute-done.143
  852.7 5.6 collective-permute-done.72
  859.0 5.7 collective-permute-start.145
  869.9 5.8 collective-permute-done.146
  877.8 4.0 collective-permute-done.147
  882.5 9.5 collective-permute-done.136
  893.9 6.9 collective-permute-done.137
  910.3 5.6 fusion
  920.2 5.3 collective-permute-done.115
  934.5 51.1 %collective-permute-done.98 = bf16[256,1024]{1,0:T(8,128)(2,1)S(1)} collective-permute-done((bf16[256,1024]{1,0:T(8,128)(2,1)}, bf16[256,1024]{1,0:T(8,128)(2,1)S(1)}, u32[]{:S(2)}, u32[]{:S(2)}) %collective-permute-start.98) | collective-permute-done | bytes 524320 | tf_op jit(solution)/shard_map/ppermute | solution.py:1081
  986.9 3.9 pad_maximum_fusion.1.bm_ref
  990.8 7.2 shard_map.179
  998.9 4.2 collective-permute-start.103
  1009.4 39.5 %psum.7 = f32[2,1024]{1,0:T(2,128)S(1)} all-reduce(f32[2,1024]{1,0:T(2,128)S(1)} %pad_maximum_fusion.13), channel_id=1, replica_groups=mesh['dp'=2,'head'=4,'ffn'=4] {'dp','ffn','head'}, use_global_device_ids=true, to_apply=%region_6.7 | all-reduce | flops 2048 | bytes 16384 | tf_op jit(solution)/shard_map/psum | solution.py:1114
  1051.0 4.7 collective-permute-done.105
  1060.3 16.9 %collective-permute-done.101 = bf16[512,256]{1,0:T(8,128)(2,1)S(1)} collective-permute-done((bf16[512,256]{1,0:T(8,128)(2,1)S(1)}, bf16[512,256]{1,0:T(8,128)(2,1)S(1)}, u32[]{:S(2)}, u32[]{:S(2)}) %collective-permute-start.101) | collective-permute-done | bytes 262176 | tf_op jit(solution)/shard_map/ppermute | solution.py:419
  (644 shorter events, 336.6 us)
Async XLA Ops:
  7.2 475.3 %all-gather.3.cloned.1.call-start = ((), (), s32[]{:S(2)}) async-start(), calls=%async_computation.4 | async-start | bytes 21086208 | tf_op jit(solution)/shard_map/all_gather | solution.py:870
  9.7 900.6 %reduce-scatter.3.cloned.1.call-start = ((), (), s32[]{:S(2)}) async-start(), calls=%async_computation.2 | async-start | bytes 20643840 | tf_op jit(solution)/shard_map/reduce_scatter | solution.py:1021
  9.8 30.1 %collective-permute-start.8 = (f32[2,256]{1,0:T(2,128)S(1)}, f32[2,256]{1,0:T(2,128)S(1)}, u32[]{:S(2)}, u32[]{:S(2)}) collective-permute-start(f32[2,256]{1,0:T(2,128)S(1)} %pad_maximum_fusion.14), channel_id=1, source_target_pairs={{0,4},{4,0},{8,12},{12,8},{1,5},{5,1},{9,13},{13,9},{2,6},{6,2},{1... | collective-permute-start | bytes 6152 | tf_op jit(solution)/shard_map/ppermute | solution.py:419
  12.9 27.0 %collective-permute-start.9 = (f32[2,256]{1,0:T(2,128)S(1)}, f32[2,256]{1,0:T(2,128)S(1)}, u32[]{:S(2)}, u32[]{:S(2)}) collective-permute-start(f32[2,256]{1,0:T(2,128)S(1)} %pad_maximum_fusion.14), channel_id=1, source_target_pairs={{0,8},{4,12},{8,0},{12,4},{1,9},{5,13},{9,1},{13,5},{2,10},{6,14},... | collective-permute-start | bytes 6152 | tf_op jit(solution)/shard_map/ppermute | solution.py:419
  15.5 24.6 %collective-permute-start.10 = (f32[2,256]{1,0:T(2,128)S(1)}, f32[2,256]{1,0:T(2,128)S(1)}, u32[]{:S(2)}, u32[]{:S(2)}) collective-permute-start(f32[2,256]{1,0:T(2,128)S(1)} %pad_maximum_fusion.14), channel_id=1, source_target_pairs={{0,12},{4,8},{8,4},{12,0},{1,13},{5,9},{9,5},{13,1},{2,14},{6,10},... | collective-permute-start | bytes 6152 | tf_op jit(solution)/shard_map/ppermute | solution.py:419
  15.5 36.3 %collective-permute-start.14 = (bf16[2,3,128,128]{3,2,1,0:T(8,128)(2,1)S(1)}, bf16[2,3,128,128]{3,2,1,0:T(8,128)(2,1)}, u32[]{:S(2)}, u32[]{:S(2)}) collective-permute-start(bf16[2,3,128,128]{3,2,1,0:T(8,128)(2,1)S(1)} %bitcast_bitcast_fusion), channel_id=1, source_target_pairs={{0,4},{4,0},{8,12},{12,8},{1,5},{5,1},{9,13},{13,9},{2,6},{6,2},{1... | collective-permute-start | bytes 589832 | tf_op jit(solution)/shard_map/ppermute | solution.py:419
  16.5 37.0 %collective-permute-start.15 = (bf16[2,3,128,128]{3,2,1,0:T(8,128)(2,1)S(1)}, bf16[2,3,128,128]{3,2,1,0:T(8,128)(2,1)}, u32[]{:S(2)}, u32[]{:S(2)}) collective-permute-start(bf16[2,3,128,128]{3,2,1,0:T(8,128)(2,1)S(1)} %bitcast_bitcast_fusion), channel_id=1, source_target_pairs={{0,8},{4,12},{8,0},{12,4},{1,9},{5,13},{9,1},{13,5},{2,10},{6,14},... | collective-permute-start | bytes 589832 | tf_op jit(solution)/shard_map/ppermute | solution.py:419
  51.8 22.7 %collective-permute-start.1 = (bf16[512,256]{1,0:T(8,128)(2,1)}, bf16[512,256]{1,0:T(8,128)(2,1)S(1)}, u32[]{:S(2)}, u32[]{:S(2)}) collective-permute-start(bf16[512,256]{1,0:T(8,128)(2,1)} %dynamic-slice_bitcast_fusion.37), channel_id=1, source_target_pairs={{0,4},{4,0},{8,12},{12,8},{1,5},{5,1},{9,13},{13,9},{2,6},{6,2},{1... | collective-permute-start | bytes 786440 | tf_op jit(solution)/shard_map/ppermute | solution.py:419
  53.5 35.7 %collective-permute-start.24 = (bf16[512,256]{0,1:T(8,128)(2,1)}, bf16[512,256]{0,1:T(8,128)(2,1)S(1)}, u32[]{:S(2)}, u32[]{:S(2)}) collective-permute-start(bf16[512,256]{0,1:T(8,128)(2,1)} %dynamic-slice_bitcast_fusion.34), channel_id=1, source_target_pairs={{0,4},{4,0},{8,12},{12,8},{1,5},{5,1},{9,13},{13,9},{2,6},{6,2},{1... | collective-permute-start | bytes 786440 | tf_op jit(solution)/shard_map/ppermute | solution.py:419
  57.2 48.0 %collective-permute-start.64 = (bf16[512,256]{1,0:T(8,128)(2,1)S(1)}, bf16[512,256]{1,0:T(8,128)(2,1)S(1)}, u32[]{:S(2)}, u32[]{:S(2)}) collective-permute-start(bf16[512,256]{1,0:T(8,128)(2,1)S(1)} %copy-done.55), channel_id=1, source_target_pairs={{0,4},{4,0},{8,12},{12,8},{1,5},{5,1},{9,13},{13,9},{2,6},{6,2},{1... | collective-permute-start | bytes 786440 | tf_op jit(solution)/shard_map/ppermute | solution.py:419
  58.8 51.1 %collective-permute-start.17 = (bf16[3,128,128]{2,1,0:T(8,128)(2,1)S(1)}, bf16[3,128,128]{2,1,0:T(8,128)(2,1)S(1)}, u32[]{:S(2)}, u32[]{:S(2)}) collective-permute-start(bf16[3,128,128]{2,1,0:T(8,128)(2,1)S(1)} %dynamic-slice_bitcast_fusion.100), channel_id=1, source_target_pairs={{0,1},{1,0},{2,3},{3,2},{16,17},{17,16},{18,19},{19,18},{4,5},{5,4... | collective-permute-start | bytes 294920 | tf_op jit(solution)/shard_map/ppermute | solution.py:419
  61.7 48.4 %collective-permute-start.47 = (bf16[256,256]{1,0:T(8,128)(2,1)S(1)}, bf16[256,256]{1,0:T(8,128)(2,1)S(1)}, u32[]{:S(2)}, u32[]{:S(2)}) collective-permute-start(bf16[256,256]{1,0:T(8,128)(2,1)S(1)} %dynamic-slice_bitcast_fusion.69), channel_id=1, source_target_pairs={{0,4},{4,0},{8,12},{12,8},{1,5},{5,1},{9,13},{13,9},{2,6},{6,2},{1... | collective-permute-start | bytes 393224 | tf_op jit(solution)/shard_map/ppermute | solution.py:419
  74.5 37.5 %collective-permute-start.5 = (bf16[256,256]{1,0:T(8,128)(2,1)S(1)}, bf16[256,256]{1,0:T(8,128)(2,1)S(1)}, u32[]{:S(2)}, u32[]{:S(2)}) collective-permute-start(bf16[256,256]{1,0:T(8,128)(2,1)S(1)} %dynamic-slice_bitcast_fusion.86), channel_id=1, source_target_pairs={{0,4},{4,0},{8,12},{12,8},{1,5},{5,1},{9,13},{13,9},{2,6},{6,2},{1... | collective-permute-start | bytes 393224 | tf_op jit(solution)/shard_map/ppermute | solution.py:419
  89.2 88.0 %collective-permute-start.2 = (bf16[512,256]{1,0:T(8,128)(2,1)S(1)}, bf16[512,256]{1,0:T(8,128)(2,1)S(1)}, u32[]{:S(2)}, u32[]{:S(2)}) collective-permute-start(bf16[512,256]{1,0:T(8,128)(2,1)S(1)} %get-tuple-element.197), channel_id=1, source_target_pairs={{0,8},{4,12},{8,0},{12,4},{1,9},{5,13},{9,1},{13,5},{2,10},{6,14},... | collective-permute-start | bytes 786440 | tf_op jit(solution)/shard_map/ppermute | solution.py:419
  105.2 72.5 %collective-permute-start.3 = (bf16[512,256]{1,0:T(8,128)(2,1)S(1)}, bf16[512,256]{1,0:T(8,128)(2,1)S(1)}, u32[]{:S(2)}, u32[]{:S(2)}) collective-permute-start(bf16[512,256]{1,0:T(8,128)(2,1)S(1)} %get-tuple-element.196), channel_id=1, source_target_pairs={{0,12},{4,8},{8,4},{12,0},{1,13},{5,9},{9,5},{13,1},{2,14},{6,10},... | collective-permute-start | bytes 786440 | tf_op jit(solution)/shard_map/ppermute | solution.py:419
  109.9 68.1 %collective-permute-start.25 = (bf16[512,256]{0,1:T(8,128)(2,1)S(1)}, bf16[512,256]{0,1:T(8,128)(2,1)S(1)}, u32[]{:S(2)}, u32[]{:S(2)}) collective-permute-start(bf16[512,256]{0,1:T(8,128)(2,1)S(1)} %get-tuple-element.194), channel_id=1, source_target_pairs={{0,8},{4,12},{8,0},{12,4},{1,9},{5,13},{9,1},{13,5},{2,10},{6,14},... | collective-permute-start | bytes 786440 | tf_op jit(solution)/shard_map/ppermute | solution.py:419
  110.2 132.9 %collective-permute-start.26 = (bf16[512,256]{0,1:T(8,128)(2,1)S(1)}, bf16[512,256]{0,1:T(8,128)(2,1)S(1)}, u32[]{:S(2)}, u32[]{:S(2)}) collective-permute-start(bf16[512,256]{0,1:T(8,128)(2,1)S(1)} %get-tuple-element.193), channel_id=1, source_target_pairs={{0,12},{4,8},{8,4},{12,0},{1,13},{5,9},{9,5},{13,1},{2,14},{6,10},... | collective-permute-start | bytes 786440 | tf_op jit(solution)/shard_map/ppermute | solution.py:419
  112.1 28.5 %collective-permute-start.68 = (bf16[256,256]{1,0:T(8,128)(2,1)S(1)}, bf16[256,256]{1,0:T(8,128)(2,1)S(1)}, u32[]{:S(2)}, u32[]{:S(2)}) collective-permute-start(bf16[256,256]{1,0:T(8,128)(2,1)S(1)} %dynamic-slice_bitcast_fusion.66), channel_id=1, source_target_pairs={{0,4},{4,0},{8,12},{12,8},{1,5},{5,1},{9,13},{13,9},{2,6},{6,2},{1... | collective-permute-start | bytes 393224 | tf_op jit(solution)/shard_map/ppermute | solution.py:419
  171.3 72.8 %collective-permute-start.65 = (bf16[512,256]{1,0:T(8,128)(2,1)S(1)}, bf16[512,256]{1,0:T(8,128)(2,1)S(1)}, u32[]{:S(2)}, u32[]{:S(2)}) collective-permute-start(bf16[512,256]{1,0:T(8,128)(2,1)S(1)} %get-tuple-element.171), channel_id=1, source_target_pairs={{0,8},{4,12},{8,0},{12,4},{1,9},{5,13},{9,1},{13,5},{2,10},{6,14},... | collective-permute-start | bytes 786440 | tf_op jit(solution)/shard_map/ppermute | solution.py:419
  177.2 73.3 %collective-permute-start.66 = (bf16[512,256]{1,0:T(8,128)(2,1)S(1)}, bf16[512,256]{1,0:T(8,128)(2,1)S(1)}, u32[]{:S(2)}, u32[]{:S(2)}) collective-permute-start(bf16[512,256]{1,0:T(8,128)(2,1)S(1)} %get-tuple-element.170), channel_id=1, source_target_pairs={{0,12},{4,8},{8,4},{12,0},{1,13},{5,9},{9,5},{13,1},{2,14},{6,10},... | collective-permute-start | bytes 786440 | tf_op jit(solution)/shard_map/ppermute | solution.py:419
  177.7 69.5 %collective-permute-start.48 = (bf16[256,256]{1,0:T(8,128)(2,1)S(1)}, bf16[256,256]{1,0:T(8,128)(2,1)S(1)}, u32[]{:S(2)}, u32[]{:S(2)}) collective-permute-start(bf16[256,256]{1,0:T(8,128)(2,1)S(1)} %get-tuple-element.265), channel_id=1, source_target_pairs={{0,8},{4,12},{8,0},{12,4},{1,9},{5,13},{9,1},{13,5},{2,10},{6,14},... | collective-permute-start | bytes 393224 | tf_op jit(solution)/shard_map/ppermute | solution.py:419
  178.1 55.1 %collective-permute-start.6 = (bf16[256,256]{1,0:T(8,128)(2,1)S(1)}, bf16[256,256]{1,0:T(8,128)(2,1)S(1)}, u32[]{:S(2)}, u32[]{:S(2)}) collective-permute-start(bf16[256,256]{1,0:T(8,128)(2,1)S(1)} %get-tuple-element.268), channel_id=1, source_target_pairs={{0,8},{4,12},{8,0},{12,4},{1,9},{5,13},{9,1},{13,5},{2,10},{6,14},... | collective-permute-start | bytes 393224 | tf_op jit(solution)/shard_map/ppermute | solution.py:419
  247.2 55.8 %collective-permute-start.42 = (bf16[256,1024]{1,0:T(8,128)(2,1)}, bf16[256,1024]{1,0:T(8,128)(2,1)}, u32[]{:S(2)}, u32[]{:S(2)}) collective-permute-start(bf16[256,1024]{1,0:T(8,128)(2,1)} %get-tuple-element.55), channel_id=1, source_target_pairs={{0,1},{1,0},{2,3},{3,2},{4,5},{5,4},{6,7},{7,6},{8,9},{9,8},{10,11... | collective-permute-start | bytes 1572872 | tf_op jit(solution)/shard_map/ppermute | solution.py:419
  248.7 59.2 %collective-permute-start.43 = (bf16[256,1024]{1,0:T(8,128)(2,1)}, bf16[256,1024]{1,0:T(8,128)(2,1)}, u32[]{:S(2)}, u32[]{:S(2)}) collective-permute-start(bf16[256,1024]{1,0:T(8,128)(2,1)} %get-tuple-element.55), channel_id=1, source_target_pairs={{0,2},{1,3},{2,0},{3,1},{4,6},{5,7},{6,4},{7,5},{8,10},{9,11},{10,... | collective-permute-start | bytes 1572872 | tf_op jit(solution)/shard_map/ppermute | solution.py:419
  250.5 59.1 %collective-permute-start.44 = (bf16[256,1024]{1,0:T(8,128)(2,1)}, bf16[256,1024]{1,0:T(8,128)(2,1)}, u32[]{:S(2)}, u32[]{:S(2)}) collective-permute-start(bf16[256,1024]{1,0:T(8,128)(2,1)} %get-tuple-element.55), channel_id=1, source_target_pairs={{0,3},{1,2},{2,1},{3,0},{4,7},{5,6},{6,5},{7,4},{8,11},{9,10},{10,... | collective-permute-start | bytes 1572872 | tf_op jit(solution)/shard_map/ppermute | solution.py:419
  254.4 20.5 %collective-permute-start.50 = (bf16[256,128]{1,0:T(8,128)(2,1)S(1)}, bf16[256,128]{1,0:T(8,128)(2,1)S(1)}, u32[]{:S(2)}, u32[]{:S(2)}) collective-permute-start(bf16[256,128]{1,0:T(8,128)(2,1)S(1)} %fusion.5), channel_id=1, source_target_pairs={{0,1},{1,0},{2,3},{3,2},{16,17},{17,16},{18,19},{19,18},{4,5},{5,4... | collective-permute-start | bytes 196616 | tf_op jit(solution)/shard_map/ppermute | solution.py:419
  259.6 51.2 %collective-permute-start.11 = (bf16[512,1024]{1,0:T(8,128)(2,1)S(1)}, bf16[512,1024]{1,0:T(8,128)(2,1)S(1)}, u32[]{:S(2)}, u32[]{:S(2)}) collective-permute-start(bf16[512,1024]{1,0:T(8,128)(2,1)S(1)} %copy-done.14), channel_id=1, source_target_pairs={{0,1},{1,0},{2,3},{3,2},{4,5},{5,4},{6,7},{7,6},{8,9},{9,8},{10,11... | collective-permute-start | bytes 3145736 | tf_op jit(solution)/shard_map/ppermute | solution.py:419
  301.9 49.8 %collective-permute-start.12 = (bf16[512,1024]{1,0:T(8,128)(2,1)S(1)}, bf16[512,1024]{1,0:T(8,128)(2,1)S(1)}, u32[]{:S(2)}, u32[]{:S(2)}) collective-permute-start(bf16[512,1024]{1,0:T(8,128)(2,1)S(1)} %copy-done.14), channel_id=1, source_target_pairs={{0,2},{1,3},{2,0},{3,1},{4,6},{5,7},{6,4},{7,5},{8,10},{9,11},{10,... | collective-permute-start | bytes 3145736 | tf_op jit(solution)/shard_map/ppermute | solution.py:419
  302.9 48.9 %collective-permute-start.13 = (bf16[512,1024]{1,0:T(8,128)(2,1)S(1)}, bf16[512,1024]{1,0:T(8,128)(2,1)S(1)}, u32[]{:S(2)}, u32[]{:S(2)}) collective-permute-start(bf16[512,1024]{1,0:T(8,128)(2,1)S(1)} %copy-done.14), channel_id=1, source_target_pairs={{0,3},{1,2},{2,1},{3,0},{4,7},{5,6},{6,5},{7,4},{8,11},{9,10},{10,... | collective-permute-start | bytes 3145736 | tf_op jit(solution)/shard_map/ppermute | solution.py:419
  307.9 44.7 %collective-permute-start.27 = (bf16[512,128]{1,0:T(8,128)(2,1)S(1)}, bf16[512,128]{1,0:T(8,128)(2,1)S(1)}, u32[]{:S(2)}, u32[]{:S(2)}) collective-permute-start(bf16[512,128]{1,0:T(8,128)(2,1)S(1)} %dynamic-slice_bitcast_fusion.83), channel_id=1, source_target_pairs={{0,1},{1,0},{2,3},{3,2},{16,17},{17,16},{18,19},{19,18},{4,5},{5,4... | collective-permute-start | bytes 393224 | tf_op jit(solution)/shard_map/ppermute | solution.py:419
  309.6 42.9 %collective-permute-start.55 = (bf16[256,128]{1,0:T(8,128)(2,1)S(1)}, bf16[256,128]{1,0:T(8,128)(2,1)S(1)}, u32[]{:S(2)}, u32[]{:S(2)}) collective-permute-start(bf16[256,128]{1,0:T(8,128)(2,1)S(1)} %get-tuple-element.258), channel_id=1, source_target_pairs={{0,18},{1,19},{2,16},{3,17},{16,2},{17,3},{18,0},{19,1},{4,22},{5,... | collective-permute-start | bytes 196616 | tf_op jit(solution)/shard_map/ppermute | solution.py:419
  310.8 42.4 %collective-permute-start.56 = (bf16[256,128]{1,0:T(8,128)(2,1)S(1)}, bf16[256,128]{1,0:T(8,128)(2,1)S(1)}, u32[]{:S(2)}, u32[]{:S(2)}) collective-permute-start(bf16[256,128]{1,0:T(8,128)(2,1)S(1)} %get-tuple-element.257), channel_id=1, source_target_pairs={{0,19},{1,18},{2,17},{3,16},{16,3},{17,2},{18,1},{19,0},{4,23},{5,... | collective-permute-start | bytes 196616 | tf_op jit(solution)/shard_map/ppermute | solution.py:419
  352.0 82.7 %collective-permute-start.34 = (bf16[4,512,1024]{2,1,0:T(8,128)(2,1)S(1)}, bf16[4,512,1024]{2,1,0:T(8,128)(2,1)S(1)}, u32[]{:S(2)}, u32[]{:S(2)}) collective-permute-start(bf16[4,512,1024]{2,1,0:T(8,128)(2,1)S(1)} %bitcast_dynamic-update-slice_fusion), channel_id=1, source_target_pairs={{0,16},{16,0},{1,17},{17,1},{2,18},{18,2},{3,19},{19,3},{4,20},{20... | collective-permute-start | bytes 12582920 | tf_op jit(solution)/shard_map/ppermute | solution.py:425
  362.9 30.9 %collective-permute-start.33 = (bf16[512,128]{1,0:T(8,128)(2,1)S(1)}, bf16[512,128]{1,0:T(8,128)(2,1)S(1)}, u32[]{:S(2)}, u32[]{:S(2)}) collective-permute-start(bf16[512,128]{1,0:T(8,128)(2,1)S(1)} %get-tuple-element.186), channel_id=1, source_target_pairs={{0,19},{1,18},{2,17},{3,16},{16,3},{17,2},{18,1},{19,0},{4,23},{5,... | collective-permute-start | bytes 393224 | tf_op jit(solution)/shard_map/ppermute | solution.py:419
  396.3 32.6 %collective-permute-start.58 = (bf16[256,128]{1,0:T(8,128)(2,1)S(1)}, bf16[256,128]{1,0:T(8,128)(2,1)S(1)}, u32[]{:S(2)}, u32[]{:S(2)}) collective-permute-start(bf16[256,128]{1,0:T(8,128)(2,1)S(1)} %get-tuple-element.255), channel_id=1, source_target_pairs={{0,2},{1,3},{2,0},{3,1},{16,18},{17,19},{18,16},{19,17},{4,6},{5,7... | collective-permute-start | bytes 196616 | tf_op jit(solution)/shard_map/ppermute | solution.py:419
  428.9 33.1 %collective-permute-start.62 = (bf16[256,128]{1,0:T(8,128)(2,1)S(1)}, bf16[256,128]{1,0:T(8,128)(2,1)S(1)}, u32[]{:S(2)}, u32[]{:S(2)}) collective-permute-start(bf16[256,128]{1,0:T(8,128)(2,1)S(1)} %get-tuple-element.251), channel_id=1, source_target_pairs={{0,18},{1,19},{2,16},{3,17},{16,2},{17,3},{18,0},{19,1},{4,22},{5,... | collective-permute-start | bytes 196616 | tf_op jit(solution)/shard_map/ppermute | solution.py:419
  431.6 35.9 %collective-permute-start.63 = (bf16[256,128]{1,0:T(8,128)(2,1)S(1)}, bf16[256,128]{1,0:T(8,128)(2,1)S(1)}, u32[]{:S(2)}, u32[]{:S(2)}) collective-permute-start(bf16[256,128]{1,0:T(8,128)(2,1)S(1)} %get-tuple-element.250), channel_id=1, source_target_pairs={{0,19},{1,18},{2,17},{3,16},{16,3},{17,2},{18,1},{19,0},{4,23},{5,... | collective-permute-start | bytes 196616 | tf_op jit(solution)/shard_map/ppermute | solution.py:419
  545.9 532.7 %reduce-scatter.5.cloned.1.call-start = ((), (), s32[]{:S(2)}) async-start(), calls=%async_computation.3 | async-start | bytes 2867200 | tf_op jit(solution)/shard_map/reduce_scatter | solution.py:1022
  562.6 67.8 %collective-permute-start.78 = (bf16[512,128]{1,0:T(8,128)(2,1)S(1)}, bf16[512,128]{1,0:T(8,128)(2,1)S(1)}, u32[]{:S(2)}, u32[]{:S(2)}) collective-permute-start(bf16[512,128]{1,0:T(8,128)(2,1)S(1)} %dynamic-slice_bitcast_fusion.60), channel_id=1, source_target_pairs={{0,1},{1,0},{2,3},{3,2},{16,17},{17,16},{18,19},{19,18},{4,5},{5,4... | collective-permute-start | bytes 393224 | tf_op jit(solution)/shard_map/ppermute | solution.py:419
  566.4 187.4 %collective-permute-start.138 = (bf16[4,256,128]{2,1,0:T(8,128)(2,1)}, bf16[4,256,128]{2,1,0:T(8,128)(2,1)}, u32[]{:S(2)}, u32[]{:S(2)}) collective-permute-start(bf16[4,256,128]{2,1,0:T(8,128)(2,1)} %dynamic-slice_bitcast_fusion.19), channel_id=1, source_target_pairs={{0,1},{1,0},{2,3},{3,2},{16,17},{17,16},{18,19},{19,18},{4,5},{5,4... | collective-permute-start | bytes 786440 | tf_op jit(solution)/shard_map/ppermute | solution.py:419
  568.1 189.2 %collective-permute-start.71 = (bf16[512,256]{1,0:T(8,128)(2,1)}, bf16[512,256]{1,0:T(8,128)(2,1)S(1)}, u32[]{:S(2)}, u32[]{:S(2)}) collective-permute-start(bf16[512,256]{1,0:T(8,128)(2,1)} %dynamic-slice_bitcast_fusion.28), channel_id=1, source_target_pairs={{0,4},{4,0},{8,12},{12,8},{1,5},{5,1},{9,13},{13,9},{2,6},{6,2},{1... | collective-permute-start | bytes 786440 | tf_op jit(solution)/shard_map/ppermute | solution.py:419
  570.0 61.4 %collective-permute-start.74 = (bf16[256,256]{1,0:T(8,128)(2,1)S(1)}, bf16[256,256]{1,0:T(8,128)(2,1)S(1)}, u32[]{:S(2)}, u32[]{:S(2)}) collective-permute-start(bf16[256,256]{1,0:T(8,128)(2,1)S(1)} %dynamic-slice_bitcast_fusion.63), channel_id=1, source_target_pairs={{0,4},{4,0},{8,12},{12,8},{1,5},{5,1},{9,13},{13,9},{2,6},{6,2},{1... | collective-permute-start | bytes 393224 | tf_op jit(solution)/shard_map/ppermute | solution.py:419
  629.3 276.0 %collective-permute-start.96 = (bf16[4,256,1024]{2,1,0:T(8,128)(2,1)}, bf16[4,256,1024]{2,1,0:T(8,128)(2,1)}, u32[]{:S(2)}, u32[]{:S(2)}) collective-permute-start(bf16[4,256,1024]{2,1,0:T(8,128)(2,1)} %dynamic-slice_bitcast_fusion), channel_id=1, source_target_pairs={{0,16},{16,0},{1,17},{17,1},{2,18},{18,2},{3,19},{19,3},{4,20},{20... | collective-permute-start | bytes 6291464 | tf_op jit(solution)/shard_map/ppermute | solution.py:425
  649.5 93.6 %collective-permute-start.75 = (bf16[256,256]{1,0:T(8,128)(2,1)S(1)}, bf16[256,256]{1,0:T(8,128)(2,1)S(1)}, u32[]{:S(2)}, u32[]{:S(2)}) collective-permute-start(bf16[256,256]{1,0:T(8,128)(2,1)S(1)} %get-tuple-element.245), channel_id=1, source_target_pairs={{0,8},{4,12},{8,0},{12,4},{1,9},{5,13},{9,1},{13,5},{2,10},{6,14},... | collective-permute-start | bytes 393224 | tf_op jit(solution)/shard_map/ppermute | solution.py:419
  680.0 61.4 %collective-permute-start.123 = (bf16[256,128]{1,0:T(8,128)(2,1)S(1)}, bf16[256,128]{1,0:T(8,128)(2,1)S(1)}, u32[]{:S(2)}, u32[]{:S(2)}) collective-permute-start(bf16[256,128]{1,0:T(8,128)(2,1)S(1)} %get-tuple-element.227), channel_id=1, source_target_pairs={{0,19},{1,18},{2,17},{3,16},{16,3},{17,2},{18,1},{19,0},{4,23},{5,... | collective-permute-start | bytes 196616 | tf_op jit(solution)/shard_map/ppermute | solution.py:419
  743.0 167.3 %collective-permute-start.85 = (bf16[4,512,1024]{2,1,0:T(8,128)(2,1)}, bf16[4,512,1024]{2,1,0:T(8,128)(2,1)}, u32[]{:S(2)}, u32[]{:S(2)}) collective-permute-start(bf16[4,512,1024]{2,1,0:T(8,128)(2,1)} %bitcast.766), channel_id=1, source_target_pairs={{0,16},{16,0},{1,17},{17,1},{2,18},{18,2},{3,19},{19,3},{4,20},{20... | collective-permute-start | bytes 12582920 | tf_op jit(solution)/shard_map/ppermute | solution.py:425
  769.2 59.0 %collective-permute-start.77 = (bf16[2,256,256]{2,1,0:T(8,128)(2,1)}, bf16[2,256,256]{2,1,0:T(8,128)(2,1)}, u32[]{:S(2)}, u32[]{:S(2)}) collective-permute-start(bf16[2,256,256]{2,1,0:T(8,128)(2,1)} %broadcast_select_fusion.10), channel_id=1, source_target_pairs={{0,16},{16,0},{1,17},{17,1},{2,18},{18,2},{3,19},{19,3},{4,20},{20... | collective-permute-start | bytes 786440 | tf_op jit(solution)/shard_map/ppermute | solution.py:425
  772.4 57.6 %collective-permute-start.139 = (bf16[4,256,128]{2,1,0:T(8,128)(2,1)}, bf16[4,256,128]{2,1,0:T(8,128)(2,1)}, u32[]{:S(2)}, u32[]{:S(2)}) collective-permute-start(bf16[4,256,128]{2,1,0:T(8,128)(2,1)} %get-tuple-element.133), channel_id=1, source_target_pairs={{0,2},{1,3},{2,0},{3,1},{16,18},{17,19},{18,16},{19,17},{4,6},{5,7... | collective-permute-start | bytes 786440 | tf_op jit(solution)/shard_map/ppermute | solution.py:419
  838.0 20.3 %collective-permute-start.72 = (bf16[512,256]{1,0:T(8,128)(2,1)S(1)}, bf16[512,256]{1,0:T(8,128)(2,1)S(1)}, u32[]{:S(2)}, u32[]{:S(2)}) collective-permute-start(bf16[512,256]{1,0:T(8,128)(2,1)S(1)} %copy-done.54), channel_id=1, source_target_pairs={{0,8},{4,12},{8,0},{12,4},{1,9},{5,13},{9,1},{13,5},{2,10},{6,14},... | collective-permute-start | bytes 786440 | tf_op jit(solution)/shard_map/ppermute | solution.py:419
  850.0 19.7 %collective-permute-start.135 = (bf16[128,3,256]{0,2,1:T(8,128)(2,1)S(1)}, bf16[128,3,256]{0,2,1:T(8,128)(2,1)S(1)}, u32[]{:S(2)}, u32[]{:S(2)}) collective-permute-start(bf16[128,3,256]{0,2,1:T(8,128)(2,1)S(1)} %dynamic-slice_bitcast_fusion.40), channel_id=1, source_target_pairs={{0,4},{4,0},{8,12},{12,8},{1,5},{5,1},{9,13},{13,9},{2,6},{6,2},{1... | collective-permute-start | bytes 589832 | tf_op jit(solution)/shard_map/ppermute | solution.py:419
  858.3 42.5 %collective-permute-start.114 = (bf16[512,256]{0,1:T(8,128)(2,1)}, bf16[512,256]{0,1:T(8,128)(2,1)S(1)}, u32[]{:S(2)}, u32[]{:S(2)}) collective-permute-start(bf16[512,256]{0,1:T(8,128)(2,1)} %dynamic-slice_bitcast_fusion.22), channel_id=1, source_target_pairs={{0,4},{4,0},{8,12},{12,8},{1,5},{5,1},{9,13},{13,9},{2,6},{6,2},{1... | collective-permute-start | bytes 786440 | tf_op jit(solution)/shard_map/ppermute | solution.py:419
  869.7 49.3 %collective-permute-start.127 = (bf16[2,256,256]{2,1,0:T(8,128)(2,1)}, bf16[2,256,256]{2,1,0:T(8,128)(2,1)}, u32[]{:S(2)}, u32[]{:S(2)}) collective-permute-start(bf16[2,256,256]{2,1,0:T(8,128)(2,1)} %broadcast_select_fusion.2), channel_id=1, source_target_pairs={{0,16},{16,0},{1,17},{17,1},{2,18},{18,2},{3,19},{19,3},{4,20},{20... | collective-permute-start | bytes 786440 | tf_op jit(solution)/shard_map/ppermute | solution.py:425
  901.6 23.9 %collective-permute-start.115 = (bf16[512,256]{0,1:T(8,128)(2,1)S(1)}, bf16[512,256]{0,1:T(8,128)(2,1)}, u32[]{:S(2)}, u32[]{:S(2)}) collective-permute-start(bf16[512,256]{0,1:T(8,128)(2,1)S(1)} %get-tuple-element.146), channel_id=1, source_target_pairs={{0,8},{4,12},{8,0},{12,4},{1,9},{5,13},{9,1},{13,5},{2,10},{6,14},... | collective-permute-start | bytes 786440 | tf_op jit(solution)/shard_map/ppermute | solution.py:419
  903.4 25.0 %collective-permute-start.116 = (bf16[512,256]{0,1:T(8,128)(2,1)}, bf16[512,256]{0,1:T(8,128)(2,1)}, u32[]{:S(2)}, u32[]{:S(2)}) collective-permute-start(bf16[512,256]{0,1:T(8,128)(2,1)} %get-tuple-element.145), channel_id=1, source_target_pairs={{0,12},{4,8},{8,4},{12,0},{1,13},{5,9},{9,5},{13,1},{2,14},{6,10},... | collective-permute-start | bytes 786440 | tf_op jit(solution)/shard_map/ppermute | solution.py:419
  909.2 20.5 %collective-permute-start.97 = (bf16[256,1024]{1,0:T(8,128)(2,1)}, bf16[256,1024]{1,0:T(8,128)(2,1)S(1)}, u32[]{:S(2)}, u32[]{:S(2)}) collective-permute-start(bf16[256,1024]{1,0:T(8,128)(2,1)} %get-tuple-element.135), channel_id=1, source_target_pairs={{0,1},{1,0},{2,3},{3,2},{4,5},{5,4},{6,7},{7,6},{8,9},{9,8},{10,11... | collective-permute-start | bytes 1572872 | tf_op jit(solution)/shard_map/ppermute | solution.py:1081
  918.0 68.9 %collective-permute-start.86 = (bf16[512,1024]{1,0:T(8,128)(2,1)}, bf16[512,1024]{1,0:T(8,128)(2,1)}, u32[]{:S(2)}, u32[]{:S(2)}) collective-permute-start(bf16[512,1024]{1,0:T(8,128)(2,1)} %get-tuple-element.122), channel_id=1, source_target_pairs={{0,1},{1,0},{2,3},{3,2},{4,5},{5,4},{6,7},{7,6},{8,9},{9,8},{10,11... | collective-permute-start | bytes 3145736 | tf_op jit(solution)/shard_map/ppermute | solution.py:1081
  918.9 68.0 %collective-permute-start.87 = (bf16[512,1024]{1,0:T(8,128)(2,1)}, bf16[512,1024]{1,0:T(8,128)(2,1)}, u32[]{:S(2)}, u32[]{:S(2)}) collective-permute-start(bf16[512,1024]{1,0:T(8,128)(2,1)} %get-tuple-element.124), channel_id=1, source_target_pairs={{0,2},{1,3},{2,0},{3,1},{4,6},{5,7},{6,4},{7,5},{8,10},{9,11},{10,... | collective-permute-start | bytes 3145736 | tf_op jit(solution)/shard_map/ppermute | solution.py:1081
  925.5 61.4 %collective-permute-start.88 = (bf16[512,1024]{1,0:T(8,128)(2,1)}, bf16[512,1024]{1,0:T(8,128)(2,1)}, u32[]{:S(2)}, u32[]{:S(2)}) collective-permute-start(bf16[512,1024]{1,0:T(8,128)(2,1)} %get-tuple-element.123), channel_id=1, source_target_pairs={{0,3},{1,2},{2,1},{3,0},{4,7},{5,6},{6,5},{7,4},{8,11},{9,10},{10,... | collective-permute-start | bytes 3145736 | tf_op jit(solution)/shard_map/ppermute | solution.py:1081
  928.5 57.1 %collective-permute-start.98 = (bf16[256,1024]{1,0:T(8,128)(2,1)}, bf16[256,1024]{1,0:T(8,128)(2,1)S(1)}, u32[]{:S(2)}, u32[]{:S(2)}) collective-permute-start(bf16[256,1024]{1,0:T(8,128)(2,1)} %get-tuple-element.137), channel_id=1, source_target_pairs={{0,2},{1,3},{2,0},{3,1},{4,6},{5,7},{6,4},{7,5},{8,10},{9,11},{10,... | collective-permute-start | bytes 1572872 | tf_op jit(solution)/shard_map/ppermute | solution.py:1081
  929.7 55.9 %collective-permute-start.99 = (bf16[256,1024]{1,0:T(8,128)(2,1)}, bf16[256,1024]{1,0:T(8,128)(2,1)S(1)}, u32[]{:S(2)}, u32[]{:S(2)}) collective-permute-start(bf16[256,1024]{1,0:T(8,128)(2,1)} %get-tuple-element.136), channel_id=1, source_target_pairs={{0,3},{1,2},{2,1},{3,0},{4,7},{5,6},{6,5},{7,4},{8,11},{9,10},{10,... | collective-permute-start | bytes 1572872 | tf_op jit(solution)/shard_map/ppermute | solution.py:1081
  1006.8 44.1 %collective-permute-start.104 = (bf16[256,256]{1,0:T(8,128)(2,1)S(1)}, bf16[256,256]{1,0:T(8,128)(2,1)S(1)}, u32[]{:S(2)}, u32[]{:S(2)}) collective-permute-start(bf16[256,256]{1,0:T(8,128)(2,1)S(1)} %get-tuple-element.235), channel_id=1, source_target_pairs={{0,8},{4,12},{8,0},{12,4},{1,9},{5,13},{9,1},{13,5},{2,10},{6,14},... | collective-permute-start | bytes 393224 | tf_op jit(solution)/shard_map/ppermute | solution.py:419
  1009.0 46.9 %collective-permute-start.100 = (bf16[512,256]{1,0:T(8,128)(2,1)S(1)}, bf16[512,256]{1,0:T(8,128)(2,1)S(1)}, u32[]{:S(2)}, u32[]{:S(2)}) collective-permute-start(bf16[512,256]{1,0:T(8,128)(2,1)S(1)} %dynamic-slice_bitcast_fusion.25), channel_id=1, source_target_pairs={{0,4},{4,0},{8,12},{12,8},{1,5},{5,1},{9,13},{13,9},{2,6},{6,2},{1... | collective-permute-start | bytes 786440 | tf_op jit(solution)/shard_map/ppermute | solution.py:419
  1055.9 21.3 %collective-permute-start.101 = (bf16[512,256]{1,0:T(8,128)(2,1)S(1)}, bf16[512,256]{1,0:T(8,128)(2,1)S(1)}, u32[]{:S(2)}, u32[]{:S(2)}) collective-permute-start(bf16[512,256]{1,0:T(8,128)(2,1)S(1)} %get-tuple-element.156), channel_id=1, source_target_pairs={{0,8},{4,12},{8,0},{12,4},{1,9},{5,13},{9,1},{13,5},{2,10},{6,14},... | collective-permute-start | bytes 786440 | tf_op jit(solution)/shard_map/ppermute | solution.py:419
  1058.5 18.8 %collective-permute-start.102 = (bf16[512,256]{1,0:T(8,128)(2,1)S(1)}, bf16[512,256]{1,0:T(8,128)(2,1)S(1)}, u32[]{:S(2)}, u32[]{:S(2)}) collective-permute-start(bf16[512,256]{1,0:T(8,128)(2,1)S(1)} %get-tuple-element.155), channel_id=1, source_target_pairs={{0,12},{4,8},{8,4},{12,0},{1,13},{5,9},{9,5},{13,1},{2,14},{6,10},... | collective-permute-start | bytes 786440 | tf_op jit(solution)/shard_map/ppermute | solution.py:419
  (154 other events, 2778.3 us)
Sparse Core Ops, SparseCore 0:
  11.4 220.1 all-gather.2
  546.0 134.2 reduce-scatter.2
  910.4 50.4 reduce-scatter.4

commit v2 on v0

--- a/solution.py
+++ b/solution.py
@@ -1,8 +1,11 @@
+import functools
 import math
 
 import jax
 import jax.numpy as jnp
 from jax import lax
+from jax.experimental import pallas as pl
+from jax.experimental.pallas import tpu as pltpu
 from jax.sharding import PartitionSpec as P
 
 HD = 64
@@ -394,6 +397,893 @@
     )
 
 
+BF16 = jnp.bfloat16
+F32 = jnp.float32
+BQ = 512
+BK = 512
+MASKED_SCORE = -1e30
+
+
+def matmul(former, latter):
+    return lax.dot_general(former, latter, (((1,), (0,)), ((), ())), preferred_element_type=F32)
+
+
+def compiler_params(mib):
+    return pltpu.CompilerParams(vmem_limit_bytes=mib * 1024 * 1024)
+
+
+def exchange(blocks, axes):
+    return lax.all_to_all(blocks, axes, 0, 0, tiled=True)
+
+
+def send_line(blocks, axis="head"):
+    count = blocks.shape[0]
+    me = lax.axis_index(axis)
+    got = []
+    for step in range(1, count):
+        send = lax.dynamic_index_in_dim(blocks, me ^ step, 0, keepdims=False)
+        got.append(lax.ppermute(send, axis, [(j, j ^ step) for j in range(count)]))
+    return blocks, got
+
+
+def join_line(blocks, got, axis="head"):
+    me = lax.axis_index(axis)
+    got = after(*got)
+    for step, piece in enumerate(got):
+        blocks = lax.dynamic_update_index_in_dim(blocks, piece, me ^ (step + 1), 0)
+    return blocks
+
+
+def exchange_line(blocks, axis="head"):
+    return join_line(*send_line(blocks, axis), axis)
+
+
+def after(values, *earlier):
+    return lax.optimization_barrier((values, *earlier))
+
+
+def send_across(blocks):
+    count = blocks.shape[0]
+    me = lax.axis_index("ffn")
+    got = []
+    for step in range(count):
+        pairs = []
+        for j in range(count * count):
+            h, f = divmod(j, count)
+            pairs.append((j, (f ^ step) * count + h))
+        send = lax.dynamic_index_in_dim(blocks, me ^ step, 0, keepdims=False)
+        got.append(lax.ppermute(send, ("head", "ffn"), pairs))
+    return got
+
+
+def join_across(got):
+    here = lax.axis_index("head")
+    a, b, c, d = after(*got)
+    return jnp.where(
+        here % 2 == 0,
+        jnp.where(here < 2, jnp.stack([a, b, c, d]), jnp.stack([c, d, a, b])),
+        jnp.where(here < 2, jnp.stack([b, a, d, c]), jnp.stack([d, c, b, a])),
+    )
+
+
+def swap(values):
+    return lax.ppermute(values, "dp", [(0, 1), (1, 0)])
+
+
+def swap_halves(values):
+    low = (lax.broadcasted_iota(jnp.int32, values.shape, 1) % HD) < HD // 2
+    lanes = values.shape[1]
+    return jnp.where(
+        low, pltpu.roll(values, lanes - HD // 2, 1), pltpu.roll(values, HD // 2, 1)
+    )
+
+
+def norm_kernel(x_ref, gain_ref, main_ref, shared_ref):
+    blocks, rows, width = x_ref.shape
+    for start in range(0, rows, 256):
+        part = pl.ds(start, 256)
+        values = [x_ref[b, part, :].astype(F32) for b in range(blocks)]
+        total = sum(jnp.sum(v * v, axis=1, keepdims=True) for v in values)
+        factor = lax.rsqrt(total / (width * blocks) + EPSILON)
+        out_ref, base = main_ref, 0
+        if start >= main_ref.shape[1]:
+            out_ref, base = shared_ref, main_ref.shape[1]
+        for b in range(blocks):
+            cols = pl.ds(b * width, width)
+            normed = (values[b] * factor * gain_ref[:, cols]).astype(BF16)
+            for copy in range(out_ref.shape[0]):
+                out_ref[copy, start - base : start - base + 256, cols] = normed
+
+
+def normalized(x, gain, copies, length):
+    shapes = [(copies, r, gain.shape[1]) for r in (length, x.shape[1] - length)]
+    return pl.pallas_call(
+        norm_kernel,
+        grid=(1,),
+        out_shape=tuple(jax.ShapeDtypeStruct(s, BF16) for s in shapes),
+        in_specs=[once(x.shape), once(gain.shape)],
+        out_specs=tuple(once(s) for s in shapes),
+        compiler_params=compiler_params(48),
+    )(x, gain)
+
+
+def head_masks():
+    lane = lax.broadcasted_iota(jnp.int32, (1, 2 * HD), 1)
+    first = jnp.where(lane < HD, 1.0, 0.0).astype(BF16)
+    return first, (1.0 - first.astype(F32)).astype(BF16)
+
+
+def row_chunks(refs, side_ref):
+    rows = refs[0].shape[1]
+    chunks = []
+    for number, ref in enumerate(refs):
+        for block in range(ref.shape[0]):
+            at = block * rows * len(refs)
+            if len(refs) == 2:
+                half = side_ref[0] if number == 0 else 1 - side_ref[0]
+                at = pl.multiple_of(at + half * rows, rows)
+            chunks.append((number, block, pl.ds(at, rows)))
+    return chunks
+
+
+def attend_kernel(count, side_ref, low_ref, *refs):
+    n_refs, fv_refs = refs[:count], refs[count : 2 * count]
+    w_ref, start_ref, cos_ref, sin_ref, q_ref, k_ref, v_ref, o_ref, lse_ref = refs[2 * count :]
+    length = q_ref.shape[0]
+    lanes = 2 * HD
+    for number, block, rows in row_chunks(n_refs, side_ref):
+        made = matmul(n_refs[number][block], w_ref[...])
+        cos, sin = cos_ref[rows, :], sin_ref[rows, :]
+        q = made[:, :lanes]
+        k = made[:, lanes : 2 * lanes]
+        q_ref[rows, :] = ((q * cos + swap_halves(q) * sin) * (1.0 / math.sqrt(HD))).astype(BF16)
+        k_ref[rows, :] = (k * cos + swap_halves(k) * sin).astype(BF16)
+        first = fv_refs[number][block].astype(F32)
+        v_ref[rows, :] = (0.5 * made[:, 2 * lanes :] + 0.5 * first).astype(BF16)
+    mask_a, mask_b = head_masks()
+    lane = lax.broadcasted_iota(jnp.int32, (BQ, lanes), 1)
+    for i in range(length // BQ):
+        rows = pl.ds(i * BQ, BQ)
+        q = q_ref[rows, :]
+        both = jnp.concatenate([q * mask_a, q * mask_b], axis=0)
+        start = start_ref[rows, :]
+        start = jnp.concatenate([start, start], axis=0)
+        place = i * BQ + lax.broadcasted_iota(jnp.int32, (BQ, 1), 0)
+        place = jnp.concatenate([place, place], axis=0)
+
+        def step(j, carry):
+            top, total, acc = carry
+            keys = pl.ds(pl.multiple_of(j * BK, BK), BK)
+            s = contract_last(both, k_ref[keys, :])
+            key = j * BK + lax.broadcasted_iota(jnp.int32, s.shape, 1)
+            s = jnp.where((key >= start) & (key <= place), s, MASKED_SCORE)
+            new_top = jnp.maximum(top, jnp.max(s, axis=1, keepdims=True))
+            p = jnp.exp(s - new_top)
+            scale = jnp.exp(top - new_top)
+            total = total * scale + jnp.sum(p, axis=1, keepdims=True)
+            acc = acc * scale + matmul(p.astype(BF16), v_ref[keys, :])
+            return new_top, total, acc
+
+        top, total, acc = lax.fori_loop(
+            low_ref[i],
+            (i * BQ + BQ - 1) // BK + 1,
+            step,
+            (
+                jnp.full((2 * BQ, 1), MASKED_SCORE, F32),
+                jnp.zeros((2 * BQ, 1), F32),
+                jnp.zeros((2 * BQ, lanes), F32),
+            ),
+        )
+        acc = acc / total
+        lse = top + jnp.log(total)
+        o_ref[rows, :] = jnp.where(lane < HD, acc[:BQ], acc[BQ:]).astype(BF16)
+        lse_ref[rows, :] = jnp.where(
+            lane < HD, jnp.broadcast_to(lse[:BQ], (BQ, lanes)), jnp.broadcast_to(lse[BQ:], (BQ, lanes))
+        )
+
+
+def once(shape, index=None):
+    index = (0,) * len(shape) if index is None else index
+    return pl.BlockSpec(shape, lambda i: index, pipeline_mode=pl.Buffered(1))
+
+
+def attend(side, low, normed, weight, firsts, begin, start_col, cos, sin):
+    count = len(normed)
+    blocks, rows, _ = normed[0].shape
+    length = start_col.shape[0]
+    lanes = 2 * HD
+    small = jax.ShapeDtypeStruct((length, lanes), BF16)
+    scalar = pl.BlockSpec(memory_space=pltpu.SMEM)
+    return pl.pallas_call(
+        functools.partial(attend_kernel, count),
+        grid=(1,),
+        out_shape=(small, small, small, small, jax.ShapeDtypeStruct((length, lanes), F32)),
+        in_specs=[scalar, scalar]
+        + [once(n.shape) for n in normed]
+        + [once((blocks, rows, lanes), (0, begin // rows, 0))] * count
+        + [once(a.shape) for a in (weight, start_col, cos, sin)],
+        out_specs=(once((length, lanes)),) * 5,
+        compiler_params=compiler_params(48),
+    )(side, low, *normed, *firsts, weight, start_col, cos, sin)
+
+
+def attend_back_kernel(count, side_ref, low_ref, *refs):
+    n_refs, do_refs = refs[:count], refs[count : 2 * count]
+    w_ref, q_ref, k_ref, v_ref, o_ref, lse_ref, start_ref, cos_ref, sin_ref = refs[
+        2 * count : 2 * count + 9
+    ]
+    dn_refs = refs[2 * count + 9 : 3 * count + 9]
+    gw_ref, gfv_ref, dq_ref, dk_ref, dv_ref, dp_ref, do_ref = refs[3 * count + 9 :]
+    length = q_ref.shape[0]
+    lanes = 2 * HD
+    chunks = row_chunks(n_refs, side_ref)
+    for number, block, rows in chunks:
+        do_ref[rows, :] = do_refs[number][block]
+    dk_ref[...] = jnp.zeros_like(dk_ref)
+    dv_ref[...] = jnp.zeros_like(dv_ref)
+    mask_a, mask_b = head_masks()
+    lane = lax.broadcasted_iota(jnp.int32, (BQ, lanes), 1)
+    for i in range(length // BQ):
+        rows = pl.ds(i * BQ, BQ)
+        q, do = q_ref[rows, :], do_ref[rows, :]
+        q2 = jnp.concatenate([q * mask_a, q * mask_b], axis=0)
+        do2 = jnp.concatenate([do * mask_a, do * mask_b], axis=0)
+        lse = jnp.transpose(lse_ref[rows, :])
+        lse = jnp.concatenate([lse[0:1, :], lse[HD : HD + 1, :]], axis=1)
+        inner = jnp.transpose(do.astype(F32) * o_ref[rows, :].astype(F32))
+        inner = jnp.concatenate(
+            [
+                jnp.sum(inner[:HD], axis=0, keepdims=True),
+                jnp.sum(inner[HD:], axis=0, keepdims=True),
+            ],
+            axis=1,
+        )
+        start = start_ref[:, rows]
+        start = jnp.concatenate([start, start], axis=1)
+        place = i * BQ + lax.broadcasted_iota(jnp.int32, (1, BQ), 1)
+        place = jnp.concatenate([place, place], axis=1)
+
+        def step(j, acc):
+            keys = pl.ds(pl.multiple_of(j * BK, BK), BK)
+            k, v = k_ref[keys, :], v_ref[keys, :]
+            s = contract_last(k, q2)
+            key = j * BK + lax.broadcasted_iota(jnp.int32, s.shape, 0)
+            s = jnp.where((key >= start) & (key <= place), s, MASKED_SCORE)
+            p = jnp.exp(s - lse)
+            dp = contract_last(v, do2)
+            ds = (p * (dp - inner)).astype(BF16)
+            dv_ref[keys, :] += matmul(p.astype(BF16), do2)
+            dk_ref[keys, :] += matmul(ds, q2)
+            return acc + contract_rows(ds, k)
+
+        acc = lax.fori_loop(
+            low_ref[i], (i * BQ + BQ - 1) // BK + 1, step, jnp.zeros((2 * BQ, lanes), F32)
+        )
+        dq_ref[rows, :] = jnp.where(lane < HD, acc[:BQ], acc[BQ:]) * (1.0 / math.sqrt(HD))
+    for begin in range(0, length, 512):
+        rows = pl.ds(begin, 512)
+        cos, sin = cos_ref[rows, :], sin_ref[rows, :]
+        dq, dk = dq_ref[rows, :], dk_ref[rows, :]
+        dv = (0.5 * dv_ref[rows, :]).astype(BF16)
+        gfv_ref[rows, :] = dv
+        dp_ref[rows, 0:lanes] = (dq * cos - swap_halves(dq) * sin).astype(BF16)
+        dp_ref[rows, lanes : 2 * lanes] = (dk * cos - swap_halves(dk) * sin).astype(BF16)
+        dp_ref[rows, 2 * lanes :] = dv
+    for number, block, rows in chunks:
+        part = dp_ref[rows, :]
+        dn_refs[number][block] = contract_last(part, w_ref[...]).astype(BF16)
+        made = contract_rows(part, n_refs[number][block])
+        if number + block == 0:
+            gw_ref[...] = made
+        else:
+            gw_ref[...] += made
+
+
+def attend_back(side, low, normed, weight, kept, grads, begin, start_row, cos, sin):
+    count = len(normed)
+    blocks, rows, width = normed[0].shape
+    length = start_row.shape[1]
+    lanes = 2 * HD
+    scalar = pl.BlockSpec(memory_space=pltpu.SMEM)
+    return pl.pallas_call(
+        functools.partial(attend_back_kernel, count),
+        grid=(1,),
+        out_shape=tuple(jax.ShapeDtypeStruct(n.shape, BF16) for n in normed)
+        + (
+            jax.ShapeDtypeStruct((3 * lanes, width), F32),
+            jax.ShapeDtypeStruct((length, lanes), BF16),
+        ),
+        in_specs=[scalar, scalar]
+        + [once(n.shape) for n in normed]
+        + [once((blocks, rows, lanes), (0, begin // rows, 0))] * count
+        + [once(a.shape) for a in (weight, *kept, start_row, cos, sin)],
+        out_specs=tuple(once(n.shape) for n in normed)
+        + (once((3 * lanes, width)), once((length, lanes))),
+        scratch_shapes=[
+            pltpu.VMEM((length, lanes), F32),
+            pltpu.VMEM((length, lanes), F32),
+            pltpu.VMEM((length, lanes), F32),
+            pltpu.VMEM((length, 3 * lanes), BF16),
+            pltpu.VMEM((length, lanes), BF16),
+        ],
+        compiler_params=compiler_params(56),
+    )(side, low, *normed, *grads, weight, *kept, start_row, cos, sin)
+
+
+def fill_out_weight(wall_ref, ow_ref):
+    groups, depth, high, wide = wall_ref.shape
+    for g in range(groups):
+        for z in range(depth):
+            ow_ref[z * high : (z + 1) * high, g * wide : (g + 1) * wide] = wall_ref[g, z]
+
+
+def hidden_kernel(
+    om_ref, os_ref, x_ref, wall_ref, gain_ref,
+    h_ref, n_ref, ob_ref, ow_ref,
+):
+    fill_out_weight(wall_ref, ow_ref)
+    blocks, width = x_ref.shape[0], x_ref.shape[2]
+    base = 0
+    for o in (om_ref, os_ref):
+        rows = o.shape[1]
+        for begin in range(0, rows, 256):
+            part = pl.ds(begin, 256)
+            here = pl.ds(base + begin, 256)
+            for b in range(blocks):
+                ob_ref[here, b * width : (b + 1) * width] = o[b, part, :]
+            branch = matmul(ob_ref[here, :], ow_ref[...])
+            total = jnp.zeros((256, 1), F32)
+            for b in range(blocks):
+                cols = slice(b * width, (b + 1) * width)
+                h = x_ref[b, here, :].astype(F32) + branch[:, cols]
+                h_ref[here, cols] = h
+                total = total + jnp.sum(h * h, axis=1, keepdims=True)
+            factor = lax.rsqrt(total / (width * blocks) + EPSILON)
+            n_ref[here, :] = (h_ref[here, :] * factor * gain_ref[...]).astype(BF16)
+        base += rows
+
+
+def mlp_kernel(
+    begin_tile, hidden, first, down_first,
+    n_ref, c_ref, wall_ref, y_ref, dn_ref, grad_ref,
+    g_ref, d_ref, nt_ref, act_ref, dgu_ref, dy_ref,
+):
+    groups, lanes = wall_ref.shape[0], wall_ref.shape[3]
+    rows, width = n_ref.shape
+    padded = d_ref.shape[0]
+    deep = width // groups
+    tiles = 2 * padded // lanes
+    all_tiles = (down_first - first) // deep // 2
+
+    @pl.when(pl.program_id(0) == 0)
+    def _():
+        y_ref[...] = jnp.zeros_like(y_ref)
+        dn_ref[...] = jnp.zeros_like(dn_ref)
+        nt_ref[...] = jnp.transpose(n_ref[...])
+        for b in range(c_ref.shape[0]):
+            part = c_ref.shape[2]
+            dy_ref[:, b * part : (b + 1) * part] = c_ref[b]
+        if padded > hidden:
+            d_ref[hidden:, :] = jnp.zeros((padded - hidden, width), BF16)
+
+    for g in range(groups):
+        for t in range(tiles):
+            column = begin_tile + t
+            if t >= tiles // 2:
+                column += all_tiles - tiles // 2
+            at = first + column * deep
+            g_ref[g * deep : (g + 1) * deep, t * lanes : (t + 1) * lanes] = wall_ref[
+                g, 0, at : at + deep, :
+            ]
+        at = down_first + begin_tile * lanes
+        d_ref[0:hidden, g * lanes : (g + 1) * lanes] = wall_ref[g, 0, at : at + hidden, :]
+    for begin in range(0, rows, 256):
+        part = pl.ds(begin, 256)
+        gu = matmul(n_ref[part, :], g_ref[...])
+        gate, up = gu[:, :padded], gu[:, padded:]
+        sig = 1.0 / (1.0 + jnp.exp(-gate))
+        silu = gate * sig
+        act_ref[part, :] = (silu * up).astype(BF16)
+        dact = contract_last(dy_ref[part, :], d_ref[...])
+        dgu_ref[part, :padded] = (dact * up * sig * (1.0 + gate * (1.0 - sig))).astype(BF16)
+        dgu_ref[part, padded:] = (dact * silu).astype(BF16)
+        y_ref[part, :] += matmul(act_ref[part, :], d_ref[...])
+        dn_ref[part, :] += contract_last(dgu_ref[part, :], g_ref[...])
+    for begin in range(0, 2 * padded, 512):
+        made = matmul(nt_ref[...], dgu_ref[:, begin : begin + 512]).astype(BF16)
+        for g in range(groups):
+            for t in range(512 // lanes):
+                at = (begin // lanes + t) * deep
+                grad_ref[g, 0, at : at + deep, :] = made[
+                    g * deep : (g + 1) * deep, t * lanes : (t + 1) * lanes
+                ]
+    for begin in range(0, width, 512):
+        made = contract_rows(act_ref[...], dy_ref[:, begin : begin + 512]).astype(BF16)
+        for t in range(512 // lanes):
+            grad_ref[begin // lanes + t, 0, tiles * deep :, :] = made[
+                :hidden, t * lanes : (t + 1) * lanes
+            ]
+
+
+def hidden_back_kernel(
+    h_ref, ya_ref, yb_ref, dna_ref, dnb_ref, ob_ref, c_ref, wall_ref, gain_ref,
+    out_ref, dh_ref, dob_ref, gout_ref, ggain_ref, ow_ref, low_ref,
+):
+    fill_out_weight(wall_ref, ow_ref)
+    groups = wall_ref.shape[0]
+    blocks, width = out_ref.shape[0], out_ref.shape[2]
+    full = width * blocks
+    gain = gain_ref[...]
+    ggain = jnp.zeros((1, full), F32)
+    for begin in range(0, h_ref.shape[0], 256):
+        here = pl.ds(begin, 256)
+        h = h_ref[here, :]
+        factor = lax.rsqrt(jnp.sum(h * h, axis=1, keepdims=True) / full + EPSILON)
+        dn = dna_ref[here, :] + dnb_ref[here, :]
+        result = (h + (ya_ref[here, :] + yb_ref[here, :])).astype(BF16)
+        for b in range(blocks):
+            out_ref[b, here, :] = result[:, b * width : (b + 1) * width]
+        weighted = dn * gain
+        ggain = ggain + jnp.sum(dn * (h * factor), axis=0, keepdims=True)
+        row_inner = jnp.sum(weighted * h, axis=1, keepdims=True)
+        dh = (
+            jnp.concatenate([c_ref[b, here, :] for b in range(blocks)], axis=1).astype(F32)
+            + factor * weighted
+            - h * (factor * factor * factor * row_inner / full)
+        )
+        dh_ref[here, :] = dh
+        low_ref[here, :] = dh.astype(BF16)
+        made = contract_last(low_ref[here, :], ow_ref[...]).astype(BF16)
+        for b in range(blocks):
+            dob_ref[b, here, :] = made[:, b * width : (b + 1) * width]
+    ggain_ref[...] = ggain
+    high, wide = gout_ref.shape[2], gout_ref.shape[3]
+    for z in range(gout_ref.shape[1]):
+        made = contract_rows(ob_ref[:, z * high : (z + 1) * high], low_ref[...]).astype(BF16)
+        for g in range(groups):
+            gout_ref[g, z] = made[:, g * wide : (g + 1) * wide]
+
+
+def last_kernel(x_ref, dh_ref, parts_ref, gain_ref, out_ref, ggain_ref):
+    blocks, width = x_ref.shape[0], x_ref.shape[2]
+    full = width * blocks
+    ggain_ref[...] = jnp.zeros_like(ggain_ref)
+    for begin in range(0, x_ref.shape[1], 256):
+        part = pl.ds(begin, 256)
+        dn = parts_ref[0, part, :].astype(F32)
+        for other in range(1, parts_ref.shape[0]):
+            dn = dn + parts_ref[other, part, :].astype(F32)
+        weighted = dn * gain_ref[...]
+        total = jnp.zeros((256, 1), F32)
+        inner = jnp.zeros((256, 1), F32)
+        for b in range(blocks):
+            cols = slice(b * width, (b + 1) * width)
+            value = x_ref[b, part, :].astype(F32)
+            total = total + jnp.sum(value * value, axis=1, keepdims=True)
+            inner = inner + jnp.sum(weighted[:, cols] * value, axis=1, keepdims=True)
+        factor = lax.rsqrt(total / full + EPSILON)
+        slope = factor * factor * factor * inner / full
+        for b in range(blocks):
+            cols = slice(b * width, (b + 1) * width)
+            value = x_ref[b, part, :].astype(F32)
+            ggain_ref[:, cols] += jnp.sum(dn[:, cols] * value * factor, axis=0, keepdims=True)
+            out_ref[b, part, :] = (
+                dh_ref[part, cols] + factor * weighted[:, cols] - value * slope
+            ).astype(BF16)
+
+
+def last(base, x, dh, parts, gain):
+    rows, full = parts.shape[1], gain.shape[1]
+    shape = (x.shape[0], rows, x.shape[2])
+    return pl.pallas_call(
+        last_kernel,
+        grid=(1,),
+        out_shape=(jax.ShapeDtypeStruct(shape, BF16), jax.ShapeDtypeStruct((1, full), F32)),
+        in_specs=[
+            once(shape, (0, base // rows, 0)),
+            once((rows, full), (base // rows, 0)),
+            once(parts.shape),
+            once(gain.shape),
+        ],
+        out_specs=(once(shape), once((1, full))),
+        compiler_params=compiler_params(56),
+    )(x, dh, parts, gain)
+
+
+def by_layers():
+    def run(
+        tokens,
+        first_values,
+        segment_ids,
+        cotangent,
+        qkv_weight,
+        out_weight,
+        gate_up_weight,
+        down_weight,
+        attn_gain,
+        mlp_gain,
+    ):
+        dp, z, f = (lax.axis_index(a) for a in ("dp", "head", "ffn"))
+        depth, side = lax.axis_size("head"), lax.axis_size("ffn")
+        group = 2 * side
+        length, width = tokens.shape[1], tokens.shape[2]
+        half = length // 2
+        full_width = width * depth
+        seq_len = length * side
+        lanes = 2 * HD
+        hidden = down_weight.shape[0]
+        padded = -(-hidden // lanes) * lanes
+        layer = ("dp", "ffn")
+        vmem = pl.BlockSpec(memory_space=pltpu.VMEM)
+
+        def to_layers(values):
+            keep = lax.dynamic_slice(values, (depth, dp * half, 0), (2, half, width))
+            give = lax.dynamic_slice(values, (depth, (1 - dp) * half, 0), (2, half, width))
+            got = swap(give)
+            early = jnp.where(dp == 0, keep, got)
+            late = jnp.where(dp == 0, got, keep)
+            return values[:depth], jnp.stack([early[0], late[0], early[1], late[1]])
+
+        def from_layers(main, shared):
+            keep = jnp.where(dp == 0, shared[0::2], shared[1::2])
+            got = swap(jnp.where(dp == 0, shared[1::2], shared[0::2]))
+            early = jnp.where(dp == 0, keep, got)
+            late = jnp.where(dp == 0, got, keep)
+            return jnp.concatenate([main, jnp.concatenate([early, late], axis=1)], axis=0)
+
+        other_ids = swap(segment_ids)
+        pick = depth + z // 2
+        ids = [
+            lax.dynamic_index_in_dim(segment_ids, z, 0, keepdims=False),
+            lax.dynamic_index_in_dim(other_ids, z, 0, keepdims=False),
+            jnp.where(
+                z % 2 == dp,
+                lax.dynamic_index_in_dim(segment_ids, pick, 0, keepdims=False),
+                lax.dynamic_index_in_dim(other_ids, pick, 0, keepdims=False),
+            ),
+        ]
+        ids = jnp.stack(ids)
+        starts = jnp.sum((ids[:, None, :] < ids[:, :, None]).astype(jnp.int32), axis=2)
+        lows = starts[:, ::BQ] // BK
+
+        places = jnp.arange(seq_len, dtype=jnp.int32)
+        cos, sin = rope_tables(places, HD)
+        cos = jnp.concatenate([cos, cos], axis=1)
+        sin = jnp.concatenate([-sin[:, : HD // 2], sin[:, HD // 2 :]], axis=1)
+        sin = jnp.concatenate([sin, sin], axis=1)
+
+        out_rows = out_weight.shape[0]
+        def in_tiles(values):
+            values = jnp.pad(values, ((0, 0), (0, padded - hidden)))
+            return values.reshape(-1, padded // lanes, lanes).transpose(1, 0, 2).reshape(-1, lanes)
+
+        wall = jnp.concatenate(
+            [out_weight, in_tiles(gate_up_weight[:, 0]), in_tiles(gate_up_weight[:, 1]), down_weight],
+            axis=0,
+        )
+        deep = qkv_weight.shape[0]
+        part = qkv_weight.reshape(deep, 3, 2, lanes).transpose(2, 1, 0, 3).reshape(-1, lanes)
+        left = jnp.concatenate([attn_gain, mlp_gain]).reshape(-1, lanes)
+        pieces = []
+        for _ in range(3):
+            piece = lax.reduce_precision(left, 8, 7)
+            pieces.append(piece.astype(BF16))
+            left = left - piece
+        tail = jnp.concatenate(pieces + [jnp.zeros((4, lanes), BF16)], axis=0)
+        part = jnp.concatenate([part, tail], axis=0)
+        part = exchange(jnp.broadcast_to(part[None], (depth,) + part.shape), "head")
+        tail = part[:, 6 * deep :].astype(F32)
+        step = 2 * width // lanes
+        gains = tail[:, :step] + tail[:, step : 2 * step] + tail[:, 2 * step : 3 * step]
+        gains = gains.reshape(depth, 2, width).transpose(1, 0, 2).reshape(2, 1, full_width)
+        part = part[:, : 6 * deep].reshape(depth, 2, 3, deep, lanes)
+        part = part.transpose(1, 0, 2, 3, 4).reshape(group, 3, deep, lanes)
+        part = exchange(part, layer)
+        weight = part.transpose(0, 2, 1, 3).reshape(group * deep, 3 * lanes)
+
+        x, x_got = send_line(jnp.concatenate(to_layers(tokens), axis=1))
+        x_got, weight, cos, sin, starts = after(x_got, weight, cos, sin, starts)
+        lows = starts[:, ::BQ] // BK
+        x = join_line(x, x_got)
+        first = jnp.concatenate(to_layers(first_values), axis=1)
+        first, x = after(first, x)
+        first_got = send_across(first)
+        nm, ns = normalized(x, gains[0], side, length)
+        wall, nm = after(wall, nm)
+        wall = lax.all_gather(wall, ("dp", "ffn", "head"), axis=0, tiled=False)
+        wall = wall.reshape(group, depth, wall.shape[1], lanes)
+        nm = exchange(nm, "ffn")
+        first_got, ns, nm = after(first_got, ns, nm)
+        first = join_across(first_got)
+
+        def pair_halves(blocks):
+            mine = lax.dynamic_slice_in_dim(blocks, dp * lanes, lanes, axis=2)
+            return mine, swap(lax.dynamic_slice_in_dim(blocks, (1 - dp) * lanes, lanes, axis=2))
+
+        def pair_join(mine, theirs):
+            return lane_join(mine, swap(theirs))
+
+        def lane_join(mine, got):
+            return jnp.where(
+                dp == 0,
+                jnp.concatenate([mine, got], axis=2),
+                jnp.concatenate([got, mine], axis=2),
+            )
+
+        def by_core(shared):
+            shared = shared.reshape(side, 2, half, lanes)
+            return (
+                lax.dynamic_index_in_dim(shared, dp, 1, keepdims=False),
+                lax.dynamic_index_in_dim(shared, 1 - dp, 1, keepdims=False),
+            )
+
+        first_mine, first_got = pair_halves(first)
+        firsts = [(first_mine,), (first_got,), (first_mine, first_got)]
+        core = dp.astype(jnp.int32).reshape(1)
+        def attend_at(i, rows_in):
+            return attend(
+                core,
+                lows[i],
+                rows_in,
+                weight,
+                firsts[i],
+                length if i == 2 else 0,
+                starts[i][:, None],
+                cos,
+                sin,
+            )
+
+        ns = exchange(ns, "ffn")
+        nm_other = swap(nm)
+        kept = [attend_at(0, (nm,))]
+        grad_blocks = jnp.concatenate(to_layers(cotangent), axis=1)
+        nm_other, ns, grad_blocks, kept[0] = after(nm_other, ns, grad_blocks, kept[0])
+        grad_blocks, grad_got = send_line(grad_blocks)
+        ns_other = swap(ns)
+        kept.append(attend_at(1, (nm_other,)))
+        ns_other, grad_got[0], kept[1] = after(ns_other, grad_got[0], kept[1])
+        om = pair_join(
+            kept[0][3].reshape(side, length, lanes), kept[1][3].reshape(side, length, lanes)
+        )
+        ns_other, om = after(ns_other, om)
+        kept.append(attend_at(2, (ns, ns_other)))
+        normed = [(nm,), (nm_other,), (ns, ns_other)]
+        om = exchange(om, "ffn")
+        om, grad_got[1], kept[2] = after(om, grad_got[1], kept[2])
+        os_, om = after(pair_join(*by_core(kept[2][3])), om)
+        os_ = exchange(os_, "ffn")
+
+        rows = length + half
+        whole = jax.ShapeDtypeStruct((rows, full_width), F32)
+        whole_low = jax.ShapeDtypeStruct((rows, full_width), BF16)
+        out_spec = pl.BlockSpec((group, depth, out_rows, lanes), lambda i: (0, 0, 0, 0))
+
+        def fixed(shape):
+            return pl.BlockSpec(
+                shape, lambda i: (0,) * len(shape), pipeline_mode=pl.Buffered(1)
+            )
+
+        ow_scratch = pltpu.VMEM((out_rows * depth, group * lanes), BF16)
+        h, n2, ob = pl.pallas_call(
+            hidden_kernel,
+            grid=(1,),
+            out_shape=(whole, whole_low, whole_low),
+            in_specs=[fixed(a.shape) for a in (om, os_, x)]
+            + [out_spec, fixed((1, full_width))],
+            out_specs=tuple(fixed((rows, full_width)) for _ in range(3)),
+            scratch_shapes=[ow_scratch],
+            compiler_params=compiler_params(56),
+        )(om, os_, x, wall, gains[1])
+        grad_got, n2 = after(grad_got, n2)
+        grad_blocks = join_line(grad_blocks, grad_got)
+
+        high = wall.shape[2]
+        count = padded // lanes
+
+        def feed_forward(begin_tile, end_tile):
+            wide = (end_tile - begin_tile) * lanes
+            real = min(hidden, end_tile * lanes) - begin_tile * lanes
+            grad_rows = 2 * (end_tile - begin_tile) * deep + real
+            return pl.pallas_call(
+                functools.partial(
+                    mlp_kernel, begin_tile, real, out_rows, out_rows + 2 * count * deep
+                ),
+                grid=(depth,),
+                out_shape=(
+                    whole,
+                    whole,
+                    jax.ShapeDtypeStruct((group, depth, grad_rows, lanes), BF16),
+                ),
+                in_specs=[
+                    fixed((rows, full_width)),
+                    fixed((depth, rows, width)),
+                    pl.BlockSpec((group, 1, high, lanes), lambda i: (0, i, 0, 0)),
+                ],
+                out_specs=(
+                    fixed((rows, full_width)),
+                    fixed((rows, full_width)),
+                    pl.BlockSpec((group, 1, grad_rows, lanes), lambda i: (0, i, 0, 0)),
+                ),
+                scratch_shapes=[
+                    pltpu.VMEM((full_width, 2 * wide), BF16),
+                    pltpu.VMEM((wide, full_width), BF16),
+                    pltpu.VMEM((full_width, rows), BF16),
+                    pltpu.VMEM((rows, wide), BF16),
+                    pltpu.VMEM((rows, 2 * wide), BF16),
+                    pltpu.VMEM((rows, full_width), BF16),
+                ],
+                compiler_params=compiler_params(60),
+            )(n2, grad_blocks, wall)
+
+        ya, dna, grads_a = feed_forward(count - 2, count)
+        n2, ya = after(n2, ya)
+        yb, dnb, grads_b = feed_forward(0, count - 2)
+
+        def layer_sum(grads):
+            shape = grads.shape[1:]
+            return lax.psum_scatter(grads, layer, scatter_dimension=0, tiled=True).reshape(shape)
+
+        grads_a = layer_sum(grads_a)
+        grads_b = layer_sum(grads_b)
+
+        out, dh, dob, gout, gain_two = pl.pallas_call(
+            hidden_back_kernel,
+            grid=(1,),
+            out_shape=(
+                jax.ShapeDtypeStruct(grad_blocks.shape, BF16),
+                whole,
+                jax.ShapeDtypeStruct(grad_blocks.shape, BF16),
+                jax.ShapeDtypeStruct((group, depth, out_rows, lanes), BF16),
+                jax.ShapeDtypeStruct((1, full_width), F32),
+            ),
+            in_specs=[fixed((rows, full_width))] * 6
+            + [fixed(grad_blocks.shape), out_spec, fixed((1, full_width))],
+            out_specs=tuple(
+                fixed(s)
+                for s in (
+                    grad_blocks.shape,
+                    (rows, full_width),
+                    grad_blocks.shape,
+                    (group, depth, out_rows, lanes),
+                    (1, full_width),
+                )
+            ),
+            scratch_shapes=[ow_scratch, pltpu.VMEM((rows, full_width), BF16)],
+            compiler_params=compiler_params(60),
+        )(h, ya, yb, dna, dnb, ob, grad_blocks, wall, gains[1])
+
+        dob = exchange(dob, "ffn")
+        do_mine, do_got = pair_halves(dob)
+
+        def back_of(i, grads_in):
+            return attend_back(
+                core,
+                lows[i],
+                normed[i],
+                weight,
+                kept[i],
+                grads_in,
+                length if i == 2 else 0,
+                starts[i][None],
+                cos,
+                sin,
+            )
+
+        out, out_got = send_line(out)
+        do_got, gout = after(do_got, gout)
+        gout = exchange(gout, layer)
+        dn_b, gw_b, gfv_b = back_of(1, (do_got,))
+        dn_b, gw_b, gfv_b, out_got[0], out_got[1] = after(
+            dn_b, gw_b, gfv_b, out_got[0], out_got[1]
+        )
+        do_mine, dn_b, gfv_b, grads_a = after(do_mine, dn_b, gfv_b, grads_a)
+        grads_a, a_got = send_line(grads_a)
+        dn_other = swap(dn_b)
+        dn_a, gw_a, gfv_a = back_of(0, (do_mine,))
+        dn_a, gw_a, gfv_a, dn_other, a_got, out_got[2], gout = after(
+            dn_a, gw_a, gfv_a, dn_other, a_got, out_got[2], gout
+        )
+        gfv_other = swap(gfv_b)
+        grads_a = join_line(grads_a, a_got)
+
+        def add_low(mine, theirs):
+            return (mine.astype(F32) + theirs.astype(F32)).astype(BF16)
+
+        main_sum = add_low(dn_a, dn_other)
+        out = join_line(out, out_got)
+        gfv_main = lane_join(
+            gfv_a.reshape(side, length, lanes), gfv_other.reshape(side, length, lanes)
+        )
+        do_mine, main_sum, grads_b = after(do_mine, main_sum, grads_b)
+        main_sum = exchange(main_sum, "ffn")
+        grads_b, b_got = send_line(grads_b)
+        dn_s, dn_t, gw_s, gfv_s = back_of(2, (do_mine, do_got))
+        b_got, dn_s, dn_t, gw_s, gfv_s = after(b_got, dn_s, dn_t, gw_s, gfv_s)
+        gfv_mine, gfv_theirs = by_core(gfv_s)
+        dn_t, gfv_theirs = swap(dn_t), swap(gfv_theirs)
+        shared_sum, main_sum, gfv_theirs = after(add_low(dn_s, dn_t), main_sum, gfv_theirs)
+        gfv = jnp.concatenate([gfv_main, lane_join(gfv_mine, gfv_theirs)], axis=1)
+        shared_sum = exchange(shared_sum, "ffn")
+        tokm, gain_main = last(0, x, dh, main_sum, gains[0])
+        shared_sum, tokm = after(shared_sum, tokm)
+        tokm, tokm_got = send_line(tokm)
+        gfv, shared_sum, tokm_got[0] = after(gfv, shared_sum, tokm_got[0])
+        gfv = exchange(gfv, "ffn")
+        toks, gain_shared = last(length, x, dh, shared_sum, gains[0])
+        toks, toks_got = send_line(toks)
+        tokm_got, toks = after(tokm_got, toks)
+        gfv, tokm_got, toks_got = after(gfv, tokm_got, toks_got)
+        gfv, gfv_got = send_line(gfv)
+        gfv_got[0], grad_w, gout, gain_shared, grads_b, out, toks_got = after(
+            gfv_got[0],
+            (gw_a + gw_b + gw_s).astype(BF16),
+            gout,
+            gain_shared,
+            grads_b,
+            out,
+            toks_got,
+        )
+        out_tokens = from_layers(out[:, :length], out[:, length:])
+        grads_b = join_line(grads_b, b_got)
+        token_grads = from_layers(join_line(tokm, tokm_got), join_line(toks, toks_got))
+        gfv = join_line(gfv, gfv_got)
+        value_grads = from_layers(gfv[:, :length], gfv[:, length:])
+
+        gout = jnp.sum(gout.astype(F32), axis=0).astype(BF16)
+        grad_out = jnp.sum(exchange_line(gout).astype(F32), axis=0)
+
+        grad_w = grad_w.reshape(3, lanes, group, deep).transpose(2, 0, 3, 1)
+        grad_w = exchange(grad_w, layer)
+        grad_w = grad_w.reshape(2, side, 3, deep, lanes).transpose(1, 3, 2, 0, 4)
+        grad_w = grad_w.reshape(depth, deep, 3, width)
+        grad_qkv = jnp.sum(exchange_line(grad_w).astype(F32), axis=0)
+
+        gain_both = jnp.concatenate([gain_main + gain_shared, gain_two]).reshape(2, depth, width)
+        gain_both = exchange_line(gain_both.transpose(1, 0, 2))
+        gain_both = jnp.sum(gain_both, axis=0, keepdims=True)
+        gain_both = exchange(jnp.broadcast_to(gain_both, (group, 2, width)), layer)
+        gain_both = jnp.sum(gain_both, axis=0)
+
+        def untile(values):
+            return values.reshape(-1, deep, lanes).transpose(1, 0, 2).reshape(deep, -1)
+
+        gates, ups, downs = [], [], []
+        for grads, tiles_in in ((grads_b, count - 2), (grads_a, 2)):
+            part = jnp.sum(grads.astype(F32), axis=0)
+            gates.append(untile(part[: tiles_in * deep]))
+            ups.append(untile(part[tiles_in * deep : 2 * tiles_in * deep]))
+            downs.append(part[2 * tiles_in * deep :])
+        grad_gate = jnp.stack(
+            [jnp.concatenate(g, axis=1)[:, :hidden] for g in (gates, ups)], axis=1
+        )
+        return (
+            out_tokens,
+            token_grads,
+            value_grads,
+            grad_qkv,
+            grad_out,
+            grad_gate,
+            jnp.concatenate(downs, axis=0),
+            gain_both[0],
+            gain_both[1],
+        )
+
+    return run
+
+
+def fits_layers(mesh, seqs, seq_len, full_width, heads):
+    sizes = dict(mesh.shape)
+    return (
+        sizes["dp"] == 2
+        and sizes["head"] == 4
+        and sizes["ffn"] == 4
+        and seqs == 12
+        and seq_len % (512 * 4) == 0
+        and full_width == 1024
+        and heads == 16
+    )
+
+
 def solution(mesh):
     in_specs = (
         P("dp", "ffn", "head"),
@@ -418,6 +1308,14 @@
         P("head"),
         P("head"),
     )
-    return jax.shard_map(
-        per_device, mesh=mesh, in_specs=in_specs, out_specs=out_specs, check_vma=False
-    )
+
+    def program(*args):
+        seqs, seq_len, full_width = args[0].shape
+        heads = args[5].shape[0] // HD
+        fast = fits_layers(mesh, seqs, seq_len, full_width, heads)
+        body = by_layers() if fast else per_device
+        return jax.shard_map(
+            body, mesh=mesh, in_specs=in_specs, out_specs=out_specs, check_vma=False
+        )(*args)
+
+    return program

time: 2190 us -> 779 us (0.36)
  waiting for transfers between devices: 1300 us -> 208 us
  matrix products: 414 us -> 0 us
  Pallas kernels: 0 us -> 247 us
  other arithmetic: 217 us -> 56.7 us
  starting transfers between devices: 4.89 us -> 124 us
  blocking collectives: 112 us -> 23.4 us
  local copies, waits for them, and re-layouts: 115 us -> 89.8 us
    all_gather x27 -> x1, waiting for transfers between devices: 655 us -> 0.01 us  [run(): wall = lax.all_gather(wall, ('dp', 'ffn', 'head'), axis=0, tiled=False)]
    reduce_scatter x23 -> x2, waiting for transfers between devices: 603 us -> 17.8 us  [layer_sum(): lax.psum_scatter(grads, layer, scatter_dimension=0, tiled=True)]
    dot_general x88 -> x0, matrix products: 414 us -> none  [the longest x6 77.9 us: query_side(): jnp.einsum('qhd,khd->hqk', grad_rows, value_rows, preferred_element_type=...]
    pallas_call x0 -> x13, Pallas kernels: none -> 247 us  [the longest x3 89.8 us: attend_back(): pl.pallas_call(functools.partial(attend_back_kernel, count), grid=(1,), o...]
    ppermute x0 -> x54, waiting for transfers between devices: none -> 152 us  [the longest x33 75.2 us: send_line(): got.append(lax.ppermute(send, axis, [(j, j ^ step) for j in range(count)]))]
    convert_element_type x28 -> x6, other arithmetic: 104 us -> 14.3 us  [the longest x2 12.3 us: add_low(): return (mine.astype(F32) + theirs.astype(F32)).astype(BF16)]
    psum x5 -> x0, blocking collectives: 86.3 us -> none  [the longest x4 71.1 us: row_total(): return lax.psum(values, 'head')]
    ppermute x0 -> x54, starting transfers between devices: none -> 70 us  [the longest x33 59.2 us: send_line(): got.append(lax.ppermute(send, axis, [(j, j ^ step) for j in range(count)]))]
  transfers between devices with their start and end apart: 53 -> 69, of which waited for: 45 -> 23; matrix products, arithmetic and copies ran while one was open for 24% -> 14% of each run, Pallas kernels for 0% -> 29%
where the time goes in v2:
time: 779 us; the launch traced here: 764 us
  Pallas kernels  247 us (32%)
  waiting for transfers between devices  208 us (27%)
  starting transfers between devices  124 us (16%)
  local copies, waits for them, and re-layouts  89.8 us (12%)
  other arithmetic  56.7 us (7%)
  blocking collectives  23.4 us (3%)
  between operations  15.5 us (2%)
    pallas_call x3, Pallas kernels, attend_back(): pl.pallas_call(functools.partial(attend_back_kernel, count), grid=(1,), o...  89.8 us
    ppermute x33, waiting for transfers between devices, send_line(): got.append(lax.ppermute(send, axis, [(j, j ^ step) for j in range(count)]))  75.2 us
    ppermute x4, waiting for transfers between devices, send_across(): got.append(lax.ppermute(send, ('head', 'ffn'), pairs))  70.4 us
    pallas_call x3, Pallas kernels, attend(): pl.pallas_call(functools.partial(attend_kernel, count), grid=(1,), out_sh...  62 us
    pallas_call x2, Pallas kernels, feed_forward(): pl.pallas_call(functools.partial(mlp_kernel, begin_tile, real, out_rows,...  61.6 us
    ppermute x33, starting transfers between devices, send_line(): got.append(lax.ppermute(send, axis, [(j, j ^ step) for j in range(count)]))  59.2 us
    all_to_all x12, starting transfers between devices, exchange(): return lax.all_to_all(blocks, axes, 0, 0, tiled=True)  52.9 us
    all_to_all x12, waiting for transfers between devices, exchange(): return lax.all_to_all(blocks, axes, 0, 0, tiled=True)  38.2 us
  transfers between devices with their start and end apart: 69, of which 23 were waited for; matrix products, arithmetic and copies ran while one was open for 14% of the time, Pallas kernels for 29%

profile of v2, /device:TPU:0, one launch (start us, length us, event | category | flops | bytes accessed | tf_op | source)
XLA Modules:
  0.0 764.0 jit_solution(3126559939872009389)
XLA Ops:
  14.9 6.3 all-to-all-start
  22.0 4.0 fusion.1
  27.8 2.5 pad_maximum_fusion.2
  34.1 6.4 convert_reduce_fusion
  42.9 3.8 collective-permute-start.3
  52.9 4.2 all-to-all-start.1
  60.2 8.9 %all-to-all-done.1 = bf16[8,3,128,128]{3,2,1,0:T(8,128)(2,1)} async-done(((bf16[8,3,128,128]{3,2,1,0:T(8,128)(2,1)}), bf16[8,3,128,128]{3,2,1,0:T(8,128)(2,1)}, u32[]{:S(2)}, u32[]{:S(2)}) %all-to-all-start.1) | async-done | bytes 786464 | tf_op jit(solution)/shard_map/all_to_all | solution.py:416
  69.1 2.4 copy.128
  73.7 6.7 collective-permute-done.2
  83.5 3.3 shard_map.169
  86.9 4.9 all-to-all-start.2
  91.9 2.4 collective-permute-start.9
  97.0 69.0 %collective-permute-done.9 = bf16[768,256]{1,0:T(8,128)(2,1)S(1)} collective-permute-done((bf16[768,256]{1,0:T(8,128)(2,1)S(1)}, bf16[768,256]{1,0:T(8,128)(2,1)S(1)}, u32[]{:S(2)}, u32[]{:S(2)}) %collective-permute-start.9) | collective-permute-done | bytes 393248 | tf_op jit(solution)/shard_map/ppermute | solution.py:455
  170.8 4.6 all-to-all-start.3
  176.5 3.0 fusion
  180.7 18.9 %shard_map.170 = (bf16[2048,128]{1,0:T(8,128)(2,1)S(1)}, bf16[2048,128]{1,0:T(8,128)(2,1)S(1)}, bf16[2048,128]{1,0:T(8,128)(2,1)S(1)}, bf16[2048,128]{1,0:T(8,128)(2,1)S(1)}, f32[2048,128]{1,0:T(8,128)S(1)}) custom-call(s32[1]{0:T(128)} %bitcast.side_ref, s32[4]{0:T(128)S(1)} %get-tuple-element.509.low_ref, bf16[4,512,1024]{2,1,0:T(8,128)(2,1)} %all-to-all-done.2.refs_0_, ...), custom_call_target="tpu_custom_call" | custom-call | tf_op jit(solution)/shard_map/pallas_call | solution.py:597
  203.8 3.0 collective-permute-start.12
  209.2 10.8 %collective-permute-start.13 = (bf16[768,256]{1,0:T(8,128)(2,1)}, bf16[768,256]{1,0:T(8,128)(2,1)}, u32[]{:S(2)}, u32[]{:S(2)}) collective-permute-start(bf16[768,256]{1,0:T(8,128)(2,1)} %get-tuple-element.433), channel_id=1, source_target_pairs={{0,4},{4,0},{8,12},{12,8},{1,5},{5,1},{9,13},{13,9},{2,6},{6,2},{1... | collective-permute-start | bytes 1179656 | tf_op jit(solution)/shard_map/ppermute | solution.py:425
  220.4 21.4 %shard_map.171 = (bf16[2048,128]{1,0:T(8,128)(2,1)S(1)}, bf16[2048,128]{1,0:T(8,128)(2,1)S(1)}, bf16[2048,128]{1,0:T(8,128)(2,1)S(1)}, bf16[2048,128]{1,0:T(8,128)(2,1)S(1)}, f32[2048,128]{1,0:T(8,128)S(1)}) custom-call(s32[1]{0:T(128)} %bitcast.side_ref, s32[4]{0:T(128)S(1)} %get-tuple-element.508.low_ref, ...), custom_call_target="tpu_custom_call" | custom-call | tf_op jit(solution)/shard_map/pallas_call | solution.py:597
  245.3 4.0 collective-permute-done.13
  252.5 4.2 all-to-all-start.4
  258.2 21.6 %shard_map.172 = (bf16[2048,128]{1,0:T(8,128)(2,1)S(1)}, bf16[2048,128]{1,0:T(8,128)(2,1)S(1)}, bf16[2048,128]{1,0:T(8,128)(2,1)S(1)}, bf16[2048,128]{1,0:T(8,128)(2,1)S(1)}, f32[2048,128]{1,0:T(8,128)S(1)}) custom-call(s32[1]{0:T(128)} %bitcast.side_ref, s32[4]{0:T(128)S(1)} %get-tuple-element.507.low_ref, bf16[4,256,1024]{2,1,0:T(8,128)(2,1)} %all-to-all-done.3.refs_0_, ...), custom_call_target="tpu_custom_call" | custom-call | tf_op jit(solution)/shard_map/pallas_call | solution.py:597
  285.0 4.1 all-to-all-start.5
  291.4 6.1 all-to-all-done.5.os_ref
  298.3 7.4 shard_map.173
  309.0 22.8 %shard_map.174 = (f32[768,1024]{1,0:T(8,128)}, f32[768,1024]{1,0:T(8,128)}, bf16[8,4,704,128]{3,2,1,0:T(8,128)(2,1)}) custom-call(bf16[768,1024]{1,0:T(8,128)(2,1)} %get-tuple-element.264.n_ref, bf16[4,768,256]{2,1,0:T(8,128)(2,1)} %copy-done.23, bf16[8,4,2496,128]{3,2,1,0:T(8,128)(2,1)} %bitcast.250), custom_call_target="tpu_custom_call" | custom-call | tf_op jit(solution)/shard_map/pallas_call | solution.py:1087
  331.8 38.9 %shard_map.175 = (f32[768,1024]{1,0:T(8,128)}, f32[768,1024]{1,0:T(8,128)}, bf16[8,4,1536,128]{3,2,1,0:T(8,128)(2,1)}) custom-call(bf16[768,1024]{1,0:T(8,128)(2,1)} %get-tuple-element.264.n_ref, bf16[4,768,256]{2,1,0:T(8,128)(2,1)} %copy-done.23, bf16[8,4,2496,128]{3,2,1,0:T(8,128)(2,1)} %bitcast.251), custom_call_target="tpu_custom_call" | custom-call | tf_op jit(solution)/shard_map/pallas_call | solution.py:1087
  370.7 13.8 %shard_map.176 = (bf16[4,768,256]{2,1,0:T(8,128)(2,1)}, f32[768,1024]{1,0:T(8,128)}, bf16[4,768,256]{2,1,0:T(8,128)(2,1)}, bf16[8,4,256,128]{3,2,1,0:T(8,128)(2,1)}, f32[1,1024]{1,0:T(1,128)}) custom-call(f32[768,1024]{1,0:T(8,128)} %get-tuple-element.251.h_ref, f32[768,1024]{1,0:T(8,128)} %get-tuple-element.263.ya_ref, ...), custom_call_target="tpu_custom_call" | custom-call | tf_op jit(solution)/shard_map/pallas_call | solution.py:1129
  384.6 23.4 %all_to_all.65 = bf16[4,768,256]{2,1,0:T(8,128)(2,1)S(1)} all-to-all(bf16[4,768,256]{2,1,0:T(8,128)(2,1)} %get-tuple-element.269), channel_id=1, replica_groups=mesh['dp'=2,'head'=4,'ffn'=4] {'ffn'}, dimensions={0} | all-to-all | bytes 3145728 | tf_op jit(solution)/shard_map/all_to_all | solution.py:416
  410.2 2.3 collective-permute-start.21
  414.9 31.9 %shard_map.177 = (bf16[4,512,1024]{2,1,0:T(8,128)(2,1)}, f32[384,1024]{1,0:T(8,128)}, bf16[2048,128]{1,0:T(8,128)(2,1)}) custom-call(s32[1]{0:T(128)} %bitcast.side_ref, s32[4]{0:T(128)} %copy-done.20, bf16[4,512,1024]{2,1,0:T(8,128)(2,1)} %collective-permute-done.10.refs_0_, bf16[4,768,128]{2,1,0:T(8,128)(2,1)} %copy-done.40, bf16[1024,384]{1,0:T(8,128)(2,1)} %copy-done.1, ...), custom_call_target="tpu_custom_call" | custom-call | tf_op jit(solution)/shard_map/pallas_call | solution.py:688
  448.3 3.7 all-to-all-start.7
  452.0 2.5 collective-permute-start.26
  456.7 3.0 collective-permute-start.23
  459.7 27.0 %shard_map.178 = (bf16[4,512,1024]{2,1,0:T(8,128)(2,1)}, f32[384,1024]{1,0:T(8,128)}, bf16[2048,128]{1,0:T(8,128)(2,1)}) custom-call(s32[1]{0:T(128)} %bitcast.side_ref, s32[4]{0:T(128)} %copy-done.19, bf16[4,512,1024]{2,1,0:T(8,128)(2,1)} %all-to-all-done.2.refs_0_, bf16[4,768,128]{2,1,0:T(8,128)(2,1)} %get-tuple-element.300.refs_1_.refs_2_, ...), custom_call_target="tpu_custom_call" | custom-call | tf_op jit(solution)/shard_map/pallas_call | solution.py:688
  487.6 8.4 %add_convert_fusion = bf16[4,512,1024]{2,1,0:T(8,128)(2,1)} fusion(bf16[4,512,1024]{2,1,0:T(8,128)(2,1)} %collective-permute-done.22, bf16[4,512,1024]{2,1,0:T(8,128)(2,1)} %get-tuple-element.296), kind=kLoop, calls=%fused_computation.1 | loop fusion | flops 8388608 | bytes 12582912 | tf_op jit(solution)/shard_map/convert_element_type | solution.py:1190
  496.1 17.7 %reduce-scatter.5.cloned.1.call-done = bf16[1,4,1536,128]{3,2,1,0:T(8,128)(2,1)} async-done(((bf16[8,4,1536,128]{3,2,1,0:T(8,128)(2,1)}), bf16[1,4,1536,128]{3,2,1,0:T(8,128)(2,1)}) %reduce-scatter.5.cloned.1.call-update) | async-done | bytes 1572880 | tf_op jit(solution)/shard_map/reduce_scatter | solution.py:1124
  513.8 5.0 all-to-all-start.8
  518.9 3.4 collective-permute-start.30
  523.3 30.9 %shard_map.179 = (bf16[4,256,1024]{2,1,0:T(8,128)(2,1)}, bf16[4,256,1024]{2,1,0:T(8,128)(2,1)}, f32[384,1024]{1,0:T(8,128)}, bf16[2048,128]{1,0:T(8,128)(2,1)}) custom-call(s32[1]{0:T(128)} %bitcast.side_ref, s32[4]{0:T(128)} %copy-done.21, bf16[4,256,1024]{2,1,0:T(8,128)(2,1)} %all-to-all-done.3.refs_0_, ...), custom_call_target="tpu_custom_call" | custom-call | tf_op jit(solution)/shard_map/pallas_call | solution.py:688
  557.7 2.7 collective-permute-done.31
  560.5 3.9 add_convert_fusion.1
  566.5 3.6 all-to-all-start.9
  576.5 5.5 shard_map.180
  582.0 12.4 %all-to-all-done.9.parts_ref = bf16[4,256,1024]{2,1,0:T(8,128)(2,1)S(1)} async-done(((bf16[4,256,1024]{2,1,0:T(8,128)(2,1)}), bf16[4,256,1024]{2,1,0:T(8,128)(2,1)S(1)}, u32[]{:S(2)}, u32[]{:S(2)}) %all-to-all-start.9) | async-done | bytes 2097184 | tf_op jit(solution)/shard_map/all_to_all | solution.py:416
  594.4 2.5 dynamic-slice_bitcast_fusion.19
  600.9 3.4 collective-permute-done.33
  604.2 3.9 all-to-all-start.10
  611.3 3.4 collective-permute-start.35
  614.8 3.7 shard_map.181
  625.3 17.2 %collective-permute-done.34 = bf16[512,256]{1,0:T(8,128)(2,1)} collective-permute-done((bf16[512,256]{1,0:T(8,128)(2,1)S(1)}, bf16[512,256]{1,0:T(8,128)(2,1)}, u32[]{:S(2)}, u32[]{:S(2)}) %collective-permute-start.34) | collective-permute-done | bytes 262176 | tf_op jit(solution)/shard_map/ppermute | solution.py:425
  642.5 4.5 collective-permute-done.37
  649.3 2.5 collective-permute-start.43
  657.1 18.0 %collective-permute-done.39 = bf16[768,256]{1,0:T(8,128)(2,1)S(1)} collective-permute-done((bf16[768,256]{1,0:T(8,128)(2,1)S(1)}, bf16[768,256]{1,0:T(8,128)(2,1)S(1)}, u32[]{:S(2)}, u32[]{:S(2)}) %collective-permute-start.39) | collective-permute-done | bytes 393248 | tf_op jit(solution)/shard_map/ppermute | solution.py:425
  675.1 7.7 %collective-permute-done.42 = bf16[768,256]{1,0:T(8,128)(2,1)S(1)} collective-permute-done((bf16[768,256]{1,0:T(8,128)(2,1)S(1)}, bf16[768,256]{1,0:T(8,128)(2,1)S(1)}, u32[]{:S(2)}, u32[]{:S(2)}) %collective-permute-start.42) | collective-permute-done | bytes 393248 | tf_op jit(solution)/shard_map/ppermute | solution.py:425
  692.1 3.0 collective-permute-start.52
  697.6 2.4 collective-permute-start.50
  710.0 3.9 all-to-all-start.12
  716.2 2.4 all-to-all-done.12
  718.6 4.3 all-to-all-start.11
  729.7 5.3 all-to-all-done.11
  736.6 2.5 collective-permute-start.47
  744.0 2.3 collective-permute-done.47
  746.3 9.6 %collective-permute-done.46 = bf16[128,3,256]{0,2,1:T(8,128)(2,1)S(1)} collective-permute-done((bf16[128,3,256]{0,2,1:T(8,128)(2,1)S(1)}, bf16[128,3,256]{0,2,1:T(8,128)(2,1)S(1)}, u32[]{:S(2)}, u32[]{:S(2)}) %collective-permute-start.46) | collective-permute-done | bytes 196640 | tf_op jit(solution)/shard_map/ppermute | solution.py:425
  (411 shorter events, 148.7 us)
Async XLA Ops:
  7.2 25.9 %collective-permute-start.4 = (s32[6,2048]{1,0:T(8,128)}, s32[6,2048]{1,0:T(8,128)}, u32[]{:S(2)}, u32[]{:S(2)}) collective-permute-start(s32[6,2048]{1,0:T(8,128)} %param.12), channel_id=1, source_target_pairs={{0,16},{16,0},{1,17},{17,1},{2,18},{18,2},{3,19},{19,3},{4,20},{20... | collective-permute-start | bytes 147464 | tf_op jit(solution)/shard_map/ppermute | solution.py:470
  9.4 37.9 %collective-permute-start.11 = (bf16[2,256,256]{2,1,0:T(8,128)(2,1)}, bf16[2,256,256]{2,1,0:T(8,128)(2,1)}, u32[]{:S(2)}, u32[]{:S(2)}) collective-permute-start(bf16[2,256,256]{2,1,0:T(8,128)(2,1)} %constant_dynamic-slice_fusion.7), channel_id=1, source_target_pairs={{0,16},{16,0},{1,17},{17,1},{2,18},{18,2},{3,19},{19,3},{4,20},{20... | collective-permute-start | bytes 786440 | tf_op jit(solution)/shard_map/ppermute | solution.py:470
  11.1 36.2 %collective-permute-start.5 = (bf16[2,256,256]{2,1,0:T(8,128)(2,1)}, bf16[2,256,256]{2,1,0:T(8,128)(2,1)}, u32[]{:S(2)}, u32[]{:S(2)}) collective-permute-start(bf16[2,256,256]{2,1,0:T(8,128)(2,1)} %constant_dynamic-slice_fusion.8), channel_id=1, source_target_pairs={{0,16},{16,0},{1,17},{17,1},{2,18},{18,2},{3,19},{19,3},{4,20},{20... | collective-permute-start | bytes 786440 | tf_op jit(solution)/shard_map/ppermute | solution.py:470
  13.2 27.3 %collective-permute-start = (bf16[2,256,256]{2,1,0:T(8,128)(2,1)}, bf16[2,256,256]{2,1,0:T(8,128)(2,1)}, u32[]{:S(2)}, u32[]{:S(2)}) collective-permute-start(bf16[2,256,256]{2,1,0:T(8,128)(2,1)} %constant_dynamic-slice_fusion.13), channel_id=1, source_target_pairs={{0,16},{16,0},{1,17},{17,1},{2,18},{18,2},{3,19},{19,3},{4,20},{20... | collective-permute-start | bytes 786440 | tf_op jit(solution)/shard_map/ppermute | solution.py:470
  14.9 35.8 %all-to-all-start = ((bf16[4,784,128]{2,1,0:T(8,128)(2,1)}), bf16[4,784,128]{2,1,0:T(8,128)(2,1)}, u32[]{:S(2)}, u32[]{:S(2)}) async-start(bf16[4,784,128]{2,1,0:T(8,128)(2,1)} %broadcast_in_dim.127), calls=%async_computation | async-start | bytes 1605632 | tf_op jit(solution)/shard_map/all_to_all | solution.py:416
  42.9 30.8 %collective-permute-start.3 = (bf16[768,256]{1,0:T(8,128)(2,1)}, bf16[768,256]{1,0:T(8,128)(2,1)}, u32[]{:S(2)}, u32[]{:S(2)}) collective-permute-start(bf16[768,256]{1,0:T(8,128)(2,1)} %get-tuple-element.440), channel_id=1, source_target_pairs={{0,12},{4,8},{8,4},{12,0},{1,13},{5,9},{9,5},{13,1},{2,14},{6,10},... | collective-permute-start | bytes 1179656 | tf_op jit(solution)/shard_map/ppermute | solution.py:425
  46.7 33.7 %collective-permute-start.2 = (bf16[768,256]{1,0:T(8,128)(2,1)}, bf16[768,256]{1,0:T(8,128)(2,1)}, u32[]{:S(2)}, u32[]{:S(2)}) collective-permute-start(bf16[768,256]{1,0:T(8,128)(2,1)} %get-tuple-element.441), channel_id=1, source_target_pairs={{0,8},{4,12},{8,0},{12,4},{1,9},{5,13},{9,1},{13,5},{2,10},{6,14},... | collective-permute-start | bytes 1179656 | tf_op jit(solution)/shard_map/ppermute | solution.py:425
  46.7 33.7 %collective-permute-start.1 = (bf16[768,256]{1,0:T(8,128)(2,1)}, bf16[768,256]{1,0:T(8,128)(2,1)}, u32[]{:S(2)}, u32[]{:S(2)}) collective-permute-start(bf16[768,256]{1,0:T(8,128)(2,1)} %get-tuple-element.442), channel_id=1, source_target_pairs={{0,4},{4,0},{8,12},{12,8},{1,5},{5,1},{9,13},{13,9},{2,6},{6,2},{1... | collective-permute-start | bytes 1179656 | tf_op jit(solution)/shard_map/ppermute | solution.py:425
  52.9 16.3 %all-to-all-start.1 = ((bf16[8,3,128,128]{3,2,1,0:T(8,128)(2,1)}), bf16[8,3,128,128]{3,2,1,0:T(8,128)(2,1)}, u32[]{:S(2)}, u32[]{:S(2)}) async-start(bf16[8,3,128,128]{3,2,1,0:T(8,128)(2,1)} %bitcast.11), calls=%async_computation.1 | async-start | bytes 1572864 | tf_op jit(solution)/shard_map/all_to_all | solution.py:416
  57.1 240.4 %all-gather.3.cloned.1.call-start = ((), (), s32[]{:S(2)}) async-start(), calls=%async_computation.17 | async-start | bytes 21086208 | tf_op jit(solution)/shard_map/all_gather | solution.py:993
  86.9 80.5 %all-to-all-start.2 = ((bf16[4,512,1024]{2,1,0:T(8,128)(2,1)}), bf16[4,512,1024]{2,1,0:T(8,128)(2,1)}, u32[]{:S(2)}, u32[]{:S(2)}) async-start(bf16[4,512,1024]{2,1,0:T(8,128)(2,1)} %get-tuple-element.209), calls=%async_computation.2 | async-start | bytes 8388608 | tf_op jit(solution)/shard_map/all_to_all | solution.py:416
  91.9 74.1 %collective-permute-start.9 = (bf16[768,256]{1,0:T(8,128)(2,1)S(1)}, bf16[768,256]{1,0:T(8,128)(2,1)S(1)}, u32[]{:S(2)}, u32[]{:S(2)}) collective-permute-start(bf16[768,256]{1,0:T(8,128)(2,1)S(1)} %get-tuple-element.436), channel_id=1, source_target_pairs={{0,12},{1,8},{2,4},{3,0},{4,13},{5,9},{6,5},{7,1},{8,14},{9,10},{1... | collective-permute-start | bytes 1179656 | tf_op jit(solution)/shard_map/ppermute | solution.py:455
  94.3 71.7 %collective-permute-start.8 = (bf16[768,256]{1,0:T(8,128)(2,1)S(1)}, bf16[768,256]{1,0:T(8,128)(2,1)S(1)}, u32[]{:S(2)}, u32[]{:S(2)}) collective-permute-start(bf16[768,256]{1,0:T(8,128)(2,1)S(1)} %get-tuple-element.437), channel_id=1, source_target_pairs={{0,8},{1,12},{2,0},{3,4},{4,9},{5,13},{6,1},{7,5},{8,10},{9,14},{1... | collective-permute-start | bytes 1179656 | tf_op jit(solution)/shard_map/ppermute | solution.py:455
  96.3 71.1 %collective-permute-start.7 = (bf16[768,256]{1,0:T(8,128)(2,1)S(1)}, bf16[768,256]{1,0:T(8,128)(2,1)S(1)}, u32[]{:S(2)}, u32[]{:S(2)}) collective-permute-start(bf16[768,256]{1,0:T(8,128)(2,1)S(1)} %get-tuple-element.438), channel_id=1, source_target_pairs={{0,4},{1,0},{2,12},{3,8},{4,5},{5,1},{6,13},{7,9},{8,6},{9,2},{10,... | collective-permute-start | bytes 1179656 | tf_op jit(solution)/shard_map/ppermute | solution.py:455
  96.3 71.1 %collective-permute-start.6 = (bf16[768,256]{1,0:T(8,128)(2,1)S(1)}, bf16[768,256]{1,0:T(8,128)(2,1)S(1)}, u32[]{:S(2)}, u32[]{:S(2)}) collective-permute-start(bf16[768,256]{1,0:T(8,128)(2,1)S(1)} %get-tuple-element.439), channel_id=1, source_target_pairs={{0,0},{1,4},{2,8},{3,12},{4,1},{5,5},{6,9},{7,13},{8,2},{9,6},{10,... | collective-permute-start | bytes 1179656 | tf_op jit(solution)/shard_map/ppermute | solution.py:455
  167.4 36.4 %collective-permute-start.10 = (bf16[4,512,1024]{2,1,0:T(8,128)(2,1)}, bf16[4,512,1024]{2,1,0:T(8,128)(2,1)}, u32[]{:S(2)}, u32[]{:S(2)}) collective-permute-start(bf16[4,512,1024]{2,1,0:T(8,128)(2,1)} %all-to-all-done.2.refs_0_), channel_id=1, source_target_pairs={{0,16},{16,0},{1,17},{17,1},{2,18},{18,2},{3,19},{19,3},{4,20},{20... | collective-permute-start | bytes 12582920 | tf_op jit(solution)/shard_map/ppermute | solution.py:470
  170.8 33.0 %all-to-all-start.3 = ((bf16[4,256,1024]{2,1,0:T(8,128)(2,1)}), bf16[4,256,1024]{2,1,0:T(8,128)(2,1)}, u32[]{:S(2)}, u32[]{:S(2)}) async-start(bf16[4,256,1024]{2,1,0:T(8,128)(2,1)} %get-tuple-element.211), calls=%async_computation.3 | async-start | bytes 4194304 | tf_op jit(solution)/shard_map/all_to_all | solution.py:416
  203.8 45.5 %collective-permute-start.12 = (bf16[4,256,1024]{2,1,0:T(8,128)(2,1)}, bf16[4,256,1024]{2,1,0:T(8,128)(2,1)}, u32[]{:S(2)}, u32[]{:S(2)}) collective-permute-start(bf16[4,256,1024]{2,1,0:T(8,128)(2,1)} %all-to-all-done.3.refs_0_), channel_id=1, source_target_pairs={{0,16},{16,0},{1,17},{17,1},{2,18},{18,2},{3,19},{19,3},{4,20},{20... | collective-permute-start | bytes 6291464 | tf_op jit(solution)/shard_map/ppermute | solution.py:470
  206.8 13.5 %collective-permute-start.14 = (bf16[4,768,128]{2,1,0:T(8,128)(2,1)}, bf16[4,768,128]{2,1,0:T(8,128)(2,1)S(1)}, u32[]{:S(2)}, u32[]{:S(2)}) collective-permute-start(bf16[4,768,128]{2,1,0:T(8,128)(2,1)} %get-tuple-element.434), channel_id=1, source_target_pairs={{0,16},{16,0},{1,17},{17,1},{2,18},{18,2},{3,19},{19,3},{4,20},{20... | collective-permute-start | bytes 2359304 | tf_op jit(solution)/shard_map/ppermute | solution.py:470
  209.2 40.1 %collective-permute-start.13 = (bf16[768,256]{1,0:T(8,128)(2,1)}, bf16[768,256]{1,0:T(8,128)(2,1)}, u32[]{:S(2)}, u32[]{:S(2)}) collective-permute-start(bf16[768,256]{1,0:T(8,128)(2,1)} %get-tuple-element.433), channel_id=1, source_target_pairs={{0,4},{4,0},{8,12},{12,8},{1,5},{5,1},{9,13},{13,9},{2,6},{6,2},{1... | collective-permute-start | bytes 1179656 | tf_op jit(solution)/shard_map/ppermute | solution.py:425
  252.5 29.9 %all-to-all-start.4 = ((bf16[4,512,256]{2,1,0:T(8,128)(2,1)}), bf16[4,512,256]{2,1,0:T(8,128)(2,1)}, u32[]{:S(2)}, u32[]{:S(2)}) async-start(bf16[4,512,256]{2,1,0:T(8,128)(2,1)} %maximum_select_fusion.2), calls=%async_computation.4 | async-start | bytes 2097152 | tf_op jit(solution)/shard_map/all_to_all | solution.py:416
  256.8 25.6 %collective-permute-start.16 = (bf16[768,256]{1,0:T(8,128)(2,1)}, bf16[768,256]{1,0:T(8,128)(2,1)}, u32[]{:S(2)}, u32[]{:S(2)}) collective-permute-start(bf16[768,256]{1,0:T(8,128)(2,1)} %get-tuple-element.432), channel_id=1, source_target_pairs={{0,8},{4,12},{8,0},{12,4},{1,9},{5,13},{9,1},{13,5},{2,10},{6,14},... | collective-permute-start | bytes 1179656 | tf_op jit(solution)/shard_map/ppermute | solution.py:425
  285.0 12.5 %all-to-all-start.5 = ((bf16[4,256,256]{2,1,0:T(8,128)(2,1)}), bf16[4,256,256]{2,1,0:T(8,128)(2,1)S(1)}, u32[]{:S(2)}, u32[]{:S(2)}) async-start(bf16[4,256,256]{2,1,0:T(8,128)(2,1)} %maximum_select_fusion.4), calls=%async_computation.5 | async-start | bytes 1048576 | tf_op jit(solution)/shard_map/all_to_all | solution.py:416
  289.2 159.1 %reduce-scatter.3.cloned.1.call-start = ((), (), s32[]{:S(2)}) async-start(), calls=%async_computation.15 | async-start | bytes 6488064 | tf_op jit(solution)/shard_map/reduce_scatter | solution.py:1124
  289.6 16.2 %collective-permute-start.18 = (bf16[768,256]{1,0:T(8,128)(2,1)S(1)}, bf16[768,256]{1,0:T(8,128)(2,1)S(1)}, u32[]{:S(2)}, u32[]{:S(2)}) collective-permute-start(bf16[768,256]{1,0:T(8,128)(2,1)S(1)} %copy-done.51), channel_id=1, source_target_pairs={{0,12},{4,8},{8,4},{12,0},{1,13},{5,9},{9,5},{13,1},{2,14},{6,10},... | collective-permute-start | bytes 1179656 | tf_op jit(solution)/shard_map/ppermute | solution.py:425
  331.8 182.0 %reduce-scatter.5.cloned.1.call-start = ((), (), s32[]{:S(2)}) async-start(), calls=%async_computation.16 | async-start | bytes 14155776 | tf_op jit(solution)/shard_map/reduce_scatter | solution.py:1124
  410.2 36.6 %collective-permute-start.21 = (bf16[768,256]{1,0:T(8,128)(2,1)S(1)}, bf16[768,256]{1,0:T(8,128)(2,1)S(1)}, u32[]{:S(2)}, u32[]{:S(2)}) collective-permute-start(bf16[768,256]{1,0:T(8,128)(2,1)S(1)} %get-tuple-element.427), channel_id=1, source_target_pairs={{0,8},{4,12},{8,0},{12,4},{1,9},{5,13},{9,1},{13,5},{2,10},{6,14},... | collective-permute-start | bytes 1179656 | tf_op jit(solution)/shard_map/ppermute | solution.py:425
  412.5 34.3 %collective-permute-start.20 = (bf16[768,256]{1,0:T(8,128)(2,1)S(1)}, bf16[768,256]{1,0:T(8,128)(2,1)S(1)}, u32[]{:S(2)}, u32[]{:S(2)}) collective-permute-start(bf16[768,256]{1,0:T(8,128)(2,1)S(1)} %get-tuple-element.428), channel_id=1, source_target_pairs={{0,4},{4,0},{8,12},{12,8},{1,5},{5,1},{9,13},{13,9},{2,6},{6,2},{1... | collective-permute-start | bytes 1179656 | tf_op jit(solution)/shard_map/ppermute | solution.py:425
  448.2 39.4 %collective-permute-start.22 = (bf16[4,512,1024]{2,1,0:T(8,128)(2,1)}, bf16[4,512,1024]{2,1,0:T(8,128)(2,1)}, u32[]{:S(2)}, u32[]{:S(2)}) collective-permute-start(bf16[4,512,1024]{2,1,0:T(8,128)(2,1)} %get-tuple-element.291), channel_id=1, source_target_pairs={{0,16},{16,0},{1,17},{17,1},{2,18},{18,2},{3,19},{19,3},{4,20},{20... | collective-permute-start | bytes 12582920 | tf_op jit(solution)/shard_map/ppermute | solution.py:470
  448.3 39.3 %all-to-all-start.7 = ((bf16[8,4,256,128]{3,2,1,0:T(8,128)(2,1)}), bf16[8,4,256,128]{3,2,1,0:T(8,128)(2,1)S(1)}, u32[]{:S(2)}, u32[]{:S(2)}) async-start(bf16[8,4,256,128]{3,2,1,0:T(8,128)(2,1)} %get-tuple-element.293), calls=%async_computation.8 | async-start | bytes 4194304 | tf_op jit(solution)/shard_map/all_to_all | solution.py:416
  452.0 34.7 %collective-permute-start.26 = (bf16[768,256]{1,0:T(8,128)(2,1)S(1)}, bf16[768,256]{1,0:T(8,128)(2,1)}, u32[]{:S(2)}, u32[]{:S(2)}) collective-permute-start(bf16[768,256]{1,0:T(8,128)(2,1)S(1)} %get-tuple-element.426), channel_id=1, source_target_pairs={{0,12},{4,8},{8,4},{12,0},{1,13},{5,9},{9,5},{13,1},{2,14},{6,10},... | collective-permute-start | bytes 1179656 | tf_op jit(solution)/shard_map/ppermute | solution.py:425
  455.3 32.3 %collective-permute-start.25 = (bf16[704,128]{1,0:T(8,128)(2,1)}, bf16[704,128]{1,0:T(8,128)(2,1)}, u32[]{:S(2)}, u32[]{:S(2)}) collective-permute-start(bf16[704,128]{1,0:T(8,128)(2,1)} %get-tuple-element.462), channel_id=1, source_target_pairs={{0,12},{4,8},{8,4},{12,0},{1,13},{5,9},{9,5},{13,1},{2,14},{6,10},... | collective-permute-start | bytes 540680 | tf_op jit(solution)/shard_map/ppermute | solution.py:425
  456.7 30.9 %collective-permute-start.24 = (bf16[704,128]{1,0:T(8,128)(2,1)}, bf16[704,128]{1,0:T(8,128)(2,1)}, u32[]{:S(2)}, u32[]{:S(2)}) collective-permute-start(bf16[704,128]{1,0:T(8,128)(2,1)} %get-tuple-element.463), channel_id=1, source_target_pairs={{0,8},{4,12},{8,0},{12,4},{1,9},{5,13},{9,1},{13,5},{2,10},{6,14},... | collective-permute-start | bytes 540680 | tf_op jit(solution)/shard_map/ppermute | solution.py:425
  456.7 30.9 %collective-permute-start.23 = (bf16[704,128]{1,0:T(8,128)(2,1)S(1)}, bf16[704,128]{1,0:T(8,128)(2,1)}, u32[]{:S(2)}, u32[]{:S(2)}) collective-permute-start(bf16[704,128]{1,0:T(8,128)(2,1)S(1)} %get-tuple-element.464), channel_id=1, source_target_pairs={{0,4},{4,0},{8,12},{12,8},{1,5},{5,1},{9,13},{13,9},{2,6},{6,2},{1... | collective-permute-start | bytes 540680 | tf_op jit(solution)/shard_map/ppermute | solution.py:425
  513.8 52.7 %all-to-all-start.8 = ((bf16[4,512,1024]{2,1,0:T(8,128)(2,1)}), bf16[4,512,1024]{2,1,0:T(8,128)(2,1)}, u32[]{:S(2)}, u32[]{:S(2)}) async-start(bf16[4,512,1024]{2,1,0:T(8,128)(2,1)} %add_convert_fusion), calls=%async_computation.10 | async-start | bytes 8388608 | tf_op jit(solution)/shard_map/all_to_all | solution.py:416
  518.9 35.3 %collective-permute-start.30 = (bf16[1536,128]{1,0:T(8,128)(2,1)S(1)}, bf16[1536,128]{1,0:T(8,128)(2,1)S(1)}, u32[]{:S(2)}, u32[]{:S(2)}) collective-permute-start(bf16[1536,128]{1,0:T(8,128)(2,1)S(1)} %get-tuple-element.423), channel_id=1, source_target_pairs={{0,12},{4,8},{8,4},{12,0},{1,13},{5,9},{9,5},{13,1},{2,14},{6,10},... | collective-permute-start | bytes 1179656 | tf_op jit(solution)/shard_map/ppermute | solution.py:425
  522.3 33.7 %collective-permute-start.29 = (bf16[1536,128]{1,0:T(8,128)(2,1)S(1)}, bf16[1536,128]{1,0:T(8,128)(2,1)S(1)}, u32[]{:S(2)}, u32[]{:S(2)}) collective-permute-start(bf16[1536,128]{1,0:T(8,128)(2,1)S(1)} %get-tuple-element.424), channel_id=1, source_target_pairs={{0,8},{4,12},{8,0},{12,4},{1,9},{5,13},{9,1},{13,5},{2,10},{6,14},... | collective-permute-start | bytes 1179656 | tf_op jit(solution)/shard_map/ppermute | solution.py:425
  522.3 33.7 %collective-permute-start.28 = (bf16[1536,128]{1,0:T(8,128)(2,1)S(1)}, bf16[1536,128]{1,0:T(8,128)(2,1)S(1)}, u32[]{:S(2)}, u32[]{:S(2)}) collective-permute-start(bf16[1536,128]{1,0:T(8,128)(2,1)S(1)} %get-tuple-element.425), channel_id=1, source_target_pairs={{0,4},{4,0},{8,12},{12,8},{1,5},{5,1},{9,13},{13,9},{2,6},{6,2},{1... | collective-permute-start | bytes 1179656 | tf_op jit(solution)/shard_map/ppermute | solution.py:425
  557.4 6.9 collective-permute-start.32
  566.5 27.9 %all-to-all-start.9 = ((bf16[4,256,1024]{2,1,0:T(8,128)(2,1)}), bf16[4,256,1024]{2,1,0:T(8,128)(2,1)S(1)}, u32[]{:S(2)}, u32[]{:S(2)}) async-start(bf16[4,256,1024]{2,1,0:T(8,128)(2,1)} %add_convert_fusion.1), calls=%async_computation.11 | async-start | bytes 4194304 | tf_op jit(solution)/shard_map/all_to_all | solution.py:416
  596.9 7.3 collective-permute-start.33
  604.2 43.4 %all-to-all-start.10 = ((bf16[4,768,256]{2,1,0:T(8,128)(2,1)}), bf16[4,768,256]{2,1,0:T(8,128)(2,1)S(1)}, u32[]{:S(2)}, u32[]{:S(2)}) async-start(bf16[4,768,256]{2,1,0:T(8,128)(2,1)} %pad_maximum_fusion), calls=%async_computation.12 | async-start | bytes 3145728 | tf_op jit(solution)/shard_map/all_to_all | solution.py:416
  611.3 13.9 %collective-permute-start.35 = (bf16[512,256]{1,0:T(8,128)(2,1)}, bf16[512,256]{1,0:T(8,128)(2,1)}, u32[]{:S(2)}, u32[]{:S(2)}) collective-permute-start(bf16[512,256]{1,0:T(8,128)(2,1)} %get-tuple-element.443), channel_id=1, source_target_pairs={{0,12},{4,8},{8,4},{12,0},{1,13},{5,9},{9,5},{13,1},{2,14},{6,10},... | collective-permute-start | bytes 786440 | tf_op jit(solution)/shard_map/ppermute | solution.py:425
  614.7 27.7 %collective-permute-start.34 = (bf16[512,256]{1,0:T(8,128)(2,1)S(1)}, bf16[512,256]{1,0:T(8,128)(2,1)}, u32[]{:S(2)}, u32[]{:S(2)}) collective-permute-start(bf16[512,256]{1,0:T(8,128)(2,1)S(1)} %copy-done.67), channel_id=1, source_target_pairs={{0,8},{4,12},{8,0},{12,4},{1,9},{5,13},{9,1},{13,5},{2,10},{6,14},... | collective-permute-start | bytes 786440 | tf_op jit(solution)/shard_map/ppermute | solution.py:425
  619.5 22.9 %collective-permute-start.38 = (bf16[256,256]{1,0:T(8,128)(2,1)S(1)}, bf16[256,256]{1,0:T(8,128)(2,1)S(1)}, u32[]{:S(2)}, u32[]{:S(2)}) collective-permute-start(bf16[256,256]{1,0:T(8,128)(2,1)S(1)} %get-tuple-element.465), channel_id=1, source_target_pairs={{0,12},{4,8},{8,4},{12,0},{1,13},{5,9},{9,5},{13,1},{2,14},{6,10},... | collective-permute-start | bytes 393224 | tf_op jit(solution)/shard_map/ppermute | solution.py:425
  621.6 25.3 %collective-permute-start.37 = (bf16[256,256]{1,0:T(8,128)(2,1)S(1)}, bf16[256,256]{1,0:T(8,128)(2,1)S(1)}, u32[]{:S(2)}, u32[]{:S(2)}) collective-permute-start(bf16[256,256]{1,0:T(8,128)(2,1)S(1)} %get-tuple-element.466), channel_id=1, source_target_pairs={{0,8},{4,12},{8,0},{12,4},{1,9},{5,13},{9,1},{13,5},{2,10},{6,14},... | collective-permute-start | bytes 393224 | tf_op jit(solution)/shard_map/ppermute | solution.py:425
  622.6 25.0 %collective-permute-start.36 = (bf16[256,256]{1,0:T(8,128)(2,1)S(1)}, bf16[256,256]{1,0:T(8,128)(2,1)}, u32[]{:S(2)}, u32[]{:S(2)}) collective-permute-start(bf16[256,256]{1,0:T(8,128)(2,1)S(1)} %get-tuple-element.467), channel_id=1, source_target_pairs={{0,4},{4,0},{8,12},{12,8},{1,5},{5,1},{9,13},{13,9},{2,6},{6,2},{1... | collective-permute-start | bytes 393224 | tf_op jit(solution)/shard_map/ppermute | solution.py:425
  649.3 25.8 %collective-permute-start.43 = (bf16[768,256]{1,0:T(8,128)(2,1)S(1)}, bf16[768,256]{1,0:T(8,128)(2,1)S(1)}, u32[]{:S(2)}, u32[]{:S(2)}) collective-permute-start(bf16[768,256]{1,0:T(8,128)(2,1)S(1)} %get-tuple-element.420), channel_id=1, source_target_pairs={{0,12},{4,8},{8,4},{12,0},{1,13},{5,9},{9,5},{13,1},{2,14},{6,10},... | collective-permute-start | bytes 1179656 | tf_op jit(solution)/shard_map/ppermute | solution.py:425
  651.8 31.1 %collective-permute-start.42 = (bf16[768,256]{1,0:T(8,128)(2,1)S(1)}, bf16[768,256]{1,0:T(8,128)(2,1)S(1)}, u32[]{:S(2)}, u32[]{:S(2)}) collective-permute-start(bf16[768,256]{1,0:T(8,128)(2,1)S(1)} %get-tuple-element.421), channel_id=1, source_target_pairs={{0,8},{4,12},{8,0},{12,4},{1,9},{5,13},{9,1},{13,5},{2,10},{6,14},... | collective-permute-start | bytes 1179656 | tf_op jit(solution)/shard_map/ppermute | solution.py:425
  651.8 23.3 %collective-permute-start.39 = (bf16[768,256]{1,0:T(8,128)(2,1)S(1)}, bf16[768,256]{1,0:T(8,128)(2,1)S(1)}, u32[]{:S(2)}, u32[]{:S(2)}) collective-permute-start(bf16[768,256]{1,0:T(8,128)(2,1)S(1)} %get-tuple-element.422), channel_id=1, source_target_pairs={{0,4},{4,0},{8,12},{12,8},{1,5},{5,1},{9,13},{13,9},{2,6},{6,2},{1... | collective-permute-start | bytes 1179656 | tf_op jit(solution)/shard_map/ppermute | solution.py:425
  692.1 13.3 %collective-permute-start.51 = (f32[2,256]{1,0:T(2,128)}, f32[2,256]{1,0:T(2,128)S(1)}, u32[]{:S(2)}, u32[]{:S(2)}) collective-permute-start(f32[2,256]{1,0:T(2,128)} %bitcast.242), channel_id=1, source_target_pairs={{0,4},{4,0},{8,12},{12,8},{1,5},{5,1},{9,13},{13,9},{2,6},{6,2},{1... | collective-permute-start | bytes 6152 | tf_op jit(solution)/shard_map/ppermute | solution.py:425
  692.1 15.2 %collective-permute-start.52 = (f32[2,256]{1,0:T(2,128)}, f32[2,256]{1,0:T(2,128)}, u32[]{:S(2)}, u32[]{:S(2)}) collective-permute-start(f32[2,256]{1,0:T(2,128)} %bitcast.241), channel_id=1, source_target_pairs={{0,8},{4,12},{8,0},{12,4},{1,9},{5,13},{9,1},{13,5},{2,10},{6,14},... | collective-permute-start | bytes 6152 | tf_op jit(solution)/shard_map/ppermute | solution.py:425
  695.1 12.3 %collective-permute-start.53 = (f32[2,256]{1,0:T(2,128)S(1)}, f32[2,256]{1,0:T(2,128)}, u32[]{:S(2)}, u32[]{:S(2)}) collective-permute-start(f32[2,256]{1,0:T(2,128)S(1)} %bitcast.289), channel_id=1, source_target_pairs={{0,12},{4,8},{8,4},{12,0},{1,13},{5,9},{9,5},{13,1},{2,14},{6,10},... | collective-permute-start | bytes 6152 | tf_op jit(solution)/shard_map/ppermute | solution.py:425
  697.6 25.9 %collective-permute-start.50 = (bf16[256,128]{1,0:T(8,128)(2,1)}, bf16[256,128]{1,0:T(8,128)(2,1)}, u32[]{:S(2)}, u32[]{:S(2)}) collective-permute-start(bf16[256,128]{1,0:T(8,128)(2,1)} %get-tuple-element.476), channel_id=1, source_target_pairs={{0,12},{4,8},{8,4},{12,0},{1,13},{5,9},{9,5},{13,1},{2,14},{6,10},... | collective-permute-start | bytes 196616 | tf_op jit(solution)/shard_map/ppermute | solution.py:425
  700.0 23.9 %collective-permute-start.49 = (bf16[256,128]{1,0:T(8,128)(2,1)}, bf16[256,128]{1,0:T(8,128)(2,1)}, u32[]{:S(2)}, u32[]{:S(2)}) collective-permute-start(bf16[256,128]{1,0:T(8,128)(2,1)} %get-tuple-element.477), channel_id=1, source_target_pairs={{0,8},{4,12},{8,0},{12,4},{1,9},{5,13},{9,1},{13,5},{2,10},{6,14},... | collective-permute-start | bytes 196616 | tf_op jit(solution)/shard_map/ppermute | solution.py:425
  705.4 18.6 %collective-permute-start.48 = (bf16[256,128]{1,0:T(8,128)(2,1)}, bf16[256,128]{1,0:T(8,128)(2,1)S(1)}, u32[]{:S(2)}, u32[]{:S(2)}) collective-permute-start(bf16[256,128]{1,0:T(8,128)(2,1)} %get-tuple-element.478), channel_id=1, source_target_pairs={{0,4},{4,0},{8,12},{12,8},{1,5},{5,1},{9,13},{13,9},{2,6},{6,2},{1... | collective-permute-start | bytes 196616 | tf_op jit(solution)/shard_map/ppermute | solution.py:425
  707.4 19.0 %collective-permute-start.41 = (bf16[2,256,256]{2,1,0:T(8,128)(2,1)}, bf16[2,256,256]{2,1,0:T(8,128)(2,1)}, u32[]{:S(2)}, u32[]{:S(2)}) collective-permute-start(bf16[2,256,256]{2,1,0:T(8,128)(2,1)} %broadcast_select_fusion.6), channel_id=1, source_target_pairs={{0,16},{16,0},{1,17},{17,1},{2,18},{18,2},{3,19},{19,3},{4,20},{20... | collective-permute-start | bytes 786440 | tf_op jit(solution)/shard_map/ppermute | solution.py:470
  707.4 21.3 %collective-permute-start.44 = (bf16[2,256,256]{2,1,0:T(8,128)(2,1)}, bf16[2,256,256]{2,1,0:T(8,128)(2,1)}, u32[]{:S(2)}, u32[]{:S(2)}) collective-permute-start(bf16[2,256,256]{2,1,0:T(8,128)(2,1)} %broadcast_select_fusion.2), channel_id=1, source_target_pairs={{0,16},{16,0},{1,17},{17,1},{2,18},{18,2},{3,19},{19,3},{4,20},{20... | collective-permute-start | bytes 786440 | tf_op jit(solution)/shard_map/ppermute | solution.py:470
  710.0 8.6 %all-to-all-start.12 = ((f32[8,2,256]{2,1,0:T(2,128)}), f32[8,2,256]{2,1,0:T(2,128)S(1)}, u32[]{:S(2)}, u32[]{:S(2)}) async-start(f32[8,2,256]{2,1,0:T(2,128)} %broadcast_in_dim.161), calls=%async_computation.14 | async-start | bytes 32768 | tf_op jit(solution)/shard_map/all_to_all | solution.py:416
  718.6 16.4 %all-to-all-start.11 = ((bf16[8,3,128,128]{3,2,1,0:T(8,128)(2,1)}), bf16[8,3,128,128]{3,2,1,0:T(8,128)(2,1)}, u32[]{:S(2)}, u32[]{:S(2)}) async-start(bf16[8,3,128,128]{3,2,1,0:T(8,128)(2,1)} %bitcast.258), calls=%async_computation.13 | async-start | bytes 1572864 | tf_op jit(solution)/shard_map/all_to_all | solution.py:416
  723.5 6.1 collective-permute-start.40
  736.6 9.7 %collective-permute-start.47 = (bf16[128,3,256]{0,2,1:T(8,128)(2,1)S(1)}, bf16[128,3,256]{0,2,1:T(8,128)(2,1)S(1)}, u32[]{:S(2)}, u32[]{:S(2)}) collective-permute-start(bf16[128,3,256]{0,2,1:T(8,128)(2,1)S(1)} %get-tuple-element.453), channel_id=1, source_target_pairs={{0,12},{4,8},{8,4},{12,0},{1,13},{5,9},{9,5},{13,1},{2,14},{6,10},... | collective-permute-start | bytes 589832 | tf_op jit(solution)/shard_map/ppermute | solution.py:425
  739.1 16.8 %collective-permute-start.46 = (bf16[128,3,256]{0,2,1:T(8,128)(2,1)S(1)}, bf16[128,3,256]{0,2,1:T(8,128)(2,1)S(1)}, u32[]{:S(2)}, u32[]{:S(2)}) collective-permute-start(bf16[128,3,256]{0,2,1:T(8,128)(2,1)S(1)} %get-tuple-element.454), channel_id=1, source_target_pairs={{0,8},{4,12},{8,0},{12,4},{1,9},{5,13},{9,1},{13,5},{2,10},{6,14},... | collective-permute-start | bytes 589832 | tf_op jit(solution)/shard_map/ppermute | solution.py:425
  739.1 16.8 %collective-permute-start.45 = (bf16[128,3,256]{0,2,1:T(8,128)(2,1)S(1)}, bf16[128,3,256]{0,2,1:T(8,128)(2,1)S(1)}, u32[]{:S(2)}, u32[]{:S(2)}) collective-permute-start(bf16[128,3,256]{0,2,1:T(8,128)(2,1)S(1)} %get-tuple-element.455), channel_id=1, source_target_pairs={{0,4},{4,0},{8,12},{12,8},{1,5},{5,1},{9,13},{13,9},{2,6},{6,2},{1... | collective-permute-start | bytes 589832 | tf_op jit(solution)/shard_map/ppermute | solution.py:425
  (87 other events, 677.0 us)
Sparse Core Ops, SparseCore 0:
  87.0 191.7 all-gather.2
  331.9 60.3 reduce-scatter.2
  396.3 117.4 reduce-scatter.4

commit v3 on v2

--- a/solution.py
+++ b/solution.py
@@ -416,14 +416,24 @@
     return lax.all_to_all(blocks, axes, 0, 0, tiled=True)
 
 
+def line_sends(blocks, axis="head"):
+    me = lax.axis_index(axis)
+    return [
+        lax.dynamic_index_in_dim(blocks, me ^ step, 0, keepdims=False)
+        for step in range(1, blocks.shape[0])
+    ]
+
+
+def line_go(sends, axis="head"):
+    count = len(sends) + 1
+    return [
+        lax.ppermute(send, axis, [(j, j ^ (step + 1)) for j in range(count)])
+        for step, send in enumerate(sends)
+    ]
+
+
 def send_line(blocks, axis="head"):
-    count = blocks.shape[0]
-    me = lax.axis_index(axis)
-    got = []
-    for step in range(1, count):
-        send = lax.dynamic_index_in_dim(blocks, me ^ step, 0, keepdims=False)
-        got.append(lax.ppermute(send, axis, [(j, j ^ step) for j in range(count)]))
-    return blocks, got
+    return blocks, line_go(line_sends(blocks, axis), axis)
 
 
 def join_line(blocks, got, axis="head"):
@@ -464,6 +474,19 @@
         jnp.where(here < 2, jnp.stack([a, b, c, d]), jnp.stack([c, d, a, b])),
         jnp.where(here < 2, jnp.stack([b, a, d, c]), jnp.stack([d, c, b, a])),
     )
+
+
+def in_pieces(values):
+    pieces = []
+    for _ in range(3):
+        piece = lax.reduce_precision(values, 8, 7)
+        pieces.append(piece.astype(BF16))
+        values = values - piece
+    return pieces
+
+
+def from_pieces(pieces):
+    return sum(p.astype(F32) for p in pieces)
 
 
 def swap(values):
@@ -806,8 +829,8 @@
 
 
 def hidden_back_kernel(
-    h_ref, ya_ref, yb_ref, dna_ref, dnb_ref, ob_ref, c_ref, wall_ref, gain_ref,
-    out_ref, dh_ref, dob_ref, gout_ref, ggain_ref, ow_ref, low_ref,
+    h_ref, ya_ref, yb_ref, dna_ref, dnb_ref, c_ref, wall_ref, gain_ref,
+    out_ref, dh_ref, dob_ref, low_ref, ggain_ref, ow_ref,
 ):
     fill_out_weight(wall_ref, ow_ref)
     groups = wall_ref.shape[0]
@@ -837,6 +860,10 @@
         for b in range(blocks):
             dob_ref[b, here, :] = made[:, b * width : (b + 1) * width]
     ggain_ref[...] = ggain
+
+
+def out_grad_kernel(ob_ref, low_ref, gout_ref):
+    groups = gout_ref.shape[0]
     high, wide = gout_ref.shape[2], gout_ref.shape[3]
     for z in range(gout_ref.shape[1]):
         made = contract_rows(ob_ref[:, z * high : (z + 1) * high], low_ref[...]).astype(BF16)
@@ -943,7 +970,9 @@
             ),
         ]
         ids = jnp.stack(ids)
-        starts = jnp.sum((ids[:, None, :] < ids[:, :, None]).astype(jnp.int32), axis=2)
+        numbers = jnp.arange(8, dtype=jnp.int32)[None, :, None]
+        lower = jnp.sum((ids[:, None, :] < numbers).astype(jnp.int32), axis=2, keepdims=True)
+        starts = jnp.sum(jnp.where(ids[:, None, :] == numbers, lower, 0), axis=1)
         lows = starts[:, ::BQ] // BK
 
         places = jnp.arange(seq_len, dtype=jnp.int32)
@@ -963,12 +992,7 @@
         )
         deep = qkv_weight.shape[0]
         part = qkv_weight.reshape(deep, 3, 2, lanes).transpose(2, 1, 0, 3).reshape(-1, lanes)
-        left = jnp.concatenate([attn_gain, mlp_gain]).reshape(-1, lanes)
-        pieces = []
-        for _ in range(3):
-            piece = lax.reduce_precision(left, 8, 7)
-            pieces.append(piece.astype(BF16))
-            left = left - piece
+        pieces = in_pieces(jnp.concatenate([attn_gain, mlp_gain]).reshape(-1, lanes))
         tail = jnp.concatenate(pieces + [jnp.zeros((4, lanes), BF16)], axis=0)
         part = jnp.concatenate([part, tail], axis=0)
         part = exchange(jnp.broadcast_to(part[None], (depth,) + part.shape), "head")
@@ -993,6 +1017,9 @@
         wall = lax.all_gather(wall, ("dp", "ffn", "head"), axis=0, tiled=False)
         wall = wall.reshape(group, depth, wall.shape[1], lanes)
         nm = exchange(nm, "ffn")
+        grad_blocks = jnp.concatenate(to_layers(cotangent), axis=1)
+        grad_sends = line_sends(grad_blocks)
+        nm, grad_blocks, grad_sends = after(nm, grad_blocks, grad_sends)
         first_got, ns, nm = after(first_got, ns, nm)
         first = join_across(first_got)
 
@@ -1036,9 +1063,8 @@
         ns = exchange(ns, "ffn")
         nm_other = swap(nm)
         kept = [attend_at(0, (nm,))]
-        grad_blocks = jnp.concatenate(to_layers(cotangent), axis=1)
-        nm_other, ns, grad_blocks, kept[0] = after(nm_other, ns, grad_blocks, kept[0])
-        grad_blocks, grad_got = send_line(grad_blocks)
+        nm_other, ns, grad_sends, kept[0] = after(nm_other, ns, grad_sends, kept[0])
+        grad_got = line_go(grad_sends)
         ns_other = swap(ns)
         kept.append(attend_at(1, (nm_other,)))
         ns_other, grad_got[0], kept[1] = after(ns_other, grad_got[0], kept[1])
@@ -1126,17 +1152,17 @@
         grads_a = layer_sum(grads_a)
         grads_b = layer_sum(grads_b)
 
-        out, dh, dob, gout, gain_two = pl.pallas_call(
+        out, dh, dob, low, gain_two = pl.pallas_call(
             hidden_back_kernel,
             grid=(1,),
             out_shape=(
                 jax.ShapeDtypeStruct(grad_blocks.shape, BF16),
                 whole,
                 jax.ShapeDtypeStruct(grad_blocks.shape, BF16),
-                jax.ShapeDtypeStruct((group, depth, out_rows, lanes), BF16),
+                whole_low,
                 jax.ShapeDtypeStruct((1, full_width), F32),
             ),
-            in_specs=[fixed((rows, full_width))] * 6
+            in_specs=[fixed((rows, full_width))] * 5
             + [fixed(grad_blocks.shape), out_spec, fixed((1, full_width))],
             out_specs=tuple(
                 fixed(s)
@@ -1144,15 +1170,26 @@
                     grad_blocks.shape,
                     (rows, full_width),
                     grad_blocks.shape,
-                    (group, depth, out_rows, lanes),
+                    (rows, full_width),
                     (1, full_width),
                 )
             ),
-            scratch_shapes=[ow_scratch, pltpu.VMEM((rows, full_width), BF16)],
+            scratch_shapes=[ow_scratch],
             compiler_params=compiler_params(60),
-        )(h, ya, yb, dna, dnb, ob, grad_blocks, wall, gains[1])
-
+        )(h, ya, yb, dna, dnb, grad_blocks, wall, gains[1])
+
+        low, dob = after(low, dob)
         dob = exchange(dob, "ffn")
+        gout_shape = (group, depth, out_rows, lanes)
+        gout = pl.pallas_call(
+            out_grad_kernel,
+            grid=(1,),
+            out_shape=jax.ShapeDtypeStruct(gout_shape, BF16),
+            in_specs=[fixed((rows, full_width))] * 2,
+            out_specs=fixed(gout_shape),
+            compiler_params=compiler_params(48),
+        )(ob, low)
+        dob, gout = after(dob, gout)
         do_mine, do_got = pair_halves(dob)
 
         def back_of(i, grads_in):
@@ -1194,7 +1231,8 @@
         gfv_main = lane_join(
             gfv_a.reshape(side, length, lanes), gfv_other.reshape(side, length, lanes)
         )
-        do_mine, main_sum, grads_b = after(do_mine, main_sum, grads_b)
+        gout = exchange_line(jnp.sum(gout.astype(F32), axis=0).astype(BF16))
+        do_mine, main_sum, grads_b, gout = after(do_mine, main_sum, grads_b, gout)
         main_sum = exchange(main_sum, "ffn")
         grads_b, b_got = send_line(grads_b)
         dn_s, dn_t, gw_s, gfv_s = back_of(2, (do_mine, do_got))
@@ -1206,43 +1244,35 @@
         shared_sum = exchange(shared_sum, "ffn")
         tokm, gain_main = last(0, x, dh, main_sum, gains[0])
         shared_sum, tokm = after(shared_sum, tokm)
+        shared_sum, tokm = after(shared_sum, tokm)
         tokm, tokm_got = send_line(tokm)
-        gfv, shared_sum, tokm_got[0] = after(gfv, shared_sum, tokm_got[0])
+        gfv, shared_sum = after(gfv, shared_sum)
         gfv = exchange(gfv, "ffn")
         toks, gain_shared = last(length, x, dh, shared_sum, gains[0])
+        grad_w = (gw_a + gw_b + gw_s).astype(BF16)
+        grad_w = grad_w.reshape(3, lanes, group, deep).transpose(2, 0, 3, 1)
+        grad_w = grad_w.reshape(group, 3 * deep, lanes)
+        gain_both = jnp.concatenate([gain_main + gain_shared, gain_two]).reshape(-1, lanes)
+        gain_rows = gain_both.shape[0]
+        tail = jnp.concatenate(in_pieces(gain_both), axis=0)
+        tail = jnp.broadcast_to(tail[None], (group,) + tail.shape)
+        grad_w = jnp.concatenate([grad_w, tail], axis=1)
+        toks, tokm_got = after(toks, tokm_got)
         toks, toks_got = send_line(toks)
-        tokm_got, toks = after(tokm_got, toks)
-        gfv, tokm_got, toks_got = after(gfv, tokm_got, toks_got)
+        grad_w, gfv = after(grad_w, gfv)
+        grad_w = exchange(grad_w, layer)
+        gfv, toks_got = after(gfv, toks_got)
         gfv, gfv_got = send_line(gfv)
-        gfv_got[0], grad_w, gout, gain_shared, grads_b, out, toks_got = after(
-            gfv_got[0],
-            (gw_a + gw_b + gw_s).astype(BF16),
-            gout,
-            gain_shared,
-            grads_b,
-            out,
-            toks_got,
-        )
+        tail = grad_w[:, 3 * deep :].astype(F32).reshape(group, 3, gain_rows, lanes)
+        tail = jnp.sum(tail, axis=(0, 1)).reshape(2, depth, -1, lanes).transpose(1, 0, 2, 3)
+        tail = jnp.concatenate(in_pieces(tail.reshape(depth, -1, lanes)), axis=1)
+        grad_w = grad_w[:, : 3 * deep].reshape(2, side, 3, deep, lanes)
+        grad_w = grad_w.transpose(1, 2, 0, 3, 4).reshape(depth, 6 * deep, lanes)
+        grad_w, w_got = send_line(jnp.concatenate([grad_w, tail], axis=1))
         out_tokens = from_layers(out[:, :length], out[:, length:])
         grads_b = join_line(grads_b, b_got)
         token_grads = from_layers(join_line(tokm, tokm_got), join_line(toks, toks_got))
-        gfv = join_line(gfv, gfv_got)
-        value_grads = from_layers(gfv[:, :length], gfv[:, length:])
-
-        gout = jnp.sum(gout.astype(F32), axis=0).astype(BF16)
-        grad_out = jnp.sum(exchange_line(gout).astype(F32), axis=0)
-
-        grad_w = grad_w.reshape(3, lanes, group, deep).transpose(2, 0, 3, 1)
-        grad_w = exchange(grad_w, layer)
-        grad_w = grad_w.reshape(2, side, 3, deep, lanes).transpose(1, 3, 2, 0, 4)
-        grad_w = grad_w.reshape(depth, deep, 3, width)
-        grad_qkv = jnp.sum(exchange_line(grad_w).astype(F32), axis=0)
-
-        gain_both = jnp.concatenate([gain_main + gain_shared, gain_two]).reshape(2, depth, width)
-        gain_both = exchange_line(gain_both.transpose(1, 0, 2))
-        gain_both = jnp.sum(gain_both, axis=0, keepdims=True)
-        gain_both = exchange(jnp.broadcast_to(gain_both, (group, 2, width)), layer)
-        gain_both = jnp.sum(gain_both, axis=0)
+        grad_out = jnp.sum(gout.astype(F32), axis=0)
 
         def untile(values):
             return values.reshape(-1, deep, lanes).transpose(1, 0, 2).reshape(deep, -1)
@@ -1256,6 +1286,17 @@
         grad_gate = jnp.stack(
             [jnp.concatenate(g, axis=1)[:, :hidden] for g in (gates, ups)], axis=1
         )
+        grad_down = jnp.concatenate(downs, axis=0)
+        gfv_got, w_got, grad_gate, grad_down, grad_out, out_tokens, token_grads = after(
+            gfv_got, w_got, grad_gate, grad_down, grad_out, out_tokens, token_grads
+        )
+        grad_w = join_line(grad_w, w_got)
+        tail = jnp.sum(grad_w[:, 6 * deep :].astype(F32).reshape(depth, 3, 2, width), axis=(0, 1))
+        grad_qkv = jnp.sum(grad_w[:, : 6 * deep].astype(F32), axis=0).reshape(3, 2, deep, lanes)
+        grad_qkv = grad_qkv.transpose(2, 0, 1, 3).reshape(deep, 3, width)
+        gfv = join_line(gfv, gfv_got)
+        value_grads = from_layers(gfv[:, :length], gfv[:, length:])
+
         return (
             out_tokens,
             token_grads,
@@ -1263,9 +1304,9 @@
             grad_qkv,
             grad_out,
             grad_gate,
-            jnp.concatenate(downs, axis=0),
-            gain_both[0],
-            gain_both[1],
+            grad_down,
+            tail[0],
+            tail[1],
         )
 
     return run

time: 779 us -> 736 us (0.945)
  blocking collectives: 23.4 us -> 0 us
    all_to_all x12, waiting for transfers between devices: 38.2 us -> 125 us  [exchange(): return lax.all_to_all(blocks, axes, 0, 0, tiled=True)]
    ppermute x4, waiting for transfers between devices: 70.4 us -> 4.37 us  [send_across(): got.append(lax.ppermute(send, ('head', 'ffn'), pairs))]
    all_to_all x1 -> x0, blocking collectives: 23.4 us -> none  [exchange(): return lax.all_to_all(blocks, axes, 0, 0, tiled=True)]
    ppermute x33 -> x30, waiting for transfers between devices: 75.2 us -> 63.4 us  [line_go(): lax.ppermute(send, axis, [(j, j ^ step + 1) for j in range(count)])]
    reduce_scatter x2, waiting for transfers between devices: 17.8 us -> 7.87 us  [layer_sum(): lax.psum_scatter(grads, layer, scatter_dimension=0, tiled=True)]
    dynamic_update_slice x33 -> x30, local copies, waits for them, and re-layouts: 21.3 us -> 17.7 us  [join_line(): blocks = lax.dynamic_update_index_in_dim(blocks, piece, me ^ step + 1, 0)]
    unnamed x169 -> x154, local copies, waits for them, and re-layouts: 23.1 us -> 26.6 us
    ppermute x33 -> x30, starting transfers between devices: 59.2 us -> 58.8 us  [line_go(): lax.ppermute(send, axis, [(j, j ^ step + 1) for j in range(count)])]
  transfers between devices with their start and end apart: 69 -> 66, of which waited for: 23 -> 24; matrix products, arithmetic and copies ran while one was open for 14% -> 14% of each run, Pallas kernels for 29% -> 29%
where the time goes in v3:
time: 736 us; the launch traced here: 727 us
  Pallas kernels  243 us (33%)
  waiting for transfers between devices  207 us (28%)
  starting transfers between devices  122 us (17%)
  local copies, waits for them, and re-layouts  83.2 us (11%)
  other arithmetic  55.3 us (8%)
  between operations  15.5 us (2%)
    all_to_all x12, waiting for transfers between devices, exchange(): return lax.all_to_all(blocks, axes, 0, 0, tiled=True)  125 us
    pallas_call x3, Pallas kernels, attend_back(): pl.pallas_call(functools.partial(attend_back_kernel, count), grid=(1,), o...  87.6 us
    ppermute x30, waiting for transfers between devices, line_go(): lax.ppermute(send, axis, [(j, j ^ step + 1) for j in range(count)])  63.4 us
    pallas_call x2, Pallas kernels, feed_forward(): pl.pallas_call(functools.partial(mlp_kernel, begin_tile, real, out_rows,...  61.5 us
    ppermute x30, starting transfers between devices, line_go(): lax.ppermute(send, axis, [(j, j ^ step + 1) for j in range(count)])  58.8 us
    pallas_call x3, Pallas kernels, attend(): pl.pallas_call(functools.partial(attend_kernel, count), grid=(1,), out_sh...  58.4 us
    all_to_all x12, starting transfers between devices, exchange(): return lax.all_to_all(blocks, axes, 0, 0, tiled=True)  53.5 us
    unnamed x154, local copies, waits for them, and re-layouts  26.6 us
  transfers between devices with their start and end apart: 66, of which 24 were waited for; matrix products, arithmetic and copies ran while one was open for 14% of the time, Pallas kernels for 29%

profile of v3, /device:TPU:0, one launch (start us, length us, event | category | flops | bytes accessed | tf_op | source)
XLA Modules:
  0.0 726.6 jit_solution(12695605734495196724)
XLA Ops:
  14.9 6.3 all-to-all-start
  22.0 4.0 fusion.1
  27.8 2.6 pad_maximum_fusion.2
  37.4 3.8 collective-permute-start.3
  45.2 13.7 %all-to-all-done = bf16[4,784,128]{2,1,0:T(8,128)(2,1)} async-done(((bf16[4,784,128]{2,1,0:T(8,128)(2,1)}), bf16[4,784,128]{2,1,0:T(8,128)(2,1)}, u32[]{:S(2)}, u32[]{:S(2)}) %all-to-all-start) | async-done | bytes 802848 | tf_op jit(solution)/shard_map/all_to_all | solution.py:416
  61.0 4.2 all-to-all-start.1
  68.2 9.1 %all-to-all-done.1 = bf16[8,3,128,128]{3,2,1,0:T(8,128)(2,1)} async-done(((bf16[8,3,128,128]{3,2,1,0:T(8,128)(2,1)}), bf16[8,3,128,128]{3,2,1,0:T(8,128)(2,1)}, u32[]{:S(2)}, u32[]{:S(2)}) %all-to-all-start.1) | async-done | bytes 786464 | tf_op jit(solution)/shard_map/all_to_all | solution.py:416
  77.3 2.4 copy.82
  85.0 3.3 shard_map.169
  88.4 4.9 all-to-all-start.2
  95.5 2.5 collective-permute-start.7
  97.9 4.5 collective-permute-start.6
  104.8 61.6 %all-to-all-done.2.refs_0_ = bf16[4,512,1024]{2,1,0:T(8,128)(2,1)} async-done(((bf16[4,512,1024]{2,1,0:T(8,128)(2,1)}), bf16[4,512,1024]{2,1,0:T(8,128)(2,1)}, u32[]{:S(2)}, u32[]{:S(2)}) %all-to-all-start.2) | async-done | bytes 4194336 | tf_op jit(solution)/shard_map/all_to_all | solution.py:416
  166.3 2.9 collective-permute-done.9
  171.4 4.9 all-to-all-start.3
  177.4 4.0 fusion
  182.7 18.5 %shard_map.170 = (bf16[2048,128]{1,0:T(8,128)(2,1)S(1)}, bf16[2048,128]{1,0:T(8,128)(2,1)S(1)}, bf16[2048,128]{1,0:T(8,128)(2,1)S(1)}, bf16[2048,128]{1,0:T(8,128)(2,1)S(1)}, f32[2048,128]{1,0:T(8,128)S(1)}) custom-call(s32[1]{0:T(128)} %bitcast.side_ref, s32[4]{0:T(128)S(1)} %get-tuple-element.521.low_ref, bf16[4,512,1024]{2,1,0:T(8,128)(2,1)} %all-to-all-done.2.refs_0_, ...), custom_call_target="tpu_custom_call" | custom-call | tf_op jit(solution)/shard_map/pallas_call | solution.py:620
  207.0 3.0 collective-permute-done.14.refs_1_.refs_3_
  210.0 18.4 %shard_map.171 = (bf16[2048,128]{1,0:T(8,128)(2,1)S(1)}, bf16[2048,128]{1,0:T(8,128)(2,1)S(1)}, bf16[2048,128]{1,0:T(8,128)(2,1)S(1)}, bf16[2048,128]{1,0:T(8,128)(2,1)S(1)}, f32[2048,128]{1,0:T(8,128)S(1)}) custom-call(s32[1]{0:T(128)} %bitcast.side_ref, s32[4]{0:T(128)S(1)} %get-tuple-element.520.low_ref, ...), custom_call_target="tpu_custom_call" | custom-call | tf_op jit(solution)/shard_map/pallas_call | solution.py:620
  231.9 9.9 %collective-permute-done.13 = bf16[768,256]{1,0:T(8,128)(2,1)} collective-permute-done((bf16[768,256]{1,0:T(8,128)(2,1)}, bf16[768,256]{1,0:T(8,128)(2,1)}, u32[]{:S(2)}, u32[]{:S(2)}) %collective-permute-start.13) | collective-permute-done | bytes 393248 | tf_op jit(solution)/shard_map/ppermute | solution.py:430
  245.0 4.5 all-to-all-start.4
  250.9 21.5 %shard_map.172 = (bf16[2048,128]{1,0:T(8,128)(2,1)S(1)}, bf16[2048,128]{1,0:T(8,128)(2,1)S(1)}, bf16[2048,128]{1,0:T(8,128)(2,1)S(1)}, bf16[2048,128]{1,0:T(8,128)(2,1)S(1)}, f32[2048,128]{1,0:T(8,128)S(1)}) custom-call(s32[1]{0:T(128)} %bitcast.side_ref, s32[4]{0:T(128)S(1)} %get-tuple-element.519.low_ref, bf16[4,256,1024]{2,1,0:T(8,128)(2,1)} %all-to-all-done.3.refs_0_, ...), custom_call_target="tpu_custom_call" | custom-call | tf_op jit(solution)/shard_map/pallas_call | solution.py:620
  275.0 6.1 collective-permute-done.16
  283.7 3.5 all-to-all-start.5
  289.1 6.6 all-to-all-done.5.os_ref
  296.5 7.4 %shard_map.173 = (f32[768,1024]{1,0:T(8,128)}, bf16[768,1024]{1,0:T(8,128)(2,1)}, bf16[768,1024]{1,0:T(8,128)(2,1)}) custom-call(bf16[4,512,256]{2,1,0:T(8,128)(2,1)} %all-to-all-done.4.om_ref, bf16[4,256,256]{2,1,0:T(8,128)(2,1)} %copy-done.43, bf16[4,768,256]{2,1,0:T(8,128)(2,1)} %copy-done, bf16[8,4,2496,128]{3,2,1,0:T(8,128)(2,1)} %bitcast.251, ...), custom_call_target="tpu_custom_call" | custom-call | tf_op jit(solution)/shard_map/pallas_call | solution.py:1093
  307.3 22.8 %shard_map.174 = (f32[768,1024]{1,0:T(8,128)}, f32[768,1024]{1,0:T(8,128)}, bf16[8,4,704,128]{3,2,1,0:T(8,128)(2,1)}) custom-call(bf16[768,1024]{1,0:T(8,128)(2,1)} %get-tuple-element.280.n_ref, bf16[4,768,256]{2,1,0:T(8,128)(2,1)} %copy-done.26, bf16[8,4,2496,128]{3,2,1,0:T(8,128)(2,1)} %bitcast.252), custom_call_target="tpu_custom_call" | custom-call | tf_op jit(solution)/shard_map/pallas_call | solution.py:1113
  330.3 38.7 %shard_map.175 = (f32[768,1024]{1,0:T(8,128)}, f32[768,1024]{1,0:T(8,128)}, bf16[8,4,1536,128]{3,2,1,0:T(8,128)(2,1)}) custom-call(bf16[768,1024]{1,0:T(8,128)(2,1)} %get-tuple-element.280.n_ref, bf16[4,768,256]{2,1,0:T(8,128)(2,1)} %copy-done.26, bf16[8,4,2496,128]{3,2,1,0:T(8,128)(2,1)} %bitcast.253), custom_call_target="tpu_custom_call" | custom-call | tf_op jit(solution)/shard_map/pallas_call | solution.py:1113
  369.1 12.6 %shard_map.176 = (bf16[4,768,256]{2,1,0:T(8,128)(2,1)}, f32[768,1024]{1,0:T(8,128)}, bf16[4,768,256]{2,1,0:T(8,128)(2,1)}, bf16[768,1024]{1,0:T(8,128)(2,1)}, f32[1,1024]{1,0:T(1,128)}) custom-call(f32[768,1024]{1,0:T(8,128)} %get-tuple-element.265.h_ref, f32[768,1024]{1,0:T(8,128)} %get-tuple-element.279.ya_ref, f32[768,1024]{1,0:T(8,128)} %get-tuple-element.281.yb_ref, ...), custom_call_target="tpu_custom_call" | custom-call | tf_op jit(solution)/shard_map/pallas_call | solution.py:1155
  381.7 4.9 all-to-all-start.6
  386.6 3.2 shard_map.177
  389.8 15.9 %all-to-all-done.6 = bf16[4,768,256]{2,1,0:T(8,128)(2,1)} async-done(((bf16[4,768,256]{2,1,0:T(8,128)(2,1)}), bf16[4,768,256]{2,1,0:T(8,128)(2,1)}, u32[]{:S(2)}, u32[]{:S(2)}) %all-to-all-start.6) | async-done | bytes 1572896 | tf_op jit(solution)/shard_map/all_to_all | solution.py:416
  405.7 2.4 constant_dynamic-slice_fusion
  408.1 2.8 collective-permute-start.21
  412.8 29.7 %shard_map.178 = (bf16[4,512,1024]{2,1,0:T(8,128)(2,1)}, f32[384,1024]{1,0:T(8,128)}, bf16[2048,128]{1,0:T(8,128)(2,1)}) custom-call(s32[1]{0:T(128)} %bitcast.side_ref, s32[4]{0:T(128)} %copy-done.22, bf16[4,512,1024]{2,1,0:T(8,128)(2,1)} %collective-permute-done.11.refs_0_, bf16[4,768,128]{2,1,0:T(8,128)(2,1)} %copy-done.40, bf16[1024,384]{1,0:T(8,128)(2,1)} %copy-done.1, ...), custom_call_target="tpu_custom_call" | custom-call | tf_op jit(solution)/shard_map/pallas_call | solution.py:711
  444.0 3.7 all-to-all-start.7
  447.8 6.5 collective-permute-start.26
  455.0 4.4 collective-permute-start.23
  459.4 26.9 %shard_map.179 = (bf16[4,512,1024]{2,1,0:T(8,128)(2,1)}, f32[384,1024]{1,0:T(8,128)}, bf16[2048,128]{1,0:T(8,128)(2,1)}) custom-call(s32[1]{0:T(128)} %bitcast.side_ref, s32[4]{0:T(128)} %copy-done.21, bf16[4,512,1024]{2,1,0:T(8,128)(2,1)} %all-to-all-done.2.refs_0_, bf16[4,768,128]{2,1,0:T(8,128)(2,1)} %get-tuple-element.324.refs_1_.refs_2_, ...), custom_call_target="tpu_custom_call" | custom-call | tf_op jit(solution)/shard_map/pallas_call | solution.py:711
  487.0 4.0 all-to-all-done.7
  491.5 3.4 collective-permute-start.29
  501.3 7.8 %add_convert_fusion = bf16[4,512,1024]{2,1,0:T(8,128)(2,1)} fusion(bf16[4,512,1024]{2,1,0:T(8,128)(2,1)} %collective-permute-done.22, bf16[4,512,1024]{2,1,0:T(8,128)(2,1)} %get-tuple-element.316), kind=kLoop, calls=%fused_computation | loop fusion | flops 8388608 | bytes 12582912 | tf_op jit(solution)/shard_map/convert_element_type | solution.py:1227
  510.3 7.9 %reduce-scatter.5.cloned.1.call-done = bf16[1,4,1536,128]{3,2,1,0:T(8,128)(2,1)} async-done(((bf16[8,4,1536,128]{3,2,1,0:T(8,128)(2,1)}), bf16[1,4,1536,128]{3,2,1,0:T(8,128)(2,1)}) %reduce-scatter.5.cloned.1.call-update) | async-done | bytes 1572880 | tf_op jit(solution)/shard_map/reduce_scatter | solution.py:1150
  518.2 5.0 all-to-all-start.8
  524.2 3.3 collective-permute-start.32
  530.9 31.0 %shard_map.180 = (bf16[4,256,1024]{2,1,0:T(8,128)(2,1)}, bf16[4,256,1024]{2,1,0:T(8,128)(2,1)}, f32[384,1024]{1,0:T(8,128)}, bf16[2048,128]{1,0:T(8,128)(2,1)}) custom-call(s32[1]{0:T(128)} %bitcast.side_ref, s32[4]{0:T(128)} %copy-done.23, bf16[4,256,1024]{2,1,0:T(8,128)(2,1)} %all-to-all-done.3.refs_0_, ...), custom_call_target="tpu_custom_call" | custom-call | tf_op jit(solution)/shard_map/pallas_call | solution.py:711
  569.4 2.4 copy.96
  574.7 4.4 add_convert_fusion.1
  579.8 4.1 all-to-all-start.9
  594.0 5.6 shard_map.181
  601.0 8.5 %all-to-all-done.9.parts_ref = bf16[4,256,1024]{2,1,0:T(8,128)(2,1)S(1)} async-done(((bf16[4,256,1024]{2,1,0:T(8,128)(2,1)}), bf16[4,256,1024]{2,1,0:T(8,128)(2,1)S(1)}, u32[]{:S(2)}, u32[]{:S(2)}) %all-to-all-start.9) | async-done | bytes 2097184 | tf_op jit(solution)/shard_map/all_to_all | solution.py:416
  610.8 3.6 shard_map.182
  615.1 3.7 all-to-all-start.10
  624.4 5.7 collective-permute-done.38
  630.1 13.7 %collective-permute-done.37 = bf16[512,256]{1,0:T(8,128)(2,1)S(1)} collective-permute-done((bf16[512,256]{1,0:T(8,128)(2,1)S(1)}, bf16[512,256]{1,0:T(8,128)(2,1)S(1)}, u32[]{:S(2)}, u32[]{:S(2)}) %collective-permute-start.37) | collective-permute-done | bytes 262176 | tf_op jit(solution)/shard_map/ppermute | solution.py:430
  645.8 3.2 collective-permute-start.39
  650.1 3.9 all-to-all-start.11
  653.9 2.3 collective-permute-done.40
  658.0 2.4 collective-permute-start.44
  662.4 4.6 all-to-all-done.11
  668.9 3.3 collective-permute-done.44
  672.2 14.6 %collective-permute-start.45 = (bf16[780,128]{1,0:T(8,128)(2,1)S(1)}, bf16[780,128]{1,0:T(8,128)(2,1)S(1)}, u32[]{:S(2)}, u32[]{:S(2)}) collective-permute-start(bf16[780,128]{1,0:T(8,128)(2,1)S(1)} %get-tuple-element.461), channel_id=1, source_target_pairs={{0,4},{4,0},{8,12},{12,8},{1,5},{5,1},{9,13},{13,9},{2,6},{6,2},{1... | collective-permute-start | bytes 599048 | tf_op jit(solution)/shard_map/ppermute | solution.py:430
  689.0 14.3 %collective-permute-done.43 = bf16[768,256]{1,0:T(8,128)(2,1)} collective-permute-done((bf16[768,256]{1,0:T(8,128)(2,1)}, bf16[768,256]{1,0:T(8,128)(2,1)}, u32[]{:S(2)}, u32[]{:S(2)}) %collective-permute-start.43) | collective-permute-done | bytes 393248 | tf_op jit(solution)/shard_map/ppermute | solution.py:430
  703.3 8.1 %collective-permute-done.46 = bf16[780,128]{1,0:T(8,128)(2,1)S(1)} collective-permute-done((bf16[780,128]{1,0:T(8,128)(2,1)S(1)}, bf16[780,128]{1,0:T(8,128)(2,1)S(1)}, u32[]{:S(2)}, u32[]{:S(2)}) %collective-permute-start.46) | collective-permute-done | bytes 199712 | tf_op jit(solution)/shard_map/ppermute | solution.py:430
  (396 shorter events, 131.9 us)
Async XLA Ops:
  7.2 26.0 %collective-permute-start.4 = (s32[6,2048]{1,0:T(8,128)}, s32[6,2048]{1,0:T(8,128)}, u32[]{:S(2)}, u32[]{:S(2)}) collective-permute-start(s32[6,2048]{1,0:T(8,128)} %param.12), channel_id=1, source_target_pairs={{0,16},{16,0},{1,17},{17,1},{2,18},{18,2},{3,19},{19,3},{4,20},{20... | collective-permute-start | bytes 147464 | tf_op jit(solution)/shard_map/ppermute | solution.py:493
  9.4 32.4 %collective-permute-start.10 = (bf16[2,256,256]{2,1,0:T(8,128)(2,1)}, bf16[2,256,256]{2,1,0:T(8,128)(2,1)}, u32[]{:S(2)}, u32[]{:S(2)}) collective-permute-start(bf16[2,256,256]{2,1,0:T(8,128)(2,1)} %constant_dynamic-slice_fusion.4), channel_id=1, source_target_pairs={{0,16},{16,0},{1,17},{17,1},{2,18},{18,2},{3,19},{19,3},{4,20},{20... | collective-permute-start | bytes 786440 | tf_op jit(solution)/shard_map/ppermute | solution.py:493
  11.1 30.7 %collective-permute-start.5 = (bf16[2,256,256]{2,1,0:T(8,128)(2,1)}, bf16[2,256,256]{2,1,0:T(8,128)(2,1)}, u32[]{:S(2)}, u32[]{:S(2)}) collective-permute-start(bf16[2,256,256]{2,1,0:T(8,128)(2,1)} %constant_dynamic-slice_fusion.5), channel_id=1, source_target_pairs={{0,16},{16,0},{1,17},{17,1},{2,18},{18,2},{3,19},{19,3},{4,20},{20... | collective-permute-start | bytes 786440 | tf_op jit(solution)/shard_map/ppermute | solution.py:493
  13.3 21.8 %collective-permute-start = (bf16[2,256,256]{2,1,0:T(8,128)(2,1)}, bf16[2,256,256]{2,1,0:T(8,128)(2,1)}, u32[]{:S(2)}, u32[]{:S(2)}) collective-permute-start(bf16[2,256,256]{2,1,0:T(8,128)(2,1)} %constant_dynamic-slice_fusion.10), channel_id=1, source_target_pairs={{0,16},{16,0},{1,17},{17,1},{2,18},{18,2},{3,19},{19,3},{4,20},{20... | collective-permute-start | bytes 786440 | tf_op jit(solution)/shard_map/ppermute | solution.py:493
  14.9 44.0 %all-to-all-start = ((bf16[4,784,128]{2,1,0:T(8,128)(2,1)}), bf16[4,784,128]{2,1,0:T(8,128)(2,1)}, u32[]{:S(2)}, u32[]{:S(2)}) async-start(bf16[4,784,128]{2,1,0:T(8,128)(2,1)} %broadcast_in_dim.131), calls=%async_computation | async-start | bytes 1605632 | tf_op jit(solution)/shard_map/all_to_all | solution.py:416
  37.4 44.5 %collective-permute-start.3 = (bf16[768,256]{1,0:T(8,128)(2,1)}, bf16[768,256]{1,0:T(8,128)(2,1)}, u32[]{:S(2)}, u32[]{:S(2)}) collective-permute-start(bf16[768,256]{1,0:T(8,128)(2,1)} %get-tuple-element.449), channel_id=1, source_target_pairs={{0,12},{4,8},{8,4},{12,0},{1,13},{5,9},{9,5},{13,1},{2,14},{6,10},... | collective-permute-start | bytes 1179656 | tf_op jit(solution)/shard_map/ppermute | solution.py:430
  41.3 40.7 %collective-permute-start.2 = (bf16[768,256]{1,0:T(8,128)(2,1)}, bf16[768,256]{1,0:T(8,128)(2,1)}, u32[]{:S(2)}, u32[]{:S(2)}) collective-permute-start(bf16[768,256]{1,0:T(8,128)(2,1)} %get-tuple-element.450), channel_id=1, source_target_pairs={{0,8},{4,12},{8,0},{12,4},{1,9},{5,13},{9,1},{13,5},{2,10},{6,14},... | collective-permute-start | bytes 1179656 | tf_op jit(solution)/shard_map/ppermute | solution.py:430
  41.3 40.7 %collective-permute-start.1 = (bf16[768,256]{1,0:T(8,128)(2,1)}, bf16[768,256]{1,0:T(8,128)(2,1)}, u32[]{:S(2)}, u32[]{:S(2)}) collective-permute-start(bf16[768,256]{1,0:T(8,128)(2,1)} %get-tuple-element.451), channel_id=1, source_target_pairs={{0,4},{4,0},{8,12},{12,8},{1,5},{5,1},{9,13},{13,9},{2,6},{6,2},{1... | collective-permute-start | bytes 1179656 | tf_op jit(solution)/shard_map/ppermute | solution.py:430
  61.0 16.3 %all-to-all-start.1 = ((bf16[8,3,128,128]{3,2,1,0:T(8,128)(2,1)}), bf16[8,3,128,128]{3,2,1,0:T(8,128)(2,1)}, u32[]{:S(2)}, u32[]{:S(2)}) async-start(bf16[8,3,128,128]{3,2,1,0:T(8,128)(2,1)} %bitcast.11), calls=%async_computation.1 | async-start | bytes 1572864 | tf_op jit(solution)/shard_map/all_to_all | solution.py:416
  65.3 230.5 %all-gather.3.cloned.1.call-start = ((), (), s32[]{:S(2)}) async-start(), calls=%async_computation.16 | async-start | bytes 21086208 | tf_op jit(solution)/shard_map/all_gather | solution.py:1017
  88.4 77.9 %all-to-all-start.2 = ((bf16[4,512,1024]{2,1,0:T(8,128)(2,1)}), bf16[4,512,1024]{2,1,0:T(8,128)(2,1)}, u32[]{:S(2)}, u32[]{:S(2)}) async-start(bf16[4,512,1024]{2,1,0:T(8,128)(2,1)} %get-tuple-element.218), calls=%async_computation.2 | async-start | bytes 8388608 | tf_op jit(solution)/shard_map/all_to_all | solution.py:416
  95.5 73.7 %collective-permute-start.9 = (bf16[768,256]{1,0:T(8,128)(2,1)}, bf16[768,256]{1,0:T(8,128)(2,1)S(1)}, u32[]{:S(2)}, u32[]{:S(2)}) collective-permute-start(bf16[768,256]{1,0:T(8,128)(2,1)} %get-tuple-element.445), channel_id=1, source_target_pairs={{0,12},{1,8},{2,4},{3,0},{4,13},{5,9},{6,5},{7,1},{8,14},{9,10},{1... | collective-permute-start | bytes 1179656 | tf_op jit(solution)/shard_map/ppermute | solution.py:465
  95.5 73.7 %collective-permute-start.8 = (bf16[768,256]{1,0:T(8,128)(2,1)}, bf16[768,256]{1,0:T(8,128)(2,1)S(1)}, u32[]{:S(2)}, u32[]{:S(2)}) collective-permute-start(bf16[768,256]{1,0:T(8,128)(2,1)} %get-tuple-element.446), channel_id=1, source_target_pairs={{0,8},{1,12},{2,0},{3,4},{4,9},{5,13},{6,1},{7,5},{8,10},{9,14},{1... | collective-permute-start | bytes 1179656 | tf_op jit(solution)/shard_map/ppermute | solution.py:465
  95.5 75.2 %collective-permute-start.7 = (bf16[768,256]{1,0:T(8,128)(2,1)}, bf16[768,256]{1,0:T(8,128)(2,1)S(1)}, u32[]{:S(2)}, u32[]{:S(2)}) collective-permute-start(bf16[768,256]{1,0:T(8,128)(2,1)} %get-tuple-element.447), channel_id=1, source_target_pairs={{0,4},{1,0},{2,12},{3,8},{4,5},{5,1},{6,13},{7,9},{8,6},{9,2},{10,... | collective-permute-start | bytes 1179656 | tf_op jit(solution)/shard_map/ppermute | solution.py:465
  97.9 72.8 %collective-permute-start.6 = (bf16[768,256]{1,0:T(8,128)(2,1)}, bf16[768,256]{1,0:T(8,128)(2,1)}, u32[]{:S(2)}, u32[]{:S(2)}) collective-permute-start(bf16[768,256]{1,0:T(8,128)(2,1)} %get-tuple-element.448), channel_id=1, source_target_pairs={{0,0},{1,4},{2,8},{3,12},{4,1},{5,5},{6,9},{7,13},{8,2},{9,6},{10,... | collective-permute-start | bytes 1179656 | tf_op jit(solution)/shard_map/ppermute | solution.py:465
  170.7 35.4 %collective-permute-start.11 = (bf16[4,512,1024]{2,1,0:T(8,128)(2,1)}, bf16[4,512,1024]{2,1,0:T(8,128)(2,1)}, u32[]{:S(2)}, u32[]{:S(2)}) collective-permute-start(bf16[4,512,1024]{2,1,0:T(8,128)(2,1)} %all-to-all-done.2.refs_0_), channel_id=1, source_target_pairs={{0,16},{16,0},{1,17},{17,1},{2,18},{18,2},{3,19},{19,3},{4,20},{20... | collective-permute-start | bytes 12582920 | tf_op jit(solution)/shard_map/ppermute | solution.py:493
  171.4 34.7 %all-to-all-start.3 = ((bf16[4,256,1024]{2,1,0:T(8,128)(2,1)}), bf16[4,256,1024]{2,1,0:T(8,128)(2,1)}, u32[]{:S(2)}, u32[]{:S(2)}) async-start(bf16[4,256,1024]{2,1,0:T(8,128)(2,1)} %get-tuple-element.221), calls=%async_computation.3 | async-start | bytes 4194304 | tf_op jit(solution)/shard_map/all_to_all | solution.py:416
  206.1 35.6 %collective-permute-start.12 = (bf16[4,256,1024]{2,1,0:T(8,128)(2,1)}, bf16[4,256,1024]{2,1,0:T(8,128)(2,1)}, u32[]{:S(2)}, u32[]{:S(2)}) collective-permute-start(bf16[4,256,1024]{2,1,0:T(8,128)(2,1)} %all-to-all-done.3.refs_0_), channel_id=1, source_target_pairs={{0,16},{16,0},{1,17},{17,1},{2,18},{18,2},{3,19},{19,3},{4,20},{20... | collective-permute-start | bytes 6291464 | tf_op jit(solution)/shard_map/ppermute | solution.py:493
  206.1 3.9 collective-permute-start.14
  206.7 35.1 %collective-permute-start.13 = (bf16[768,256]{1,0:T(8,128)(2,1)}, bf16[768,256]{1,0:T(8,128)(2,1)}, u32[]{:S(2)}, u32[]{:S(2)}) collective-permute-start(bf16[768,256]{1,0:T(8,128)(2,1)} %get-tuple-element.242), channel_id=1, source_target_pairs={{0,4},{4,0},{8,12},{12,8},{1,5},{5,1},{9,13},{13,9},{2,6},{6,2},{1... | collective-permute-start | bytes 1179656 | tf_op jit(solution)/shard_map/ppermute | solution.py:430
  241.8 2.0 collective-permute-start.15
  245.0 36.0 %all-to-all-start.4 = ((bf16[4,512,256]{2,1,0:T(8,128)(2,1)}), bf16[4,512,256]{2,1,0:T(8,128)(2,1)}, u32[]{:S(2)}, u32[]{:S(2)}) async-start(bf16[4,512,256]{2,1,0:T(8,128)(2,1)} %maximum_select_fusion.2), calls=%async_computation.4 | async-start | bytes 2097152 | tf_op jit(solution)/shard_map/all_to_all | solution.py:416
  249.5 31.6 %collective-permute-start.16 = (bf16[768,256]{1,0:T(8,128)(2,1)}, bf16[768,256]{1,0:T(8,128)(2,1)}, u32[]{:S(2)}, u32[]{:S(2)}) collective-permute-start(bf16[768,256]{1,0:T(8,128)(2,1)} %get-tuple-element.253), channel_id=1, source_target_pairs={{0,8},{4,12},{8,0},{12,4},{1,9},{5,13},{9,1},{13,5},{2,10},{6,14},... | collective-permute-start | bytes 1179656 | tf_op jit(solution)/shard_map/ppermute | solution.py:430
  283.7 12.0 %all-to-all-start.5 = ((bf16[4,256,256]{2,1,0:T(8,128)(2,1)}), bf16[4,256,256]{2,1,0:T(8,128)(2,1)S(1)}, u32[]{:S(2)}, u32[]{:S(2)}) async-start(bf16[4,256,256]{2,1,0:T(8,128)(2,1)} %maximum_select_fusion.4), calls=%async_computation.5 | async-start | bytes 1048576 | tf_op jit(solution)/shard_map/all_to_all | solution.py:416
  287.2 156.8 %reduce-scatter.3.cloned.1.call-start = ((), (), s32[]{:S(2)}) async-start(), calls=%async_computation.14 | async-start | bytes 6488064 | tf_op jit(solution)/shard_map/reduce_scatter | solution.py:1150
  287.6 16.4 %collective-permute-start.18 = (bf16[768,256]{1,0:T(8,128)(2,1)S(1)}, bf16[768,256]{1,0:T(8,128)(2,1)S(1)}, u32[]{:S(2)}, u32[]{:S(2)}) collective-permute-start(bf16[768,256]{1,0:T(8,128)(2,1)S(1)} %copy-done.55), channel_id=1, source_target_pairs={{0,12},{4,8},{8,4},{12,0},{1,13},{5,9},{9,5},{13,1},{2,14},{6,10},... | collective-permute-start | bytes 1179656 | tf_op jit(solution)/shard_map/ppermute | solution.py:430
  330.1 188.1 %reduce-scatter.5.cloned.1.call-start = ((), (), s32[]{:S(2)}) async-start(), calls=%async_computation.15 | async-start | bytes 14155776 | tf_op jit(solution)/shard_map/reduce_scatter | solution.py:1150
  381.7 24.0 %all-to-all-start.6 = ((bf16[4,768,256]{2,1,0:T(8,128)(2,1)}), bf16[4,768,256]{2,1,0:T(8,128)(2,1)}, u32[]{:S(2)}, u32[]{:S(2)}) async-start(bf16[4,768,256]{2,1,0:T(8,128)(2,1)} %get-tuple-element.286), calls=%async_computation.6 | async-start | bytes 3145728 | tf_op jit(solution)/shard_map/all_to_all | solution.py:416
  408.0 3.9 collective-permute-start.19
  408.1 34.4 %collective-permute-start.21 = (bf16[768,256]{1,0:T(8,128)(2,1)S(1)}, bf16[768,256]{1,0:T(8,128)(2,1)S(1)}, u32[]{:S(2)}, u32[]{:S(2)}) collective-permute-start(bf16[768,256]{1,0:T(8,128)(2,1)S(1)} %get-tuple-element.436), channel_id=1, source_target_pairs={{0,8},{4,12},{8,0},{12,4},{1,9},{5,13},{9,1},{13,5},{2,10},{6,14},... | collective-permute-start | bytes 1179656 | tf_op jit(solution)/shard_map/ppermute | solution.py:430
  410.9 31.6 %collective-permute-start.20 = (bf16[768,256]{1,0:T(8,128)(2,1)S(1)}, bf16[768,256]{1,0:T(8,128)(2,1)S(1)}, u32[]{:S(2)}, u32[]{:S(2)}) collective-permute-start(bf16[768,256]{1,0:T(8,128)(2,1)S(1)} %get-tuple-element.437), channel_id=1, source_target_pairs={{0,4},{4,0},{8,12},{12,8},{1,5},{5,1},{9,13},{13,9},{2,6},{6,2},{1... | collective-permute-start | bytes 1179656 | tf_op jit(solution)/shard_map/ppermute | solution.py:430
  444.0 47.1 %collective-permute-start.22 = (bf16[4,512,1024]{2,1,0:T(8,128)(2,1)}, bf16[4,512,1024]{2,1,0:T(8,128)(2,1)}, u32[]{:S(2)}, u32[]{:S(2)}) collective-permute-start(bf16[4,512,1024]{2,1,0:T(8,128)(2,1)} %get-tuple-element.311), channel_id=1, source_target_pairs={{0,16},{16,0},{1,17},{17,1},{2,18},{18,2},{3,19},{19,3},{4,20},{20... | collective-permute-start | bytes 12582920 | tf_op jit(solution)/shard_map/ppermute | solution.py:493
  444.0 47.1 %all-to-all-start.7 = ((bf16[8,4,256,128]{3,2,1,0:T(8,128)(2,1)}), bf16[8,4,256,128]{3,2,1,0:T(8,128)(2,1)S(1)}, u32[]{:S(2)}, u32[]{:S(2)}) async-start(bf16[8,4,256,128]{3,2,1,0:T(8,128)(2,1)} %shard_map.177), calls=%async_computation.8 | async-start | bytes 4194304 | tf_op jit(solution)/shard_map/all_to_all | solution.py:416
  447.8 38.5 %collective-permute-start.26 = (bf16[768,256]{1,0:T(8,128)(2,1)S(1)}, bf16[768,256]{1,0:T(8,128)(2,1)S(1)}, u32[]{:S(2)}, u32[]{:S(2)}) collective-permute-start(bf16[768,256]{1,0:T(8,128)(2,1)S(1)} %get-tuple-element.435), channel_id=1, source_target_pairs={{0,12},{4,8},{8,4},{12,0},{1,13},{5,9},{9,5},{13,1},{2,14},{6,10},... | collective-permute-start | bytes 1179656 | tf_op jit(solution)/shard_map/ppermute | solution.py:430
  455.0 36.1 %collective-permute-start.25 = (bf16[704,128]{1,0:T(8,128)(2,1)}, bf16[704,128]{1,0:T(8,128)(2,1)}, u32[]{:S(2)}, u32[]{:S(2)}) collective-permute-start(bf16[704,128]{1,0:T(8,128)(2,1)} %get-tuple-element.471), channel_id=1, source_target_pairs={{0,12},{4,8},{8,4},{12,0},{1,13},{5,9},{9,5},{13,1},{2,14},{6,10},... | collective-permute-start | bytes 540680 | tf_op jit(solution)/shard_map/ppermute | solution.py:430
  455.0 36.1 %collective-permute-start.24 = (bf16[704,128]{1,0:T(8,128)(2,1)}, bf16[704,128]{1,0:T(8,128)(2,1)}, u32[]{:S(2)}, u32[]{:S(2)}) collective-permute-start(bf16[704,128]{1,0:T(8,128)(2,1)} %get-tuple-element.472), channel_id=1, source_target_pairs={{0,8},{4,12},{8,0},{12,4},{1,9},{5,13},{9,1},{13,5},{2,10},{6,14},... | collective-permute-start | bytes 540680 | tf_op jit(solution)/shard_map/ppermute | solution.py:430
  455.0 36.1 %collective-permute-start.23 = (bf16[704,128]{1,0:T(8,128)(2,1)S(1)}, bf16[704,128]{1,0:T(8,128)(2,1)}, u32[]{:S(2)}, u32[]{:S(2)}) collective-permute-start(bf16[704,128]{1,0:T(8,128)(2,1)S(1)} %get-tuple-element.473), channel_id=1, source_target_pairs={{0,4},{4,0},{8,12},{12,8},{1,5},{5,1},{9,13},{13,9},{2,6},{6,2},{1... | collective-permute-start | bytes 540680 | tf_op jit(solution)/shard_map/ppermute | solution.py:430
  487.0 75.4 %collective-permute-start.35 = (bf16[2048,128]{1,0:T(8,128)(2,1)}, bf16[2048,128]{1,0:T(8,128)(2,1)}, u32[]{:S(2)}, u32[]{:S(2)}) collective-permute-start(bf16[2048,128]{1,0:T(8,128)(2,1)} %get-tuple-element.342), channel_id=1, source_target_pairs={{0,16},{16,0},{1,17},{17,1},{2,18},{18,2},{3,19},{19,3},{4,20},{20... | collective-permute-start | bytes 1572872 | tf_op jit(solution)/shard_map/ppermute | solution.py:493
  491.5 18.7 %collective-permute-start.29 = (bf16[256,128]{1,0:T(8,128)(2,1)S(1)}, bf16[256,128]{1,0:T(8,128)(2,1)S(1)}, u32[]{:S(2)}, u32[]{:S(2)}) collective-permute-start(bf16[256,128]{1,0:T(8,128)(2,1)S(1)} %get-tuple-element.485), channel_id=1, source_target_pairs={{0,12},{4,8},{8,4},{12,0},{1,13},{5,9},{9,5},{13,1},{2,14},{6,10},... | collective-permute-start | bytes 196616 | tf_op jit(solution)/shard_map/ppermute | solution.py:430
  494.9 15.3 %collective-permute-start.28 = (bf16[256,128]{1,0:T(8,128)(2,1)S(1)}, bf16[256,128]{1,0:T(8,128)(2,1)S(1)}, u32[]{:S(2)}, u32[]{:S(2)}) collective-permute-start(bf16[256,128]{1,0:T(8,128)(2,1)S(1)} %get-tuple-element.486), channel_id=1, source_target_pairs={{0,8},{4,12},{8,0},{12,4},{1,9},{5,13},{9,1},{13,5},{2,10},{6,14},... | collective-permute-start | bytes 196616 | tf_op jit(solution)/shard_map/ppermute | solution.py:430
  494.9 15.3 %collective-permute-start.27 = (bf16[256,128]{1,0:T(8,128)(2,1)S(1)}, bf16[256,128]{1,0:T(8,128)(2,1)S(1)}, u32[]{:S(2)}, u32[]{:S(2)}) collective-permute-start(bf16[256,128]{1,0:T(8,128)(2,1)S(1)} %get-tuple-element.487), channel_id=1, source_target_pairs={{0,4},{4,0},{8,12},{12,8},{1,5},{5,1},{9,13},{13,9},{2,6},{6,2},{1... | collective-permute-start | bytes 196616 | tf_op jit(solution)/shard_map/ppermute | solution.py:430
  518.2 61.0 %all-to-all-start.8 = ((bf16[4,512,1024]{2,1,0:T(8,128)(2,1)}), bf16[4,512,1024]{2,1,0:T(8,128)(2,1)}, u32[]{:S(2)}, u32[]{:S(2)}) async-start(bf16[4,512,1024]{2,1,0:T(8,128)(2,1)} %add_convert_fusion), calls=%async_computation.10 | async-start | bytes 8388608 | tf_op jit(solution)/shard_map/all_to_all | solution.py:416
  524.2 37.7 %collective-permute-start.32 = (bf16[1536,128]{1,0:T(8,128)(2,1)}, bf16[1536,128]{1,0:T(8,128)(2,1)}, u32[]{:S(2)}, u32[]{:S(2)}) collective-permute-start(bf16[1536,128]{1,0:T(8,128)(2,1)} %get-tuple-element.432), channel_id=1, source_target_pairs={{0,12},{4,8},{8,4},{12,0},{1,13},{5,9},{9,5},{13,1},{2,14},{6,10},... | collective-permute-start | bytes 1179656 | tf_op jit(solution)/shard_map/ppermute | solution.py:430
  527.5 34.4 %collective-permute-start.31 = (bf16[1536,128]{1,0:T(8,128)(2,1)}, bf16[1536,128]{1,0:T(8,128)(2,1)}, u32[]{:S(2)}, u32[]{:S(2)}) collective-permute-start(bf16[1536,128]{1,0:T(8,128)(2,1)} %get-tuple-element.433), channel_id=1, source_target_pairs={{0,8},{4,12},{8,0},{12,4},{1,9},{5,13},{9,1},{13,5},{2,10},{6,14},... | collective-permute-start | bytes 1179656 | tf_op jit(solution)/shard_map/ppermute | solution.py:430
  527.5 34.4 %collective-permute-start.30 = (bf16[1536,128]{1,0:T(8,128)(2,1)S(1)}, bf16[1536,128]{1,0:T(8,128)(2,1)}, u32[]{:S(2)}, u32[]{:S(2)}) collective-permute-start(bf16[1536,128]{1,0:T(8,128)(2,1)S(1)} %get-tuple-element.434), channel_id=1, source_target_pairs={{0,4},{4,0},{8,12},{12,8},{1,5},{5,1},{9,13},{13,9},{2,6},{6,2},{1... | collective-permute-start | bytes 1179656 | tf_op jit(solution)/shard_map/ppermute | solution.py:430
  529.3 34.7 %collective-permute-start.48 = (bf16[2,256,256]{2,1,0:T(8,128)(2,1)}, bf16[2,256,256]{2,1,0:T(8,128)(2,1)}, u32[]{:S(2)}, u32[]{:S(2)}) collective-permute-start(bf16[2,256,256]{2,1,0:T(8,128)(2,1)} %broadcast_select_fusion.10), channel_id=1, source_target_pairs={{0,16},{16,0},{1,17},{17,1},{2,18},{18,2},{3,19},{19,3},{4,20},{20... | collective-permute-start | bytes 786440 | tf_op jit(solution)/shard_map/ppermute | solution.py:493
  561.9 12.8 %collective-permute-start.33 = (bf16[4,256,1024]{2,1,0:T(8,128)(2,1)}, bf16[4,256,1024]{2,1,0:T(8,128)(2,1)}, u32[]{:S(2)}, u32[]{:S(2)}) collective-permute-start(bf16[4,256,1024]{2,1,0:T(8,128)(2,1)} %get-tuple-element.336), channel_id=1, source_target_pairs={{0,16},{16,0},{1,17},{17,1},{2,18},{18,2},{3,19},{19,3},{4,20},{20... | collective-permute-start | bytes 6291464 | tf_op jit(solution)/shard_map/ppermute | solution.py:493
  572.5 6.6 collective-permute-start.34
  579.8 29.6 %all-to-all-start.9 = ((bf16[4,256,1024]{2,1,0:T(8,128)(2,1)}), bf16[4,256,1024]{2,1,0:T(8,128)(2,1)S(1)}, u32[]{:S(2)}, u32[]{:S(2)}) async-start(bf16[4,256,1024]{2,1,0:T(8,128)(2,1)} %add_convert_fusion.1), calls=%async_computation.11 | async-start | bytes 4194304 | tf_op jit(solution)/shard_map/all_to_all | solution.py:416
  615.1 34.0 %all-to-all-start.10 = ((bf16[4,768,256]{2,1,0:T(8,128)(2,1)}), bf16[4,768,256]{2,1,0:T(8,128)(2,1)S(1)}, u32[]{:S(2)}, u32[]{:S(2)}) async-start(bf16[4,768,256]{2,1,0:T(8,128)(2,1)} %pad_maximum_fusion), calls=%async_computation.12 | async-start | bytes 3145728 | tf_op jit(solution)/shard_map/all_to_all | solution.py:416
  618.9 11.2 %collective-permute-start.38 = (bf16[512,256]{1,0:T(8,128)(2,1)S(1)}, bf16[512,256]{1,0:T(8,128)(2,1)S(1)}, u32[]{:S(2)}, u32[]{:S(2)}) collective-permute-start(bf16[512,256]{1,0:T(8,128)(2,1)S(1)} %get-tuple-element.452), channel_id=1, source_target_pairs={{0,12},{4,8},{8,4},{12,0},{1,13},{5,9},{9,5},{13,1},{2,14},{6,10},... | collective-permute-start | bytes 786440 | tf_op jit(solution)/shard_map/ppermute | solution.py:430
  620.3 23.6 %collective-permute-start.37 = (bf16[512,256]{1,0:T(8,128)(2,1)S(1)}, bf16[512,256]{1,0:T(8,128)(2,1)S(1)}, u32[]{:S(2)}, u32[]{:S(2)}) collective-permute-start(bf16[512,256]{1,0:T(8,128)(2,1)S(1)} %get-tuple-element.453), channel_id=1, source_target_pairs={{0,8},{4,12},{8,0},{12,4},{1,9},{5,13},{9,1},{13,5},{2,10},{6,14},... | collective-permute-start | bytes 786440 | tf_op jit(solution)/shard_map/ppermute | solution.py:430
  621.5 22.4 %collective-permute-start.36 = (bf16[512,256]{1,0:T(8,128)(2,1)S(1)}, bf16[512,256]{1,0:T(8,128)(2,1)S(1)}, u32[]{:S(2)}, u32[]{:S(2)}) collective-permute-start(bf16[512,256]{1,0:T(8,128)(2,1)S(1)} %get-tuple-element.454), channel_id=1, source_target_pairs={{0,4},{4,0},{8,12},{12,8},{1,5},{5,1},{9,13},{13,9},{2,6},{6,2},{1... | collective-permute-start | bytes 786440 | tf_op jit(solution)/shard_map/ppermute | solution.py:430
  644.6 9.3 %collective-permute-start.41 = (bf16[256,256]{1,0:T(8,128)(2,1)}, bf16[256,256]{1,0:T(8,128)(2,1)S(1)}, u32[]{:S(2)}, u32[]{:S(2)}) collective-permute-start(bf16[256,256]{1,0:T(8,128)(2,1)} %get-tuple-element.474), channel_id=1, source_target_pairs={{0,12},{4,8},{8,4},{12,0},{1,13},{5,9},{9,5},{13,1},{2,14},{6,10},... | collective-permute-start | bytes 393224 | tf_op jit(solution)/shard_map/ppermute | solution.py:430
  645.8 10.5 %collective-permute-start.40 = (bf16[256,256]{1,0:T(8,128)(2,1)}, bf16[256,256]{1,0:T(8,128)(2,1)S(1)}, u32[]{:S(2)}, u32[]{:S(2)}) collective-permute-start(bf16[256,256]{1,0:T(8,128)(2,1)} %get-tuple-element.475), channel_id=1, source_target_pairs={{0,8},{4,12},{8,0},{12,4},{1,9},{5,13},{9,1},{13,5},{2,10},{6,14},... | collective-permute-start | bytes 393224 | tf_op jit(solution)/shard_map/ppermute | solution.py:430
  645.8 10.5 %collective-permute-start.39 = (bf16[256,256]{1,0:T(8,128)(2,1)}, bf16[256,256]{1,0:T(8,128)(2,1)S(1)}, u32[]{:S(2)}, u32[]{:S(2)}) collective-permute-start(bf16[256,256]{1,0:T(8,128)(2,1)} %get-tuple-element.476), channel_id=1, source_target_pairs={{0,4},{4,0},{8,12},{12,8},{1,5},{5,1},{9,13},{13,9},{2,6},{6,2},{1... | collective-permute-start | bytes 393224 | tf_op jit(solution)/shard_map/ppermute | solution.py:430
  650.1 17.0 %all-to-all-start.11 = ((bf16[8,432,128]{2,1,0:T(8,128)(2,1)}), bf16[8,432,128]{2,1,0:T(8,128)(2,1)S(1)}, u32[]{:S(2)}, u32[]{:S(2)}) async-start(bf16[8,432,128]{2,1,0:T(8,128)(2,1)} %pad_maximum_fusion.4), calls=%async_computation.13 | async-start | bytes 1769472 | tf_op jit(solution)/shard_map/all_to_all | solution.py:416
  657.1 11.6 %collective-permute-start.49 = (bf16[2,256,256]{2,1,0:T(8,128)(2,1)}, bf16[2,256,256]{2,1,0:T(8,128)(2,1)}, u32[]{:S(2)}, u32[]{:S(2)}) collective-permute-start(bf16[2,256,256]{2,1,0:T(8,128)(2,1)} %broadcast_select_fusion.6), channel_id=1, source_target_pairs={{0,16},{16,0},{1,17},{17,1},{2,18},{18,2},{3,19},{19,3},{4,20},{20... | collective-permute-start | bytes 786440 | tf_op jit(solution)/shard_map/ppermute | solution.py:493
  658.0 14.2 %collective-permute-start.44 = (bf16[768,256]{1,0:T(8,128)(2,1)}, bf16[768,256]{1,0:T(8,128)(2,1)}, u32[]{:S(2)}, u32[]{:S(2)}) collective-permute-start(bf16[768,256]{1,0:T(8,128)(2,1)} %get-tuple-element.429), channel_id=1, source_target_pairs={{0,12},{4,8},{8,4},{12,0},{1,13},{5,9},{9,5},{13,1},{2,14},{6,10},... | collective-permute-start | bytes 1179656 | tf_op jit(solution)/shard_map/ppermute | solution.py:430
  660.4 42.9 %collective-permute-start.43 = (bf16[768,256]{1,0:T(8,128)(2,1)}, bf16[768,256]{1,0:T(8,128)(2,1)}, u32[]{:S(2)}, u32[]{:S(2)}) collective-permute-start(bf16[768,256]{1,0:T(8,128)(2,1)} %get-tuple-element.430), channel_id=1, source_target_pairs={{0,8},{4,12},{8,0},{12,4},{1,9},{5,13},{9,1},{13,5},{2,10},{6,14},... | collective-permute-start | bytes 1179656 | tf_op jit(solution)/shard_map/ppermute | solution.py:430
  660.4 42.9 %collective-permute-start.42 = (bf16[768,256]{1,0:T(8,128)(2,1)S(1)}, bf16[768,256]{1,0:T(8,128)(2,1)}, u32[]{:S(2)}, u32[]{:S(2)}) collective-permute-start(bf16[768,256]{1,0:T(8,128)(2,1)S(1)} %get-tuple-element.431), channel_id=1, source_target_pairs={{0,4},{4,0},{8,12},{12,8},{1,5},{5,1},{9,13},{13,9},{2,6},{6,2},{1... | collective-permute-start | bytes 1179656 | tf_op jit(solution)/shard_map/ppermute | solution.py:430
  667.4 35.9 %collective-permute-start.47 = (bf16[780,128]{1,0:T(8,128)(2,1)S(1)}, bf16[780,128]{1,0:T(8,128)(2,1)S(1)}, u32[]{:S(2)}, u32[]{:S(2)}) collective-permute-start(bf16[780,128]{1,0:T(8,128)(2,1)S(1)} %get-tuple-element.459), channel_id=1, source_target_pairs={{0,12},{4,8},{8,4},{12,0},{1,13},{5,9},{9,5},{13,1},{2,14},{6,10},... | collective-permute-start | bytes 599048 | tf_op jit(solution)/shard_map/ppermute | solution.py:430
  668.6 42.8 %collective-permute-start.46 = (bf16[780,128]{1,0:T(8,128)(2,1)S(1)}, bf16[780,128]{1,0:T(8,128)(2,1)S(1)}, u32[]{:S(2)}, u32[]{:S(2)}) collective-permute-start(bf16[780,128]{1,0:T(8,128)(2,1)S(1)} %get-tuple-element.460), channel_id=1, source_target_pairs={{0,8},{4,12},{8,0},{12,4},{1,9},{5,13},{9,1},{13,5},{2,10},{6,14},... | collective-permute-start | bytes 599048 | tf_op jit(solution)/shard_map/ppermute | solution.py:430
  672.2 39.2 %collective-permute-start.45 = (bf16[780,128]{1,0:T(8,128)(2,1)S(1)}, bf16[780,128]{1,0:T(8,128)(2,1)S(1)}, u32[]{:S(2)}, u32[]{:S(2)}) collective-permute-start(bf16[780,128]{1,0:T(8,128)(2,1)S(1)} %get-tuple-element.461), channel_id=1, source_target_pairs={{0,4},{4,0},{8,12},{12,8},{1,5},{5,1},{9,13},{13,9},{2,6},{6,2},{1... | collective-permute-start | bytes 599048 | tf_op jit(solution)/shard_map/ppermute | solution.py:430
  (79 other events, 705.3 us)
Sparse Core Ops, SparseCore 0:
  88.5 191.2 all-gather.2
  330.2 59.6 reduce-scatter.2
  393.8 124.3 reduce-scatter.4

commit v4 on v3

--- a/solution.py
+++ b/solution.py
@@ -1237,16 +1237,15 @@
         grads_b, b_got = send_line(grads_b)
         dn_s, dn_t, gw_s, gfv_s = back_of(2, (do_mine, do_got))
         b_got, dn_s, dn_t, gw_s, gfv_s = after(b_got, dn_s, dn_t, gw_s, gfv_s)
+        dn_t = swap(dn_t)
+        tokm, gain_main = last(0, x, dh, main_sum, gains[0])
+        shared_sum, tokm, gfv_s, gw_s = after(add_low(dn_s, dn_t), tokm, gfv_s, gw_s)
+        shared_sum = exchange(shared_sum, "ffn")
+        tokm, tokm_got = send_line(tokm)
         gfv_mine, gfv_theirs = by_core(gfv_s)
-        dn_t, gfv_theirs = swap(dn_t), swap(gfv_theirs)
-        shared_sum, main_sum, gfv_theirs = after(add_low(dn_s, dn_t), main_sum, gfv_theirs)
-        gfv = jnp.concatenate([gfv_main, lane_join(gfv_mine, gfv_theirs)], axis=1)
-        shared_sum = exchange(shared_sum, "ffn")
-        tokm, gain_main = last(0, x, dh, main_sum, gains[0])
-        shared_sum, tokm = after(shared_sum, tokm)
-        shared_sum, tokm = after(shared_sum, tokm)
-        tokm, tokm_got = send_line(tokm)
-        gfv, shared_sum = after(gfv, shared_sum)
+        gfv = lane_join(gfv_mine, swap(gfv_theirs))
+        gfv = jnp.concatenate([gfv_main, gfv], axis=1)
+        gfv, shared_sum, tokm_got = after(gfv, shared_sum, tokm_got)
         gfv = exchange(gfv, "ffn")
         toks, gain_shared = last(length, x, dh, shared_sum, gains[0])
         grad_w = (gw_a + gw_b + gw_s).astype(BF16)
@@ -1257,7 +1256,6 @@
         tail = jnp.concatenate(in_pieces(gain_both), axis=0)
         tail = jnp.broadcast_to(tail[None], (group,) + tail.shape)
         grad_w = jnp.concatenate([grad_w, tail], axis=1)
-        toks, tokm_got = after(toks, tokm_got)
         toks, toks_got = send_line(toks)
         grad_w, gfv = after(grad_w, gfv)
         grad_w = exchange(grad_w, layer)

time: 736 us -> 739 us (level)
    unnamed x154 -> x148, local copies, waits for them, and re-layouts: 26.6 us -> 24.4 us
  transfers between devices with their start and end apart: 66 -> 66, of which waited for: 24 -> 24; matrix products, arithmetic and copies ran while one was open for 14% -> 15% of each run, Pallas kernels for 29% -> 28%
where the time goes in v4:
time: 739 us; the launch traced here: 731 us
  Pallas kernels  243 us (33%)
  waiting for transfers between devices  201 us (27%)
  starting transfers between devices  127 us (17%)
  local copies, waits for them, and re-layouts  90.3 us (12%)
  other arithmetic  53.8 us (7%)
  between operations  15.5 us (2%)
    all_to_all x12, waiting for transfers between devices, exchange(): return lax.all_to_all(blocks, axes, 0, 0, tiled=True)  126 us
    pallas_call x3, Pallas kernels, attend_back(): pl.pallas_call(functools.partial(attend_back_kernel, count), grid=(1,), o...  87.4 us
    pallas_call x2, Pallas kernels, feed_forward(): pl.pallas_call(functools.partial(mlp_kernel, begin_tile, real, out_rows,...  61.5 us
    ppermute x30, starting transfers between devices, line_go(): lax.ppermute(send, axis, [(j, j ^ step + 1) for j in range(count)])  58.6 us
    pallas_call x3, Pallas kernels, attend(): pl.pallas_call(functools.partial(attend_kernel, count), grid=(1,), out_sh...  58.3 us
    ppermute x30, waiting for transfers between devices, line_go(): lax.ppermute(send, axis, [(j, j ^ step + 1) for j in range(count)])  56.4 us
    all_to_all x12, starting transfers between devices, exchange(): return lax.all_to_all(blocks, axes, 0, 0, tiled=True)  53.6 us
    unnamed x148, local copies, waits for them, and re-layouts  24.4 us
  transfers between devices with their start and end apart: 66, of which 24 were waited for; matrix products, arithmetic and copies ran while one was open for 15% of the time, Pallas kernels for 28%

profile of v4, /device:TPU:0, one launch (start us, length us, event | category | flops | bytes accessed | tf_op | source)
XLA Modules:
  0.0 730.7 jit_solution(16901544619582642890)
XLA Ops:
  14.9 6.3 all-to-all-start
  22.0 4.0 fusion.1
  27.9 2.5 pad_maximum_fusion.2
  37.5 3.8 collective-permute-start.3
  45.3 13.6 %all-to-all-done = bf16[4,784,128]{2,1,0:T(8,128)(2,1)} async-done(((bf16[4,784,128]{2,1,0:T(8,128)(2,1)}), bf16[4,784,128]{2,1,0:T(8,128)(2,1)}, u32[]{:S(2)}, u32[]{:S(2)}) %all-to-all-start) | async-done | bytes 802848 | tf_op jit(solution)/shard_map/all_to_all | solution.py:416
  61.1 4.2 all-to-all-start.1
  68.2 9.1 %all-to-all-done.1 = bf16[8,3,128,128]{3,2,1,0:T(8,128)(2,1)} async-done(((bf16[8,3,128,128]{3,2,1,0:T(8,128)(2,1)}), bf16[8,3,128,128]{3,2,1,0:T(8,128)(2,1)}, u32[]{:S(2)}, u32[]{:S(2)}) %all-to-all-start.1) | async-done | bytes 786464 | tf_op jit(solution)/shard_map/all_to_all | solution.py:416
  77.4 2.4 copy.82
  85.1 3.3 shard_map.169
  88.4 4.9 all-to-all-start.2
  95.5 2.5 collective-permute-start.7
  98.0 4.5 collective-permute-start.6
  104.7 61.6 %all-to-all-done.2.refs_0_ = bf16[4,512,1024]{2,1,0:T(8,128)(2,1)} async-done(((bf16[4,512,1024]{2,1,0:T(8,128)(2,1)}), bf16[4,512,1024]{2,1,0:T(8,128)(2,1)}, u32[]{:S(2)}, u32[]{:S(2)}) %all-to-all-start.2) | async-done | bytes 4194336 | tf_op jit(solution)/shard_map/all_to_all | solution.py:416
  166.3 2.9 collective-permute-done.9
  171.4 4.9 all-to-all-start.3
  177.4 4.0 fusion
  182.6 18.5 %shard_map.170 = (bf16[2048,128]{1,0:T(8,128)(2,1)S(1)}, bf16[2048,128]{1,0:T(8,128)(2,1)S(1)}, bf16[2048,128]{1,0:T(8,128)(2,1)S(1)}, bf16[2048,128]{1,0:T(8,128)(2,1)S(1)}, f32[2048,128]{1,0:T(8,128)S(1)}) custom-call(s32[1]{0:T(128)} %bitcast.side_ref, s32[4]{0:T(128)S(1)} %get-tuple-element.517.low_ref, bf16[4,512,1024]{2,1,0:T(8,128)(2,1)} %all-to-all-done.2.refs_0_, ...), custom_call_target="tpu_custom_call" | custom-call | tf_op jit(solution)/shard_map/pallas_call | solution.py:620
  208.8 4.7 collective-permute-done.14.refs_1_.refs_3_
  213.4 21.1 %shard_map.171 = (bf16[2048,128]{1,0:T(8,128)(2,1)S(1)}, bf16[2048,128]{1,0:T(8,128)(2,1)S(1)}, bf16[2048,128]{1,0:T(8,128)(2,1)S(1)}, bf16[2048,128]{1,0:T(8,128)(2,1)S(1)}, f32[2048,128]{1,0:T(8,128)S(1)}) custom-call(s32[1]{0:T(128)} %bitcast.side_ref, s32[4]{0:T(128)S(1)} %get-tuple-element.516.low_ref, ...), custom_call_target="tpu_custom_call" | custom-call | tf_op jit(solution)/shard_map/pallas_call | solution.py:620
  238.0 4.3 collective-permute-done.13
  245.5 4.5 all-to-all-start.4
  251.4 18.7 %shard_map.172 = (bf16[2048,128]{1,0:T(8,128)(2,1)S(1)}, bf16[2048,128]{1,0:T(8,128)(2,1)S(1)}, bf16[2048,128]{1,0:T(8,128)(2,1)S(1)}, bf16[2048,128]{1,0:T(8,128)(2,1)S(1)}, f32[2048,128]{1,0:T(8,128)S(1)}) custom-call(s32[1]{0:T(128)} %bitcast.side_ref, s32[4]{0:T(128)S(1)} %get-tuple-element.515.low_ref, bf16[4,256,1024]{2,1,0:T(8,128)(2,1)} %all-to-all-done.3.refs_0_, ...), custom_call_target="tpu_custom_call" | custom-call | tf_op jit(solution)/shard_map/pallas_call | solution.py:620
  272.7 8.4 %collective-permute-done.16 = bf16[768,256]{1,0:T(8,128)(2,1)} collective-permute-done((bf16[768,256]{1,0:T(8,128)(2,1)}, bf16[768,256]{1,0:T(8,128)(2,1)}, u32[]{:S(2)}, u32[]{:S(2)}) %collective-permute-start.16) | collective-permute-done | bytes 393248 | tf_op jit(solution)/shard_map/ppermute | solution.py:430
  283.7 3.5 all-to-all-start.5
  289.1 6.6 all-to-all-done.5.os_ref
  296.6 7.4 %shard_map.173 = (f32[768,1024]{1,0:T(8,128)}, bf16[768,1024]{1,0:T(8,128)(2,1)}, bf16[768,1024]{1,0:T(8,128)(2,1)}) custom-call(bf16[4,512,256]{2,1,0:T(8,128)(2,1)} %all-to-all-done.4.om_ref, bf16[4,256,256]{2,1,0:T(8,128)(2,1)} %copy-done.45, bf16[4,768,256]{2,1,0:T(8,128)(2,1)} %copy-done, bf16[8,4,2496,128]{3,2,1,0:T(8,128)(2,1)} %bitcast.251, ...), custom_call_target="tpu_custom_call" | custom-call | tf_op jit(solution)/shard_map/pallas_call | solution.py:1093
  307.3 22.8 %shard_map.174 = (f32[768,1024]{1,0:T(8,128)}, f32[768,1024]{1,0:T(8,128)}, bf16[8,4,704,128]{3,2,1,0:T(8,128)(2,1)}) custom-call(bf16[768,1024]{1,0:T(8,128)(2,1)} %get-tuple-element.278.n_ref, bf16[4,768,256]{2,1,0:T(8,128)(2,1)} %copy-done.26, bf16[8,4,2496,128]{3,2,1,0:T(8,128)(2,1)} %bitcast.252), custom_call_target="tpu_custom_call" | custom-call | tf_op jit(solution)/shard_map/pallas_call | solution.py:1113
  330.3 38.7 %shard_map.175 = (f32[768,1024]{1,0:T(8,128)}, f32[768,1024]{1,0:T(8,128)}, bf16[8,4,1536,128]{3,2,1,0:T(8,128)(2,1)}) custom-call(bf16[768,1024]{1,0:T(8,128)(2,1)} %get-tuple-element.278.n_ref, bf16[4,768,256]{2,1,0:T(8,128)(2,1)} %copy-done.26, bf16[8,4,2496,128]{3,2,1,0:T(8,128)(2,1)} %bitcast.253), custom_call_target="tpu_custom_call" | custom-call | tf_op jit(solution)/shard_map/pallas_call | solution.py:1113
  369.1 12.6 %shard_map.176 = (bf16[4,768,256]{2,1,0:T(8,128)(2,1)}, f32[768,1024]{1,0:T(8,128)}, bf16[4,768,256]{2,1,0:T(8,128)(2,1)}, bf16[768,1024]{1,0:T(8,128)(2,1)}, f32[1,1024]{1,0:T(1,128)}) custom-call(f32[768,1024]{1,0:T(8,128)} %get-tuple-element.263.h_ref, f32[768,1024]{1,0:T(8,128)} %get-tuple-element.277.ya_ref, f32[768,1024]{1,0:T(8,128)} %get-tuple-element.279.yb_ref, ...), custom_call_target="tpu_custom_call" | custom-call | tf_op jit(solution)/shard_map/pallas_call | solution.py:1155
  381.7 4.9 all-to-all-start.6
  386.6 3.2 shard_map.177
  389.8 15.9 %all-to-all-done.6 = bf16[4,768,256]{2,1,0:T(8,128)(2,1)} async-done(((bf16[4,768,256]{2,1,0:T(8,128)(2,1)}), bf16[4,768,256]{2,1,0:T(8,128)(2,1)}, u32[]{:S(2)}, u32[]{:S(2)}) %all-to-all-start.6) | async-done | bytes 1572896 | tf_op jit(solution)/shard_map/all_to_all | solution.py:416
  408.2 2.8 collective-permute-start.21
  412.9 33.3 %shard_map.178 = (bf16[4,512,1024]{2,1,0:T(8,128)(2,1)}, f32[384,1024]{1,0:T(8,128)}, bf16[2048,128]{1,0:T(8,128)(2,1)}) custom-call(s32[1]{0:T(128)} %bitcast.side_ref, s32[4]{0:T(128)} %copy-done.22, bf16[4,512,1024]{2,1,0:T(8,128)(2,1)} %collective-permute-done.11.refs_0_, bf16[4,768,128]{2,1,0:T(8,128)(2,1)} %copy-done.40, bf16[1024,384]{1,0:T(8,128)(2,1)} %copy-done.1, ...), custom_call_target="tpu_custom_call" | custom-call | tf_op jit(solution)/shard_map/pallas_call | solution.py:711
  447.0 3.7 all-to-all-start.7
  450.8 2.8 collective-permute-start.26
  455.8 3.0 collective-permute-start.23
  458.7 26.7 %shard_map.179 = (bf16[4,512,1024]{2,1,0:T(8,128)(2,1)}, f32[384,1024]{1,0:T(8,128)}, bf16[2048,128]{1,0:T(8,128)(2,1)}) custom-call(s32[1]{0:T(128)} %bitcast.side_ref, s32[4]{0:T(128)} %copy-done.21, bf16[4,512,1024]{2,1,0:T(8,128)(2,1)} %all-to-all-done.2.refs_0_, bf16[4,768,128]{2,1,0:T(8,128)(2,1)} %get-tuple-element.322.refs_1_.refs_2_, ...), custom_call_target="tpu_custom_call" | custom-call | tf_op jit(solution)/shard_map/pallas_call | solution.py:711
  486.2 2.9 collective-permute-start.34
  491.5 3.4 collective-permute-start.29
  504.7 6.5 add_convert_fusion
  512.2 6.0 reduce-scatter.5.cloned.1.call-done
  518.2 5.0 all-to-all-start.8
  524.3 3.3 collective-permute-start.32
  533.2 27.3 %shard_map.180 = (bf16[4,256,1024]{2,1,0:T(8,128)(2,1)}, bf16[4,256,1024]{2,1,0:T(8,128)(2,1)}, f32[384,1024]{1,0:T(8,128)}, bf16[2048,128]{1,0:T(8,128)(2,1)}) custom-call(s32[1]{0:T(128)} %bitcast.side_ref, s32[4]{0:T(128)} %copy-done.23, bf16[4,256,1024]{2,1,0:T(8,128)(2,1)} %all-to-all-done.3.refs_0_, ...), custom_call_target="tpu_custom_call" | custom-call | tf_op jit(solution)/shard_map/pallas_call | solution.py:711
  569.1 2.4 add_convert_fusion.1
  571.5 5.6 shard_map.181
  577.1 3.8 all-to-all-start.9
  593.4 2.4 copy.96
  597.0 2.9 collective-permute-start.38
  599.9 2.7 collective-permute-start.37
  605.1 3.0 collective-permute-done.38
  608.1 16.0 %collective-permute-done.37 = bf16[512,256]{1,0:T(8,128)(2,1)S(1)} collective-permute-done((bf16[512,256]{1,0:T(8,128)(2,1)S(1)}, bf16[512,256]{1,0:T(8,128)(2,1)S(1)}, u32[]{:S(2)}, u32[]{:S(2)}) %collective-permute-start.37) | collective-permute-done | bytes 262176 | tf_op jit(solution)/shard_map/ppermute | solution.py:430
  626.2 3.6 shard_map.182
  630.5 4.3 all-to-all-start.10
  635.6 3.1 collective-permute-start.41
  642.3 12.0 %all-to-all-done.10 = bf16[4,768,256]{2,1,0:T(8,128)(2,1)S(1)} async-done(((bf16[4,768,256]{2,1,0:T(8,128)(2,1)}), bf16[4,768,256]{2,1,0:T(8,128)(2,1)S(1)}, u32[]{:S(2)}, u32[]{:S(2)}) %all-to-all-start.10) | async-done | bytes 1572896 | tf_op jit(solution)/shard_map/all_to_all | solution.py:416
  654.3 3.6 all-to-all-start.11
  661.9 3.2 collective-permute-start.44
  666.3 4.7 all-to-all-done.11
  671.3 3.2 collective-permute-start.47
  676.1 15.2 %collective-permute-start.45 = (bf16[780,128]{1,0:T(8,128)(2,1)S(1)}, bf16[780,128]{1,0:T(8,128)(2,1)S(1)}, u32[]{:S(2)}, u32[]{:S(2)}) collective-permute-start(bf16[780,128]{1,0:T(8,128)(2,1)S(1)} %get-tuple-element.457), channel_id=1, source_target_pairs={{0,4},{4,0},{8,12},{12,8},{1,5},{5,1},{9,13},{13,9},{2,6},{6,2},{1... | collective-permute-start | bytes 599048 | tf_op jit(solution)/shard_map/ppermute | solution.py:430
  693.6 14.3 %collective-permute-done.43 = bf16[768,256]{1,0:T(8,128)(2,1)} collective-permute-done((bf16[768,256]{1,0:T(8,128)(2,1)}, bf16[768,256]{1,0:T(8,128)(2,1)}, u32[]{:S(2)}, u32[]{:S(2)}) %collective-permute-start.43) | collective-permute-done | bytes 393248 | tf_op jit(solution)/shard_map/ppermute | solution.py:430
  707.9 7.6 %collective-permute-done.46 = bf16[780,128]{1,0:T(8,128)(2,1)S(1)} collective-permute-done((bf16[780,128]{1,0:T(8,128)(2,1)S(1)}, bf16[780,128]{1,0:T(8,128)(2,1)S(1)}, u32[]{:S(2)}, u32[]{:S(2)}) %collective-permute-start.46) | collective-permute-done | bytes 199712 | tf_op jit(solution)/shard_map/ppermute | solution.py:430
  (390 shorter events, 144.4 us)
Async XLA Ops:
  7.2 26.0 %collective-permute-start.4 = (s32[6,2048]{1,0:T(8,128)}, s32[6,2048]{1,0:T(8,128)}, u32[]{:S(2)}, u32[]{:S(2)}) collective-permute-start(s32[6,2048]{1,0:T(8,128)} %param.12), channel_id=1, source_target_pairs={{0,16},{16,0},{1,17},{17,1},{2,18},{18,2},{3,19},{19,3},{4,20},{20... | collective-permute-start | bytes 147464 | tf_op jit(solution)/shard_map/ppermute | solution.py:493
  9.4 32.4 %collective-permute-start.10 = (bf16[2,256,256]{2,1,0:T(8,128)(2,1)}, bf16[2,256,256]{2,1,0:T(8,128)(2,1)}, u32[]{:S(2)}, u32[]{:S(2)}) collective-permute-start(bf16[2,256,256]{2,1,0:T(8,128)(2,1)} %constant_dynamic-slice_fusion.4), channel_id=1, source_target_pairs={{0,16},{16,0},{1,17},{17,1},{2,18},{18,2},{3,19},{19,3},{4,20},{20... | collective-permute-start | bytes 786440 | tf_op jit(solution)/shard_map/ppermute | solution.py:493
  11.2 30.7 %collective-permute-start.5 = (bf16[2,256,256]{2,1,0:T(8,128)(2,1)}, bf16[2,256,256]{2,1,0:T(8,128)(2,1)}, u32[]{:S(2)}, u32[]{:S(2)}) collective-permute-start(bf16[2,256,256]{2,1,0:T(8,128)(2,1)} %constant_dynamic-slice_fusion.5), channel_id=1, source_target_pairs={{0,16},{16,0},{1,17},{17,1},{2,18},{18,2},{3,19},{19,3},{4,20},{20... | collective-permute-start | bytes 786440 | tf_op jit(solution)/shard_map/ppermute | solution.py:493
  13.3 21.8 %collective-permute-start = (bf16[2,256,256]{2,1,0:T(8,128)(2,1)}, bf16[2,256,256]{2,1,0:T(8,128)(2,1)}, u32[]{:S(2)}, u32[]{:S(2)}) collective-permute-start(bf16[2,256,256]{2,1,0:T(8,128)(2,1)} %constant_dynamic-slice_fusion.10), channel_id=1, source_target_pairs={{0,16},{16,0},{1,17},{17,1},{2,18},{18,2},{3,19},{19,3},{4,20},{20... | collective-permute-start | bytes 786440 | tf_op jit(solution)/shard_map/ppermute | solution.py:493
  14.9 44.0 %all-to-all-start = ((bf16[4,784,128]{2,1,0:T(8,128)(2,1)}), bf16[4,784,128]{2,1,0:T(8,128)(2,1)}, u32[]{:S(2)}, u32[]{:S(2)}) async-start(bf16[4,784,128]{2,1,0:T(8,128)(2,1)} %broadcast_in_dim.131), calls=%async_computation | async-start | bytes 1605632 | tf_op jit(solution)/shard_map/all_to_all | solution.py:416
  37.5 44.5 %collective-permute-start.3 = (bf16[768,256]{1,0:T(8,128)(2,1)}, bf16[768,256]{1,0:T(8,128)(2,1)}, u32[]{:S(2)}, u32[]{:S(2)}) collective-permute-start(bf16[768,256]{1,0:T(8,128)(2,1)} %get-tuple-element.445), channel_id=1, source_target_pairs={{0,12},{4,8},{8,4},{12,0},{1,13},{5,9},{9,5},{13,1},{2,14},{6,10},... | collective-permute-start | bytes 1179656 | tf_op jit(solution)/shard_map/ppermute | solution.py:430
  41.3 40.7 %collective-permute-start.2 = (bf16[768,256]{1,0:T(8,128)(2,1)}, bf16[768,256]{1,0:T(8,128)(2,1)}, u32[]{:S(2)}, u32[]{:S(2)}) collective-permute-start(bf16[768,256]{1,0:T(8,128)(2,1)} %get-tuple-element.446), channel_id=1, source_target_pairs={{0,8},{4,12},{8,0},{12,4},{1,9},{5,13},{9,1},{13,5},{2,10},{6,14},... | collective-permute-start | bytes 1179656 | tf_op jit(solution)/shard_map/ppermute | solution.py:430
  41.3 40.7 %collective-permute-start.1 = (bf16[768,256]{1,0:T(8,128)(2,1)}, bf16[768,256]{1,0:T(8,128)(2,1)}, u32[]{:S(2)}, u32[]{:S(2)}) collective-permute-start(bf16[768,256]{1,0:T(8,128)(2,1)} %get-tuple-element.447), channel_id=1, source_target_pairs={{0,4},{4,0},{8,12},{12,8},{1,5},{5,1},{9,13},{13,9},{2,6},{6,2},{1... | collective-permute-start | bytes 1179656 | tf_op jit(solution)/shard_map/ppermute | solution.py:430
  61.1 16.3 %all-to-all-start.1 = ((bf16[8,3,128,128]{3,2,1,0:T(8,128)(2,1)}), bf16[8,3,128,128]{3,2,1,0:T(8,128)(2,1)}, u32[]{:S(2)}, u32[]{:S(2)}) async-start(bf16[8,3,128,128]{3,2,1,0:T(8,128)(2,1)} %bitcast.11), calls=%async_computation.1 | async-start | bytes 1572864 | tf_op jit(solution)/shard_map/all_to_all | solution.py:416
  65.3 230.5 %all-gather.3.cloned.1.call-start = ((), (), s32[]{:S(2)}) async-start(), calls=%async_computation.16 | async-start | bytes 21086208 | tf_op jit(solution)/shard_map/all_gather | solution.py:1017
  88.4 77.9 %all-to-all-start.2 = ((bf16[4,512,1024]{2,1,0:T(8,128)(2,1)}), bf16[4,512,1024]{2,1,0:T(8,128)(2,1)}, u32[]{:S(2)}, u32[]{:S(2)}) async-start(bf16[4,512,1024]{2,1,0:T(8,128)(2,1)} %get-tuple-element.216), calls=%async_computation.2 | async-start | bytes 8388608 | tf_op jit(solution)/shard_map/all_to_all | solution.py:416
  95.5 73.7 %collective-permute-start.9 = (bf16[768,256]{1,0:T(8,128)(2,1)}, bf16[768,256]{1,0:T(8,128)(2,1)S(1)}, u32[]{:S(2)}, u32[]{:S(2)}) collective-permute-start(bf16[768,256]{1,0:T(8,128)(2,1)} %get-tuple-element.441), channel_id=1, source_target_pairs={{0,12},{1,8},{2,4},{3,0},{4,13},{5,9},{6,5},{7,1},{8,14},{9,10},{1... | collective-permute-start | bytes 1179656 | tf_op jit(solution)/shard_map/ppermute | solution.py:465
  95.5 73.7 %collective-permute-start.8 = (bf16[768,256]{1,0:T(8,128)(2,1)}, bf16[768,256]{1,0:T(8,128)(2,1)S(1)}, u32[]{:S(2)}, u32[]{:S(2)}) collective-permute-start(bf16[768,256]{1,0:T(8,128)(2,1)} %get-tuple-element.442), channel_id=1, source_target_pairs={{0,8},{1,12},{2,0},{3,4},{4,9},{5,13},{6,1},{7,5},{8,10},{9,14},{1... | collective-permute-start | bytes 1179656 | tf_op jit(solution)/shard_map/ppermute | solution.py:465
  95.5 75.2 %collective-permute-start.7 = (bf16[768,256]{1,0:T(8,128)(2,1)}, bf16[768,256]{1,0:T(8,128)(2,1)S(1)}, u32[]{:S(2)}, u32[]{:S(2)}) collective-permute-start(bf16[768,256]{1,0:T(8,128)(2,1)} %get-tuple-element.443), channel_id=1, source_target_pairs={{0,4},{1,0},{2,12},{3,8},{4,5},{5,1},{6,13},{7,9},{8,6},{9,2},{10,... | collective-permute-start | bytes 1179656 | tf_op jit(solution)/shard_map/ppermute | solution.py:465
  98.0 72.7 %collective-permute-start.6 = (bf16[768,256]{1,0:T(8,128)(2,1)}, bf16[768,256]{1,0:T(8,128)(2,1)}, u32[]{:S(2)}, u32[]{:S(2)}) collective-permute-start(bf16[768,256]{1,0:T(8,128)(2,1)} %get-tuple-element.444), channel_id=1, source_target_pairs={{0,0},{1,4},{2,8},{3,12},{4,1},{5,5},{6,9},{7,13},{8,2},{9,6},{10,... | collective-permute-start | bytes 1179656 | tf_op jit(solution)/shard_map/ppermute | solution.py:465
  170.7 35.5 %collective-permute-start.11 = (bf16[4,512,1024]{2,1,0:T(8,128)(2,1)}, bf16[4,512,1024]{2,1,0:T(8,128)(2,1)}, u32[]{:S(2)}, u32[]{:S(2)}) collective-permute-start(bf16[4,512,1024]{2,1,0:T(8,128)(2,1)} %all-to-all-done.2.refs_0_), channel_id=1, source_target_pairs={{0,16},{16,0},{1,17},{17,1},{2,18},{18,2},{3,19},{19,3},{4,20},{20... | collective-permute-start | bytes 12582920 | tf_op jit(solution)/shard_map/ppermute | solution.py:493
  171.4 34.7 %all-to-all-start.3 = ((bf16[4,256,1024]{2,1,0:T(8,128)(2,1)}), bf16[4,256,1024]{2,1,0:T(8,128)(2,1)}, u32[]{:S(2)}, u32[]{:S(2)}) async-start(bf16[4,256,1024]{2,1,0:T(8,128)(2,1)} %get-tuple-element.219), calls=%async_computation.3 | async-start | bytes 4194304 | tf_op jit(solution)/shard_map/all_to_all | solution.py:416
  206.2 36.2 %collective-permute-start.12 = (bf16[4,256,1024]{2,1,0:T(8,128)(2,1)}, bf16[4,256,1024]{2,1,0:T(8,128)(2,1)}, u32[]{:S(2)}, u32[]{:S(2)}) collective-permute-start(bf16[4,256,1024]{2,1,0:T(8,128)(2,1)} %all-to-all-done.3.refs_0_), channel_id=1, source_target_pairs={{0,16},{16,0},{1,17},{17,1},{2,18},{18,2},{3,19},{19,3},{4,20},{20... | collective-permute-start | bytes 6291464 | tf_op jit(solution)/shard_map/ppermute | solution.py:493
  208.3 5.1 collective-permute-start.14
  208.4 33.9 %collective-permute-start.13 = (bf16[768,256]{1,0:T(8,128)(2,1)}, bf16[768,256]{1,0:T(8,128)(2,1)}, u32[]{:S(2)}, u32[]{:S(2)}) collective-permute-start(bf16[768,256]{1,0:T(8,128)(2,1)} %get-tuple-element.240), channel_id=1, source_target_pairs={{0,4},{4,0},{8,12},{12,8},{1,5},{5,1},{9,13},{13,9},{2,6},{6,2},{1... | collective-permute-start | bytes 1179656 | tf_op jit(solution)/shard_map/ppermute | solution.py:430
  242.3 1.9 collective-permute-start.15
  245.5 35.6 %all-to-all-start.4 = ((bf16[4,512,256]{2,1,0:T(8,128)(2,1)}), bf16[4,512,256]{2,1,0:T(8,128)(2,1)}, u32[]{:S(2)}, u32[]{:S(2)}) async-start(bf16[4,512,256]{2,1,0:T(8,128)(2,1)} %maximum_select_fusion.2), calls=%async_computation.4 | async-start | bytes 2097152 | tf_op jit(solution)/shard_map/all_to_all | solution.py:416
  250.0 31.1 %collective-permute-start.16 = (bf16[768,256]{1,0:T(8,128)(2,1)}, bf16[768,256]{1,0:T(8,128)(2,1)}, u32[]{:S(2)}, u32[]{:S(2)}) collective-permute-start(bf16[768,256]{1,0:T(8,128)(2,1)} %get-tuple-element.251), channel_id=1, source_target_pairs={{0,8},{4,12},{8,0},{12,4},{1,9},{5,13},{9,1},{13,5},{2,10},{6,14},... | collective-permute-start | bytes 1179656 | tf_op jit(solution)/shard_map/ppermute | solution.py:430
  283.7 12.0 %all-to-all-start.5 = ((bf16[4,256,256]{2,1,0:T(8,128)(2,1)}), bf16[4,256,256]{2,1,0:T(8,128)(2,1)S(1)}, u32[]{:S(2)}, u32[]{:S(2)}) async-start(bf16[4,256,256]{2,1,0:T(8,128)(2,1)} %maximum_select_fusion.4), calls=%async_computation.5 | async-start | bytes 1048576 | tf_op jit(solution)/shard_map/all_to_all | solution.py:416
  287.2 159.8 %reduce-scatter.3.cloned.1.call-start = ((), (), s32[]{:S(2)}) async-start(), calls=%async_computation.14 | async-start | bytes 6488064 | tf_op jit(solution)/shard_map/reduce_scatter | solution.py:1150
  287.7 16.4 %collective-permute-start.18 = (bf16[768,256]{1,0:T(8,128)(2,1)S(1)}, bf16[768,256]{1,0:T(8,128)(2,1)S(1)}, u32[]{:S(2)}, u32[]{:S(2)}) collective-permute-start(bf16[768,256]{1,0:T(8,128)(2,1)S(1)} %copy-done.52), channel_id=1, source_target_pairs={{0,12},{4,8},{8,4},{12,0},{1,13},{5,9},{9,5},{13,1},{2,14},{6,10},... | collective-permute-start | bytes 1179656 | tf_op jit(solution)/shard_map/ppermute | solution.py:430
  330.1 188.1 %reduce-scatter.5.cloned.1.call-start = ((), (), s32[]{:S(2)}) async-start(), calls=%async_computation.15 | async-start | bytes 14155776 | tf_op jit(solution)/shard_map/reduce_scatter | solution.py:1150
  381.7 24.0 %all-to-all-start.6 = ((bf16[4,768,256]{2,1,0:T(8,128)(2,1)}), bf16[4,768,256]{2,1,0:T(8,128)(2,1)}, u32[]{:S(2)}, u32[]{:S(2)}) async-start(bf16[4,768,256]{2,1,0:T(8,128)(2,1)} %get-tuple-element.284), calls=%async_computation.6 | async-start | bytes 3145728 | tf_op jit(solution)/shard_map/all_to_all | solution.py:416
  408.1 3.9 collective-permute-start.19
  408.2 38.0 %collective-permute-start.21 = (bf16[768,256]{1,0:T(8,128)(2,1)S(1)}, bf16[768,256]{1,0:T(8,128)(2,1)S(1)}, u32[]{:S(2)}, u32[]{:S(2)}) collective-permute-start(bf16[768,256]{1,0:T(8,128)(2,1)S(1)} %get-tuple-element.432), channel_id=1, source_target_pairs={{0,8},{4,12},{8,0},{12,4},{1,9},{5,13},{9,1},{13,5},{2,10},{6,14},... | collective-permute-start | bytes 1179656 | tf_op jit(solution)/shard_map/ppermute | solution.py:430
  411.0 35.2 %collective-permute-start.20 = (bf16[768,256]{1,0:T(8,128)(2,1)S(1)}, bf16[768,256]{1,0:T(8,128)(2,1)S(1)}, u32[]{:S(2)}, u32[]{:S(2)}) collective-permute-start(bf16[768,256]{1,0:T(8,128)(2,1)S(1)} %get-tuple-element.433), channel_id=1, source_target_pairs={{0,4},{4,0},{8,12},{12,8},{1,5},{5,1},{9,13},{13,9},{2,6},{6,2},{1... | collective-permute-start | bytes 1179656 | tf_op jit(solution)/shard_map/ppermute | solution.py:430
  447.0 44.1 %collective-permute-start.22 = (bf16[4,512,1024]{2,1,0:T(8,128)(2,1)}, bf16[4,512,1024]{2,1,0:T(8,128)(2,1)}, u32[]{:S(2)}, u32[]{:S(2)}) collective-permute-start(bf16[4,512,1024]{2,1,0:T(8,128)(2,1)} %get-tuple-element.309), channel_id=1, source_target_pairs={{0,16},{16,0},{1,17},{17,1},{2,18},{18,2},{3,19},{19,3},{4,20},{20... | collective-permute-start | bytes 12582920 | tf_op jit(solution)/shard_map/ppermute | solution.py:493
  447.0 44.0 %all-to-all-start.7 = ((bf16[8,4,256,128]{3,2,1,0:T(8,128)(2,1)}), bf16[8,4,256,128]{3,2,1,0:T(8,128)(2,1)S(1)}, u32[]{:S(2)}, u32[]{:S(2)}) async-start(bf16[8,4,256,128]{3,2,1,0:T(8,128)(2,1)} %shard_map.177), calls=%async_computation.8 | async-start | bytes 4194304 | tf_op jit(solution)/shard_map/all_to_all | solution.py:416
  450.8 34.7 %collective-permute-start.26 = (bf16[768,256]{1,0:T(8,128)(2,1)S(1)}, bf16[768,256]{1,0:T(8,128)(2,1)S(1)}, u32[]{:S(2)}, u32[]{:S(2)}) collective-permute-start(bf16[768,256]{1,0:T(8,128)(2,1)S(1)} %get-tuple-element.431), channel_id=1, source_target_pairs={{0,12},{4,8},{8,4},{12,0},{1,13},{5,9},{9,5},{13,1},{2,14},{6,10},... | collective-permute-start | bytes 1179656 | tf_op jit(solution)/shard_map/ppermute | solution.py:430
  454.4 36.7 %collective-permute-start.25 = (bf16[704,128]{1,0:T(8,128)(2,1)}, bf16[704,128]{1,0:T(8,128)(2,1)}, u32[]{:S(2)}, u32[]{:S(2)}) collective-permute-start(bf16[704,128]{1,0:T(8,128)(2,1)} %get-tuple-element.467), channel_id=1, source_target_pairs={{0,12},{4,8},{8,4},{12,0},{1,13},{5,9},{9,5},{13,1},{2,14},{6,10},... | collective-permute-start | bytes 540680 | tf_op jit(solution)/shard_map/ppermute | solution.py:430
  455.5 35.6 %collective-permute-start.24 = (bf16[704,128]{1,0:T(8,128)(2,1)}, bf16[704,128]{1,0:T(8,128)(2,1)}, u32[]{:S(2)}, u32[]{:S(2)}) collective-permute-start(bf16[704,128]{1,0:T(8,128)(2,1)} %get-tuple-element.468), channel_id=1, source_target_pairs={{0,8},{4,12},{8,0},{12,4},{1,9},{5,13},{9,1},{13,5},{2,10},{6,14},... | collective-permute-start | bytes 540680 | tf_op jit(solution)/shard_map/ppermute | solution.py:430
  455.8 35.3 %collective-permute-start.23 = (bf16[704,128]{1,0:T(8,128)(2,1)S(1)}, bf16[704,128]{1,0:T(8,128)(2,1)}, u32[]{:S(2)}, u32[]{:S(2)}) collective-permute-start(bf16[704,128]{1,0:T(8,128)(2,1)S(1)} %get-tuple-element.469), channel_id=1, source_target_pairs={{0,4},{4,0},{8,12},{12,8},{1,5},{5,1},{9,13},{13,9},{2,6},{6,2},{1... | collective-permute-start | bytes 540680 | tf_op jit(solution)/shard_map/ppermute | solution.py:430
  486.2 45.2 %collective-permute-start.34 = (bf16[2048,128]{1,0:T(8,128)(2,1)}, bf16[2048,128]{1,0:T(8,128)(2,1)}, u32[]{:S(2)}, u32[]{:S(2)}) collective-permute-start(bf16[2048,128]{1,0:T(8,128)(2,1)} %get-tuple-element.341), channel_id=1, source_target_pairs={{0,16},{16,0},{1,17},{17,1},{2,18},{18,2},{3,19},{19,3},{4,20},{20... | collective-permute-start | bytes 1572872 | tf_op jit(solution)/shard_map/ppermute | solution.py:493
  491.5 20.6 %collective-permute-start.29 = (bf16[256,128]{1,0:T(8,128)(2,1)S(1)}, bf16[256,128]{1,0:T(8,128)(2,1)S(1)}, u32[]{:S(2)}, u32[]{:S(2)}) collective-permute-start(bf16[256,128]{1,0:T(8,128)(2,1)S(1)} %get-tuple-element.481), channel_id=1, source_target_pairs={{0,12},{4,8},{8,4},{12,0},{1,13},{5,9},{9,5},{13,1},{2,14},{6,10},... | collective-permute-start | bytes 196616 | tf_op jit(solution)/shard_map/ppermute | solution.py:430
  494.9 17.2 %collective-permute-start.28 = (bf16[256,128]{1,0:T(8,128)(2,1)S(1)}, bf16[256,128]{1,0:T(8,128)(2,1)S(1)}, u32[]{:S(2)}, u32[]{:S(2)}) collective-permute-start(bf16[256,128]{1,0:T(8,128)(2,1)S(1)} %get-tuple-element.482), channel_id=1, source_target_pairs={{0,8},{4,12},{8,0},{12,4},{1,9},{5,13},{9,1},{13,5},{2,10},{6,14},... | collective-permute-start | bytes 196616 | tf_op jit(solution)/shard_map/ppermute | solution.py:430
  494.9 17.2 %collective-permute-start.27 = (bf16[256,128]{1,0:T(8,128)(2,1)S(1)}, bf16[256,128]{1,0:T(8,128)(2,1)S(1)}, u32[]{:S(2)}, u32[]{:S(2)}) collective-permute-start(bf16[256,128]{1,0:T(8,128)(2,1)S(1)} %get-tuple-element.483), channel_id=1, source_target_pairs={{0,4},{4,0},{8,12},{12,8},{1,5},{5,1},{9,13},{13,9},{2,6},{6,2},{1... | collective-permute-start | bytes 196616 | tf_op jit(solution)/shard_map/ppermute | solution.py:430
  518.2 53.4 %all-to-all-start.8 = ((bf16[4,512,1024]{2,1,0:T(8,128)(2,1)}), bf16[4,512,1024]{2,1,0:T(8,128)(2,1)}, u32[]{:S(2)}, u32[]{:S(2)}) async-start(bf16[4,512,1024]{2,1,0:T(8,128)(2,1)} %add_convert_fusion), calls=%async_computation.10 | async-start | bytes 8388608 | tf_op jit(solution)/shard_map/all_to_all | solution.py:416
  524.3 36.3 %collective-permute-start.32 = (bf16[1536,128]{1,0:T(8,128)(2,1)}, bf16[1536,128]{1,0:T(8,128)(2,1)}, u32[]{:S(2)}, u32[]{:S(2)}) collective-permute-start(bf16[1536,128]{1,0:T(8,128)(2,1)} %get-tuple-element.428), channel_id=1, source_target_pairs={{0,12},{4,8},{8,4},{12,0},{1,13},{5,9},{9,5},{13,1},{2,14},{6,10},... | collective-permute-start | bytes 1179656 | tf_op jit(solution)/shard_map/ppermute | solution.py:430
  527.6 34.0 %collective-permute-start.31 = (bf16[1536,128]{1,0:T(8,128)(2,1)}, bf16[1536,128]{1,0:T(8,128)(2,1)}, u32[]{:S(2)}, u32[]{:S(2)}) collective-permute-start(bf16[1536,128]{1,0:T(8,128)(2,1)} %get-tuple-element.429), channel_id=1, source_target_pairs={{0,8},{4,12},{8,0},{12,4},{1,9},{5,13},{9,1},{13,5},{2,10},{6,14},... | collective-permute-start | bytes 1179656 | tf_op jit(solution)/shard_map/ppermute | solution.py:430
  527.6 34.0 %collective-permute-start.30 = (bf16[1536,128]{1,0:T(8,128)(2,1)}, bf16[1536,128]{1,0:T(8,128)(2,1)}, u32[]{:S(2)}, u32[]{:S(2)}) collective-permute-start(bf16[1536,128]{1,0:T(8,128)(2,1)} %get-tuple-element.430), channel_id=1, source_target_pairs={{0,4},{4,0},{8,12},{12,8},{1,5},{5,1},{9,13},{13,9},{2,6},{6,2},{1... | collective-permute-start | bytes 1179656 | tf_op jit(solution)/shard_map/ppermute | solution.py:430
  529.9 31.8 %collective-permute-start.48 = (bf16[2,256,256]{2,1,0:T(8,128)(2,1)}, bf16[2,256,256]{2,1,0:T(8,128)(2,1)}, u32[]{:S(2)}, u32[]{:S(2)}) collective-permute-start(bf16[2,256,256]{2,1,0:T(8,128)(2,1)} %broadcast_select_fusion.10), channel_id=1, source_target_pairs={{0,16},{16,0},{1,17},{17,1},{2,18},{18,2},{3,19},{19,3},{4,20},{20... | collective-permute-start | bytes 786440 | tf_op jit(solution)/shard_map/ppermute | solution.py:493
  561.7 7.5 %collective-permute-start.33 = (bf16[4,256,1024]{2,1,0:T(8,128)(2,1)}, bf16[4,256,1024]{2,1,0:T(8,128)(2,1)S(1)}, u32[]{:S(2)}, u32[]{:S(2)}) collective-permute-start(bf16[4,256,1024]{2,1,0:T(8,128)(2,1)} %get-tuple-element.332), channel_id=1, source_target_pairs={{0,16},{16,0},{1,17},{17,1},{2,18},{18,2},{3,19},{19,3},{4,20},{20... | collective-permute-start | bytes 6291464 | tf_op jit(solution)/shard_map/ppermute | solution.py:493
  577.1 47.7 %all-to-all-start.9 = ((bf16[4,256,1024]{2,1,0:T(8,128)(2,1)}), bf16[4,256,1024]{2,1,0:T(8,128)(2,1)S(1)}, u32[]{:S(2)}, u32[]{:S(2)}) async-start(bf16[4,256,1024]{2,1,0:T(8,128)(2,1)} %add_convert_fusion.1), calls=%async_computation.11 | async-start | bytes 4194304 | tf_op jit(solution)/shard_map/all_to_all | solution.py:416
  591.5 11.1 %collective-permute-start.35 = (bf16[4,256,128]{2,1,0:T(8,128)(2,1)}, bf16[4,256,128]{2,1,0:T(8,128)(2,1)}, u32[]{:S(2)}, u32[]{:S(2)}) collective-permute-start(bf16[4,256,128]{2,1,0:T(8,128)(2,1)} %get-tuple-element.474), channel_id=1, source_target_pairs={{0,16},{16,0},{1,17},{17,1},{2,18},{18,2},{3,19},{19,3},{4,20},{20... | collective-permute-start | bytes 786440 | tf_op jit(solution)/shard_map/ppermute | solution.py:493
  597.0 11.1 %collective-permute-start.38 = (bf16[512,256]{1,0:T(8,128)(2,1)S(1)}, bf16[512,256]{1,0:T(8,128)(2,1)S(1)}, u32[]{:S(2)}, u32[]{:S(2)}) collective-permute-start(bf16[512,256]{1,0:T(8,128)(2,1)S(1)} %get-tuple-element.448), channel_id=1, source_target_pairs={{0,12},{4,8},{8,4},{12,0},{1,13},{5,9},{9,5},{13,1},{2,14},{6,10},... | collective-permute-start | bytes 786440 | tf_op jit(solution)/shard_map/ppermute | solution.py:430
  599.9 24.2 %collective-permute-start.37 = (bf16[512,256]{1,0:T(8,128)(2,1)S(1)}, bf16[512,256]{1,0:T(8,128)(2,1)S(1)}, u32[]{:S(2)}, u32[]{:S(2)}) collective-permute-start(bf16[512,256]{1,0:T(8,128)(2,1)S(1)} %get-tuple-element.449), channel_id=1, source_target_pairs={{0,8},{4,12},{8,0},{12,4},{1,9},{5,13},{9,1},{13,5},{2,10},{6,14},... | collective-permute-start | bytes 786440 | tf_op jit(solution)/shard_map/ppermute | solution.py:430
  602.6 22.2 %collective-permute-start.36 = (bf16[512,256]{1,0:T(8,128)(2,1)S(1)}, bf16[512,256]{1,0:T(8,128)(2,1)}, u32[]{:S(2)}, u32[]{:S(2)}) collective-permute-start(bf16[512,256]{1,0:T(8,128)(2,1)S(1)} %get-tuple-element.450), channel_id=1, source_target_pairs={{0,4},{4,0},{8,12},{12,8},{1,5},{5,1},{9,13},{13,9},{2,6},{6,2},{1... | collective-permute-start | bytes 786440 | tf_op jit(solution)/shard_map/ppermute | solution.py:430
  630.5 23.8 %all-to-all-start.10 = ((bf16[4,768,256]{2,1,0:T(8,128)(2,1)}), bf16[4,768,256]{2,1,0:T(8,128)(2,1)S(1)}, u32[]{:S(2)}, u32[]{:S(2)}) async-start(bf16[4,768,256]{2,1,0:T(8,128)(2,1)} %pad_maximum_fusion), calls=%async_computation.12 | async-start | bytes 3145728 | tf_op jit(solution)/shard_map/all_to_all | solution.py:416
  635.6 22.3 %collective-permute-start.41 = (bf16[256,256]{1,0:T(8,128)(2,1)}, bf16[256,256]{1,0:T(8,128)(2,1)S(1)}, u32[]{:S(2)}, u32[]{:S(2)}) collective-permute-start(bf16[256,256]{1,0:T(8,128)(2,1)} %get-tuple-element.470), channel_id=1, source_target_pairs={{0,12},{4,8},{8,4},{12,0},{1,13},{5,9},{9,5},{13,1},{2,14},{6,10},... | collective-permute-start | bytes 393224 | tf_op jit(solution)/shard_map/ppermute | solution.py:430
  638.7 19.1 %collective-permute-start.40 = (bf16[256,256]{1,0:T(8,128)(2,1)}, bf16[256,256]{1,0:T(8,128)(2,1)}, u32[]{:S(2)}, u32[]{:S(2)}) collective-permute-start(bf16[256,256]{1,0:T(8,128)(2,1)} %get-tuple-element.471), channel_id=1, source_target_pairs={{0,8},{4,12},{8,0},{12,4},{1,9},{5,13},{9,1},{13,5},{2,10},{6,14},... | collective-permute-start | bytes 393224 | tf_op jit(solution)/shard_map/ppermute | solution.py:430
  638.7 19.2 %collective-permute-start.39 = (bf16[256,256]{1,0:T(8,128)(2,1)}, bf16[256,256]{1,0:T(8,128)(2,1)}, u32[]{:S(2)}, u32[]{:S(2)}) collective-permute-start(bf16[256,256]{1,0:T(8,128)(2,1)} %get-tuple-element.472), channel_id=1, source_target_pairs={{0,4},{4,0},{8,12},{12,8},{1,5},{5,1},{9,13},{13,9},{2,6},{6,2},{1... | collective-permute-start | bytes 393224 | tf_op jit(solution)/shard_map/ppermute | solution.py:430
  654.3 16.6 %all-to-all-start.11 = ((bf16[8,432,128]{2,1,0:T(8,128)(2,1)}), bf16[8,432,128]{2,1,0:T(8,128)(2,1)S(1)}, u32[]{:S(2)}, u32[]{:S(2)}) async-start(bf16[8,432,128]{2,1,0:T(8,128)(2,1)} %pad_maximum_fusion.4), calls=%async_computation.13 | async-start | bytes 1769472 | tf_op jit(solution)/shard_map/all_to_all | solution.py:416
  660.5 14.0 %collective-permute-start.49 = (bf16[2,256,256]{2,1,0:T(8,128)(2,1)}, bf16[2,256,256]{2,1,0:T(8,128)(2,1)}, u32[]{:S(2)}, u32[]{:S(2)}) collective-permute-start(bf16[2,256,256]{2,1,0:T(8,128)(2,1)} %broadcast_select_fusion.6), channel_id=1, source_target_pairs={{0,16},{16,0},{1,17},{17,1},{2,18},{18,2},{3,19},{19,3},{4,20},{20... | collective-permute-start | bytes 786440 | tf_op jit(solution)/shard_map/ppermute | solution.py:493
  661.9 14.2 %collective-permute-start.44 = (bf16[768,256]{1,0:T(8,128)(2,1)}, bf16[768,256]{1,0:T(8,128)(2,1)}, u32[]{:S(2)}, u32[]{:S(2)}) collective-permute-start(bf16[768,256]{1,0:T(8,128)(2,1)} %get-tuple-element.425), channel_id=1, source_target_pairs={{0,12},{4,8},{8,4},{12,0},{1,13},{5,9},{9,5},{13,1},{2,14},{6,10},... | collective-permute-start | bytes 1179656 | tf_op jit(solution)/shard_map/ppermute | solution.py:430
  665.0 42.8 %collective-permute-start.43 = (bf16[768,256]{1,0:T(8,128)(2,1)}, bf16[768,256]{1,0:T(8,128)(2,1)}, u32[]{:S(2)}, u32[]{:S(2)}) collective-permute-start(bf16[768,256]{1,0:T(8,128)(2,1)} %get-tuple-element.426), channel_id=1, source_target_pairs={{0,8},{4,12},{8,0},{12,4},{1,9},{5,13},{9,1},{13,5},{2,10},{6,14},... | collective-permute-start | bytes 1179656 | tf_op jit(solution)/shard_map/ppermute | solution.py:430
  665.0 42.8 %collective-permute-start.42 = (bf16[768,256]{1,0:T(8,128)(2,1)S(1)}, bf16[768,256]{1,0:T(8,128)(2,1)}, u32[]{:S(2)}, u32[]{:S(2)}) collective-permute-start(bf16[768,256]{1,0:T(8,128)(2,1)S(1)} %get-tuple-element.427), channel_id=1, source_target_pairs={{0,4},{4,0},{8,12},{12,8},{1,5},{5,1},{9,13},{13,9},{2,6},{6,2},{1... | collective-permute-start | bytes 1179656 | tf_op jit(solution)/shard_map/ppermute | solution.py:430
  671.3 36.6 %collective-permute-start.47 = (bf16[780,128]{1,0:T(8,128)(2,1)S(1)}, bf16[780,128]{1,0:T(8,128)(2,1)S(1)}, u32[]{:S(2)}, u32[]{:S(2)}) collective-permute-start(bf16[780,128]{1,0:T(8,128)(2,1)S(1)} %get-tuple-element.455), channel_id=1, source_target_pairs={{0,12},{4,8},{8,4},{12,0},{1,13},{5,9},{9,5},{13,1},{2,14},{6,10},... | collective-permute-start | bytes 599048 | tf_op jit(solution)/shard_map/ppermute | solution.py:430
  674.5 41.0 %collective-permute-start.46 = (bf16[780,128]{1,0:T(8,128)(2,1)S(1)}, bf16[780,128]{1,0:T(8,128)(2,1)S(1)}, u32[]{:S(2)}, u32[]{:S(2)}) collective-permute-start(bf16[780,128]{1,0:T(8,128)(2,1)S(1)} %get-tuple-element.456), channel_id=1, source_target_pairs={{0,8},{4,12},{8,0},{12,4},{1,9},{5,13},{9,1},{13,5},{2,10},{6,14},... | collective-permute-start | bytes 599048 | tf_op jit(solution)/shard_map/ppermute | solution.py:430
  676.1 39.4 %collective-permute-start.45 = (bf16[780,128]{1,0:T(8,128)(2,1)S(1)}, bf16[780,128]{1,0:T(8,128)(2,1)S(1)}, u32[]{:S(2)}, u32[]{:S(2)}) collective-permute-start(bf16[780,128]{1,0:T(8,128)(2,1)S(1)} %get-tuple-element.457), channel_id=1, source_target_pairs={{0,4},{4,0},{8,12},{12,8},{1,5},{5,1},{9,13},{13,9},{2,6},{6,2},{1... | collective-permute-start | bytes 599048 | tf_op jit(solution)/shard_map/ppermute | solution.py:430
  (76 other events, 727.0 us)
Sparse Core Ops, SparseCore 0:
  88.5 190.8 all-gather.2
  330.2 59.6 reduce-scatter.2
  393.8 124.2 reduce-scatter.4

commit v5 on v4

--- a/solution.py
+++ b/solution.py
@@ -1239,9 +1239,10 @@
         b_got, dn_s, dn_t, gw_s, gfv_s = after(b_got, dn_s, dn_t, gw_s, gfv_s)
         dn_t = swap(dn_t)
         tokm, gain_main = last(0, x, dh, main_sum, gains[0])
-        shared_sum, tokm, gfv_s, gw_s = after(add_low(dn_s, dn_t), tokm, gfv_s, gw_s)
+        shared_sum, tokm = after(add_low(dn_s, dn_t), tokm)
         shared_sum = exchange(shared_sum, "ffn")
         tokm, tokm_got = send_line(tokm)
+        tokm_got, gfv_s, gw_s, b_got = after(tokm_got, gfv_s, gw_s, b_got)
         gfv_mine, gfv_theirs = by_core(gfv_s)
         gfv = lane_join(gfv_mine, swap(gfv_theirs))
         gfv = jnp.concatenate([gfv_main, gfv], axis=1)

time: 739 us -> 742 us (level)
  starting transfers between devices: 127 us -> 114 us
  waiting for transfers between devices: 201 us -> 209 us
    ppermute x30, starting transfers between devices: 58.6 us -> 51.1 us  [line_go(): lax.ppermute(send, axis, [(j, j ^ step + 1) for j in range(count)])]
    reduce_scatter x2, waiting for transfers between devices: 5.97 us -> 13.5 us  [layer_sum(): lax.psum_scatter(grads, layer, scatter_dimension=0, tiled=True)]
  transfers between devices with their start and end apart: 66 -> 66, of which waited for: 24 -> 23; matrix products, arithmetic and copies ran while one was open for 15% -> 15% of each run, Pallas kernels for 28% -> 29%
where the time goes in v5:
time: 742 us; the launch traced here: 732 us
  Pallas kernels  249 us (34%)
  waiting for transfers between devices  209 us (28%)
  starting transfers between devices  114 us (15%)
  local copies, waits for them, and re-layouts  84.4 us (11%)
  other arithmetic  59.7 us (8%)
  between operations  15.5 us (2%)
    all_to_all x12, waiting for transfers between devices, exchange(): return lax.all_to_all(blocks, axes, 0, 0, tiled=True)  128 us
    pallas_call x3, Pallas kernels, attend_back(): pl.pallas_call(functools.partial(attend_back_kernel, count), grid=(1,), o...  90.9 us
    pallas_call x2, Pallas kernels, feed_forward(): pl.pallas_call(functools.partial(mlp_kernel, begin_tile, real, out_rows,...  61.5 us
    pallas_call x3, Pallas kernels, attend(): pl.pallas_call(functools.partial(attend_kernel, count), grid=(1,), out_sh...  61.3 us
    ppermute x30, waiting for transfers between devices, line_go(): lax.ppermute(send, axis, [(j, j ^ step + 1) for j in range(count)])  54.8 us
    all_to_all x12, starting transfers between devices, exchange(): return lax.all_to_all(blocks, axes, 0, 0, tiled=True)  53 us
    ppermute x30, starting transfers between devices, line_go(): lax.ppermute(send, axis, [(j, j ^ step + 1) for j in range(count)])  51.1 us
    unnamed x148, local copies, waits for them, and re-layouts  24.4 us
  transfers between devices with their start and end apart: 66, of which 23 were waited for; matrix products, arithmetic and copies ran while one was open for 15% of the time, Pallas kernels for 29%

profile of v5, /device:TPU:0, one launch (start us, length us, event | category | flops | bytes accessed | tf_op | source)
XLA Modules:
  0.0 732.3 jit_solution(14969031205457785918)
XLA Ops:
  14.9 6.3 all-to-all-start
  22.0 4.0 fusion.1
  27.9 2.5 pad_maximum_fusion.2
  37.5 3.8 collective-permute-start.3
  45.3 13.6 %all-to-all-done = bf16[4,784,128]{2,1,0:T(8,128)(2,1)} async-done(((bf16[4,784,128]{2,1,0:T(8,128)(2,1)}), bf16[4,784,128]{2,1,0:T(8,128)(2,1)}, u32[]{:S(2)}, u32[]{:S(2)}) %all-to-all-start) | async-done | bytes 802848 | tf_op jit(solution)/shard_map/all_to_all | solution.py:416
  61.1 4.2 all-to-all-start.1
  68.2 9.1 %all-to-all-done.1 = bf16[8,3,128,128]{3,2,1,0:T(8,128)(2,1)} async-done(((bf16[8,3,128,128]{3,2,1,0:T(8,128)(2,1)}), bf16[8,3,128,128]{3,2,1,0:T(8,128)(2,1)}, u32[]{:S(2)}, u32[]{:S(2)}) %all-to-all-start.1) | async-done | bytes 786464 | tf_op jit(solution)/shard_map/all_to_all | solution.py:416
  77.4 2.4 copy.82
  79.7 2.2 copy.114
  85.1 3.3 shard_map.169
  88.4 4.9 all-to-all-start.2
  95.5 2.5 collective-permute-start.7
  98.0 4.5 collective-permute-start.6
  104.7 61.6 %all-to-all-done.2.refs_0_ = bf16[4,512,1024]{2,1,0:T(8,128)(2,1)} async-done(((bf16[4,512,1024]{2,1,0:T(8,128)(2,1)}), bf16[4,512,1024]{2,1,0:T(8,128)(2,1)}, u32[]{:S(2)}, u32[]{:S(2)}) %all-to-all-start.2) | async-done | bytes 4194336 | tf_op jit(solution)/shard_map/all_to_all | solution.py:416
  166.3 2.9 collective-permute-done.9
  171.4 4.7 all-to-all-start.3
  177.2 4.0 fusion
  182.3 21.5 %shard_map.170 = (bf16[2048,128]{1,0:T(8,128)(2,1)S(1)}, bf16[2048,128]{1,0:T(8,128)(2,1)S(1)}, bf16[2048,128]{1,0:T(8,128)(2,1)S(1)}, bf16[2048,128]{1,0:T(8,128)(2,1)S(1)}, f32[2048,128]{1,0:T(8,128)S(1)}) custom-call(s32[1]{0:T(128)} %bitcast.side_ref, s32[4]{0:T(128)S(1)} %get-tuple-element.529.low_ref, bf16[4,512,1024]{2,1,0:T(8,128)(2,1)} %all-to-all-done.2.refs_0_, ...), custom_call_target="tpu_custom_call" | custom-call | tf_op jit(solution)/shard_map/pallas_call | solution.py:620
  208.9 4.8 collective-permute-done.14.refs_1_.refs_3_
  213.7 21.1 %shard_map.171 = (bf16[2048,128]{1,0:T(8,128)(2,1)S(1)}, bf16[2048,128]{1,0:T(8,128)(2,1)S(1)}, bf16[2048,128]{1,0:T(8,128)(2,1)S(1)}, bf16[2048,128]{1,0:T(8,128)(2,1)S(1)}, f32[2048,128]{1,0:T(8,128)S(1)}) custom-call(s32[1]{0:T(128)} %bitcast.side_ref, s32[4]{0:T(128)S(1)} %get-tuple-element.528.low_ref, ...), custom_call_target="tpu_custom_call" | custom-call | tf_op jit(solution)/shard_map/pallas_call | solution.py:620
  238.2 3.8 collective-permute-done.13
  245.2 4.4 all-to-all-start.4
  251.1 18.8 %shard_map.172 = (bf16[2048,128]{1,0:T(8,128)(2,1)S(1)}, bf16[2048,128]{1,0:T(8,128)(2,1)S(1)}, bf16[2048,128]{1,0:T(8,128)(2,1)S(1)}, bf16[2048,128]{1,0:T(8,128)(2,1)S(1)}, f32[2048,128]{1,0:T(8,128)S(1)}) custom-call(s32[1]{0:T(128)} %bitcast.side_ref, s32[4]{0:T(128)S(1)} %get-tuple-element.527.low_ref, bf16[4,256,1024]{2,1,0:T(8,128)(2,1)} %all-to-all-done.3.refs_0_, ...), custom_call_target="tpu_custom_call" | custom-call | tf_op jit(solution)/shard_map/pallas_call | solution.py:620
  272.5 8.9 %collective-permute-done.16 = bf16[768,256]{1,0:T(8,128)(2,1)} collective-permute-done((bf16[768,256]{1,0:T(8,128)(2,1)}, bf16[768,256]{1,0:T(8,128)(2,1)}, u32[]{:S(2)}, u32[]{:S(2)}) %collective-permute-start.16) | collective-permute-done | bytes 393248 | tf_op jit(solution)/shard_map/ppermute | solution.py:430
  283.9 3.5 all-to-all-start.5
  289.2 6.8 all-to-all-done.5.os_ref
  296.8 7.4 %shard_map.173 = (f32[768,1024]{1,0:T(8,128)}, bf16[768,1024]{1,0:T(8,128)(2,1)}, bf16[768,1024]{1,0:T(8,128)(2,1)}) custom-call(bf16[4,512,256]{2,1,0:T(8,128)(2,1)} %all-to-all-done.4.om_ref, bf16[4,256,256]{2,1,0:T(8,128)(2,1)} %copy-done.41, bf16[4,768,256]{2,1,0:T(8,128)(2,1)} %copy-done, bf16[8,4,2496,128]{3,2,1,0:T(8,128)(2,1)} %bitcast.251, ...), custom_call_target="tpu_custom_call" | custom-call | tf_op jit(solution)/shard_map/pallas_call | solution.py:1093
  307.6 22.8 %shard_map.174 = (f32[768,1024]{1,0:T(8,128)}, f32[768,1024]{1,0:T(8,128)}, bf16[8,4,704,128]{3,2,1,0:T(8,128)(2,1)}) custom-call(bf16[768,1024]{1,0:T(8,128)(2,1)} %get-tuple-element.284.n_ref, bf16[4,768,256]{2,1,0:T(8,128)(2,1)} %copy-done.26, bf16[8,4,2496,128]{3,2,1,0:T(8,128)(2,1)} %bitcast.252), custom_call_target="tpu_custom_call" | custom-call | tf_op jit(solution)/shard_map/pallas_call | solution.py:1113
  330.8 38.7 %shard_map.175 = (f32[768,1024]{1,0:T(8,128)}, f32[768,1024]{1,0:T(8,128)}, bf16[8,4,1536,128]{3,2,1,0:T(8,128)(2,1)}) custom-call(bf16[768,1024]{1,0:T(8,128)(2,1)} %get-tuple-element.284.n_ref, bf16[4,768,256]{2,1,0:T(8,128)(2,1)} %copy-done.26, bf16[8,4,2496,128]{3,2,1,0:T(8,128)(2,1)} %bitcast.253), custom_call_target="tpu_custom_call" | custom-call | tf_op jit(solution)/shard_map/pallas_call | solution.py:1113
  369.5 12.5 %shard_map.176 = (bf16[4,768,256]{2,1,0:T(8,128)(2,1)}, f32[768,1024]{1,0:T(8,128)}, bf16[4,768,256]{2,1,0:T(8,128)(2,1)}, bf16[768,1024]{1,0:T(8,128)(2,1)}, f32[1,1024]{1,0:T(1,128)}) custom-call(f32[768,1024]{1,0:T(8,128)} %get-tuple-element.269.h_ref, f32[768,1024]{1,0:T(8,128)} %get-tuple-element.283.ya_ref, f32[768,1024]{1,0:T(8,128)} %get-tuple-element.285.yb_ref, ...), custom_call_target="tpu_custom_call" | custom-call | tf_op jit(solution)/shard_map/pallas_call | solution.py:1155
  382.1 4.8 all-to-all-start.6
  386.9 3.2 shard_map.177
  390.2 15.8 %all-to-all-done.6 = bf16[4,768,256]{2,1,0:T(8,128)(2,1)} async-done(((bf16[4,768,256]{2,1,0:T(8,128)(2,1)}), bf16[4,768,256]{2,1,0:T(8,128)(2,1)}, u32[]{:S(2)}, u32[]{:S(2)}) %all-to-all-start.6) | async-done | bytes 1572896 | tf_op jit(solution)/shard_map/all_to_all | solution.py:416
  406.0 2.4 constant_dynamic-slice_fusion
  408.5 2.7 collective-permute-start.21
  412.9 33.2 %shard_map.178 = (bf16[4,512,1024]{2,1,0:T(8,128)(2,1)}, f32[384,1024]{1,0:T(8,128)}, bf16[2048,128]{1,0:T(8,128)(2,1)}) custom-call(s32[1]{0:T(128)} %bitcast.side_ref, s32[4]{0:T(128)} %copy-done.22, bf16[4,512,1024]{2,1,0:T(8,128)(2,1)} %collective-permute-done.11.refs_0_, bf16[4,768,128]{2,1,0:T(8,128)(2,1)} %copy-done.38, bf16[1024,384]{1,0:T(8,128)(2,1)} %copy-done.1, ...), custom_call_target="tpu_custom_call" | custom-call | tf_op jit(solution)/shard_map/pallas_call | solution.py:711
  447.6 3.7 all-to-all-start.7
  452.2 3.8 collective-permute-start.25
  456.6 30.5 %shard_map.179 = (bf16[4,512,1024]{2,1,0:T(8,128)(2,1)}, f32[384,1024]{1,0:T(8,128)}, bf16[2048,128]{1,0:T(8,128)(2,1)}) custom-call(s32[1]{0:T(128)} %bitcast.side_ref, s32[4]{0:T(128)} %copy-done.21, bf16[4,512,1024]{2,1,0:T(8,128)(2,1)} %all-to-all-done.2.refs_0_, bf16[4,768,128]{2,1,0:T(8,128)(2,1)} %get-tuple-element.328.refs_1_.refs_2_, ...), custom_call_target="tpu_custom_call" | custom-call | tf_op jit(solution)/shard_map/pallas_call | solution.py:711
  487.1 3.7 all-to-all-done.7
  491.3 3.4 collective-permute-start.29
  495.7 8.7 %add_convert_fusion = bf16[4,512,1024]{2,1,0:T(8,128)(2,1)} fusion(bf16[4,512,1024]{2,1,0:T(8,128)(2,1)} %collective-permute-done.22, bf16[4,512,1024]{2,1,0:T(8,128)(2,1)} %get-tuple-element.320), kind=kLoop, calls=%fused_computation | loop fusion | flops 8388608 | bytes 12582912 | tf_op jit(solution)/shard_map/convert_element_type | solution.py:1227
  504.5 13.5 %reduce-scatter.5.cloned.1.call-done = bf16[1,4,1536,128]{3,2,1,0:T(8,128)(2,1)} async-done(((bf16[8,4,1536,128]{3,2,1,0:T(8,128)(2,1)}), bf16[1,4,1536,128]{3,2,1,0:T(8,128)(2,1)}) %reduce-scatter.5.cloned.1.call-update) | async-done | bytes 1572880 | tf_op jit(solution)/shard_map/reduce_scatter | solution.py:1150
  518.0 5.0 all-to-all-start.8
  523.1 3.4 collective-permute-start.32
  528.5 27.2 %shard_map.180 = (bf16[4,256,1024]{2,1,0:T(8,128)(2,1)}, bf16[4,256,1024]{2,1,0:T(8,128)(2,1)}, f32[384,1024]{1,0:T(8,128)}, bf16[2048,128]{1,0:T(8,128)(2,1)}) custom-call(s32[1]{0:T(128)} %bitcast.side_ref, s32[4]{0:T(128)} %copy-done.23, bf16[4,256,1024]{2,1,0:T(8,128)(2,1)} %all-to-all-done.3.refs_0_, ...), custom_call_target="tpu_custom_call" | custom-call | tf_op jit(solution)/shard_map/pallas_call | solution.py:711
  555.8 4.4 collective-permute-done.31
  570.8 3.9 add_convert_fusion.1
  574.8 5.6 shard_map.181
  582.4 3.0 collective-permute-start.36
  588.7 4.0 all-to-all-start.9
  593.8 13.2 %collective-permute-done.35 = bf16[512,256]{1,0:T(8,128)(2,1)} collective-permute-done((bf16[512,256]{1,0:T(8,128)(2,1)}, bf16[512,256]{1,0:T(8,128)(2,1)}, u32[]{:S(2)}, u32[]{:S(2)}) %collective-permute-start.35) | collective-permute-done | bytes 262176 | tf_op jit(solution)/shard_map/ppermute | solution.py:430
  617.4 2.4 fusion.3
  620.9 2.4 copy.96
  630.9 3.6 shard_map.182
  635.2 4.0 all-to-all-start.10
  641.4 3.0 collective-permute-start.39
  648.5 10.8 %all-to-all-done.10 = bf16[4,768,256]{2,1,0:T(8,128)(2,1)S(1)} async-done(((bf16[4,768,256]{2,1,0:T(8,128)(2,1)}), bf16[4,768,256]{2,1,0:T(8,128)(2,1)S(1)}, u32[]{:S(2)}, u32[]{:S(2)}) %all-to-all-start.10) | async-done | bytes 1572896 | tf_op jit(solution)/shard_map/all_to_all | solution.py:416
  659.4 3.6 all-to-all-start.11
  666.6 3.0 collective-permute-start.42
  669.5 6.5 all-to-all-done.11
  679.4 13.6 %collective-permute-start.45 = (bf16[780,128]{1,0:T(8,128)(2,1)S(1)}, bf16[780,128]{1,0:T(8,128)(2,1)S(1)}, u32[]{:S(2)}, u32[]{:S(2)}) collective-permute-start(bf16[780,128]{1,0:T(8,128)(2,1)S(1)} %get-tuple-element.469), channel_id=1, source_target_pairs={{0,4},{4,0},{8,12},{12,8},{1,5},{5,1},{9,13},{13,9},{2,6},{6,2},{1... | collective-permute-start | bytes 599048 | tf_op jit(solution)/shard_map/ppermute | solution.py:430
  695.2 14.3 %collective-permute-done.43 = bf16[768,256]{1,0:T(8,128)(2,1)} collective-permute-done((bf16[768,256]{1,0:T(8,128)(2,1)}, bf16[768,256]{1,0:T(8,128)(2,1)}, u32[]{:S(2)}, u32[]{:S(2)}) %collective-permute-start.43) | collective-permute-done | bytes 393248 | tf_op jit(solution)/shard_map/ppermute | solution.py:430
  709.5 7.6 %collective-permute-done.46 = bf16[780,128]{1,0:T(8,128)(2,1)S(1)} collective-permute-done((bf16[780,128]{1,0:T(8,128)(2,1)S(1)}, bf16[780,128]{1,0:T(8,128)(2,1)S(1)}, u32[]{:S(2)}, u32[]{:S(2)}) %collective-permute-start.46) | collective-permute-done | bytes 199712 | tf_op jit(solution)/shard_map/ppermute | solution.py:430
  (390 shorter events, 131.6 us)
Async XLA Ops:
  7.2 26.0 %collective-permute-start.4 = (s32[6,2048]{1,0:T(8,128)}, s32[6,2048]{1,0:T(8,128)}, u32[]{:S(2)}, u32[]{:S(2)}) collective-permute-start(s32[6,2048]{1,0:T(8,128)} %param.12), channel_id=1, source_target_pairs={{0,16},{16,0},{1,17},{17,1},{2,18},{18,2},{3,19},{19,3},{4,20},{20... | collective-permute-start | bytes 147464 | tf_op jit(solution)/shard_map/ppermute | solution.py:493
  9.4 32.4 %collective-permute-start.10 = (bf16[2,256,256]{2,1,0:T(8,128)(2,1)}, bf16[2,256,256]{2,1,0:T(8,128)(2,1)}, u32[]{:S(2)}, u32[]{:S(2)}) collective-permute-start(bf16[2,256,256]{2,1,0:T(8,128)(2,1)} %constant_dynamic-slice_fusion.4), channel_id=1, source_target_pairs={{0,16},{16,0},{1,17},{17,1},{2,18},{18,2},{3,19},{19,3},{4,20},{20... | collective-permute-start | bytes 786440 | tf_op jit(solution)/shard_map/ppermute | solution.py:493
  11.2 30.7 %collective-permute-start.5 = (bf16[2,256,256]{2,1,0:T(8,128)(2,1)}, bf16[2,256,256]{2,1,0:T(8,128)(2,1)}, u32[]{:S(2)}, u32[]{:S(2)}) collective-permute-start(bf16[2,256,256]{2,1,0:T(8,128)(2,1)} %constant_dynamic-slice_fusion.5), channel_id=1, source_target_pairs={{0,16},{16,0},{1,17},{17,1},{2,18},{18,2},{3,19},{19,3},{4,20},{20... | collective-permute-start | bytes 786440 | tf_op jit(solution)/shard_map/ppermute | solution.py:493
  13.3 21.8 %collective-permute-start = (bf16[2,256,256]{2,1,0:T(8,128)(2,1)}, bf16[2,256,256]{2,1,0:T(8,128)(2,1)}, u32[]{:S(2)}, u32[]{:S(2)}) collective-permute-start(bf16[2,256,256]{2,1,0:T(8,128)(2,1)} %constant_dynamic-slice_fusion.10), channel_id=1, source_target_pairs={{0,16},{16,0},{1,17},{17,1},{2,18},{18,2},{3,19},{19,3},{4,20},{20... | collective-permute-start | bytes 786440 | tf_op jit(solution)/shard_map/ppermute | solution.py:493
  14.9 44.0 %all-to-all-start = ((bf16[4,784,128]{2,1,0:T(8,128)(2,1)}), bf16[4,784,128]{2,1,0:T(8,128)(2,1)}, u32[]{:S(2)}, u32[]{:S(2)}) async-start(bf16[4,784,128]{2,1,0:T(8,128)(2,1)} %broadcast_in_dim.131), calls=%async_computation | async-start | bytes 1605632 | tf_op jit(solution)/shard_map/all_to_all | solution.py:416
  37.5 44.5 %collective-permute-start.3 = (bf16[768,256]{1,0:T(8,128)(2,1)}, bf16[768,256]{1,0:T(8,128)(2,1)}, u32[]{:S(2)}, u32[]{:S(2)}) collective-permute-start(bf16[768,256]{1,0:T(8,128)(2,1)} %get-tuple-element.457), channel_id=1, source_target_pairs={{0,12},{4,8},{8,4},{12,0},{1,13},{5,9},{9,5},{13,1},{2,14},{6,10},... | collective-permute-start | bytes 1179656 | tf_op jit(solution)/shard_map/ppermute | solution.py:430
  41.3 40.7 %collective-permute-start.2 = (bf16[768,256]{1,0:T(8,128)(2,1)}, bf16[768,256]{1,0:T(8,128)(2,1)}, u32[]{:S(2)}, u32[]{:S(2)}) collective-permute-start(bf16[768,256]{1,0:T(8,128)(2,1)} %get-tuple-element.458), channel_id=1, source_target_pairs={{0,8},{4,12},{8,0},{12,4},{1,9},{5,13},{9,1},{13,5},{2,10},{6,14},... | collective-permute-start | bytes 1179656 | tf_op jit(solution)/shard_map/ppermute | solution.py:430
  41.3 40.7 %collective-permute-start.1 = (bf16[768,256]{1,0:T(8,128)(2,1)}, bf16[768,256]{1,0:T(8,128)(2,1)}, u32[]{:S(2)}, u32[]{:S(2)}) collective-permute-start(bf16[768,256]{1,0:T(8,128)(2,1)} %get-tuple-element.459), channel_id=1, source_target_pairs={{0,4},{4,0},{8,12},{12,8},{1,5},{5,1},{9,13},{13,9},{2,6},{6,2},{1... | collective-permute-start | bytes 1179656 | tf_op jit(solution)/shard_map/ppermute | solution.py:430
  61.1 16.3 %all-to-all-start.1 = ((bf16[8,3,128,128]{3,2,1,0:T(8,128)(2,1)}), bf16[8,3,128,128]{3,2,1,0:T(8,128)(2,1)}, u32[]{:S(2)}, u32[]{:S(2)}) async-start(bf16[8,3,128,128]{3,2,1,0:T(8,128)(2,1)} %bitcast.11), calls=%async_computation.1 | async-start | bytes 1572864 | tf_op jit(solution)/shard_map/all_to_all | solution.py:416
  65.3 230.7 %all-gather.3.cloned.1.call-start = ((), (), s32[]{:S(2)}) async-start(), calls=%async_computation.16 | async-start | bytes 21086208 | tf_op jit(solution)/shard_map/all_gather | solution.py:1017
  88.4 77.9 %all-to-all-start.2 = ((bf16[4,512,1024]{2,1,0:T(8,128)(2,1)}), bf16[4,512,1024]{2,1,0:T(8,128)(2,1)}, u32[]{:S(2)}, u32[]{:S(2)}) async-start(bf16[4,512,1024]{2,1,0:T(8,128)(2,1)} %get-tuple-element.222), calls=%async_computation.2 | async-start | bytes 8388608 | tf_op jit(solution)/shard_map/all_to_all | solution.py:416
  95.5 73.7 %collective-permute-start.9 = (bf16[768,256]{1,0:T(8,128)(2,1)}, bf16[768,256]{1,0:T(8,128)(2,1)S(1)}, u32[]{:S(2)}, u32[]{:S(2)}) collective-permute-start(bf16[768,256]{1,0:T(8,128)(2,1)} %get-tuple-element.453), channel_id=1, source_target_pairs={{0,12},{1,8},{2,4},{3,0},{4,13},{5,9},{6,5},{7,1},{8,14},{9,10},{1... | collective-permute-start | bytes 1179656 | tf_op jit(solution)/shard_map/ppermute | solution.py:465
  95.5 73.7 %collective-permute-start.8 = (bf16[768,256]{1,0:T(8,128)(2,1)}, bf16[768,256]{1,0:T(8,128)(2,1)S(1)}, u32[]{:S(2)}, u32[]{:S(2)}) collective-permute-start(bf16[768,256]{1,0:T(8,128)(2,1)} %get-tuple-element.454), channel_id=1, source_target_pairs={{0,8},{1,12},{2,0},{3,4},{4,9},{5,13},{6,1},{7,5},{8,10},{9,14},{1... | collective-permute-start | bytes 1179656 | tf_op jit(solution)/shard_map/ppermute | solution.py:465
  95.5 75.2 %collective-permute-start.7 = (bf16[768,256]{1,0:T(8,128)(2,1)}, bf16[768,256]{1,0:T(8,128)(2,1)S(1)}, u32[]{:S(2)}, u32[]{:S(2)}) collective-permute-start(bf16[768,256]{1,0:T(8,128)(2,1)} %get-tuple-element.455), channel_id=1, source_target_pairs={{0,4},{1,0},{2,12},{3,8},{4,5},{5,1},{6,13},{7,9},{8,6},{9,2},{10,... | collective-permute-start | bytes 1179656 | tf_op jit(solution)/shard_map/ppermute | solution.py:465
  98.0 72.7 %collective-permute-start.6 = (bf16[768,256]{1,0:T(8,128)(2,1)}, bf16[768,256]{1,0:T(8,128)(2,1)}, u32[]{:S(2)}, u32[]{:S(2)}) collective-permute-start(bf16[768,256]{1,0:T(8,128)(2,1)} %get-tuple-element.456), channel_id=1, source_target_pairs={{0,0},{1,4},{2,8},{3,12},{4,1},{5,5},{6,9},{7,13},{8,2},{9,6},{10,... | collective-permute-start | bytes 1179656 | tf_op jit(solution)/shard_map/ppermute | solution.py:465
  170.7 37.3 %collective-permute-start.11 = (bf16[4,512,1024]{2,1,0:T(8,128)(2,1)}, bf16[4,512,1024]{2,1,0:T(8,128)(2,1)}, u32[]{:S(2)}, u32[]{:S(2)}) collective-permute-start(bf16[4,512,1024]{2,1,0:T(8,128)(2,1)} %all-to-all-done.2.refs_0_), channel_id=1, source_target_pairs={{0,16},{16,0},{1,17},{17,1},{2,18},{18,2},{3,19},{19,3},{4,20},{20... | collective-permute-start | bytes 12582920 | tf_op jit(solution)/shard_map/ppermute | solution.py:493
  171.4 36.6 %all-to-all-start.3 = ((bf16[4,256,1024]{2,1,0:T(8,128)(2,1)}), bf16[4,256,1024]{2,1,0:T(8,128)(2,1)}, u32[]{:S(2)}, u32[]{:S(2)}) async-start(bf16[4,256,1024]{2,1,0:T(8,128)(2,1)} %get-tuple-element.225), calls=%async_computation.3 | async-start | bytes 4194304 | tf_op jit(solution)/shard_map/all_to_all | solution.py:416
  208.0 34.0 %collective-permute-start.12 = (bf16[4,256,1024]{2,1,0:T(8,128)(2,1)}, bf16[4,256,1024]{2,1,0:T(8,128)(2,1)}, u32[]{:S(2)}, u32[]{:S(2)}) collective-permute-start(bf16[4,256,1024]{2,1,0:T(8,128)(2,1)} %all-to-all-done.3.refs_0_), channel_id=1, source_target_pairs={{0,16},{16,0},{1,17},{17,1},{2,18},{18,2},{3,19},{19,3},{4,20},{20... | collective-permute-start | bytes 6291464 | tf_op jit(solution)/shard_map/ppermute | solution.py:493
  208.3 5.4 collective-permute-start.14
  208.5 33.5 %collective-permute-start.13 = (bf16[768,256]{1,0:T(8,128)(2,1)}, bf16[768,256]{1,0:T(8,128)(2,1)}, u32[]{:S(2)}, u32[]{:S(2)}) collective-permute-start(bf16[768,256]{1,0:T(8,128)(2,1)} %get-tuple-element.246), channel_id=1, source_target_pairs={{0,4},{4,0},{8,12},{12,8},{1,5},{5,1},{9,13},{13,9},{2,6},{6,2},{1... | collective-permute-start | bytes 1179656 | tf_op jit(solution)/shard_map/ppermute | solution.py:430
  242.0 1.9 collective-permute-start.15
  245.2 36.1 %all-to-all-start.4 = ((bf16[4,512,256]{2,1,0:T(8,128)(2,1)}), bf16[4,512,256]{2,1,0:T(8,128)(2,1)}, u32[]{:S(2)}, u32[]{:S(2)}) async-start(bf16[4,512,256]{2,1,0:T(8,128)(2,1)} %maximum_select_fusion.2), calls=%async_computation.4 | async-start | bytes 2097152 | tf_op jit(solution)/shard_map/all_to_all | solution.py:416
  249.7 31.7 %collective-permute-start.16 = (bf16[768,256]{1,0:T(8,128)(2,1)}, bf16[768,256]{1,0:T(8,128)(2,1)}, u32[]{:S(2)}, u32[]{:S(2)}) collective-permute-start(bf16[768,256]{1,0:T(8,128)(2,1)} %get-tuple-element.257), channel_id=1, source_target_pairs={{0,8},{4,12},{8,0},{12,4},{1,9},{5,13},{9,1},{13,5},{2,10},{6,14},... | collective-permute-start | bytes 1179656 | tf_op jit(solution)/shard_map/ppermute | solution.py:430
  283.9 12.0 %all-to-all-start.5 = ((bf16[4,256,256]{2,1,0:T(8,128)(2,1)}), bf16[4,256,256]{2,1,0:T(8,128)(2,1)S(1)}, u32[]{:S(2)}, u32[]{:S(2)}) async-start(bf16[4,256,256]{2,1,0:T(8,128)(2,1)} %maximum_select_fusion.4), calls=%async_computation.5 | async-start | bytes 1048576 | tf_op jit(solution)/shard_map/all_to_all | solution.py:416
  287.4 160.2 %reduce-scatter.3.cloned.1.call-start = ((), (), s32[]{:S(2)}) async-start(), calls=%async_computation.14 | async-start | bytes 6488064 | tf_op jit(solution)/shard_map/reduce_scatter | solution.py:1150
  287.7 16.6 %collective-permute-start.18 = (bf16[768,256]{1,0:T(8,128)(2,1)S(1)}, bf16[768,256]{1,0:T(8,128)(2,1)S(1)}, u32[]{:S(2)}, u32[]{:S(2)}) collective-permute-start(bf16[768,256]{1,0:T(8,128)(2,1)S(1)} %copy-done.51), channel_id=1, source_target_pairs={{0,12},{4,8},{8,4},{12,0},{1,13},{5,9},{9,5},{13,1},{2,14},{6,10},... | collective-permute-start | bytes 1179656 | tf_op jit(solution)/shard_map/ppermute | solution.py:430
  330.4 187.6 %reduce-scatter.5.cloned.1.call-start = ((), (), s32[]{:S(2)}) async-start(), calls=%async_computation.15 | async-start | bytes 14155776 | tf_op jit(solution)/shard_map/reduce_scatter | solution.py:1150
  382.1 23.9 %all-to-all-start.6 = ((bf16[4,768,256]{2,1,0:T(8,128)(2,1)}), bf16[4,768,256]{2,1,0:T(8,128)(2,1)}, u32[]{:S(2)}, u32[]{:S(2)}) async-start(bf16[4,768,256]{2,1,0:T(8,128)(2,1)} %get-tuple-element.290), calls=%async_computation.6 | async-start | bytes 3145728 | tf_op jit(solution)/shard_map/all_to_all | solution.py:416
  408.4 3.6 collective-permute-start.19
  408.5 37.6 %collective-permute-start.21 = (bf16[768,256]{1,0:T(8,128)(2,1)S(1)}, bf16[768,256]{1,0:T(8,128)(2,1)S(1)}, u32[]{:S(2)}, u32[]{:S(2)}) collective-permute-start(bf16[768,256]{1,0:T(8,128)(2,1)S(1)} %get-tuple-element.444), channel_id=1, source_target_pairs={{0,8},{4,12},{8,0},{12,4},{1,9},{5,13},{9,1},{13,5},{2,10},{6,14},... | collective-permute-start | bytes 1179656 | tf_op jit(solution)/shard_map/ppermute | solution.py:430
  411.1 35.0 %collective-permute-start.20 = (bf16[768,256]{1,0:T(8,128)(2,1)S(1)}, bf16[768,256]{1,0:T(8,128)(2,1)S(1)}, u32[]{:S(2)}, u32[]{:S(2)}) collective-permute-start(bf16[768,256]{1,0:T(8,128)(2,1)S(1)} %get-tuple-element.445), channel_id=1, source_target_pairs={{0,4},{4,0},{8,12},{12,8},{1,5},{5,1},{9,13},{13,9},{2,6},{6,2},{1... | collective-permute-start | bytes 1179656 | tf_op jit(solution)/shard_map/ppermute | solution.py:430
  447.6 43.3 %collective-permute-start.22 = (bf16[4,512,1024]{2,1,0:T(8,128)(2,1)}, bf16[4,512,1024]{2,1,0:T(8,128)(2,1)}, u32[]{:S(2)}, u32[]{:S(2)}) collective-permute-start(bf16[4,512,1024]{2,1,0:T(8,128)(2,1)} %get-tuple-element.315), channel_id=1, source_target_pairs={{0,16},{16,0},{1,17},{17,1},{2,18},{18,2},{3,19},{19,3},{4,20},{20... | collective-permute-start | bytes 12582920 | tf_op jit(solution)/shard_map/ppermute | solution.py:493
  447.6 43.3 %all-to-all-start.7 = ((bf16[8,4,256,128]{3,2,1,0:T(8,128)(2,1)}), bf16[8,4,256,128]{3,2,1,0:T(8,128)(2,1)S(1)}, u32[]{:S(2)}, u32[]{:S(2)}) async-start(bf16[8,4,256,128]{3,2,1,0:T(8,128)(2,1)} %shard_map.177), calls=%async_computation.8 | async-start | bytes 4194304 | tf_op jit(solution)/shard_map/all_to_all | solution.py:416
  451.4 35.8 %collective-permute-start.26 = (bf16[768,256]{1,0:T(8,128)(2,1)S(1)}, bf16[768,256]{1,0:T(8,128)(2,1)}, u32[]{:S(2)}, u32[]{:S(2)}) collective-permute-start(bf16[768,256]{1,0:T(8,128)(2,1)S(1)} %get-tuple-element.443), channel_id=1, source_target_pairs={{0,12},{4,8},{8,4},{12,0},{1,13},{5,9},{9,5},{13,1},{2,14},{6,10},... | collective-permute-start | bytes 1179656 | tf_op jit(solution)/shard_map/ppermute | solution.py:430
  452.2 38.6 %collective-permute-start.25 = (bf16[704,128]{1,0:T(8,128)(2,1)}, bf16[704,128]{1,0:T(8,128)(2,1)}, u32[]{:S(2)}, u32[]{:S(2)}) collective-permute-start(bf16[704,128]{1,0:T(8,128)(2,1)} %get-tuple-element.479), channel_id=1, source_target_pairs={{0,12},{4,8},{8,4},{12,0},{1,13},{5,9},{9,5},{13,1},{2,14},{6,10},... | collective-permute-start | bytes 540680 | tf_op jit(solution)/shard_map/ppermute | solution.py:430
  456.1 34.8 %collective-permute-start.24 = (bf16[704,128]{1,0:T(8,128)(2,1)}, bf16[704,128]{1,0:T(8,128)(2,1)}, u32[]{:S(2)}, u32[]{:S(2)}) collective-permute-start(bf16[704,128]{1,0:T(8,128)(2,1)} %get-tuple-element.480), channel_id=1, source_target_pairs={{0,8},{4,12},{8,0},{12,4},{1,9},{5,13},{9,1},{13,5},{2,10},{6,14},... | collective-permute-start | bytes 540680 | tf_op jit(solution)/shard_map/ppermute | solution.py:430
  456.1 34.8 %collective-permute-start.23 = (bf16[704,128]{1,0:T(8,128)(2,1)S(1)}, bf16[704,128]{1,0:T(8,128)(2,1)}, u32[]{:S(2)}, u32[]{:S(2)}) collective-permute-start(bf16[704,128]{1,0:T(8,128)(2,1)S(1)} %get-tuple-element.481), channel_id=1, source_target_pairs={{0,4},{4,0},{8,12},{12,8},{1,5},{5,1},{9,13},{13,9},{2,6},{6,2},{1... | collective-permute-start | bytes 540680 | tf_op jit(solution)/shard_map/ppermute | solution.py:430
  491.3 13.2 %collective-permute-start.29 = (bf16[256,128]{1,0:T(8,128)(2,1)S(1)}, bf16[256,128]{1,0:T(8,128)(2,1)S(1)}, u32[]{:S(2)}, u32[]{:S(2)}) collective-permute-start(bf16[256,128]{1,0:T(8,128)(2,1)S(1)} %get-tuple-element.493), channel_id=1, source_target_pairs={{0,12},{4,8},{8,4},{12,0},{1,13},{5,9},{9,5},{13,1},{2,14},{6,10},... | collective-permute-start | bytes 196616 | tf_op jit(solution)/shard_map/ppermute | solution.py:430
  494.7 9.8 %collective-permute-start.28 = (bf16[256,128]{1,0:T(8,128)(2,1)S(1)}, bf16[256,128]{1,0:T(8,128)(2,1)S(1)}, u32[]{:S(2)}, u32[]{:S(2)}) collective-permute-start(bf16[256,128]{1,0:T(8,128)(2,1)S(1)} %get-tuple-element.494), channel_id=1, source_target_pairs={{0,8},{4,12},{8,0},{12,4},{1,9},{5,13},{9,1},{13,5},{2,10},{6,14},... | collective-permute-start | bytes 196616 | tf_op jit(solution)/shard_map/ppermute | solution.py:430
  494.7 9.8 %collective-permute-start.27 = (bf16[256,128]{1,0:T(8,128)(2,1)S(1)}, bf16[256,128]{1,0:T(8,128)(2,1)S(1)}, u32[]{:S(2)}, u32[]{:S(2)}) collective-permute-start(bf16[256,128]{1,0:T(8,128)(2,1)S(1)} %get-tuple-element.495), channel_id=1, source_target_pairs={{0,4},{4,0},{8,12},{12,8},{1,5},{5,1},{9,13},{13,9},{2,6},{6,2},{1... | collective-permute-start | bytes 196616 | tf_op jit(solution)/shard_map/ppermute | solution.py:430
  518.0 56.8 %all-to-all-start.8 = ((bf16[4,512,1024]{2,1,0:T(8,128)(2,1)}), bf16[4,512,1024]{2,1,0:T(8,128)(2,1)}, u32[]{:S(2)}, u32[]{:S(2)}) async-start(bf16[4,512,1024]{2,1,0:T(8,128)(2,1)} %add_convert_fusion), calls=%async_computation.10 | async-start | bytes 8388608 | tf_op jit(solution)/shard_map/all_to_all | solution.py:416
  523.1 32.7 %collective-permute-start.32 = (bf16[1536,128]{1,0:T(8,128)(2,1)S(1)}, bf16[1536,128]{1,0:T(8,128)(2,1)S(1)}, u32[]{:S(2)}, u32[]{:S(2)}) collective-permute-start(bf16[1536,128]{1,0:T(8,128)(2,1)S(1)} %get-tuple-element.440), channel_id=1, source_target_pairs={{0,12},{4,8},{8,4},{12,0},{1,13},{5,9},{9,5},{13,1},{2,14},{6,10},... | collective-permute-start | bytes 1179656 | tf_op jit(solution)/shard_map/ppermute | solution.py:430
  526.5 33.7 %collective-permute-start.31 = (bf16[1536,128]{1,0:T(8,128)(2,1)S(1)}, bf16[1536,128]{1,0:T(8,128)(2,1)S(1)}, u32[]{:S(2)}, u32[]{:S(2)}) collective-permute-start(bf16[1536,128]{1,0:T(8,128)(2,1)S(1)} %get-tuple-element.441), channel_id=1, source_target_pairs={{0,8},{4,12},{8,0},{12,4},{1,9},{5,13},{9,1},{13,5},{2,10},{6,14},... | collective-permute-start | bytes 1179656 | tf_op jit(solution)/shard_map/ppermute | solution.py:430
  526.5 33.7 %collective-permute-start.30 = (bf16[1536,128]{1,0:T(8,128)(2,1)S(1)}, bf16[1536,128]{1,0:T(8,128)(2,1)S(1)}, u32[]{:S(2)}, u32[]{:S(2)}) collective-permute-start(bf16[1536,128]{1,0:T(8,128)(2,1)S(1)} %get-tuple-element.442), channel_id=1, source_target_pairs={{0,4},{4,0},{8,12},{12,8},{1,5},{5,1},{9,13},{13,9},{2,6},{6,2},{1... | collective-permute-start | bytes 1179656 | tf_op jit(solution)/shard_map/ppermute | solution.py:430
  527.5 38.8 %collective-permute-start.37 = (bf16[2048,128]{1,0:T(8,128)(2,1)}, bf16[2048,128]{1,0:T(8,128)(2,1)S(1)}, u32[]{:S(2)}, u32[]{:S(2)}) collective-permute-start(bf16[2048,128]{1,0:T(8,128)(2,1)} %get-tuple-element.351), channel_id=1, source_target_pairs={{0,16},{16,0},{1,17},{17,1},{2,18},{18,2},{3,19},{19,3},{4,20},{20... | collective-permute-start | bytes 1572872 | tf_op jit(solution)/shard_map/ppermute | solution.py:493
  560.2 10.6 %collective-permute-start.33 = (bf16[4,256,1024]{2,1,0:T(8,128)(2,1)}, bf16[4,256,1024]{2,1,0:T(8,128)(2,1)}, u32[]{:S(2)}, u32[]{:S(2)}) collective-permute-start(bf16[4,256,1024]{2,1,0:T(8,128)(2,1)} %get-tuple-element.338), channel_id=1, source_target_pairs={{0,16},{16,0},{1,17},{17,1},{2,18},{18,2},{3,19},{19,3},{4,20},{20... | collective-permute-start | bytes 6291464 | tf_op jit(solution)/shard_map/ppermute | solution.py:493
  564.6 4.5 collective-permute-start.48
  582.4 11.4 %collective-permute-start.36 = (bf16[512,256]{1,0:T(8,128)(2,1)}, bf16[512,256]{1,0:T(8,128)(2,1)}, u32[]{:S(2)}, u32[]{:S(2)}) collective-permute-start(bf16[512,256]{1,0:T(8,128)(2,1)} %get-tuple-element.460), channel_id=1, source_target_pairs={{0,12},{4,8},{8,4},{12,0},{1,13},{5,9},{9,5},{13,1},{2,14},{6,10},... | collective-permute-start | bytes 786440 | tf_op jit(solution)/shard_map/ppermute | solution.py:430
  585.4 21.6 %collective-permute-start.35 = (bf16[512,256]{1,0:T(8,128)(2,1)}, bf16[512,256]{1,0:T(8,128)(2,1)}, u32[]{:S(2)}, u32[]{:S(2)}) collective-permute-start(bf16[512,256]{1,0:T(8,128)(2,1)} %get-tuple-element.461), channel_id=1, source_target_pairs={{0,8},{4,12},{8,0},{12,4},{1,9},{5,13},{9,1},{13,5},{2,10},{6,14},... | collective-permute-start | bytes 786440 | tf_op jit(solution)/shard_map/ppermute | solution.py:430
  585.4 21.6 %collective-permute-start.34 = (bf16[512,256]{1,0:T(8,128)(2,1)}, bf16[512,256]{1,0:T(8,128)(2,1)}, u32[]{:S(2)}, u32[]{:S(2)}) collective-permute-start(bf16[512,256]{1,0:T(8,128)(2,1)} %get-tuple-element.462), channel_id=1, source_target_pairs={{0,4},{4,0},{8,12},{12,8},{1,5},{5,1},{9,13},{13,9},{2,6},{6,2},{1... | collective-permute-start | bytes 786440 | tf_op jit(solution)/shard_map/ppermute | solution.py:430
  588.7 40.8 %all-to-all-start.9 = ((bf16[4,256,1024]{2,1,0:T(8,128)(2,1)}), bf16[4,256,1024]{2,1,0:T(8,128)(2,1)S(1)}, u32[]{:S(2)}, u32[]{:S(2)}) async-start(bf16[4,256,1024]{2,1,0:T(8,128)(2,1)} %add_convert_fusion.1), calls=%async_computation.11 | async-start | bytes 4194304 | tf_op jit(solution)/shard_map/all_to_all | solution.py:416
  615.7 11.5 %collective-permute-start.38 = (bf16[4,256,128]{2,1,0:T(8,128)(2,1)}, bf16[4,256,128]{2,1,0:T(8,128)(2,1)}, u32[]{:S(2)}, u32[]{:S(2)}) collective-permute-start(bf16[4,256,128]{2,1,0:T(8,128)(2,1)} %get-tuple-element.486), channel_id=1, source_target_pairs={{0,16},{16,0},{1,17},{17,1},{2,18},{18,2},{3,19},{19,3},{4,20},{20... | collective-permute-start | bytes 786440 | tf_op jit(solution)/shard_map/ppermute | solution.py:493
  635.2 24.1 %all-to-all-start.10 = ((bf16[4,768,256]{2,1,0:T(8,128)(2,1)}), bf16[4,768,256]{2,1,0:T(8,128)(2,1)S(1)}, u32[]{:S(2)}, u32[]{:S(2)}) async-start(bf16[4,768,256]{2,1,0:T(8,128)(2,1)} %pad_maximum_fusion), calls=%async_computation.12 | async-start | bytes 3145728 | tf_op jit(solution)/shard_map/all_to_all | solution.py:416
  640.0 23.0 %collective-permute-start.41 = (bf16[256,256]{1,0:T(8,128)(2,1)}, bf16[256,256]{1,0:T(8,128)(2,1)S(1)}, u32[]{:S(2)}, u32[]{:S(2)}) collective-permute-start(bf16[256,256]{1,0:T(8,128)(2,1)} %get-tuple-element.482), channel_id=1, source_target_pairs={{0,12},{4,8},{8,4},{12,0},{1,13},{5,9},{9,5},{13,1},{2,14},{6,10},... | collective-permute-start | bytes 393224 | tf_op jit(solution)/shard_map/ppermute | solution.py:430
  641.4 21.5 %collective-permute-start.40 = (bf16[256,256]{1,0:T(8,128)(2,1)}, bf16[256,256]{1,0:T(8,128)(2,1)S(1)}, u32[]{:S(2)}, u32[]{:S(2)}) collective-permute-start(bf16[256,256]{1,0:T(8,128)(2,1)} %get-tuple-element.483), channel_id=1, source_target_pairs={{0,8},{4,12},{8,0},{12,4},{1,9},{5,13},{9,1},{13,5},{2,10},{6,14},... | collective-permute-start | bytes 393224 | tf_op jit(solution)/shard_map/ppermute | solution.py:430
  641.4 21.5 %collective-permute-start.39 = (bf16[256,256]{1,0:T(8,128)(2,1)}, bf16[256,256]{1,0:T(8,128)(2,1)S(1)}, u32[]{:S(2)}, u32[]{:S(2)}) collective-permute-start(bf16[256,256]{1,0:T(8,128)(2,1)} %get-tuple-element.484), channel_id=1, source_target_pairs={{0,4},{4,0},{8,12},{12,8},{1,5},{5,1},{9,13},{13,9},{2,6},{6,2},{1... | collective-permute-start | bytes 393224 | tf_op jit(solution)/shard_map/ppermute | solution.py:430
  659.4 16.6 %all-to-all-start.11 = ((bf16[8,432,128]{2,1,0:T(8,128)(2,1)}), bf16[8,432,128]{2,1,0:T(8,128)(2,1)S(1)}, u32[]{:S(2)}, u32[]{:S(2)}) async-start(bf16[8,432,128]{2,1,0:T(8,128)(2,1)} %pad_maximum_fusion.4), calls=%async_computation.13 | async-start | bytes 1769472 | tf_op jit(solution)/shard_map/all_to_all | solution.py:416
  663.8 14.1 %collective-permute-start.49 = (bf16[2,256,256]{2,1,0:T(8,128)(2,1)}, bf16[2,256,256]{2,1,0:T(8,128)(2,1)}, u32[]{:S(2)}, u32[]{:S(2)}) collective-permute-start(bf16[2,256,256]{2,1,0:T(8,128)(2,1)} %broadcast_select_fusion.6), channel_id=1, source_target_pairs={{0,16},{16,0},{1,17},{17,1},{2,18},{18,2},{3,19},{19,3},{4,20},{20... | collective-permute-start | bytes 786440 | tf_op jit(solution)/shard_map/ppermute | solution.py:493
  665.1 14.2 %collective-permute-start.44 = (bf16[768,256]{1,0:T(8,128)(2,1)}, bf16[768,256]{1,0:T(8,128)(2,1)}, u32[]{:S(2)}, u32[]{:S(2)}) collective-permute-start(bf16[768,256]{1,0:T(8,128)(2,1)} %get-tuple-element.437), channel_id=1, source_target_pairs={{0,12},{4,8},{8,4},{12,0},{1,13},{5,9},{9,5},{13,1},{2,14},{6,10},... | collective-permute-start | bytes 1179656 | tf_op jit(solution)/shard_map/ppermute | solution.py:430
  666.6 42.9 %collective-permute-start.43 = (bf16[768,256]{1,0:T(8,128)(2,1)}, bf16[768,256]{1,0:T(8,128)(2,1)}, u32[]{:S(2)}, u32[]{:S(2)}) collective-permute-start(bf16[768,256]{1,0:T(8,128)(2,1)} %get-tuple-element.438), channel_id=1, source_target_pairs={{0,8},{4,12},{8,0},{12,4},{1,9},{5,13},{9,1},{13,5},{2,10},{6,14},... | collective-permute-start | bytes 1179656 | tf_op jit(solution)/shard_map/ppermute | solution.py:430
  666.6 42.9 %collective-permute-start.42 = (bf16[768,256]{1,0:T(8,128)(2,1)S(1)}, bf16[768,256]{1,0:T(8,128)(2,1)}, u32[]{:S(2)}, u32[]{:S(2)}) collective-permute-start(bf16[768,256]{1,0:T(8,128)(2,1)S(1)} %get-tuple-element.439), channel_id=1, source_target_pairs={{0,4},{4,0},{8,12},{12,8},{1,5},{5,1},{9,13},{13,9},{2,6},{6,2},{1... | collective-permute-start | bytes 1179656 | tf_op jit(solution)/shard_map/ppermute | solution.py:430
  676.3 33.1 %collective-permute-start.47 = (bf16[780,128]{1,0:T(8,128)(2,1)S(1)}, bf16[780,128]{1,0:T(8,128)(2,1)S(1)}, u32[]{:S(2)}, u32[]{:S(2)}) collective-permute-start(bf16[780,128]{1,0:T(8,128)(2,1)S(1)} %get-tuple-element.467), channel_id=1, source_target_pairs={{0,12},{4,8},{8,4},{12,0},{1,13},{5,9},{9,5},{13,1},{2,14},{6,10},... | collective-permute-start | bytes 599048 | tf_op jit(solution)/shard_map/ppermute | solution.py:430
  677.8 39.3 %collective-permute-start.46 = (bf16[780,128]{1,0:T(8,128)(2,1)S(1)}, bf16[780,128]{1,0:T(8,128)(2,1)S(1)}, u32[]{:S(2)}, u32[]{:S(2)}) collective-permute-start(bf16[780,128]{1,0:T(8,128)(2,1)S(1)} %get-tuple-element.468), channel_id=1, source_target_pairs={{0,8},{4,12},{8,0},{12,4},{1,9},{5,13},{9,1},{13,5},{2,10},{6,14},... | collective-permute-start | bytes 599048 | tf_op jit(solution)/shard_map/ppermute | solution.py:430
  679.4 37.7 %collective-permute-start.45 = (bf16[780,128]{1,0:T(8,128)(2,1)S(1)}, bf16[780,128]{1,0:T(8,128)(2,1)S(1)}, u32[]{:S(2)}, u32[]{:S(2)}) collective-permute-start(bf16[780,128]{1,0:T(8,128)(2,1)S(1)} %get-tuple-element.469), channel_id=1, source_target_pairs={{0,4},{4,0},{8,12},{12,8},{1,5},{5,1},{9,13},{13,9},{2,6},{6,2},{1... | collective-permute-start | bytes 599048 | tf_op jit(solution)/shard_map/ppermute | solution.py:430
  (76 other events, 739.6 us)
Sparse Core Ops, SparseCore 0:
  88.5 191.7 all-gather.2
  330.5 59.4 reduce-scatter.2
  393.9 124.0 reduce-scatter.4

commit v6 on v4

--- a/solution.py
+++ b/solution.py
@@ -1232,21 +1232,24 @@
             gfv_a.reshape(side, length, lanes), gfv_other.reshape(side, length, lanes)
         )
         gout = exchange_line(jnp.sum(gout.astype(F32), axis=0).astype(BF16))
-        do_mine, main_sum, grads_b, gout = after(do_mine, main_sum, grads_b, gout)
+        do_mine, main_sum, gout = after(do_mine, main_sum, gout)
         main_sum = exchange(main_sum, "ffn")
+        dn_s, dn_t, gw_s, gfv_s = back_of(2, (do_mine, do_got))
+        grads_b, dn_s, dn_t, gw_s, gfv_s = after(grads_b, dn_s, dn_t, gw_s, gfv_s)
         grads_b, b_got = send_line(grads_b)
-        dn_s, dn_t, gw_s, gfv_s = back_of(2, (do_mine, do_got))
-        b_got, dn_s, dn_t, gw_s, gfv_s = after(b_got, dn_s, dn_t, gw_s, gfv_s)
         dn_t = swap(dn_t)
+        shared_sum, main_sum, b_got[0], b_got[1] = after(
+            add_low(dn_s, dn_t), main_sum, b_got[0], b_got[1]
+        )
+        shared_sum = exchange(shared_sum, "ffn")
         tokm, gain_main = last(0, x, dh, main_sum, gains[0])
-        shared_sum, tokm, gfv_s, gw_s = after(add_low(dn_s, dn_t), tokm, gfv_s, gw_s)
-        shared_sum = exchange(shared_sum, "ffn")
+        tokm, b_got[2], gfv_s, gw_s, gfv_main, shared_sum = after(
+            tokm, b_got[2], gfv_s, gw_s, gfv_main, shared_sum
+        )
         tokm, tokm_got = send_line(tokm)
         gfv_mine, gfv_theirs = by_core(gfv_s)
         gfv = lane_join(gfv_mine, swap(gfv_theirs))
-        gfv = jnp.concatenate([gfv_main, gfv], axis=1)
-        gfv, shared_sum, tokm_got = after(gfv, shared_sum, tokm_got)
-        gfv = exchange(gfv, "ffn")
+        gfv = exchange(jnp.concatenate([gfv_main, gfv], axis=1), "ffn")
         toks, gain_shared = last(length, x, dh, shared_sum, gains[0])
         grad_w = (gw_a + gw_b + gw_s).astype(BF16)
         grad_w = grad_w.reshape(3, lanes, group, deep).transpose(2, 0, 3, 1)
@@ -1256,6 +1259,7 @@
         tail = jnp.concatenate(in_pieces(gain_both), axis=0)
         tail = jnp.broadcast_to(tail[None], (group,) + tail.shape)
         grad_w = jnp.concatenate([grad_w, tail], axis=1)
+        toks, tokm_got = after(toks, tokm_got)
         toks, toks_got = send_line(toks)
         grad_w, gfv = after(grad_w, gfv)
         grad_w = exchange(grad_w, layer)

time: 739 us -> 733 us (level)
  local copies, waits for them, and re-layouts: 90.3 us -> 81 us
    ppermute x30, starting transfers between devices: 58.6 us -> 66.2 us  [line_go(): lax.ppermute(send, axis, [(j, j ^ step + 1) for j in range(count)])]
    unnamed x148 -> x156, local copies, waits for them, and re-layouts: 24.4 us -> 24.4 us
  transfers between devices with their start and end apart: 66 -> 66, of which waited for: 24 -> 27; matrix products, arithmetic and copies ran while one was open for 15% -> 13% of each run, Pallas kernels for 28% -> 29%
where the time goes in v6:
time: 733 us; the launch traced here: 724 us
  Pallas kernels  243 us (33%)
  waiting for transfers between devices  202 us (28%)
  starting transfers between devices  130 us (18%)
  local copies, waits for them, and re-layouts  81 us (11%)
  other arithmetic  52.4 us (7%)
  between operations  15.5 us (2%)
    all_to_all x12, waiting for transfers between devices, exchange(): return lax.all_to_all(blocks, axes, 0, 0, tiled=True)  127 us
    pallas_call x3, Pallas kernels, attend_back(): pl.pallas_call(functools.partial(attend_back_kernel, count), grid=(1,), o...  87.3 us
    ppermute x30, starting transfers between devices, line_go(): lax.ppermute(send, axis, [(j, j ^ step + 1) for j in range(count)])  66.2 us
    pallas_call x2, Pallas kernels, feed_forward(): pl.pallas_call(functools.partial(mlp_kernel, begin_tile, real, out_rows,...  61.5 us
    pallas_call x3, Pallas kernels, attend(): pl.pallas_call(functools.partial(attend_kernel, count), grid=(1,), out_sh...  58.4 us
    ppermute x30, waiting for transfers between devices, line_go(): lax.ppermute(send, axis, [(j, j ^ step + 1) for j in range(count)])  57.4 us
    all_to_all x12, starting transfers between devices, exchange(): return lax.all_to_all(blocks, axes, 0, 0, tiled=True)  53.6 us
    unnamed x156, local copies, waits for them, and re-layouts  24.4 us
  transfers between devices with their start and end apart: 66, of which 27 were waited for; matrix products, arithmetic and copies ran while one was open for 13% of the time, Pallas kernels for 29%

profile of v6, /device:TPU:0, one launch (start us, length us, event | category | flops | bytes accessed | tf_op | source)
XLA Modules:
  0.0 723.9 jit_solution(10636422886022946654)
XLA Ops:
  14.9 6.3 all-to-all-start
  22.0 4.0 fusion.1
  27.9 2.6 pad_maximum_fusion.2
  37.5 3.8 collective-permute-start.3
  45.3 13.6 %all-to-all-done = bf16[4,784,128]{2,1,0:T(8,128)(2,1)} async-done(((bf16[4,784,128]{2,1,0:T(8,128)(2,1)}), bf16[4,784,128]{2,1,0:T(8,128)(2,1)}, u32[]{:S(2)}, u32[]{:S(2)}) %all-to-all-start) | async-done | bytes 802848 | tf_op jit(solution)/shard_map/all_to_all | solution.py:416
  61.0 4.2 all-to-all-start.1
  68.2 9.1 %all-to-all-done.1 = bf16[8,3,128,128]{3,2,1,0:T(8,128)(2,1)} async-done(((bf16[8,3,128,128]{3,2,1,0:T(8,128)(2,1)}), bf16[8,3,128,128]{3,2,1,0:T(8,128)(2,1)}, u32[]{:S(2)}, u32[]{:S(2)}) %all-to-all-start.1) | async-done | bytes 786464 | tf_op jit(solution)/shard_map/all_to_all | solution.py:416
  85.0 3.3 shard_map.169
  88.3 4.9 all-to-all-start.2
  95.4 2.5 collective-permute-start.7
  97.9 4.5 collective-permute-start.6
  104.7 61.6 %all-to-all-done.2.refs_0_ = bf16[4,512,1024]{2,1,0:T(8,128)(2,1)} async-done(((bf16[4,512,1024]{2,1,0:T(8,128)(2,1)}), bf16[4,512,1024]{2,1,0:T(8,128)(2,1)}, u32[]{:S(2)}, u32[]{:S(2)}) %all-to-all-start.2) | async-done | bytes 4194336 | tf_op jit(solution)/shard_map/all_to_all | solution.py:416
  166.3 2.9 collective-permute-done.9
  171.4 4.9 all-to-all-start.3
  177.4 4.0 fusion
  182.7 18.5 %shard_map.170 = (bf16[2048,128]{1,0:T(8,128)(2,1)S(1)}, bf16[2048,128]{1,0:T(8,128)(2,1)S(1)}, bf16[2048,128]{1,0:T(8,128)(2,1)S(1)}, bf16[2048,128]{1,0:T(8,128)(2,1)S(1)}, f32[2048,128]{1,0:T(8,128)S(1)}) custom-call(s32[1]{0:T(128)} %bitcast.side_ref, s32[4]{0:T(128)S(1)} %get-tuple-element.521.low_ref, bf16[4,512,1024]{2,1,0:T(8,128)(2,1)} %all-to-all-done.2.refs_0_, ...), custom_call_target="tpu_custom_call" | custom-call | tf_op jit(solution)/shard_map/pallas_call | solution.py:620
  207.0 4.8 collective-permute-done.14.refs_1_.refs_3_
  211.8 18.4 %shard_map.171 = (bf16[2048,128]{1,0:T(8,128)(2,1)S(1)}, bf16[2048,128]{1,0:T(8,128)(2,1)S(1)}, bf16[2048,128]{1,0:T(8,128)(2,1)S(1)}, bf16[2048,128]{1,0:T(8,128)(2,1)S(1)}, f32[2048,128]{1,0:T(8,128)S(1)}) custom-call(s32[1]{0:T(128)} %bitcast.side_ref, s32[4]{0:T(128)S(1)} %get-tuple-element.520.low_ref, ...), custom_call_target="tpu_custom_call" | custom-call | tf_op jit(solution)/shard_map/pallas_call | solution.py:620
  233.6 8.0 %collective-permute-done.13 = bf16[768,256]{1,0:T(8,128)(2,1)} collective-permute-done((bf16[768,256]{1,0:T(8,128)(2,1)}, bf16[768,256]{1,0:T(8,128)(2,1)}, u32[]{:S(2)}, u32[]{:S(2)}) %collective-permute-start.13) | collective-permute-done | bytes 393248 | tf_op jit(solution)/shard_map/ppermute | solution.py:430
  244.9 4.5 all-to-all-start.4
  250.8 21.5 %shard_map.172 = (bf16[2048,128]{1,0:T(8,128)(2,1)S(1)}, bf16[2048,128]{1,0:T(8,128)(2,1)S(1)}, bf16[2048,128]{1,0:T(8,128)(2,1)S(1)}, bf16[2048,128]{1,0:T(8,128)(2,1)S(1)}, f32[2048,128]{1,0:T(8,128)S(1)}) custom-call(s32[1]{0:T(128)} %bitcast.side_ref, s32[4]{0:T(128)S(1)} %get-tuple-element.519.low_ref, bf16[4,256,1024]{2,1,0:T(8,128)(2,1)} %all-to-all-done.3.refs_0_, ...), custom_call_target="tpu_custom_call" | custom-call | tf_op jit(solution)/shard_map/pallas_call | solution.py:620
  274.8 6.2 collective-permute-done.16
  283.6 3.5 all-to-all-start.5
  289.1 6.6 all-to-all-done.5.os_ref
  296.5 7.4 %shard_map.173 = (f32[768,1024]{1,0:T(8,128)}, bf16[768,1024]{1,0:T(8,128)(2,1)}, bf16[768,1024]{1,0:T(8,128)(2,1)}) custom-call(bf16[4,512,256]{2,1,0:T(8,128)(2,1)} %all-to-all-done.4.om_ref, bf16[4,256,256]{2,1,0:T(8,128)(2,1)} %copy-done.44, bf16[4,768,256]{2,1,0:T(8,128)(2,1)} %copy-done, bf16[8,4,2496,128]{3,2,1,0:T(8,128)(2,1)} %bitcast.251, ...), custom_call_target="tpu_custom_call" | custom-call | tf_op jit(solution)/shard_map/pallas_call | solution.py:1093
  307.2 22.8 %shard_map.174 = (f32[768,1024]{1,0:T(8,128)}, f32[768,1024]{1,0:T(8,128)}, bf16[8,4,704,128]{3,2,1,0:T(8,128)(2,1)}) custom-call(bf16[768,1024]{1,0:T(8,128)(2,1)} %get-tuple-element.280.n_ref, bf16[4,768,256]{2,1,0:T(8,128)(2,1)} %copy-done.26, bf16[8,4,2496,128]{3,2,1,0:T(8,128)(2,1)} %bitcast.252), custom_call_target="tpu_custom_call" | custom-call | tf_op jit(solution)/shard_map/pallas_call | solution.py:1113
  330.3 38.7 %shard_map.175 = (f32[768,1024]{1,0:T(8,128)}, f32[768,1024]{1,0:T(8,128)}, bf16[8,4,1536,128]{3,2,1,0:T(8,128)(2,1)}) custom-call(bf16[768,1024]{1,0:T(8,128)(2,1)} %get-tuple-element.280.n_ref, bf16[4,768,256]{2,1,0:T(8,128)(2,1)} %copy-done.26, bf16[8,4,2496,128]{3,2,1,0:T(8,128)(2,1)} %bitcast.253), custom_call_target="tpu_custom_call" | custom-call | tf_op jit(solution)/shard_map/pallas_call | solution.py:1113
  369.0 12.6 %shard_map.176 = (bf16[4,768,256]{2,1,0:T(8,128)(2,1)}, f32[768,1024]{1,0:T(8,128)}, bf16[4,768,256]{2,1,0:T(8,128)(2,1)}, bf16[768,1024]{1,0:T(8,128)(2,1)}, f32[1,1024]{1,0:T(1,128)}) custom-call(f32[768,1024]{1,0:T(8,128)} %get-tuple-element.265.h_ref, f32[768,1024]{1,0:T(8,128)} %get-tuple-element.279.ya_ref, f32[768,1024]{1,0:T(8,128)} %get-tuple-element.281.yb_ref, ...), custom_call_target="tpu_custom_call" | custom-call | tf_op jit(solution)/shard_map/pallas_call | solution.py:1155
  381.6 4.9 all-to-all-start.6
  386.5 3.2 shard_map.177
  389.7 15.9 %all-to-all-done.6 = bf16[4,768,256]{2,1,0:T(8,128)(2,1)} async-done(((bf16[4,768,256]{2,1,0:T(8,128)(2,1)}), bf16[4,768,256]{2,1,0:T(8,128)(2,1)}, u32[]{:S(2)}, u32[]{:S(2)}) %all-to-all-start.6) | async-done | bytes 1572896 | tf_op jit(solution)/shard_map/all_to_all | solution.py:416
  408.1 2.8 collective-permute-start.21
  412.8 29.7 %shard_map.178 = (bf16[4,512,1024]{2,1,0:T(8,128)(2,1)}, f32[384,1024]{1,0:T(8,128)}, bf16[2048,128]{1,0:T(8,128)(2,1)}) custom-call(s32[1]{0:T(128)} %bitcast.side_ref, s32[4]{0:T(128)} %copy-done.22, bf16[4,512,1024]{2,1,0:T(8,128)(2,1)} %collective-permute-done.11.refs_0_, bf16[4,768,128]{2,1,0:T(8,128)(2,1)} %copy-done.41, bf16[1024,384]{1,0:T(8,128)(2,1)} %copy-done.1, ...), custom_call_target="tpu_custom_call" | custom-call | tf_op jit(solution)/shard_map/pallas_call | solution.py:711
  443.9 3.7 all-to-all-start.7
  447.7 2.7 collective-permute-start.26
  452.4 4.1 collective-permute-start.24
  456.4 26.8 %shard_map.179 = (bf16[4,512,1024]{2,1,0:T(8,128)(2,1)}, f32[384,1024]{1,0:T(8,128)}, bf16[2048,128]{1,0:T(8,128)(2,1)}) custom-call(s32[1]{0:T(128)} %bitcast.side_ref, s32[4]{0:T(128)} %copy-done.21, bf16[4,512,1024]{2,1,0:T(8,128)(2,1)} %all-to-all-done.2.refs_0_, bf16[4,768,128]{2,1,0:T(8,128)(2,1)} %get-tuple-element.324.refs_1_.refs_2_, ...), custom_call_target="tpu_custom_call" | custom-call | tf_op jit(solution)/shard_map/pallas_call | solution.py:711
  483.3 7.8 %all-to-all-done.7 = bf16[8,4,256,128]{3,2,1,0:T(8,128)(2,1)S(1)} async-done(((bf16[8,4,256,128]{3,2,1,0:T(8,128)(2,1)}), bf16[8,4,256,128]{3,2,1,0:T(8,128)(2,1)S(1)}, u32[]{:S(2)}, u32[]{:S(2)}) %all-to-all-start.7) | async-done | bytes 2097184 | tf_op jit(solution)/shard_map/all_to_all | solution.py:416
  491.4 3.4 collective-permute-start.29
  495.9 8.7 %add_convert_fusion = bf16[4,512,1024]{2,1,0:T(8,128)(2,1)} fusion(bf16[4,512,1024]{2,1,0:T(8,128)(2,1)} %collective-permute-done.22, bf16[4,512,1024]{2,1,0:T(8,128)(2,1)} %get-tuple-element.318), kind=kLoop, calls=%fused_computation | loop fusion | flops 8388608 | bytes 12582912 | tf_op jit(solution)/shard_map/convert_element_type | solution.py:1227
  504.7 4.8 all-to-all-start.8
  509.5 30.8 %shard_map.180 = (bf16[4,256,1024]{2,1,0:T(8,128)(2,1)}, bf16[4,256,1024]{2,1,0:T(8,128)(2,1)}, f32[384,1024]{1,0:T(8,128)}, bf16[2048,128]{1,0:T(8,128)(2,1)}) custom-call(s32[1]{0:T(128)} %bitcast.side_ref, s32[4]{0:T(128)} %copy-done.23, bf16[4,256,1024]{2,1,0:T(8,128)(2,1)} %all-to-all-done.3.refs_0_, ...), custom_call_target="tpu_custom_call" | custom-call | tf_op jit(solution)/shard_map/pallas_call | solution.py:711
  540.3 4.7 reduce-scatter.5.cloned.1.call-done
  548.8 3.1 collective-permute-start.32
  553.9 2.4 add_convert_fusion.1
  556.3 4.9 all-to-all-done.8.parts_ref
  561.3 8.5 %collective-permute-done.32 = bf16[1536,128]{1,0:T(8,128)(2,1)S(1)} collective-permute-done((bf16[1536,128]{1,0:T(8,128)(2,1)S(1)}, bf16[1536,128]{1,0:T(8,128)(2,1)S(1)}, u32[]{:S(2)}, u32[]{:S(2)}) %collective-permute-start.32) | collective-permute-done | bytes 393248 | tf_op jit(solution)/shard_map/ppermute | solution.py:430
  570.6 3.9 all-to-all-start.9
  583.1 2.9 maximum_select_fusion.3
  586.7 3.0 collective-permute-start.33
  591.0 5.5 shard_map.181
  596.5 3.6 collective-permute-done.33
  601.5 3.7 shard_map.182
  610.4 3.0 collective-permute-start.38
  613.4 6.6 collective-permute-start.37
  624.1 4.2 all-to-all-start.10
  631.2 7.0 collective-permute-done.37
  638.9 2.9 collective-permute-start.41
  647.6 3.8 all-to-all-start.11
  658.7 5.8 all-to-all-done.11
  664.8 2.9 collective-permute-start.47
  668.5 15.7 %collective-permute-start.45 = (bf16[780,128]{1,0:T(8,128)(2,1)S(1)}, bf16[780,128]{1,0:T(8,128)(2,1)S(1)}, u32[]{:S(2)}, u32[]{:S(2)}) collective-permute-start(bf16[780,128]{1,0:T(8,128)(2,1)S(1)} %get-tuple-element.461), channel_id=1, source_target_pairs={{0,4},{4,0},{8,12},{12,8},{1,5},{5,1},{9,13},{13,9},{2,6},{6,2},{1... | collective-permute-start | bytes 599048 | tf_op jit(solution)/shard_map/ppermute | solution.py:430
  686.5 14.3 %collective-permute-done.43 = bf16[768,256]{1,0:T(8,128)(2,1)} collective-permute-done((bf16[768,256]{1,0:T(8,128)(2,1)}, bf16[768,256]{1,0:T(8,128)(2,1)}, u32[]{:S(2)}, u32[]{:S(2)}) %collective-permute-start.43) | collective-permute-done | bytes 393248 | tf_op jit(solution)/shard_map/ppermute | solution.py:430
  700.7 7.9 %collective-permute-done.46 = bf16[780,128]{1,0:T(8,128)(2,1)S(1)} collective-permute-done((bf16[780,128]{1,0:T(8,128)(2,1)S(1)}, bf16[780,128]{1,0:T(8,128)(2,1)S(1)}, u32[]{:S(2)}, u32[]{:S(2)}) %collective-permute-start.46) | collective-permute-done | bytes 199712 | tf_op jit(solution)/shard_map/ppermute | solution.py:430
  (398 shorter events, 133.3 us)
Async XLA Ops:
  7.2 26.0 %collective-permute-start.4 = (s32[6,2048]{1,0:T(8,128)}, s32[6,2048]{1,0:T(8,128)}, u32[]{:S(2)}, u32[]{:S(2)}) collective-permute-start(s32[6,2048]{1,0:T(8,128)} %param.12), channel_id=1, source_target_pairs={{0,16},{16,0},{1,17},{17,1},{2,18},{18,2},{3,19},{19,3},{4,20},{20... | collective-permute-start | bytes 147464 | tf_op jit(solution)/shard_map/ppermute | solution.py:493
  9.4 32.4 %collective-permute-start.10 = (bf16[2,256,256]{2,1,0:T(8,128)(2,1)}, bf16[2,256,256]{2,1,0:T(8,128)(2,1)}, u32[]{:S(2)}, u32[]{:S(2)}) collective-permute-start(bf16[2,256,256]{2,1,0:T(8,128)(2,1)} %constant_dynamic-slice_fusion.4), channel_id=1, source_target_pairs={{0,16},{16,0},{1,17},{17,1},{2,18},{18,2},{3,19},{19,3},{4,20},{20... | collective-permute-start | bytes 786440 | tf_op jit(solution)/shard_map/ppermute | solution.py:493
  11.1 30.7 %collective-permute-start.5 = (bf16[2,256,256]{2,1,0:T(8,128)(2,1)}, bf16[2,256,256]{2,1,0:T(8,128)(2,1)}, u32[]{:S(2)}, u32[]{:S(2)}) collective-permute-start(bf16[2,256,256]{2,1,0:T(8,128)(2,1)} %constant_dynamic-slice_fusion.5), channel_id=1, source_target_pairs={{0,16},{16,0},{1,17},{17,1},{2,18},{18,2},{3,19},{19,3},{4,20},{20... | collective-permute-start | bytes 786440 | tf_op jit(solution)/shard_map/ppermute | solution.py:493
  13.3 21.8 %collective-permute-start = (bf16[2,256,256]{2,1,0:T(8,128)(2,1)}, bf16[2,256,256]{2,1,0:T(8,128)(2,1)}, u32[]{:S(2)}, u32[]{:S(2)}) collective-permute-start(bf16[2,256,256]{2,1,0:T(8,128)(2,1)} %constant_dynamic-slice_fusion.10), channel_id=1, source_target_pairs={{0,16},{16,0},{1,17},{17,1},{2,18},{18,2},{3,19},{19,3},{4,20},{20... | collective-permute-start | bytes 786440 | tf_op jit(solution)/shard_map/ppermute | solution.py:493
  14.9 44.0 %all-to-all-start = ((bf16[4,784,128]{2,1,0:T(8,128)(2,1)}), bf16[4,784,128]{2,1,0:T(8,128)(2,1)}, u32[]{:S(2)}, u32[]{:S(2)}) async-start(bf16[4,784,128]{2,1,0:T(8,128)(2,1)} %broadcast_in_dim.131), calls=%async_computation | async-start | bytes 1605632 | tf_op jit(solution)/shard_map/all_to_all | solution.py:416
  37.5 44.4 %collective-permute-start.3 = (bf16[768,256]{1,0:T(8,128)(2,1)}, bf16[768,256]{1,0:T(8,128)(2,1)}, u32[]{:S(2)}, u32[]{:S(2)}) collective-permute-start(bf16[768,256]{1,0:T(8,128)(2,1)} %get-tuple-element.449), channel_id=1, source_target_pairs={{0,12},{4,8},{8,4},{12,0},{1,13},{5,9},{9,5},{13,1},{2,14},{6,10},... | collective-permute-start | bytes 1179656 | tf_op jit(solution)/shard_map/ppermute | solution.py:430
  41.3 40.6 %collective-permute-start.2 = (bf16[768,256]{1,0:T(8,128)(2,1)}, bf16[768,256]{1,0:T(8,128)(2,1)}, u32[]{:S(2)}, u32[]{:S(2)}) collective-permute-start(bf16[768,256]{1,0:T(8,128)(2,1)} %get-tuple-element.450), channel_id=1, source_target_pairs={{0,8},{4,12},{8,0},{12,4},{1,9},{5,13},{9,1},{13,5},{2,10},{6,14},... | collective-permute-start | bytes 1179656 | tf_op jit(solution)/shard_map/ppermute | solution.py:430
  41.3 40.6 %collective-permute-start.1 = (bf16[768,256]{1,0:T(8,128)(2,1)}, bf16[768,256]{1,0:T(8,128)(2,1)}, u32[]{:S(2)}, u32[]{:S(2)}) collective-permute-start(bf16[768,256]{1,0:T(8,128)(2,1)} %get-tuple-element.451), channel_id=1, source_target_pairs={{0,4},{4,0},{8,12},{12,8},{1,5},{5,1},{9,13},{13,9},{2,6},{6,2},{1... | collective-permute-start | bytes 1179656 | tf_op jit(solution)/shard_map/ppermute | solution.py:430
  61.0 16.3 %all-to-all-start.1 = ((bf16[8,3,128,128]{3,2,1,0:T(8,128)(2,1)}), bf16[8,3,128,128]{3,2,1,0:T(8,128)(2,1)}, u32[]{:S(2)}, u32[]{:S(2)}) async-start(bf16[8,3,128,128]{3,2,1,0:T(8,128)(2,1)} %bitcast.11), calls=%async_computation.1 | async-start | bytes 1572864 | tf_op jit(solution)/shard_map/all_to_all | solution.py:416
  65.2 230.4 %all-gather.3.cloned.1.call-start = ((), (), s32[]{:S(2)}) async-start(), calls=%async_computation.16 | async-start | bytes 21086208 | tf_op jit(solution)/shard_map/all_gather | solution.py:1017
  88.3 77.9 %all-to-all-start.2 = ((bf16[4,512,1024]{2,1,0:T(8,128)(2,1)}), bf16[4,512,1024]{2,1,0:T(8,128)(2,1)}, u32[]{:S(2)}, u32[]{:S(2)}) async-start(bf16[4,512,1024]{2,1,0:T(8,128)(2,1)} %get-tuple-element.218), calls=%async_computation.2 | async-start | bytes 8388608 | tf_op jit(solution)/shard_map/all_to_all | solution.py:416
  95.4 73.8 %collective-permute-start.9 = (bf16[768,256]{1,0:T(8,128)(2,1)}, bf16[768,256]{1,0:T(8,128)(2,1)S(1)}, u32[]{:S(2)}, u32[]{:S(2)}) collective-permute-start(bf16[768,256]{1,0:T(8,128)(2,1)} %get-tuple-element.445), channel_id=1, source_target_pairs={{0,12},{1,8},{2,4},{3,0},{4,13},{5,9},{6,5},{7,1},{8,14},{9,10},{1... | collective-permute-start | bytes 1179656 | tf_op jit(solution)/shard_map/ppermute | solution.py:465
  95.4 73.8 %collective-permute-start.8 = (bf16[768,256]{1,0:T(8,128)(2,1)}, bf16[768,256]{1,0:T(8,128)(2,1)S(1)}, u32[]{:S(2)}, u32[]{:S(2)}) collective-permute-start(bf16[768,256]{1,0:T(8,128)(2,1)} %get-tuple-element.446), channel_id=1, source_target_pairs={{0,8},{1,12},{2,0},{3,4},{4,9},{5,13},{6,1},{7,5},{8,10},{9,14},{1... | collective-permute-start | bytes 1179656 | tf_op jit(solution)/shard_map/ppermute | solution.py:465
  95.4 75.3 %collective-permute-start.7 = (bf16[768,256]{1,0:T(8,128)(2,1)}, bf16[768,256]{1,0:T(8,128)(2,1)S(1)}, u32[]{:S(2)}, u32[]{:S(2)}) collective-permute-start(bf16[768,256]{1,0:T(8,128)(2,1)} %get-tuple-element.447), channel_id=1, source_target_pairs={{0,4},{1,0},{2,12},{3,8},{4,5},{5,1},{6,13},{7,9},{8,6},{9,2},{10,... | collective-permute-start | bytes 1179656 | tf_op jit(solution)/shard_map/ppermute | solution.py:465
  97.9 72.8 %collective-permute-start.6 = (bf16[768,256]{1,0:T(8,128)(2,1)}, bf16[768,256]{1,0:T(8,128)(2,1)}, u32[]{:S(2)}, u32[]{:S(2)}) collective-permute-start(bf16[768,256]{1,0:T(8,128)(2,1)} %get-tuple-element.448), channel_id=1, source_target_pairs={{0,0},{1,4},{2,8},{3,12},{4,1},{5,5},{6,9},{7,13},{8,2},{9,6},{10,... | collective-permute-start | bytes 1179656 | tf_op jit(solution)/shard_map/ppermute | solution.py:465
  170.7 35.4 %collective-permute-start.11 = (bf16[4,512,1024]{2,1,0:T(8,128)(2,1)}, bf16[4,512,1024]{2,1,0:T(8,128)(2,1)}, u32[]{:S(2)}, u32[]{:S(2)}) collective-permute-start(bf16[4,512,1024]{2,1,0:T(8,128)(2,1)} %all-to-all-done.2.refs_0_), channel_id=1, source_target_pairs={{0,16},{16,0},{1,17},{17,1},{2,18},{18,2},{3,19},{19,3},{4,20},{20... | collective-permute-start | bytes 12582920 | tf_op jit(solution)/shard_map/ppermute | solution.py:493
  171.4 34.7 %all-to-all-start.3 = ((bf16[4,256,1024]{2,1,0:T(8,128)(2,1)}), bf16[4,256,1024]{2,1,0:T(8,128)(2,1)}, u32[]{:S(2)}, u32[]{:S(2)}) async-start(bf16[4,256,1024]{2,1,0:T(8,128)(2,1)} %get-tuple-element.221), calls=%async_computation.3 | async-start | bytes 4194304 | tf_op jit(solution)/shard_map/all_to_all | solution.py:416
  206.1 35.5 %collective-permute-start.12 = (bf16[4,256,1024]{2,1,0:T(8,128)(2,1)}, bf16[4,256,1024]{2,1,0:T(8,128)(2,1)}, u32[]{:S(2)}, u32[]{:S(2)}) collective-permute-start(bf16[4,256,1024]{2,1,0:T(8,128)(2,1)} %all-to-all-done.3.refs_0_), channel_id=1, source_target_pairs={{0,16},{16,0},{1,17},{17,1},{2,18},{18,2},{3,19},{19,3},{4,20},{20... | collective-permute-start | bytes 6291464 | tf_op jit(solution)/shard_map/ppermute | solution.py:493
  206.1 5.7 collective-permute-start.14
  206.7 35.0 %collective-permute-start.13 = (bf16[768,256]{1,0:T(8,128)(2,1)}, bf16[768,256]{1,0:T(8,128)(2,1)}, u32[]{:S(2)}, u32[]{:S(2)}) collective-permute-start(bf16[768,256]{1,0:T(8,128)(2,1)} %get-tuple-element.242), channel_id=1, source_target_pairs={{0,4},{4,0},{8,12},{12,8},{1,5},{5,1},{9,13},{13,9},{2,6},{6,2},{1... | collective-permute-start | bytes 1179656 | tf_op jit(solution)/shard_map/ppermute | solution.py:430
  241.6 1.9 collective-permute-start.15
  244.9 36.1 %all-to-all-start.4 = ((bf16[4,512,256]{2,1,0:T(8,128)(2,1)}), bf16[4,512,256]{2,1,0:T(8,128)(2,1)}, u32[]{:S(2)}, u32[]{:S(2)}) async-start(bf16[4,512,256]{2,1,0:T(8,128)(2,1)} %maximum_select_fusion.2), calls=%async_computation.4 | async-start | bytes 2097152 | tf_op jit(solution)/shard_map/all_to_all | solution.py:416
  249.3 31.7 %collective-permute-start.16 = (bf16[768,256]{1,0:T(8,128)(2,1)}, bf16[768,256]{1,0:T(8,128)(2,1)}, u32[]{:S(2)}, u32[]{:S(2)}) collective-permute-start(bf16[768,256]{1,0:T(8,128)(2,1)} %get-tuple-element.253), channel_id=1, source_target_pairs={{0,8},{4,12},{8,0},{12,4},{1,9},{5,13},{9,1},{13,5},{2,10},{6,14},... | collective-permute-start | bytes 1179656 | tf_op jit(solution)/shard_map/ppermute | solution.py:430
  283.6 12.0 %all-to-all-start.5 = ((bf16[4,256,256]{2,1,0:T(8,128)(2,1)}), bf16[4,256,256]{2,1,0:T(8,128)(2,1)S(1)}, u32[]{:S(2)}, u32[]{:S(2)}) async-start(bf16[4,256,256]{2,1,0:T(8,128)(2,1)} %maximum_select_fusion.4), calls=%async_computation.5 | async-start | bytes 1048576 | tf_op jit(solution)/shard_map/all_to_all | solution.py:416
  287.1 156.8 %reduce-scatter.3.cloned.1.call-start = ((), (), s32[]{:S(2)}) async-start(), calls=%async_computation.14 | async-start | bytes 6488064 | tf_op jit(solution)/shard_map/reduce_scatter | solution.py:1150
  287.6 16.4 %collective-permute-start.18 = (bf16[768,256]{1,0:T(8,128)(2,1)S(1)}, bf16[768,256]{1,0:T(8,128)(2,1)S(1)}, u32[]{:S(2)}, u32[]{:S(2)}) collective-permute-start(bf16[768,256]{1,0:T(8,128)(2,1)S(1)} %copy-done.54), channel_id=1, source_target_pairs={{0,12},{4,8},{8,4},{12,0},{1,13},{5,9},{9,5},{13,1},{2,14},{6,10},... | collective-permute-start | bytes 1179656 | tf_op jit(solution)/shard_map/ppermute | solution.py:430
  330.0 214.9 %reduce-scatter.5.cloned.1.call-start = ((), (), s32[]{:S(2)}) async-start(), calls=%async_computation.15 | async-start | bytes 14155776 | tf_op jit(solution)/shard_map/reduce_scatter | solution.py:1150
  381.6 24.0 %all-to-all-start.6 = ((bf16[4,768,256]{2,1,0:T(8,128)(2,1)}), bf16[4,768,256]{2,1,0:T(8,128)(2,1)}, u32[]{:S(2)}, u32[]{:S(2)}) async-start(bf16[4,768,256]{2,1,0:T(8,128)(2,1)} %get-tuple-element.286), calls=%async_computation.6 | async-start | bytes 3145728 | tf_op jit(solution)/shard_map/all_to_all | solution.py:416
  408.0 3.9 collective-permute-start.19
  408.1 34.4 %collective-permute-start.21 = (bf16[768,256]{1,0:T(8,128)(2,1)S(1)}, bf16[768,256]{1,0:T(8,128)(2,1)S(1)}, u32[]{:S(2)}, u32[]{:S(2)}) collective-permute-start(bf16[768,256]{1,0:T(8,128)(2,1)S(1)} %get-tuple-element.436), channel_id=1, source_target_pairs={{0,8},{4,12},{8,0},{12,4},{1,9},{5,13},{9,1},{13,5},{2,10},{6,14},... | collective-permute-start | bytes 1179656 | tf_op jit(solution)/shard_map/ppermute | solution.py:430
  410.8 31.6 %collective-permute-start.20 = (bf16[768,256]{1,0:T(8,128)(2,1)S(1)}, bf16[768,256]{1,0:T(8,128)(2,1)S(1)}, u32[]{:S(2)}, u32[]{:S(2)}) collective-permute-start(bf16[768,256]{1,0:T(8,128)(2,1)S(1)} %get-tuple-element.437), channel_id=1, source_target_pairs={{0,4},{4,0},{8,12},{12,8},{1,5},{5,1},{9,13},{13,9},{2,6},{6,2},{1... | collective-permute-start | bytes 1179656 | tf_op jit(solution)/shard_map/ppermute | solution.py:430
  443.9 47.1 %collective-permute-start.22 = (bf16[4,512,1024]{2,1,0:T(8,128)(2,1)}, bf16[4,512,1024]{2,1,0:T(8,128)(2,1)}, u32[]{:S(2)}, u32[]{:S(2)}) collective-permute-start(bf16[4,512,1024]{2,1,0:T(8,128)(2,1)} %get-tuple-element.311), channel_id=1, source_target_pairs={{0,16},{16,0},{1,17},{17,1},{2,18},{18,2},{3,19},{19,3},{4,20},{20... | collective-permute-start | bytes 12582920 | tf_op jit(solution)/shard_map/ppermute | solution.py:493
  443.9 47.1 %all-to-all-start.7 = ((bf16[8,4,256,128]{3,2,1,0:T(8,128)(2,1)}), bf16[8,4,256,128]{3,2,1,0:T(8,128)(2,1)S(1)}, u32[]{:S(2)}, u32[]{:S(2)}) async-start(bf16[8,4,256,128]{3,2,1,0:T(8,128)(2,1)} %shard_map.177), calls=%async_computation.8 | async-start | bytes 4194304 | tf_op jit(solution)/shard_map/all_to_all | solution.py:416
  447.7 35.6 %collective-permute-start.26 = (bf16[768,256]{1,0:T(8,128)(2,1)S(1)}, bf16[768,256]{1,0:T(8,128)(2,1)}, u32[]{:S(2)}, u32[]{:S(2)}) collective-permute-start(bf16[768,256]{1,0:T(8,128)(2,1)S(1)} %get-tuple-element.435), channel_id=1, source_target_pairs={{0,12},{4,8},{8,4},{12,0},{1,13},{5,9},{9,5},{13,1},{2,14},{6,10},... | collective-permute-start | bytes 1179656 | tf_op jit(solution)/shard_map/ppermute | solution.py:430
  451.2 39.8 %collective-permute-start.25 = (bf16[704,128]{1,0:T(8,128)(2,1)}, bf16[704,128]{1,0:T(8,128)(2,1)}, u32[]{:S(2)}, u32[]{:S(2)}) collective-permute-start(bf16[704,128]{1,0:T(8,128)(2,1)} %get-tuple-element.471), channel_id=1, source_target_pairs={{0,12},{4,8},{8,4},{12,0},{1,13},{5,9},{9,5},{13,1},{2,14},{6,10},... | collective-permute-start | bytes 540680 | tf_op jit(solution)/shard_map/ppermute | solution.py:430
  452.4 38.7 %collective-permute-start.24 = (bf16[704,128]{1,0:T(8,128)(2,1)}, bf16[704,128]{1,0:T(8,128)(2,1)}, u32[]{:S(2)}, u32[]{:S(2)}) collective-permute-start(bf16[704,128]{1,0:T(8,128)(2,1)} %get-tuple-element.472), channel_id=1, source_target_pairs={{0,8},{4,12},{8,0},{12,4},{1,9},{5,13},{9,1},{13,5},{2,10},{6,14},... | collective-permute-start | bytes 540680 | tf_op jit(solution)/shard_map/ppermute | solution.py:430
  456.4 34.6 %collective-permute-start.23 = (bf16[704,128]{1,0:T(8,128)(2,1)S(1)}, bf16[704,128]{1,0:T(8,128)(2,1)}, u32[]{:S(2)}, u32[]{:S(2)}) collective-permute-start(bf16[704,128]{1,0:T(8,128)(2,1)S(1)} %get-tuple-element.473), channel_id=1, source_target_pairs={{0,4},{4,0},{8,12},{12,8},{1,5},{5,1},{9,13},{13,9},{2,6},{6,2},{1... | collective-permute-start | bytes 540680 | tf_op jit(solution)/shard_map/ppermute | solution.py:430
  491.4 13.2 %collective-permute-start.29 = (bf16[256,128]{1,0:T(8,128)(2,1)S(1)}, bf16[256,128]{1,0:T(8,128)(2,1)S(1)}, u32[]{:S(2)}, u32[]{:S(2)}) collective-permute-start(bf16[256,128]{1,0:T(8,128)(2,1)S(1)} %get-tuple-element.485), channel_id=1, source_target_pairs={{0,12},{4,8},{8,4},{12,0},{1,13},{5,9},{9,5},{13,1},{2,14},{6,10},... | collective-permute-start | bytes 196616 | tf_op jit(solution)/shard_map/ppermute | solution.py:430
  494.8 9.8 %collective-permute-start.28 = (bf16[256,128]{1,0:T(8,128)(2,1)S(1)}, bf16[256,128]{1,0:T(8,128)(2,1)S(1)}, u32[]{:S(2)}, u32[]{:S(2)}) collective-permute-start(bf16[256,128]{1,0:T(8,128)(2,1)S(1)} %get-tuple-element.486), channel_id=1, source_target_pairs={{0,8},{4,12},{8,0},{12,4},{1,9},{5,13},{9,1},{13,5},{2,10},{6,14},... | collective-permute-start | bytes 196616 | tf_op jit(solution)/shard_map/ppermute | solution.py:430
  494.8 9.8 %collective-permute-start.27 = (bf16[256,128]{1,0:T(8,128)(2,1)S(1)}, bf16[256,128]{1,0:T(8,128)(2,1)S(1)}, u32[]{:S(2)}, u32[]{:S(2)}) collective-permute-start(bf16[256,128]{1,0:T(8,128)(2,1)S(1)} %get-tuple-element.487), channel_id=1, source_target_pairs={{0,4},{4,0},{8,12},{12,8},{1,5},{5,1},{9,13},{13,9},{2,6},{6,2},{1... | collective-permute-start | bytes 196616 | tf_op jit(solution)/shard_map/ppermute | solution.py:430
  504.7 56.6 %all-to-all-start.8 = ((bf16[4,512,1024]{2,1,0:T(8,128)(2,1)}), bf16[4,512,1024]{2,1,0:T(8,128)(2,1)}, u32[]{:S(2)}, u32[]{:S(2)}) async-start(bf16[4,512,1024]{2,1,0:T(8,128)(2,1)} %add_convert_fusion), calls=%async_computation.10 | async-start | bytes 8388608 | tf_op jit(solution)/shard_map/all_to_all | solution.py:416
  545.0 8.9 %collective-permute-start.30 = (bf16[4,256,1024]{2,1,0:T(8,128)(2,1)}, bf16[4,256,1024]{2,1,0:T(8,128)(2,1)S(1)}, u32[]{:S(2)}, u32[]{:S(2)}) collective-permute-start(bf16[4,256,1024]{2,1,0:T(8,128)(2,1)} %get-tuple-element.334), channel_id=1, source_target_pairs={{0,16},{16,0},{1,17},{17,1},{2,18},{18,2},{3,19},{19,3},{4,20},{20... | collective-permute-start | bytes 6291464 | tf_op jit(solution)/shard_map/ppermute | solution.py:493
  545.0 38.2 %collective-permute-start.34 = (bf16[2048,128]{1,0:T(8,128)(2,1)}, bf16[2048,128]{1,0:T(8,128)(2,1)}, u32[]{:S(2)}, u32[]{:S(2)}) collective-permute-start(bf16[2048,128]{1,0:T(8,128)(2,1)} %get-tuple-element.342), channel_id=1, source_target_pairs={{0,16},{16,0},{1,17},{17,1},{2,18},{18,2},{3,19},{19,3},{4,20},{20... | collective-permute-start | bytes 1572872 | tf_op jit(solution)/shard_map/ppermute | solution.py:493
  548.8 20.9 %collective-permute-start.32 = (bf16[1536,128]{1,0:T(8,128)(2,1)S(1)}, bf16[1536,128]{1,0:T(8,128)(2,1)S(1)}, u32[]{:S(2)}, u32[]{:S(2)}) collective-permute-start(bf16[1536,128]{1,0:T(8,128)(2,1)S(1)} %get-tuple-element.433), channel_id=1, source_target_pairs={{0,8},{4,12},{8,0},{12,4},{1,9},{5,13},{9,1},{13,5},{2,10},{6,14},... | collective-permute-start | bytes 1179656 | tf_op jit(solution)/shard_map/ppermute | solution.py:430
  551.9 18.0 %collective-permute-start.31 = (bf16[1536,128]{1,0:T(8,128)(2,1)S(1)}, bf16[1536,128]{1,0:T(8,128)(2,1)S(1)}, u32[]{:S(2)}, u32[]{:S(2)}) collective-permute-start(bf16[1536,128]{1,0:T(8,128)(2,1)S(1)} %get-tuple-element.434), channel_id=1, source_target_pairs={{0,4},{4,0},{8,12},{12,8},{1,5},{5,1},{9,13},{13,9},{2,6},{6,2},{1... | collective-permute-start | bytes 1179656 | tf_op jit(solution)/shard_map/ppermute | solution.py:430
  570.6 29.5 %all-to-all-start.9 = ((bf16[4,256,1024]{2,1,0:T(8,128)(2,1)}), bf16[4,256,1024]{2,1,0:T(8,128)(2,1)S(1)}, u32[]{:S(2)}, u32[]{:S(2)}) async-start(bf16[4,256,1024]{2,1,0:T(8,128)(2,1)} %add_convert_fusion.1), calls=%async_computation.11 | async-start | bytes 4194304 | tf_op jit(solution)/shard_map/all_to_all | solution.py:416
  583.0 6.6 collective-permute-start.48
  586.7 13.4 %collective-permute-start.33 = (bf16[1536,128]{1,0:T(8,128)(2,1)S(1)}, bf16[1536,128]{1,0:T(8,128)(2,1)S(1)}, u32[]{:S(2)}, u32[]{:S(2)}) collective-permute-start(bf16[1536,128]{1,0:T(8,128)(2,1)S(1)} %copy-done.55), channel_id=1, source_target_pairs={{0,12},{4,8},{8,4},{12,0},{1,13},{5,9},{9,5},{13,1},{2,14},{6,10},... | collective-permute-start | bytes 1179656 | tf_op jit(solution)/shard_map/ppermute | solution.py:430
  609.5 12.1 %collective-permute-start.35 = (bf16[4,256,128]{2,1,0:T(8,128)(2,1)}, bf16[4,256,128]{2,1,0:T(8,128)(2,1)}, u32[]{:S(2)}, u32[]{:S(2)}) collective-permute-start(bf16[4,256,128]{2,1,0:T(8,128)(2,1)} %get-tuple-element.478), channel_id=1, source_target_pairs={{0,16},{16,0},{1,17},{17,1},{2,18},{18,2},{3,19},{19,3},{4,20},{20... | collective-permute-start | bytes 786440 | tf_op jit(solution)/shard_map/ppermute | solution.py:493
  610.4 20.8 %collective-permute-start.38 = (bf16[512,256]{1,0:T(8,128)(2,1)}, bf16[512,256]{1,0:T(8,128)(2,1)}, u32[]{:S(2)}, u32[]{:S(2)}) collective-permute-start(bf16[512,256]{1,0:T(8,128)(2,1)} %get-tuple-element.452), channel_id=1, source_target_pairs={{0,12},{4,8},{8,4},{12,0},{1,13},{5,9},{9,5},{13,1},{2,14},{6,10},... | collective-permute-start | bytes 786440 | tf_op jit(solution)/shard_map/ppermute | solution.py:430
  613.4 24.8 %collective-permute-start.37 = (bf16[512,256]{1,0:T(8,128)(2,1)}, bf16[512,256]{1,0:T(8,128)(2,1)}, u32[]{:S(2)}, u32[]{:S(2)}) collective-permute-start(bf16[512,256]{1,0:T(8,128)(2,1)} %get-tuple-element.453), channel_id=1, source_target_pairs={{0,8},{4,12},{8,0},{12,4},{1,9},{5,13},{9,1},{13,5},{2,10},{6,14},... | collective-permute-start | bytes 786440 | tf_op jit(solution)/shard_map/ppermute | solution.py:430
  619.9 18.2 %collective-permute-start.36 = (bf16[512,256]{1,0:T(8,128)(2,1)}, bf16[512,256]{1,0:T(8,128)(2,1)}, u32[]{:S(2)}, u32[]{:S(2)}) collective-permute-start(bf16[512,256]{1,0:T(8,128)(2,1)} %get-tuple-element.454), channel_id=1, source_target_pairs={{0,4},{4,0},{8,12},{12,8},{1,5},{5,1},{9,13},{13,9},{2,6},{6,2},{1... | collective-permute-start | bytes 786440 | tf_op jit(solution)/shard_map/ppermute | solution.py:430
  624.1 23.5 %all-to-all-start.10 = ((bf16[4,768,256]{2,1,0:T(8,128)(2,1)}), bf16[4,768,256]{2,1,0:T(8,128)(2,1)S(1)}, u32[]{:S(2)}, u32[]{:S(2)}) async-start(bf16[4,768,256]{2,1,0:T(8,128)(2,1)} %pad_maximum_fusion), calls=%async_computation.12 | async-start | bytes 3145728 | tf_op jit(solution)/shard_map/all_to_all | solution.py:416
  638.9 12.5 %collective-permute-start.41 = (bf16[256,256]{1,0:T(8,128)(2,1)}, bf16[256,256]{1,0:T(8,128)(2,1)S(1)}, u32[]{:S(2)}, u32[]{:S(2)}) collective-permute-start(bf16[256,256]{1,0:T(8,128)(2,1)} %get-tuple-element.474), channel_id=1, source_target_pairs={{0,12},{4,8},{8,4},{12,0},{1,13},{5,9},{9,5},{13,1},{2,14},{6,10},... | collective-permute-start | bytes 393224 | tf_op jit(solution)/shard_map/ppermute | solution.py:430
  641.8 10.7 %collective-permute-start.40 = (bf16[256,256]{1,0:T(8,128)(2,1)}, bf16[256,256]{1,0:T(8,128)(2,1)S(1)}, u32[]{:S(2)}, u32[]{:S(2)}) collective-permute-start(bf16[256,256]{1,0:T(8,128)(2,1)} %get-tuple-element.475), channel_id=1, source_target_pairs={{0,8},{4,12},{8,0},{12,4},{1,9},{5,13},{9,1},{13,5},{2,10},{6,14},... | collective-permute-start | bytes 393224 | tf_op jit(solution)/shard_map/ppermute | solution.py:430
  641.8 10.7 %collective-permute-start.39 = (bf16[256,256]{1,0:T(8,128)(2,1)}, bf16[256,256]{1,0:T(8,128)(2,1)S(1)}, u32[]{:S(2)}, u32[]{:S(2)}) collective-permute-start(bf16[256,256]{1,0:T(8,128)(2,1)} %get-tuple-element.476), channel_id=1, source_target_pairs={{0,4},{4,0},{8,12},{12,8},{1,5},{5,1},{9,13},{13,9},{2,6},{6,2},{1... | collective-permute-start | bytes 393224 | tf_op jit(solution)/shard_map/ppermute | solution.py:430
  647.6 16.9 %all-to-all-start.11 = ((bf16[8,432,128]{2,1,0:T(8,128)(2,1)}), bf16[8,432,128]{2,1,0:T(8,128)(2,1)S(1)}, u32[]{:S(2)}, u32[]{:S(2)}) async-start(bf16[8,432,128]{2,1,0:T(8,128)(2,1)} %pad_maximum_fusion.4), calls=%async_computation.13 | async-start | bytes 1769472 | tf_op jit(solution)/shard_map/all_to_all | solution.py:416
  653.4 14.4 %collective-permute-start.49 = (bf16[2,256,256]{2,1,0:T(8,128)(2,1)}, bf16[2,256,256]{2,1,0:T(8,128)(2,1)}, u32[]{:S(2)}, u32[]{:S(2)}) collective-permute-start(bf16[2,256,256]{2,1,0:T(8,128)(2,1)} %broadcast_select_fusion.6), channel_id=1, source_target_pairs={{0,16},{16,0},{1,17},{17,1},{2,18},{18,2},{3,19},{19,3},{4,20},{20... | collective-permute-start | bytes 786440 | tf_op jit(solution)/shard_map/ppermute | solution.py:493
  654.3 14.2 %collective-permute-start.44 = (bf16[768,256]{1,0:T(8,128)(2,1)}, bf16[768,256]{1,0:T(8,128)(2,1)}, u32[]{:S(2)}, u32[]{:S(2)}) collective-permute-start(bf16[768,256]{1,0:T(8,128)(2,1)} %get-tuple-element.429), channel_id=1, source_target_pairs={{0,12},{4,8},{8,4},{12,0},{1,13},{5,9},{9,5},{13,1},{2,14},{6,10},... | collective-permute-start | bytes 1179656 | tf_op jit(solution)/shard_map/ppermute | solution.py:430
  656.6 44.1 %collective-permute-start.43 = (bf16[768,256]{1,0:T(8,128)(2,1)}, bf16[768,256]{1,0:T(8,128)(2,1)}, u32[]{:S(2)}, u32[]{:S(2)}) collective-permute-start(bf16[768,256]{1,0:T(8,128)(2,1)} %get-tuple-element.430), channel_id=1, source_target_pairs={{0,8},{4,12},{8,0},{12,4},{1,9},{5,13},{9,1},{13,5},{2,10},{6,14},... | collective-permute-start | bytes 1179656 | tf_op jit(solution)/shard_map/ppermute | solution.py:430
  656.6 44.1 %collective-permute-start.42 = (bf16[768,256]{1,0:T(8,128)(2,1)S(1)}, bf16[768,256]{1,0:T(8,128)(2,1)}, u32[]{:S(2)}, u32[]{:S(2)}) collective-permute-start(bf16[768,256]{1,0:T(8,128)(2,1)S(1)} %get-tuple-element.431), channel_id=1, source_target_pairs={{0,4},{4,0},{8,12},{12,8},{1,5},{5,1},{9,13},{13,9},{2,6},{6,2},{1... | collective-permute-start | bytes 1179656 | tf_op jit(solution)/shard_map/ppermute | solution.py:430
  664.8 35.9 %collective-permute-start.47 = (bf16[780,128]{1,0:T(8,128)(2,1)S(1)}, bf16[780,128]{1,0:T(8,128)(2,1)S(1)}, u32[]{:S(2)}, u32[]{:S(2)}) collective-permute-start(bf16[780,128]{1,0:T(8,128)(2,1)S(1)} %get-tuple-element.459), channel_id=1, source_target_pairs={{0,12},{4,8},{8,4},{12,0},{1,13},{5,9},{9,5},{13,1},{2,14},{6,10},... | collective-permute-start | bytes 599048 | tf_op jit(solution)/shard_map/ppermute | solution.py:430
  667.8 40.9 %collective-permute-start.46 = (bf16[780,128]{1,0:T(8,128)(2,1)S(1)}, bf16[780,128]{1,0:T(8,128)(2,1)S(1)}, u32[]{:S(2)}, u32[]{:S(2)}) collective-permute-start(bf16[780,128]{1,0:T(8,128)(2,1)S(1)} %get-tuple-element.460), channel_id=1, source_target_pairs={{0,8},{4,12},{8,0},{12,4},{1,9},{5,13},{9,1},{13,5},{2,10},{6,14},... | collective-permute-start | bytes 599048 | tf_op jit(solution)/shard_map/ppermute | solution.py:430
  668.5 40.2 %collective-permute-start.45 = (bf16[780,128]{1,0:T(8,128)(2,1)S(1)}, bf16[780,128]{1,0:T(8,128)(2,1)S(1)}, u32[]{:S(2)}, u32[]{:S(2)}) collective-permute-start(bf16[780,128]{1,0:T(8,128)(2,1)S(1)} %get-tuple-element.461), channel_id=1, source_target_pairs={{0,4},{4,0},{8,12},{12,8},{1,5},{5,1},{9,13},{13,9},{2,6},{6,2},{1... | collective-permute-start | bytes 599048 | tf_op jit(solution)/shard_map/ppermute | solution.py:430
  (80 other events, 748.0 us)
Sparse Core Ops, SparseCore 0:
  88.5 191.4 all-gather.2
  330.2 59.6 reduce-scatter.2
  393.7 151.1 reduce-scatter.4
